TPU v7x, 32 devices: a whole 2x2x4 slice. The times are simulated.
32 devices in a mesh: row: 4 (over y, x), col: 8 (over z, core).
Axes of the slice: x: 2, y: 2, z: 4, core: 2. Of those that a mesh axis runs over, the one named last changes fastest.
Arguments:
- image: bfloat16 [128, 256, 180], P('row', 'col'), may hold values from -6 to 6
- norm1_gain: float32 [180], replicated, may hold values from 0.5 to 1.5
- norm2_gain: float32 [180], replicated, may hold values from 0.5 to 1.5
- qkv_weight: bfloat16 [180, 540], replicated, may hold values from -2 to 2
- proj_weight: bfloat16 [180, 180], replicated, may hold values from -0.4375 to 0.4375
- rel_table: float32 [961, 6], replicated, may hold values from -4 to 4
- conv_weight: bfloat16 [3, 3, 180, 180], replicated, may hold values from -0.15625 to 0.15625
- fc1_weight: bfloat16 [180, 360], replicated, may hold values from -0.4375 to 0.4375
- fc2_weight: bfloat16 [360, 180], replicated, may hold values from -0.3125 to 0.3125
Outputs:
- mixed_out: bfloat16 [128, 256, 180], P('row', 'col')
All inputs are finite; a program needn't handle non-finite values.
Results may differ from a plain program's by a relative error of at most 0.012.
The roundings to bfloat16 on the way count: a program that leaves them out, or rounds other values in their place, can miss the bound.
Values may be sent and summed in bfloat16 or wider, within the bound.
No kernel may reach another device: no remote copies, remote signals or barrier semaphores. Data moves between devices by JAX's collectives and lax.ppermute only.
A program may use at most 128 MiB of HBM per device.

v0:
```python
import jax
import jax.numpy as jnp
from jax import lax
from jax.sharding import PartitionSpec as P

HEADS = 6
WIN = 16
SHIFT = 8


def from_behind(block, axis, distance):
    devices = range(lax.axis_size(axis))
    route = [((i - distance) % len(devices), i) for i in devices]
    return lax.ppermute(block, axis, route)


def padded_2(cells, sides, width):
    for axis, dim in sides:
        count = lax.axis_size(axis)
        ends = count - 1
        head = lax.slice_in_dim(cells, 0, width, axis=dim)
        tail = lax.slice_in_dim(cells, cells.shape[dim] - width, cells.shape[dim], axis=dim)
        cells = jnp.concatenate(
            [
                lax.ppermute(tail, axis, [(i, (i + 1) % count) for i in range(ends)]),
                cells,
                lax.ppermute(head, axis, [((i + 1) % count, i) for i in range(ends)]),
            ],
            axis=dim,
        )
    return cells


def layer_norm(values, norm_gain):
    centre = jnp.mean(values, axis=-1, keepdims=True)
    spread = jnp.mean((values - centre) ** 2, axis=-1, keepdims=True)
    return (values - centre) * lax.rsqrt(spread + 1e-05) * norm_gain


def to_windows(field):
    rows_n, cols_n = (field.shape[0], field.shape[1])
    shaped = field.reshape(rows_n // WIN, WIN, cols_n // WIN, WIN, field.shape[2])
    return shaped.transpose(0, 2, 1, 3, 4).reshape(-1, WIN * WIN, field.shape[2])


def from_windows(windowed, rows_n, cols_n):
    shaped = windowed.reshape(rows_n // WIN, cols_n // WIN, WIN, WIN, windowed.shape[2])
    return shaped.transpose(0, 2, 1, 3, 4).reshape(rows_n, cols_n, windowed.shape[2])


def region(position, extent):
    return (position >= extent - WIN).astype(jnp.int32) + (position >= extent - WIN // 2).astype(
        jnp.int32
    )


def position_bias(rel_table):
    span = 2 * WIN - 1
    heads_n = rel_table.shape[1]
    table_grid = rel_table.reshape(span, span, heads_n)
    inside = jnp.arange(WIN, dtype=jnp.int32)
    offset_ids = jnp.arange(span, dtype=jnp.int32)
    one_hot = (
        inside[:, None, None] - inside[None, :, None] + WIN - 1 == offset_ids[None, None, :]
    ).astype(jnp.float32)
    by_rows = jnp.einsum("abk,kch->abch", one_hot, table_grid, precision=lax.Precision.HIGHEST)
    full_bias = jnp.einsum("abch,dec->hadbe", by_rows, one_hot, precision=lax.Precision.HIGHEST)
    return lax.optimization_barrier(full_bias.reshape(heads_n, WIN * WIN, WIN * WIN))


def attend(windowed, win_labels, qkv_weight, proj_weight, pos_bias):
    count_win, pixels, channels = windowed.shape
    head_dim = channels // HEADS
    qkv_rows = jnp.dot(
        windowed.reshape(-1, channels), qkv_weight, preferred_element_type=jnp.float32
    )
    qkv_rows = qkv_rows.astype(jnp.bfloat16).reshape(count_win, pixels, 3, HEADS, head_dim)
    queries = qkv_rows[:, :, 0]
    keys_all = qkv_rows[:, :, 1]
    values_all = qkv_rows[:, :, 2]
    scores = jnp.einsum("wphd,wqhd->whpq", queries, keys_all, preferred_element_type=jnp.float32)
    scores = scores * head_dim ** (-0.5) + pos_bias[None]
    same_region = win_labels[:, :, None] == win_labels[:, None, :]
    scores = jnp.where(same_region[:, None], scores, -1000000000.0)
    scores = scores - jnp.max(scores, axis=-1, keepdims=True)
    exp_scores = jnp.exp(scores)
    soft_weights = (exp_scores / jnp.sum(exp_scores, axis=-1, keepdims=True)).astype(jnp.bfloat16)
    heads_out = jnp.einsum(
        "whpq,wqhd->wphd", soft_weights, values_all, preferred_element_type=jnp.float32
    ).astype(jnp.bfloat16)
    heads_out = heads_out.reshape(count_win * pixels, channels)
    projected = jnp.dot(heads_out, proj_weight, preferred_element_type=jnp.float32).astype(
        jnp.bfloat16
    )
    return projected.reshape(count_win, pixels, channels)


def on_device(
    image,
    norm1_gain,
    norm2_gain,
    qkv_weight,
    proj_weight,
    rel_table,
    conv_weight,
    fc1_weight,
    fc2_weight,
):
    tile_rows, tile_cols, channels = image.shape
    rows_total = tile_rows * lax.axis_size("row")
    cols_total = tile_cols * lax.axis_size("col")
    state = image.astype(jnp.float32)
    normed1 = layer_norm(state, norm1_gain).astype(jnp.bfloat16)
    lower_band = from_behind(image[:SHIFT], "row", -1)
    tall_tile = jnp.concatenate([image[SHIFT:], lower_band], axis=0)
    outgoing = tall_tile[:, :SHIFT]
    received = from_behind(outgoing, "col", -1)
    moved = jnp.concatenate([tall_tile[:, SHIFT:], received], axis=1)
    shifted = layer_norm(moved.astype(jnp.float32), norm1_gain).astype(jnp.bfloat16)
    row_pos = lax.axis_index("row") * tile_rows + jnp.arange(tile_rows, dtype=jnp.int32)
    col_pos = lax.axis_index("col") * tile_cols + jnp.arange(tile_cols, dtype=jnp.int32)
    labels = region(row_pos, rows_total)[:, None] * 3 + region(col_pos, cols_total)[None, :]
    windowed = to_windows(shifted)
    win_labels = to_windows(labels[:, :, None])[:, :, 0]
    count_win = windowed.shape[0]
    pos_bias = position_bias(rel_table)
    grouped = windowed.reshape(count_win // 4, 4, WIN * WIN, channels)
    grouped_labels = win_labels.reshape(count_win // 4, 4, WIN * WIN)

    def one_group(group_args):
        return attend(group_args[0], group_args[1], qkv_weight, proj_weight, pos_bias)

    attended = lax.map(one_group, (grouped, grouped_labels)).reshape(count_win, WIN * WIN, channels)
    attended = from_windows(attended, tile_rows, tile_cols)
    upper_band = from_behind(attended[tile_rows - SHIFT :], "row", 1)
    tall_back = jnp.concatenate([upper_band, attended[: tile_rows - SHIFT]], axis=0)
    left_band = from_behind(tall_back[:, tile_cols - SHIFT :], "col", 1)
    returned = jnp.concatenate([left_band, tall_back[:, : tile_cols - SHIFT]], axis=1)
    padded = padded_2(normed1, (("row", 0), ("col", 1)), 1)
    conv_sum = jnp.zeros((tile_rows * tile_cols, channels), jnp.float32)
    for row_tap in range(3):
        for col_tap in range(3):
            piece = padded[row_tap : row_tap + tile_rows, col_tap : col_tap + tile_cols].reshape(
                -1, channels
            )
            conv_sum = conv_sum + jnp.dot(
                piece, conv_weight[row_tap, col_tap], preferred_element_type=jnp.float32
            )
    state1 = state + returned.astype(jnp.float32) + conv_sum.reshape(tile_rows, tile_cols, channels)
    normed2 = layer_norm(state1, norm2_gain).astype(jnp.bfloat16).reshape(-1, channels)
    hidden = jax.nn.gelu(
        jnp.dot(normed2, fc1_weight, preferred_element_type=jnp.float32), approximate=False
    ).astype(jnp.bfloat16)
    mlp_out = jnp.dot(hidden, fc2_weight, preferred_element_type=jnp.float32).reshape(state1.shape)
    return (state1 + mlp_out).astype(jnp.bfloat16)


def solution(mesh):
    placed = (P("row", "col", None), P(), P(), P(), P(), P(), P(), P(), P())
    return jax.shard_map(
        on_device, mesh=mesh, in_specs=placed, out_specs=P("row", "col", None), check_vma=False
    )
```

profile of v0, /device:TPU:0, one launch (start us, length us, event | category | flops | bytes accessed | tf_op | source)
XLA Modules:
  0.0 95.2 jit_solution(12942594642970960825)
XLA Ops:
  0.0 1.3 %convert_reduce_fusion = f32[32,32]{1,0:T(8,128)S(1)} fusion(bf16[32,32,180]{2,1,0:T(8,128)(2,1)} %param.9), kind=kLoop, calls=%fused_computation.14 | loop fusion | flops 367616 | bytes 372736 | tf_op jit(solution)/shard_map/reduce_sum | solution.py:35
  1.3 1.4 %fusion.25 = f32[32,32]{1,0:T(8,128)S(1)} fusion(bf16[32,32,180]{2,1,0:T(8,128)(2,1)} %param.9, f32[32,32]{1,0:T(8,128)S(1)} %broadcast_multiply_fusion.1), kind=kLoop, calls=%fused_computation.50 | loop fusion | flops 736256 | bytes 376832 | tf_op jit(solution)/shard_map/reduce_sum | solution.py:36
  4.4 1.3 %collective-permute-start.5 = (bf16[1,32,180]{2,1,0:T(8,128)(2,1)}, bf16[1,32,180]{2,1,0:T(8,128)(2,1)S(1)}, u32[]{:S(2)}, u32[]{:S(2)}) collective-permute-start(bf16[1,32,180]{2,1,0:T(8,128)(2,1)} %get-tuple-element.44), channel_id=1, source_target_pairs={{8,0},{16,8},{24,16},{9,1},{17,9},{25,17},{10,2},{18,10},{26,18},{... | collective-permute-start | bytes 34568 | tf_op jit(solution)/shard_map/ppermute | solution.py:27
  5.7 5.5 %collective-permute-start.4 = (bf16[1,32,180]{2,1,0:T(8,128)(2,1)}, bf16[1,32,180]{2,1,0:T(8,128)(2,1)S(1)}, u32[]{:S(2)}, u32[]{:S(2)}) collective-permute-start(bf16[1,32,180]{2,1,0:T(8,128)(2,1)} %get-tuple-element.43), channel_id=1, source_target_pairs={{0,8},{8,16},{16,24},{1,9},{9,17},{17,25},{2,10},{10,18},{18,26},{... | collective-permute-start | bytes 34568 | tf_op jit(solution)/shard_map/ppermute | solution.py:25
  12.8 8.0 %convolution_bitcast_fusion = f32[6,16,16,16,16]{3,4,0,1,2:T(8,128)} fusion(f32[16,16,31,6,1]{2,1,3,0,4:T(8,128)S(1)} %convolution_bitcast_fusion.1, s32[16,16]{1,0:T(8,128)S(1)} %subtract_add_fusion), kind=kOutput, calls=%fused_computation.4 | convolution fusion | flops 146284288 | bytes 1764352 | tf_op jit(solution)/shard_map/abch,dec->hadbe/dot_general | solution.py:67
  21.9 12.7 %copy.36 = f32[6,16,16,16,16]{4,3,2,1,0:T(8,128)} copy(f32[6,16,16,16,16]{3,4,0,1,2:T(8,128)} %convolution_bitcast_fusion) | data formatting | bytes 3145728 | tf_op jit(solution)/shard_map/abch,dec->hadbe/transpose | solution.py:67
  34.6 8.7 %reshape.183 = f32[6,256,256]{2,1,0:T(8,128)S(1)} reshape(f32[6,16,16,16,16]{4,3,2,1,0:T(8,128)} %copy.36) | data formatting | bytes 3145728 | tf_op jit(solution)/shard_map/reshape | solution.py:68
  43.4 1.6 %copy.37 = f32[6,256,256]{1,2,0:T(8,128)} copy(f32[6,256,256]{2,1,0:T(8,128)S(1)} %reshape.183) | data formatting | bytes 3145728 | tf_op jit(solution)/shard_map/optimization_barrier | solution.py:68
  45.1 1.4 %collective-permute-start.6 = (bf16[34,1,180]{2,1,0:T(2,128)(2,1)S(1)}, bf16[34,1,180]{2,1,0:T(2,128)(2,1)S(1)}, u32[]{:S(2)}, u32[]{:S(2)}) collective-permute-start(bf16[34,1,180]{2,1,0:T(2,128)(2,1)S(1)} %get-tuple-element.39), channel_id=1, source_target_pairs={{0,1},{1,2},{2,3},{3,4},{4,5},{5,6},{6,7},{8,9},{9,10},{10,11},{11... | collective-permute-start | bytes 36728 | tf_op jit(solution)/shard_map/ppermute | solution.py:25
  46.5 1.3 %collective-permute-start.7 = (bf16[34,1,180]{2,1,0:T(2,128)(2,1)S(1)}, bf16[34,1,180]{2,1,0:T(2,128)(2,1)S(1)}, u32[]{:S(2)}, u32[]{:S(2)}) collective-permute-start(bf16[34,1,180]{2,1,0:T(2,128)(2,1)S(1)} %get-tuple-element.40), channel_id=1, source_target_pairs={{1,0},{2,1},{3,2},{4,3},{5,4},{6,5},{7,6},{9,8},{10,9},{11,10},{12... | collective-permute-start | bytes 36728 | tf_op jit(solution)/shard_map/ppermute | solution.py:27
  47.8 1.0 %pad_maximum_fusion.1 = (bf16[32,32,180]{2,1,0:T(8,128)(2,1)}, bf16[32,32,180]{2,1,0:T(8,128)(2,1)S(1)}) fusion(bf16[1,32,180]{2,1,0:T(8,128)(2,1)S(1)} %collective-permute-done.5, bf16[32,32,180]{2,1,0:T(8,128)(2,1)S(1)} %fusion.27, bf16[1,32,180]{2,1,0:T(8,128)(2,1)S(1)} %collective-permute-done.4), kind=kLoop, calls=%fused_computation.94 | loop fusion | flops 368640 | bytes 1128960 | tf_op jit(solution)/shard_map/concatenate | solution.py:23
  49.2 2.2 %collective-permute-done.7 = bf16[34,1,180]{2,1,0:T(2,128)(2,1)S(1)} collective-permute-done((bf16[34,1,180]{2,1,0:T(2,128)(2,1)S(1)}, bf16[34,1,180]{2,1,0:T(2,128)(2,1)S(1)}, u32[]{:S(2)}, u32[]{:S(2)}) %collective-permute-start.7) | collective-permute-done | bytes 12272 | tf_op jit(solution)/shard_map/ppermute | solution.py:27
  51.8 1.2 %fusion.130 = (bf16[32,32,180]{2,1,0:T(8,128)(2,1)S(1)}, bf16[32,32,180]{2,1,0:T(8,128)(2,1)S(1)}, bf16[32,32,180]{2,1,0:T(8,128)(2,1)S(1)}, bf16[32,32,180]{2,1...) fusion(bf16[34,33,180]{2,1,0:T(8,128)(2,1)S(1)} %get-tuple-element.37, ...), kind=kLoop, calls=%fused_computation.188 | loop fusion | bytes 4423680 | tf_op jit(solution)/shard_map/slice | solution.py:143
  54.7 1.3 %convolution_add_fusion.1 = f32[1024,180]{0,1:T(8,128)} fusion(f32[1024,180]{0,1:T(8,128)S(1)} %convolution_add_fusion.2, bf16[1024,180]{1,0:T(8,128)(2,1)S(1)} %bitcast.132, bf16[3,3,180,180]{3,2,1,0:T(8,128)(2,1)S(1)} %copy-done.5), kind=kOutput, calls=%fused_computation.38 | convolution fusion | flops 66539520 | bytes 2109440 | tf_op jit(solution)/shard_map/dot_general | solution.py:146
  56.0 3.0 %collective-permute-start.1 = (bf16[32,8,180]{2,1,0:T(8,128)(2,1)S(1)}, bf16[32,8,180]{2,1,0:T(8,128)(2,1)S(1)}, u32[]{:S(2)}, u32[]{:S(2)}) collective-permute-start(bf16[32,8,180]{2,1,0:T(8,128)(2,1)S(1)} %pad_maximum_fusion.5), channel_id=1, source_target_pairs={{1,0},{2,1},{3,2},{4,3},{5,4},{6,5},{7,6},{0,7},{9,8},{10,9},{11,1... | collective-permute-start | bytes 276488 | tf_op jit(solution)/shard_map/ppermute | solution.py:14
  59.0 2.4 %collective-permute-done.1 = bf16[32,8,180]{2,1,0:T(8,128)(2,1)S(1)} collective-permute-done((bf16[32,8,180]{2,1,0:T(8,128)(2,1)S(1)}, bf16[32,8,180]{2,1,0:T(8,128)(2,1)S(1)}, u32[]{:S(2)}, u32[]{:S(2)}) %collective-permute-start.1) | collective-permute-done | bytes 92192 | tf_op jit(solution)/shard_map/ppermute | solution.py:14
  64.8 6.5 %fusion.133 = (f32[4,6,256]{2,1,0:T(8,128)S(1)}, f32[4,6,256,256]{2,3,1,0:T(8,128)}) fusion(f32[6,256,256]{1,2,0:T(8,128)} %copy.37, pred[4,256,256]{1,2,0:T(8,128)(4,1)S(1)} %copy-done.6, bf16[4,256,1,6,30]{1,0,4,3,2:T(4,128)(2,1)S(1)} %get-tuple-element.20, bf16[4,256,1,6,30]{1,0,4,3,2:T(4,128)(2,1)S(1)} %get-tuple-element.28), kind=kOutput, calls=%fused_computation.191 | convolution fusion | flops 102236416 | bytes 8888320 | tf_op jit(solution)/shard_map/while/body/eval_jaxpr/sub | solution.py:85
  71.4 3.4 %fusion.24 = bf16[4,256,6,30]{1,3,2,0:T(8,128)(2,1)S(1)} fusion(f32[4,6,256,256]{2,3,1,0:T(8,128)} %get-tuple-element.46, f32[4,6,256]{2,1,0:T(8,128)S(1)} %get-tuple-element.45, bf16[4,256,1,6,30]{1,0,4,3,2:T(4,128)(2,1)S(1)} %get-tuple-element.19), kind=kOutput, calls=%fused_computation.49 | convolution fusion | flops 97701888 | bytes 7053312 | tf_op jit(solution)/shard_map/while/body/eval_jaxpr/whpq,wqhd->wphd/dot_general | solution.py:88
  76.3 2.1 %collective-permute-start.2 = (bf16[8,32,180]{2,1,0:T(8,128)(2,1)S(1)}, bf16[8,32,180]{2,1,0:T(8,128)(2,1)S(1)}, u32[]{:S(2)}, u32[]{:S(2)}) collective-permute-start(bf16[8,32,180]{2,1,0:T(8,128)(2,1)S(1)} %slice.144), channel_id=1, source_target_pairs={{24,0},{0,8},{8,16},{16,24},{25,1},{1,9},{9,17},{17,25},{26,2},{2,... | collective-permute-start | bytes 276488 | tf_op jit(solution)/shard_map/ppermute | solution.py:14
  78.4 1.2 %fusion.70 = f32[1024,180]{0,1:T(8,128)S(1)} fusion(bf16[1024,180]{1,0:T(8,128)(2,1)S(1)} %bitcast.131, bf16[3,3,180,180]{3,2,1,0:T(8,128)(2,1)} %param.15), kind=kOutput, calls=%fused_computation.113 | convolution fusion | flops 66355200 | bytes 1200128 | tf_op jit(solution)/shard_map/dot_general | solution.py:146
  79.7 3.1 %collective-permute-done.2 = bf16[8,32,180]{2,1,0:T(8,128)(2,1)S(1)} collective-permute-done((bf16[8,32,180]{2,1,0:T(8,128)(2,1)S(1)}, bf16[8,32,180]{2,1,0:T(8,128)(2,1)S(1)}, u32[]{:S(2)}, u32[]{:S(2)}) %collective-permute-start.2) | collective-permute-done | bytes 92192 | tf_op jit(solution)/shard_map/ppermute | solution.py:14
  83.7 1.2 %fusion.19 = f32[1024,180]{0,1:T(8,128)S(1)} fusion(f32[1024,180]{0,1:T(8,128)S(1)} %fusion.70, f32[1024,180]{0,1:T(8,128)S(1)} %copy-done.2, bf16[1024,180]{1,0:T(8,128)(2,1)S(1)} %bitcast.130, bf16[3,3,180,180]{3,2,1,0:T(8,128)(2,1)} %param.15), kind=kOutput, calls=%fused_computation.37 | convolution fusion | flops 66723840 | bytes 2674688 | tf_op jit(solution)/shard_map/dot_general | solution.py:146
  85.3 4.0 %collective-permute-done.3 = bf16[32,8,180]{2,1,0:T(8,128)(2,1)S(1)} collective-permute-done((bf16[32,8,180]{2,1,0:T(8,128)(2,1)S(1)}, bf16[32,8,180]{2,1,0:T(8,128)(2,1)S(1)}, u32[]{:S(2)}, u32[]{:S(2)}) %collective-permute-start.3) | collective-permute-done | bytes 92192 | tf_op jit(solution)/shard_map/ppermute | solution.py:14
  90.6 3.7 %fusion.20 = f32[1024,180]{1,0:T(8,128)S(1)} fusion(bf16[360,180]{0,1:T(8,128)(2,1)S(1)} %copy-done.11, bf16[1024,180]{1,0:T(8,128)(2,1)S(1)} %bitcast.143, bf16[180,360]{1,0:T(8,128)(2,1)S(1)} %copy-done.12), kind=kOutput, calls=%fused_computation.44 | convolution fusion | flops 289382400 | bytes 1365120 | tf_op jit(solution)/shard_map/dot_general | solution.py:154
  (84 shorter events, 15.1 us)
Async XLA Ops:
  0.0 62.8 %copy-start = (bf16[180,540]{1,0:T(8,128)(2,1)S(1)}, bf16[180,540]{1,0:T(8,128)(2,1)}, u32[]{:S(2)}) copy-start(bf16[180,540]{1,0:T(8,128)(2,1)} %param.12) | copy-start | bytes 583204
  0.0 2.8 %copy-start.1 = (bf16[32,32,180]{2,1,0:T(8,128)(2,1)S(1)}, bf16[32,32,180]{2,1,0:T(8,128)(2,1)}, u32[]{:S(2)}) copy-start(bf16[32,32,180]{2,1,0:T(8,128)(2,1)} %param.9) | copy-start | bytes 1105924
  0.0 12.2 %copy-start.8 = (f32[961,6]{0,1:T(8,128)S(1)}, f32[961,6]{0,1:T(8,128)}, u32[]{:S(2)}) copy-start(f32[961,6]{0,1:T(8,128)} %param.14) | copy-start | bytes 69196
  4.4 40.6 %collective-permute-start.5 = (bf16[1,32,180]{2,1,0:T(8,128)(2,1)}, bf16[1,32,180]{2,1,0:T(8,128)(2,1)S(1)}, u32[]{:S(2)}, u32[]{:S(2)}) collective-permute-start(bf16[1,32,180]{2,1,0:T(8,128)(2,1)} %get-tuple-element.44), channel_id=1, source_target_pairs={{8,0},{16,8},{24,16},{9,1},{17,9},{25,17},{10,2},{18,10},{26,18},{... | collective-permute-start | bytes 34568 | tf_op jit(solution)/shard_map/ppermute | solution.py:27
  5.7 39.3 %collective-permute-start.4 = (bf16[1,32,180]{2,1,0:T(8,128)(2,1)}, bf16[1,32,180]{2,1,0:T(8,128)(2,1)S(1)}, u32[]{:S(2)}, u32[]{:S(2)}) collective-permute-start(bf16[1,32,180]{2,1,0:T(8,128)(2,1)} %get-tuple-element.43), channel_id=1, source_target_pairs={{0,8},{8,16},{16,24},{1,9},{9,17},{17,25},{2,10},{10,18},{18,26},{... | collective-permute-start | bytes 34568 | tf_op jit(solution)/shard_map/ppermute | solution.py:25
  11.2 44.7 %collective-permute-start = (bf16[8,32,180]{2,1,0:T(8,128)(2,1)S(1)}, bf16[8,32,180]{2,1,0:T(8,128)(2,1)S(1)}, u32[]{:S(2)}, u32[]{:S(2)}) collective-permute-start(bf16[8,32,180]{2,1,0:T(8,128)(2,1)S(1)} %slice.108), channel_id=1, source_target_pairs={{8,0},{16,8},{24,16},{0,24},{9,1},{17,9},{25,17},{1,25},{10,2},{18... | collective-permute-start | bytes 276488 | tf_op jit(solution)/shard_map/ppermute | solution.py:14
  45.0 3.9 %copy-start.5 = (bf16[3,3,180,180]{3,2,1,0:T(8,128)(2,1)S(1)}, bf16[3,3,180,180]{3,2,1,0:T(8,128)(2,1)}, u32[]{:S(2)}) copy-start(bf16[3,3,180,180]{3,2,1,0:T(8,128)(2,1)} %param.15) | copy-start | bytes 1749604
  45.1 4.1 %collective-permute-start.6 = (bf16[34,1,180]{2,1,0:T(2,128)(2,1)S(1)}, bf16[34,1,180]{2,1,0:T(2,128)(2,1)S(1)}, u32[]{:S(2)}, u32[]{:S(2)}) collective-permute-start(bf16[34,1,180]{2,1,0:T(2,128)(2,1)S(1)} %get-tuple-element.39), channel_id=1, source_target_pairs={{0,1},{1,2},{2,3},{3,4},{4,5},{5,6},{6,7},{8,9},{9,10},{10,11},{11... | collective-permute-start | bytes 36728 | tf_op jit(solution)/shard_map/ppermute | solution.py:25
  46.5 4.9 %collective-permute-start.7 = (bf16[34,1,180]{2,1,0:T(2,128)(2,1)S(1)}, bf16[34,1,180]{2,1,0:T(2,128)(2,1)S(1)}, u32[]{:S(2)}, u32[]{:S(2)}) collective-permute-start(bf16[34,1,180]{2,1,0:T(2,128)(2,1)S(1)} %get-tuple-element.40), channel_id=1, source_target_pairs={{1,0},{2,1},{3,2},{4,3},{5,4},{6,5},{7,6},{9,8},{10,9},{11,10},{12... | collective-permute-start | bytes 36728 | tf_op jit(solution)/shard_map/ppermute | solution.py:27
  56.0 5.5 %collective-permute-start.1 = (bf16[32,8,180]{2,1,0:T(8,128)(2,1)S(1)}, bf16[32,8,180]{2,1,0:T(8,128)(2,1)S(1)}, u32[]{:S(2)}, u32[]{:S(2)}) collective-permute-start(bf16[32,8,180]{2,1,0:T(8,128)(2,1)S(1)} %pad_maximum_fusion.5), channel_id=1, source_target_pairs={{1,0},{2,1},{3,2},{4,3},{5,4},{6,5},{7,6},{0,7},{9,8},{10,9},{11,1... | collective-permute-start | bytes 276488 | tf_op jit(solution)/shard_map/ppermute | solution.py:14
  59.0 3.4 %copy-start.9 = (f32[180]{0:T(256)S(1)}, f32[180]{0:T(256)}, u32[]{:S(2)}) copy-start(f32[180]{0:T(256)} %param.10) | copy-start | bytes 2164
  63.9 1.0 copy-start.6
  74.8 0.9 copy-start.7
  75.7 2.8 %copy-start.4 = (bf16[32,32,180]{2,1,0:T(8,128)(2,1)S(1)}, bf16[32,32,180]{2,1,0:T(8,128)(2,1)}, u32[]{:S(2)}) copy-start(bf16[32,32,180]{2,1,0:T(8,128)(2,1)} %get-tuple-element.48) | copy-start | bytes 1105924
  76.3 7.5 %copy-start.2 = (f32[1024,180]{0,1:T(8,128)S(1)}, f32[1024,180]{0,1:T(8,128)}, u32[]{:S(2)}) copy-start(f32[1024,180]{0,1:T(8,128)} %convolution_add_fusion.1) | copy-start | bytes 2211844
  76.3 7.5 %copy-start.3 = (bf16[32,32,180]{2,1,0:T(8,128)(2,1)S(1)}, bf16[32,32,180]{2,1,0:T(8,128)(2,1)}, u32[]{:S(2)}) copy-start(bf16[32,32,180]{2,1,0:T(8,128)(2,1)} %get-tuple-element.41) | copy-start | bytes 1105924
  76.3 6.5 %collective-permute-start.2 = (bf16[8,32,180]{2,1,0:T(8,128)(2,1)S(1)}, bf16[8,32,180]{2,1,0:T(8,128)(2,1)S(1)}, u32[]{:S(2)}, u32[]{:S(2)}) collective-permute-start(bf16[8,32,180]{2,1,0:T(8,128)(2,1)S(1)} %slice.144), channel_id=1, source_target_pairs={{24,0},{0,8},{8,16},{16,24},{25,1},{1,9},{9,17},{17,25},{26,2},{2,... | collective-permute-start | bytes 276488 | tf_op jit(solution)/shard_map/ppermute | solution.py:14
  82.8 6.5 %collective-permute-start.3 = (bf16[32,8,180]{2,1,0:T(8,128)(2,1)S(1)}, bf16[32,8,180]{2,1,0:T(8,128)(2,1)S(1)}, u32[]{:S(2)}, u32[]{:S(2)}) collective-permute-start(bf16[32,8,180]{2,1,0:T(8,128)(2,1)S(1)} %pad_maximum_fusion.4), channel_id=1, source_target_pairs={{7,0},{0,1},{1,2},{2,3},{3,4},{4,5},{5,6},{6,7},{15,8},{8,9},{9,10... | collective-permute-start | bytes 276488 | tf_op jit(solution)/shard_map/ppermute | solution.py:14
  89.3 0.7 copy-start.10
  89.6 0.9 copy-start.11
  89.6 1.0 %copy-start.12 = (bf16[180,360]{1,0:T(8,128)(2,1)S(1)}, bf16[180,360]{1,0:T(8,128)(2,1)}, u32[]{:S(2)}) copy-start(bf16[180,360]{1,0:T(8,128)(2,1)} %param.16) | copy-start | bytes 388804
where the time goes:
time: 96.5 us; the launch traced here: 95.2 us
  matrix products  28.7 us (30%)
  local copies, waits for them, and re-layouts  28.5 us (30%)
  starting transfers between devices  16.4 us (17%)
  waiting for transfers between devices  11.8 us (12%)
  other arithmetic  9.39 us (10%)
    transpose x1, local copies, waits for them, and re-layouts, position_bias(): jnp.einsum('abch,dec->hadbe', by_rows, one_hot, precision=lax.Precision.H...  12.7 us
    ppermute x4, waiting for transfers between devices, from_behind(): return lax.ppermute(block, axis, route)  9.56 us
    reshape x1, local copies, waits for them, and re-layouts, position_bias(): full_bias.reshape(heads_n, WIN * WIN, WIN * WIN)  8.72 us
    dot_general x1, matrix products, position_bias(): jnp.einsum('abch,dec->hadbe', by_rows, one_hot, precision=lax.Precision.H...  7.97 us
    ppermute x4, starting transfers between devices, from_behind(): return lax.ppermute(block, axis, route)  6.91 us
    ppermute x2, starting transfers between devices, padded_2(): lax.ppermute(tail, axis, [(i, (i + 1) % count) for i in range(ends)])  6.9 us
    sub x1, matrix products, attend(): scores = scores - jnp.max(scores, axis=-1, keepdims=True)  6.51 us
    dot_general x9, matrix products, on_device(): jnp.dot(piece, conv_weight[row_tap, col_tap], preferred_element_type=jnp....  5.77 us
  transfers between devices with their start and end apart: 8, of which 4 were waited for; matrix products, arithmetic and copies ran while one was open for 44% of the time, Pallas kernels for 0%

commit v1 on v0

v1 whole, which is shorter than its diff:
```python
import functools
import math

import jax
import jax.numpy as jnp
from jax import lax
from jax.experimental import pallas as pl
from jax.experimental.pallas import tpu as pltpu
from jax.sharding import PartitionSpec as P

HEADS = 6
WIN = 16
SHIFT = 8
LANES = 256
F32 = jnp.float32
BF16 = jnp.bfloat16
LOG2E = math.log2(math.e)
MASKED = -4.0e9


def layer_norm(values, norm_gain):
    centre = jnp.mean(values, axis=-1, keepdims=True)
    values = values - centre
    spread = jnp.mean(values * values, axis=-1, keepdims=True)
    return values * lax.rsqrt(spread + 1e-05) * norm_gain


def dot(a, b):
    return jnp.dot(a, b, preferred_element_type=F32)


def dot_nt(a, b):
    return lax.dot_general(a, b, (((1,), (1,)), ((), ())), preferred_element_type=F32)


def one_hot(condition):
    return jnp.where(condition, 1.0, 0.0).astype(BF16)


def expand_bias(table_ref, padded, strip, bias):
    span = 2 * WIN - 1
    padded[...] = jnp.zeros_like(padded)
    padded[0:HEADS, 0 : span * span] = table_ref[...] * LOG2E
    table = padded[...]
    width = padded.shape[1]
    shifted = jnp.concatenate(
        [table if px == 0 else pltpu.roll(table, width - px, 1) for px in range(WIN)], axis=0
    )
    high = shifted.astype(BF16)
    low = (shifted - high.astype(F32)).astype(BF16)
    entry = lax.broadcasted_iota(jnp.int32, (width, 512), 0)
    place = lax.broadcasted_iota(jnp.int32, (1, 512), 1)
    wanted = (2 * WIN - 2 - lax.div(place, WIN)) * span + WIN - 1 - lax.rem(place, WIN)
    picked = dot(jnp.concatenate([high, low], axis=0), one_hot(entry == wanted))
    half = 8 * WIN
    picked = picked[:half] + picked[half:]
    for tile in range(4):
        strip[tile] = picked[:, 128 * tile : 128 * (tile + 1)]
    for head in range(HEADS):
        rows = jnp.concatenate(
            [strip[tile, pl.ds(head, WIN, stride=8), :] for tile in range(4)], axis=1
        )
        for turn in range(8):
            rolled = rows if turn == 0 else pltpu.roll(rows, 512 - 16 * turn, 1)
            bias[head, 15 - turn] = rolled[:, 0:256]
            bias[head, 7 - turn] = rolled[:, 128:384]


def kernel(
    image_ref, top_ref, bottom_ref, left_ref, right_ref, gain1_ref, gain2_ref,
    qkv_ref, proj_ref, table_ref, conv_ref, fc1_ref, fc2_ref, out_ref,
    normed, kv, query, heads, bias, shifted, padded, strip, wq, wkv, wp, wc,
):
    rows, cols, channels = image_ref.shape
    head_dim = channels // HEADS
    row, col = lax.axis_index("row"), lax.axis_index("col")
    last_row, last_col = lax.axis_size("row") - 1, lax.axis_size("col") - 1
    lane = lax.broadcasted_iota(jnp.int32, (1, LANES), 1)
    flag_lane, one_lane = channels, channels + 1

    expand_bias(table_ref, padded, strip, bias)

    for ref in (wq, wkv, wp, wc):
        ref[...] = jnp.zeros_like(ref)
    special = lax.broadcasted_iota(jnp.int32, (16, LANES), 0) + 176
    lanes16 = lax.broadcasted_iota(jnp.int32, (16, LANES), 1)
    wq[176:192, :] = one_hot((special == one_lane) & (lanes16 == flag_lane))
    wkv[176:192, 0:LANES] = jnp.where(
        (special == flag_lane) & (lanes16 == flag_lane), MASKED, 0.0
    ).astype(BF16)
    wkv[176:192, LANES:] = one_hot(
        (special == one_lane) & (lanes16 >= channels) & (lanes16 < channels + HEADS)
    )
    wq[0:channels, 0:channels] = qkv_ref[:, 0:channels]
    wkv[0:channels, 0:channels] = qkv_ref[:, channels : 2 * channels]
    wkv[0:channels, LANES : LANES + channels] = qkv_ref[:, 2 * channels :]
    wp[0:channels, :] = proj_ref[...]
    for row_tap in range(3):
        for col_tap in range(3):
            wc[row_tap, col_tap, 0:channels, :] = conv_ref[row_tap, col_tap]

    half = lane[:, LANES // 2 :]
    one_mark = jnp.where(half == one_lane, 1.0, 0.0)
    flag_mark = jnp.where(half == flag_lane, 1.0, 0.0)
    outside_r = [(row == 0).astype(F32), 0.0, (row == last_row).astype(F32)]
    outside_c = [(col == 0).astype(F32), 0.0, (col == last_col).astype(F32)]
    spans_r = [(0, SHIFT), (SHIFT, SHIFT + rows), (SHIFT + rows, 2 * SHIFT + rows)]
    spans_c = [(0, SHIFT), (SHIFT, SHIFT + cols), (SHIFT + cols, 2 * SHIFT + cols)]
    for (r0, r1), out_r in zip(spans_r, outside_r):
        for (c0, c1), out_c in zip(spans_c, outside_c):
            mark = one_mark + flag_mark * (out_r + out_c)
            normed[r0:r1, c0:c1, LANES // 2 :] = jnp.broadcast_to(
                mark[None], (r1 - r0, c1 - c0, LANES // 2)
            )
    gain1 = gain1_ref[...]
    for r in range(0, rows, 8):
        normed[SHIFT + r : SHIFT + r + 8, SHIFT : SHIFT + cols, 0:channels] = layer_norm(
            image_ref[r : r + 8].astype(F32), gain1
        )
    for r0, ref in ((0, top_ref), (SHIFT + rows, bottom_ref)):
        normed[r0 : r0 + SHIFT, SHIFT : SHIFT + cols, 0:channels] = layer_norm(
            ref[...].astype(F32), gain1
        )
    for c0, ref in ((0, left_ref), (SHIFT + cols, right_ref)):
        for r in range(0, rows + 2 * SHIFT, WIN):
            normed[r : r + WIN, c0 : c0 + SHIFT, 0:channels] = layer_norm(
                ref[r : r + WIN].astype(F32), gain1
            )

    scale = head_dim**-0.5 * LOG2E
    for r in range(0, rows, 8):
        pixels = normed[SHIFT + r : SHIFT + r + 8, SHIFT : SHIFT + cols, :].astype(BF16)
        query[r : r + 8] = (dot(pixels.reshape(-1, LANES), wq[...]) * scale).reshape(8, cols, LANES)
    wide = cols + 2 * SHIFT
    for r in range(0, rows + 2 * SHIFT, 8):
        pixels = normed[r : r + 8].astype(BF16).reshape(-1, LANES)
        kv[r : r + 8] = dot(pixels, wkv[...]).astype(BF16).reshape(8, wide, 2 * LANES)

    def spans(extent):
        cuts = []
        for window in range((extent + 2 * SHIFT) // WIN):
            start = max(window * WIN, SHIFT)
            stop = min((window + 1) * WIN, extent + SHIFT)
            cuts.append((window * WIN, start, stop))
        return cuts

    own = [(lane >= h * head_dim) & (lane < (h + 1) * head_dim) for h in range(HEADS)]
    for key_r, r0, r1 in spans(rows):
        for key_c, c0, c1 in spans(cols):
            pair = kv[key_r : key_r + WIN, key_c : key_c + WIN, :].reshape(WIN * WIN, 2 * LANES)
            keys, values = pair[:, :LANES], pair[:, LANES:]
            step = max(8, 128 // (c1 - c0))
            for q0 in range(r0, r1, step):
                q1 = min(q0 + step, r1)
                count = (q1 - q0) * (c1 - c0)
                part = query[q0 - SHIFT : q1 - SHIFT, c0 - SHIFT : c1 - SHIFT, :]
                part = part.reshape(count, LANES)
                stacked = jnp.concatenate(
                    [
                        jnp.where(own[h] | (lane == flag_lane), part, 0.0).astype(BF16)
                        for h in range(HEADS)
                    ],
                    axis=0,
                )
                scores = dot_nt(stacked, keys).reshape(HEADS, count, WIN * WIN)
                part_bias = bias[:, q0 - key_r : q1 - key_r, c0 - key_c : c1 - key_c, :]
                scores = scores + part_bias.reshape(HEADS, count, WIN * WIN)
                scores = scores - jnp.max(scores, axis=-1, keepdims=True)
                soft = jnp.exp2(scores).astype(BF16).reshape(HEADS * count, WIN * WIN)
                mixed = dot(soft, values)
                result = mixed[0:count]
                for h in range(1, HEADS):
                    mine = own[h] | (lane == channels + h)
                    result = jnp.where(mine, mixed[h * count : (h + 1) * count], result)
                heads[q0 - SHIFT : q1 - SHIFT, c0 - SHIFT : c1 - SHIFT, :] = result.reshape(
                    q1 - q0, c1 - c0, LANES
                )

    for tap in range(3):
        for r in range(0, rows + 2, 8):
            stop = min(r + 8, rows + 2)
            shifted[tap, r:stop] = normed[
                SHIFT - 1 + r : SHIFT - 1 + stop, SHIFT - 1 + tap : SHIFT - 1 + tap + cols, :
            ].astype(BF16)

    @pl.when(row == 0)
    def _():
        shifted[:, 0] = jnp.zeros_like(shifted[:, 0])

    @pl.when(row == last_row)
    def _():
        shifted[:, rows + 1] = jnp.zeros_like(shifted[:, rows + 1])

    @pl.when(col == 0)
    def _():
        edge = lax.broadcasted_iota(jnp.int32, (1, cols, LANES), 1) == 0
        shifted[0] = jnp.where(edge, 0.0, shifted[0].astype(F32)).astype(BF16)

    @pl.when(col == last_col)
    def _():
        edge = lax.broadcasted_iota(jnp.int32, (1, cols, LANES), 1) == cols - 1
        shifted[2] = jnp.where(edge, 0.0, shifted[2].astype(F32)).astype(BF16)

    sum_row = lax.broadcasted_iota(jnp.int32, (LANES // 2, LANES), 0) + LANES // 2 - channels
    lane_wide = lax.broadcasted_iota(jnp.int32, (LANES // 2, LANES), 1)
    spread = one_hot(
        (sum_row >= 0) & (lane_wide >= sum_row * head_dim) & (lane_wide < (sum_row + 1) * head_dim)
        & (lane_wide < channels)
    )
    is_sum = (half >= channels) & (half < channels + HEADS)
    gain2 = gain2_ref[...]
    band = 8
    for r in range(0, rows, band):
        raw = heads[r : r + band].reshape(band * cols, LANES)
        inverse = jnp.where(is_sum, 1.0 / raw[:, LANES // 2 :], 0.0)
        high = inverse.astype(BF16)
        low = (inverse - high.astype(F32)).astype(BF16)
        heads_out = (raw * (dot(high, spread) + dot(low, spread))).astype(BF16)
        attended = dot(heads_out, wp[...]).astype(BF16).astype(F32)
        conv_sum = None
        for row_tap in range(3):
            for col_tap in range(3):
                piece = shifted[col_tap, r + row_tap : r + row_tap + band].reshape(-1, LANES)
                term = dot(piece, wc[row_tap, col_tap])
                conv_sum = term if conv_sum is None else conv_sum + term
        state1 = image_ref[r : r + band].astype(F32).reshape(-1, channels) + attended + conv_sum
        normed2 = layer_norm(state1, gain2).astype(BF16)
        hidden = dot(normed2, fc1_ref[...])
        hidden = (0.5 * hidden * (1.0 + lax.erf(hidden * math.sqrt(0.5)))).astype(BF16)
        mixed_out = state1 + dot_nt(hidden, fc2_ref[...])
        out_ref[r : r + band] = mixed_out.astype(BF16).reshape(band, cols, channels)


def neighbour(block, axis, step):
    count = lax.axis_size(axis)
    return lax.ppermute(block, axis, [(i, (i + step) % count) for i in range(count)])


def on_device(
    image, norm1_gain, norm2_gain, qkv_weight, proj_weight, rel_table, conv_weight, fc1_weight,
    fc2_weight,
):
    rows, cols, channels = image.shape
    top = neighbour(image[rows - SHIFT :], "row", 1)
    bottom = neighbour(image[:SHIFT], "row", -1)
    tall = jnp.concatenate([top, image, bottom], axis=0)
    left = neighbour(tall[:, cols - SHIFT :], "col", 1)
    right = neighbour(tall[:, :SHIFT], "col", -1)
    tall_rows, wide_cols = rows + 2 * SHIFT, cols + 2 * SHIFT
    vmem = pl.BlockSpec(memory_space=pltpu.VMEM)
    return pl.pallas_call(
        kernel,
        out_shape=jax.ShapeDtypeStruct(image.shape, BF16),
        in_specs=[vmem] * 13,
        out_specs=vmem,
        scratch_shapes=[
            pltpu.VMEM((tall_rows, wide_cols, LANES), F32),
            pltpu.VMEM((tall_rows, wide_cols, 2 * LANES), BF16),
            pltpu.VMEM((rows, cols, LANES), F32),
            pltpu.VMEM((rows, cols, LANES), F32),
            pltpu.VMEM((HEADS, WIN, WIN, WIN * WIN), F32),
            pltpu.VMEM((3, rows + 2, cols, LANES), BF16),
            pltpu.VMEM((8, 1024), F32),
            pltpu.VMEM((4, 8 * WIN, 128), F32),
            pltpu.VMEM((LANES, LANES), BF16),
            pltpu.VMEM((LANES, 2 * LANES), BF16),
            pltpu.VMEM((LANES, channels), BF16),
            pltpu.VMEM((3, 3, LANES, channels), BF16),
        ],
        compiler_params=pltpu.CompilerParams(vmem_limit_bytes=48 * 1024 * 1024),
        name="block",
    )(
        image, top, bottom, left, right, norm1_gain[None], norm2_gain[None],
        qkv_weight, proj_weight, rel_table.T, conv_weight, fc1_weight, fc2_weight.T,
    )


def solution(mesh):
    placed = (P("row", "col", None), P(), P(), P(), P(), P(), P(), P(), P())
    return jax.shard_map(
        on_device, mesh=mesh, in_specs=placed, out_specs=P("row", "col", None), check_vma=False
    )
```

time: 96.5 us -> 35.8 us (0.37); the launches traced: 95.2 us -> 35.6 us
  matrix products: 28.7 us -> 0 us
  local copies, waits for them, and re-layouts: 28.5 us -> 1.8 us
  Pallas kernels: 0 us -> 13.9 us
  starting transfers between devices: 16.4 us -> 6.24 us
  other arithmetic: 9.39 us -> 0 us
  waiting for transfers between devices: 11.8 us -> 13.6 us
    dot_general x15 -> x0, matrix products: 22.2 us -> none  [the longest x1 7.97 us: position_bias(): jnp.einsum('abch,dec->hadbe', by_rows, one_hot, precision=lax.Precision.H...]
    pallas_call x0 -> x1, Pallas kernels: none -> 13.9 us  [on_device(): pl.pallas_call(kernel, out_shape=jax.ShapeDtypeStruct(image.shape, BF16),...]
    transpose x2 -> x0, local copies, waits for them, and re-layouts: 12.8 us -> none  [the longest x1 12.7 us: position_bias(): jnp.einsum('abch,dec->hadbe', by_rows, one_hot, precision=lax.Precision.H...]
    ppermute x8 -> x4, starting transfers between devices: 16.4 us -> 6.24 us  [neighbour(): lax.ppermute(block, axis, [(i, (i + step) % count) for i in range(count)])]
    reshape x3 -> x0, local copies, waits for them, and re-layouts: 9.41 us -> none  [the longest x1 8.72 us: position_bias(): full_bias.reshape(heads_n, WIN * WIN, WIN * WIN)]
    sub x1 -> x0, matrix products: 6.51 us -> none  [attend(): scores = scores - jnp.max(scores, axis=-1, keepdims=True)]
    reduce_sum x6 -> x0, other arithmetic: 4 us -> none  [the longest x3 2.21 us: layer_norm(): spread = jnp.mean((values - centre) ** 2, axis=-1, keepdims=True)]
    convert_element_type x5 -> x0, other arithmetic: 2.76 us -> none  [the longest x1 1.02 us: on_device(): normed1 = layer_norm(state, norm1_gain).astype(jnp.bfloat16)]
  transfers between devices with their start and end apart: 8 -> 4, of which waited for: 4 -> 4; matrix products, arithmetic and copies ran while one was open for 44% -> 0% of each run, Pallas kernels for 0% -> 0%
where the time goes in v1:
time: 35.8 us; the launch traced here: 35.6 us
  Pallas kernels  13.9 us (39%)
  waiting for transfers between devices  13.6 us (38%)
  starting transfers between devices  6.24 us (17%)
  local copies, waits for them, and re-layouts  1.8 us (5%)
    pallas_call x1, Pallas kernels, on_device(): pl.pallas_call(kernel, out_shape=jax.ShapeDtypeStruct(image.shape, BF16),...  13.9 us
    ppermute x4, waiting for transfers between devices, neighbour(): lax.ppermute(block, axis, [(i, (i + step) % count) for i in range(count)])  13.6 us
    ppermute x4, starting transfers between devices, neighbour(): lax.ppermute(block, axis, [(i, (i + step) % count) for i in range(count)])  6.24 us
    slice x1, local copies, waits for them, and re-layouts, on_device(): bottom = neighbour(image[:SHIFT], 'row', -1)  1.04 us
    unnamed x20, local copies, waits for them, and re-layouts  0.72 us
  transfers between devices with their start and end apart: 4, of which 4 were waited for; matrix products, arithmetic and copies ran while one was open for 0% of the time, Pallas kernels for 0%

profile of v1, /device:TPU:0, one launch (start us, length us, event | category | flops | bytes accessed | tf_op | source)
XLA Modules:
  0.0 35.6 jit_solution(6250191433085899005)
XLA Ops:
  0.0 1.0 %fusion.1 = (bf16[8,32,180]{2,1,0:T(8,128)(2,1)S(1)}, bf16[8,32,180]{2,1,0:T(8,128)(2,1)S(1)}) fusion(bf16[32,32,180]{2,1,0:T(8,128)(2,1)} %image_ref.1), kind=kLoop, calls=%fused_computation.4 | loop fusion | bytes 368640 | tf_op jit(solution)/shard_map/slice | solution.py:245
  1.0 3.0 %collective-permute-start = (bf16[8,32,180]{2,1,0:T(8,128)(2,1)S(1)}, bf16[8,32,180]{2,1,0:T(8,128)(2,1)S(1)}, u32[]{:S(2)}, u32[]{:S(2)}) collective-permute-start(bf16[8,32,180]{2,1,0:T(8,128)(2,1)S(1)} %get-tuple-element.8), channel_id=1, source_target_pairs={{0,8},{8,16},{16,24},{24,0},{1,9},{9,17},{17,25},{25,1},{2,10},{10... | collective-permute-start | bytes 276488 | tf_op jit(solution)/shard_map/ppermute | solution.py:236
  4.0 1.0 %collective-permute-start.1 = (bf16[8,32,180]{2,1,0:T(8,128)(2,1)S(1)}, bf16[8,32,180]{2,1,0:T(8,128)(2,1)S(1)}, u32[]{:S(2)}, u32[]{:S(2)}) collective-permute-start(bf16[8,32,180]{2,1,0:T(8,128)(2,1)S(1)} %get-tuple-element.7), channel_id=1, source_target_pairs={{0,24},{8,0},{16,8},{24,16},{1,25},{9,1},{17,9},{25,17},{2,26},{10... | collective-permute-start | bytes 276488 | tf_op jit(solution)/shard_map/ppermute | solution.py:236
  5.1 4.3 %collective-permute-done.top_ref = bf16[8,32,180]{2,1,0:T(8,128)(2,1)S(1)} collective-permute-done((bf16[8,32,180]{2,1,0:T(8,128)(2,1)S(1)}, bf16[8,32,180]{2,1,0:T(8,128)(2,1)S(1)}, u32[]{:S(2)}, u32[]{:S(2)}) %collective-permute-start) | collective-permute-done | bytes 92192 | tf_op jit(solution)/shard_map/ppermute | solution.py:236
  9.3 0.0 copy-done
  9.3 0.0 copy-start.1
  9.4 2.1 %collective-permute-done.1.bottom_ref = bf16[8,32,180]{2,1,0:T(8,128)(2,1)S(1)} collective-permute-done((bf16[8,32,180]{2,1,0:T(8,128)(2,1)S(1)}, bf16[8,32,180]{2,1,0:T(8,128)(2,1)S(1)}, u32[]{:S(2)}, u32[]{:S(2)}) %collective-permute-start.1) | collective-permute-done | bytes 92192 | tf_op jit(solution)/shard_map/ppermute | solution.py:236
  11.6 0.0 copy-start.2
  11.6 0.0 copy-start.3
  11.6 0.0 copy-start.4
  11.6 0.0 copy-start.5
  11.6 0.0 copy-start.6
  11.6 0.0 copy-start.8
  11.7 2.2 %collective-permute-start.3 = (bf16[48,8,180]{2,1,0:T(8,128)(2,1)S(1)}, bf16[48,8,180]{2,1,0:T(8,128)(2,1)S(1)}, u32[]{:S(2)}, u32[]{:S(2)}) collective-permute-start(bf16[48,8,180]{2,1,0:T(8,128)(2,1)S(1)} %get-tuple-element.5), channel_id=1, source_target_pairs={{0,7},{1,0},{2,1},{3,2},{4,3},{5,4},{6,5},{7,6},{8,15},{9,8},{10,9... | collective-permute-start | bytes 414728 | tf_op jit(solution)/shard_map/ppermute | solution.py:236
  13.9 0.0 collective-permute-start.2
  13.9 4.2 %collective-permute-done.3.right_ref = bf16[48,8,180]{2,1,0:T(8,128)(2,1)S(1)} collective-permute-done((bf16[48,8,180]{2,1,0:T(8,128)(2,1)S(1)}, bf16[48,8,180]{2,1,0:T(8,128)(2,1)S(1)}, u32[]{:S(2)}, u32[]{:S(2)}) %collective-permute-start.3) | collective-permute-done | bytes 138272 | tf_op jit(solution)/shard_map/ppermute | solution.py:236
  18.1 3.0 %collective-permute-done.2.left_ref = bf16[48,8,180]{2,1,0:T(8,128)(2,1)S(1)} collective-permute-done((bf16[48,8,180]{2,1,0:T(8,128)(2,1)S(1)}, bf16[48,8,180]{2,1,0:T(8,128)(2,1)S(1)}, u32[]{:S(2)}, u32[]{:S(2)}) %collective-permute-start.2) | collective-permute-done | bytes 138272 | tf_op jit(solution)/shard_map/ppermute | solution.py:236
  21.1 0.0 copy-done.1
  21.1 0.0 copy-done.2
  21.1 0.0 copy-done.3
  21.1 0.0 copy-done.4
  21.1 0.0 copy-done.5
  21.1 0.6 %copy-done.7 = f32[180]{0:T(256)S(1)} copy-done((f32[180]{0:T(256)S(1)}, f32[180]{0:T(256)}, u32[]{:S(2)}) %copy-start.7) | copy-done | bytes 744
  21.8 13.9 %block.1 = bf16[32,32,180]{2,1,0:T(8,128)(2,1)} custom-call(bf16[32,32,180]{2,1,0:T(8,128)(2,1)S(1)} %copy-done, bf16[8,32,180]{2,1,0:T(8,128)(2,1)S(1)} %collective-permute-done.top_ref, bf16[8,32,180]{2,1,0:T(8,128)(2,1)S(1)} %collective-permute-done.1.bottom_ref, bf16[48,8,180]{2,1,0:T(8,128)(2,1)S(1)} %collective-permute-done.2.left_ref, ...), custom_call_target="tpu_custom_call" | custom-call | tf_op jit(solution)/shard_map/block/pallas_call | solution.py:251
  (8 shorter events, 0.1 us)
Async XLA Ops:
  0.0 9.3 %copy-start = (bf16[32,32,180]{2,1,0:T(8,128)(2,1)S(1)}, bf16[32,32,180]{2,1,0:T(8,128)(2,1)}, u32[]{:S(2)}) copy-start(bf16[32,32,180]{2,1,0:T(8,128)(2,1)} %image_ref.1) | copy-start | bytes 1105924
  1.0 8.3 %collective-permute-start = (bf16[8,32,180]{2,1,0:T(8,128)(2,1)S(1)}, bf16[8,32,180]{2,1,0:T(8,128)(2,1)S(1)}, u32[]{:S(2)}, u32[]{:S(2)}) collective-permute-start(bf16[8,32,180]{2,1,0:T(8,128)(2,1)S(1)} %get-tuple-element.8), channel_id=1, source_target_pairs={{0,8},{8,16},{16,24},{24,0},{1,9},{9,17},{17,25},{25,1},{2,10},{10... | collective-permute-start | bytes 276488 | tf_op jit(solution)/shard_map/ppermute | solution.py:236
  4.0 7.5 %collective-permute-start.1 = (bf16[8,32,180]{2,1,0:T(8,128)(2,1)S(1)}, bf16[8,32,180]{2,1,0:T(8,128)(2,1)S(1)}, u32[]{:S(2)}, u32[]{:S(2)}) collective-permute-start(bf16[8,32,180]{2,1,0:T(8,128)(2,1)S(1)} %get-tuple-element.7), channel_id=1, source_target_pairs={{0,24},{8,0},{16,8},{24,16},{1,25},{9,1},{17,9},{25,17},{2,26},{10... | collective-permute-start | bytes 276488 | tf_op jit(solution)/shard_map/ppermute | solution.py:236
  9.3 11.7 %copy-start.1 = (bf16[3,3,180,180]{3,2,1,0:T(8,128)(2,1)S(1)}, bf16[3,3,180,180]{3,2,1,0:T(8,128)(2,1)}, u32[]{:S(2)}) copy-start(bf16[3,3,180,180]{3,2,1,0:T(8,128)(2,1)} %conv_ref.1) | copy-start | bytes 1749604
  11.6 9.5 %copy-start.2 = (bf16[180,540]{1,0:T(8,128)(2,1)S(1)}, bf16[180,540]{1,0:T(8,128)(2,1)}, u32[]{:S(2)}) copy-start(bf16[180,540]{1,0:T(8,128)(2,1)} %qkv_ref.1) | copy-start | bytes 583204
  11.6 9.5 %copy-start.3 = (bf16[180,360]{1,0:T(8,128)(2,1)S(1)}, bf16[180,360]{1,0:T(8,128)(2,1)}, u32[]{:S(2)}) copy-start(bf16[180,360]{1,0:T(8,128)(2,1)} %fc1_ref.1) | copy-start | bytes 388804
  11.6 9.5 %copy-start.4 = (bf16[360,180]{0,1:T(8,128)(2,1)S(1)}, bf16[360,180]{0,1:T(8,128)(2,1)}, u32[]{:S(2)}) copy-start(bf16[360,180]{0,1:T(8,128)(2,1)} %param.17) | copy-start | bytes 388804
  11.6 9.5 %copy-start.5 = (bf16[180,180]{1,0:T(8,128)(2,1)S(1)}, bf16[180,180]{1,0:T(8,128)(2,1)}, u32[]{:S(2)}) copy-start(bf16[180,180]{1,0:T(8,128)(2,1)} %proj_ref.1) | copy-start | bytes 194404
  11.6 9.5 %copy-start.6 = (f32[961,6]{0,1:T(8,128)S(1)}, f32[961,6]{0,1:T(8,128)}, u32[]{:S(2)}) copy-start(f32[961,6]{0,1:T(8,128)} %param.14) | copy-start | bytes 69196
  11.6 9.5 %copy-start.8 = (f32[180]{0:T(256)S(1)}, f32[180]{0:T(256)}, u32[]{:S(2)}) copy-start(f32[180]{0:T(256)} %param.11) | copy-start | bytes 2164
  11.7 6.5 %collective-permute-start.3 = (bf16[48,8,180]{2,1,0:T(8,128)(2,1)S(1)}, bf16[48,8,180]{2,1,0:T(8,128)(2,1)S(1)}, u32[]{:S(2)}, u32[]{:S(2)}) collective-permute-start(bf16[48,8,180]{2,1,0:T(8,128)(2,1)S(1)} %get-tuple-element.5), channel_id=1, source_target_pairs={{0,7},{1,0},{2,1},{3,2},{4,3},{5,4},{6,5},{7,6},{8,15},{9,8},{10,9... | collective-permute-start | bytes 414728 | tf_op jit(solution)/shard_map/ppermute | solution.py:236
  13.9 7.2 %collective-permute-start.2 = (bf16[48,8,180]{2,1,0:T(8,128)(2,1)S(1)}, bf16[48,8,180]{2,1,0:T(8,128)(2,1)S(1)}, u32[]{:S(2)}, u32[]{:S(2)}) collective-permute-start(bf16[48,8,180]{2,1,0:T(8,128)(2,1)S(1)} %get-tuple-element.6), channel_id=1, source_target_pairs={{0,1},{1,2},{2,3},{3,4},{4,5},{5,6},{6,7},{7,0},{8,9},{9,10},{10,1... | collective-permute-start | bytes 414728 | tf_op jit(solution)/shard_map/ppermute | solution.py:236
  21.1 0.7 %copy-start.7 = (f32[180]{0:T(256)S(1)}, f32[180]{0:T(256)}, u32[]{:S(2)}) copy-start(f32[180]{0:T(256)} %param.10) | copy-start | bytes 2164

commit v2 on v1

v2 whole, which is shorter than its diff:
```python
import functools
import math

import jax
import jax.numpy as jnp
from jax import lax
from jax.experimental import pallas as pl
from jax.experimental.pallas import tpu as pltpu
from jax.sharding import PartitionSpec as P

HEADS = 6
WIN = 16
SHIFT = 8
LANES = 256
HALF = LANES // 2
F32 = jnp.float32
BF16 = jnp.bfloat16
LOG2E = math.log2(math.e)
MASKED = -4.0e9


def layer_norm(values, norm_gain):
    centre = jnp.mean(values, axis=-1, keepdims=True)
    values = values - centre
    spread = jnp.mean(values * values, axis=-1, keepdims=True)
    return values * lax.rsqrt(spread + 1e-05) * norm_gain


def dot(a, b):
    return jnp.dot(a, b, preferred_element_type=F32)


def dot_nt(a, b):
    return lax.dot_general(a, b, (((1,), (1,)), ((), ())), preferred_element_type=F32)


def one_hot(condition):
    return jnp.where(condition, 1.0, 0.0).astype(BF16)


def lanes_of(width=LANES):
    return lax.broadcasted_iota(jnp.int32, (1, width), 1)


def mark_lanes(ref, place, shape, channels, outside):
    half = lanes_of()[:, HALF:]
    mark = jnp.where(half == channels + 1, 1.0, 0.0) + jnp.where(half == channels, outside, 0.0)
    ref[(*place, slice(HALF, LANES))] = jnp.broadcast_to(mark[None], (*shape, HALF))


def expand_bias(table_ref, padded, strip, bias):
    span = 2 * WIN - 1
    padded[...] = jnp.zeros_like(padded)
    padded[0:HEADS, 0 : span * span] = table_ref[...] * LOG2E
    table = padded[...]
    width = padded.shape[1]
    shifted = jnp.concatenate(
        [table if px == 0 else pltpu.roll(table, width - px, 1) for px in range(WIN)], axis=0
    )
    high = shifted.astype(BF16)
    low = (shifted - high.astype(F32)).astype(BF16)
    entry = lax.broadcasted_iota(jnp.int32, (width, 512), 0)
    place = lax.broadcasted_iota(jnp.int32, (1, 512), 1)
    wanted = (2 * WIN - 2 - lax.div(place, WIN)) * span + WIN - 1 - lax.rem(place, WIN)
    picked = dot(jnp.concatenate([high, low], axis=0), one_hot(entry == wanted))
    half = 8 * WIN
    picked = picked[:half] + picked[half:]
    for tile in range(4):
        strip[tile] = picked[:, 128 * tile : 128 * (tile + 1)]
    for head in range(HEADS):
        rows = jnp.concatenate(
            [strip[tile, pl.ds(head, WIN, stride=8), :] for tile in range(4)], axis=1
        )
        for turn in range(8):
            rolled = rows if turn == 0 else pltpu.roll(rows, 512 - 16 * turn, 1)
            bias[head, 15 - turn] = rolled[:, 0:256]
            bias[head, 7 - turn] = rolled[:, 128:384]


def own_kernel(
    image_ref, gain1_ref, qkv_ref, proj_ref, table_ref, conv_ref,
    bias, normed, q_mid, q_left, q_right, kv_mid, wkv, wp, wc,
    padded, strip, wq,
):
    rows, cols, channels = image_ref.shape
    head_dim = channels // HEADS
    flag_lane, one_lane = channels, channels + 1
    expand_bias(table_ref, padded, strip, bias)

    for ref in (wq, wkv, wp, wc):
        ref[...] = jnp.zeros_like(ref)
    special = lax.broadcasted_iota(jnp.int32, (16, LANES), 0) + 176
    lanes16 = lax.broadcasted_iota(jnp.int32, (16, LANES), 1)
    wq[176:192, :] = one_hot((special == one_lane) & (lanes16 == flag_lane))
    wkv[176:192, 0:LANES] = jnp.where(
        (special == flag_lane) & (lanes16 == flag_lane), MASKED, 0.0
    ).astype(BF16)
    wkv[176:192, LANES:] = one_hot(
        (special == one_lane) & (lanes16 >= channels) & (lanes16 < channels + HEADS)
    )
    wq[0:channels, 0:channels] = qkv_ref[:, 0:channels]
    wkv[0:channels, 0:channels] = qkv_ref[:, channels : 2 * channels]
    wkv[0:channels, LANES : LANES + channels] = qkv_ref[:, 2 * channels :]
    wp[0:channels, :] = proj_ref[...]
    for row_tap in range(3):
        for col_tap in range(3):
            wc[row_tap, col_tap, 0:channels, :] = conv_ref[row_tap, col_tap]

    mark_lanes(normed, (slice(0, rows), slice(0, cols)), (rows, cols), channels, 0.0)
    gain1 = gain1_ref[...]
    for r in range(0, rows, 8):
        normed[r : r + 8, :, 0:channels] = layer_norm(image_ref[r : r + 8].astype(F32), gain1)

    scale = head_dim**-0.5 * LOG2E
    for r in range(0, rows, 8):
        pixels = normed[r : r + 8].astype(BF16).reshape(-1, LANES)
        q = (dot(pixels, wq[...]) * scale).reshape(8, cols, LANES)
        q_left[r : r + 8] = q[:, :SHIFT]
        q_mid[r : r + 8] = q[:, SHIFT : cols - SHIFT]
        q_right[r : r + 8] = q[:, cols - SHIFT :]
        middle = normed[r : r + 8, SHIFT : cols - SHIFT].astype(BF16).reshape(-1, LANES)
        kv = dot(middle, wkv[...]).astype(BF16)
        kv_mid[r : r + 8] = kv.reshape(8, cols - 2 * SHIFT, 2 * LANES)


def attend(part, pair, part_bias, head_dim, channels):
    lane = lanes_of()
    keys, values = pair[:, :LANES], pair[:, LANES:]
    count = part.shape[0]
    own = [(lane >= h * head_dim) & (lane < (h + 1) * head_dim) for h in range(HEADS)]
    stacked = jnp.concatenate(
        [jnp.where(own[h] | (lane == channels), part, 0.0).astype(BF16) for h in range(HEADS)],
        axis=0,
    )
    scores = dot_nt(stacked, keys).reshape(HEADS, count, WIN * WIN)
    scores = scores + part_bias.reshape(HEADS, count, WIN * WIN)
    scores = scores - jnp.max(scores, axis=-1, keepdims=True)
    soft = jnp.exp2(scores).astype(BF16).reshape(HEADS * count, WIN * WIN)
    mixed = dot(soft, values)
    result = mixed[0:count]
    for h in range(1, HEADS):
        mine = own[h] | (lane == channels + h)
        result = jnp.where(mine, mixed[h * count : (h + 1) * count], result)
    return result


def finish(raw, pieces, image, wp, wc, gain2, fc1, fc2, channels):
    head_dim = channels // HEADS
    half = lanes_of()[:, HALF:]
    sum_row = lax.broadcasted_iota(jnp.int32, (HALF, LANES), 0) + HALF - channels
    lane_wide = lax.broadcasted_iota(jnp.int32, (HALF, LANES), 1)
    spread = one_hot(
        (sum_row >= 0) & (lane_wide >= sum_row * head_dim) & (lane_wide < (sum_row + 1) * head_dim)
        & (lane_wide < channels)
    )
    is_sum = (half >= channels) & (half < channels + HEADS)
    inverse = jnp.where(is_sum, 1.0 / raw[:, HALF:], 0.0)
    high = inverse.astype(BF16)
    low = (inverse - high.astype(F32)).astype(BF16)
    heads_out = (raw * (dot(high, spread) + dot(low, spread))).astype(BF16)
    attended = dot(heads_out, wp[...]).astype(BF16).astype(F32)
    conv_sum = None
    for row_tap in range(3):
        for col_tap in range(3):
            term = dot(pieces(row_tap, col_tap), wc[row_tap, col_tap])
            conv_sum = term if conv_sum is None else conv_sum + term
    state1 = image + attended + conv_sum
    normed2 = layer_norm(state1, gain2).astype(BF16)
    hidden = dot(normed2, fc1[...])
    hidden = (0.5 * hidden * (1.0 + lax.erf(hidden * math.sqrt(0.5)))).astype(BF16)
    return state1 + dot_nt(hidden, fc2[...])


def middle_kernel(
    image_ref, top_ref, bottom_ref, gain1_ref, gain2_ref, fc1_ref, fc2_ref,
    bias, normed, q_mid, kv_mid, wkv, wp, wc, out_ref,
    bands, shifted, heads,
):
    rows, cols, channels = image_ref.shape
    head_dim = channels // HEADS
    wide = cols - 2 * SHIFT
    row, last_row = lax.axis_index("row"), lax.axis_size("row") - 1
    gain1 = gain1_ref[...]
    kv_band = []
    for i, (ref, edge) in enumerate(((top_ref, 0), (bottom_ref, last_row))):
        mark_lanes(
            bands, (i, slice(0, SHIFT), slice(0, cols)), (SHIFT, cols), channels, (row == edge).astype(F32)
        )
        bands[i, :, :, 0:channels] = layer_norm(ref[...].astype(F32), gain1)
        pixels = bands[i, :, SHIFT : cols - SHIFT].astype(BF16).reshape(-1, LANES)
        kv_band.append(dot(pixels, wkv[...]).astype(BF16))

    for window in range(rows // WIN + 1):
        start, stop = max(window * WIN - SHIFT, 0), min((window + 1) * WIN - SHIFT, rows)
        first = start - (window * WIN - SHIFT)
        pair = kv_mid[start:stop].reshape(-1, 2 * LANES)
        if window == 0:
            pair = jnp.concatenate([kv_band[0], pair], axis=0)
        if window == rows // WIN:
            pair = jnp.concatenate([pair, kv_band[1]], axis=0)
        for r in range(start, stop, SHIFT):
            part_bias = bias[:, first + r - start : first + r - start + SHIFT]
            part = q_mid[r : r + SHIFT].reshape(-1, LANES)
            result = attend(part, pair, part_bias, head_dim, channels)
            heads[r : r + SHIFT] = result.reshape(SHIFT, wide, LANES)

    for tap in range(3):
        c0 = SHIFT - 1 + tap
        shifted[tap, 0] = bands[0, SHIFT - 1, c0 : c0 + wide].astype(BF16)
        for r in range(0, rows, 8):
            shifted[tap, 1 + r : 9 + r] = normed[r : r + 8, c0 : c0 + wide].astype(BF16)
        shifted[tap, 1 + rows] = bands[1, 0, c0 : c0 + wide].astype(BF16)

    gain2 = gain2_ref[...]
    band = 16
    for r in range(0, rows, band):
        image = image_ref[r : r + band].astype(F32)[:, SHIFT : cols - SHIFT].reshape(-1, channels)
        raw = heads[r : r + band].reshape(-1, LANES)

        def pieces(row_tap, col_tap):
            return shifted[col_tap, r + row_tap : r + row_tap + band].reshape(-1, LANES)

        mixed = finish(raw, pieces, image, wp, wc, gain2, fc1_ref, fc2_ref, channels)
        out_ref[r : r + band] = mixed.reshape(band, wide, channels)


def side_kernel(
    image_ref, top_ref, bottom_ref, left_ref, right_ref, gain1_ref, gain2_ref, fc1_ref, fc2_ref,
    bias, normed, q_left, q_right, wkv, wp, wc, middle_ref, out_ref,
    side, kv, shifted, heads,
):
    rows, cols, channels = image_ref.shape
    head_dim = channels // HEADS
    tall = rows + 2 * SHIFT
    row, last_row = lax.axis_index("row"), lax.axis_size("row") - 1
    col, last_col = lax.axis_index("col"), lax.axis_size("col") - 1
    gain1 = gain1_ref[...]
    out_row = [(row == 0).astype(F32), (row == last_row).astype(F32)]
    out_col = [(col == 0).astype(F32), (col == last_col).astype(F32)]
    for s, (ref, halo, own, c0) in enumerate(
        ((left_ref, 0, SHIFT, 0), (right_ref, 2 * SHIFT, 0, cols - 2 * SHIFT))
    ):
        mark_lanes(side, (s, slice(0, SHIFT), slice(halo, halo + SHIFT)), (SHIFT, SHIFT), channels,
                   out_col[s] + out_row[0])
        mark_lanes(side, (s, slice(SHIFT, SHIFT + rows), slice(halo, halo + SHIFT)), (rows, SHIFT), channels,
                   out_col[s])
        mark_lanes(side, (s, slice(SHIFT + rows, tall), slice(halo, halo + SHIFT)), (SHIFT, SHIFT), channels,
                   out_col[s] + out_row[1])
        for r in range(0, tall, WIN):
            side[s, r : r + WIN, halo : halo + SHIFT, 0:channels] = layer_norm(
                ref[r : r + WIN].astype(F32), gain1
            )
        for i, (r0, band_ref) in enumerate(((0, top_ref), (SHIFT + rows, bottom_ref))):
            values = band_ref[...].astype(F32)[:, c0 : c0 + 2 * SHIFT]
            mark_lanes(side, (s, slice(r0, r0 + SHIFT), slice(own, own + 2 * SHIFT)), (SHIFT, 2 * SHIFT),
                       channels, out_row[i])
            side[s, r0 : r0 + SHIFT, own : own + 2 * SHIFT, 0:channels] = layer_norm(values, gain1)
        side[s, SHIFT : SHIFT + rows, own : own + 2 * SHIFT] = normed[:, c0 : c0 + 2 * SHIFT]

        k0 = 0 if s == 0 else SHIFT
        for r in range(0, tall, WIN):
            pixels = side[s, r : r + WIN, k0 : k0 + WIN].astype(BF16).reshape(-1, LANES)
            kv[s, r : r + WIN] = dot(pixels, wkv[...]).astype(BF16).reshape(WIN, WIN, 2 * LANES)

    for s, q_ref in enumerate((q_left, q_right)):
        px = SHIFT if s == 0 else 0
        for window in range(rows // WIN + 1):
            start, stop = max(window * WIN - SHIFT, 0), min((window + 1) * WIN - SHIFT, rows)
            first = start - (window * WIN - SHIFT)
            pair = kv[s, window * WIN : (window + 1) * WIN].reshape(-1, 2 * LANES)
            part_bias = bias[:, first : first + stop - start, px : px + SHIFT]
            part = q_ref[start:stop].reshape(-1, LANES)
            result = attend(part, pair, part_bias, head_dim, channels)
            heads[s, start:stop] = result.reshape(stop - start, SHIFT, LANES)

    for s in range(2):
        for tap in range(3):
            c0 = (SHIFT if s == 0 else SHIFT) - 1 + tap
            for r in range(0, rows + 2, 8):
                stop = min(r + 8, rows + 2)
                shifted[tap, s, r:stop] = side[s, SHIFT - 1 + r : SHIFT - 1 + stop, c0 : c0 + SHIFT]

    gain2 = gain2_ref[...]
    band = 16
    for r in range(0, rows, band):
        whole = image_ref[r : r + band].astype(F32)
        image = jnp.concatenate(
            [whole[:, :SHIFT].reshape(-1, channels), whole[:, cols - SHIFT :].reshape(-1, channels)], axis=0
        )
        raw = heads[:, r : r + band].reshape(-1, LANES)

        def pieces(row_tap, col_tap):
            piece = shifted[col_tap, :, r + row_tap : r + row_tap + band]
            return piece.reshape(-1, LANES).astype(BF16)

        mixed = finish(raw, pieces, image, wp, wc, gain2, fc1_ref, fc2_ref, channels)
        mixed = mixed.reshape(2, band, SHIFT, channels)
        whole = jnp.concatenate([mixed[0], middle_ref[r : r + band], mixed[1]], axis=1)
        out_ref[r : r + band] = whole.astype(BF16)


def from_neighbour(block, axis, step):
    count = lax.axis_size(axis)
    pairs = [(i, i + step) for i in range(count) if 0 <= i + step < count]
    return lax.ppermute(block, axis, pairs)


def call(kernel, name, outs, scratch, flops, operands):
    vmem = pl.BlockSpec(memory_space=pltpu.VMEM)
    return pl.pallas_call(
        kernel,
        out_shape=[jax.ShapeDtypeStruct(shape, kind) for shape, kind in outs],
        in_specs=[vmem] * len(operands),
        out_specs=[vmem] * len(outs),
        scratch_shapes=[pltpu.VMEM(shape, kind) for shape, kind in scratch],
        cost_estimate=pl.CostEstimate(flops=flops, bytes_accessed=4_000_000, transcendentals=1_000_000),
        compiler_params=pltpu.CompilerParams(vmem_limit_bytes=24 * 1024 * 1024),
        name=name,
    )(*operands)


def on_device(
    image, norm1_gain, norm2_gain, qkv_weight, proj_weight, rel_table, conv_weight, fc1_weight,
    fc2_weight,
):
    rows, cols, channels = image.shape
    tall, wide = rows + 2 * SHIFT, cols - 2 * SHIFT
    gain1, gain2, fc2 = norm1_gain[None], norm2_gain[None], fc2_weight.T
    top = from_neighbour(image[rows - SHIFT :], "row", 1)
    bottom = from_neighbour(image[:SHIFT], "row", -1)
    bias, normed, q_mid, q_left, q_right, kv_mid, wkv, wp, wc = call(
        own_kernel,
        "own_tile",
        [
            ((HEADS, WIN, WIN, WIN * WIN), F32),
            ((rows, cols, LANES), F32),
            ((rows, wide, LANES), F32),
            ((rows, SHIFT, LANES), F32),
            ((rows, SHIFT, LANES), F32),
            ((rows, wide, 2 * LANES), BF16),
            ((LANES, 2 * LANES), BF16),
            ((LANES, channels), BF16),
            ((3, 3, LANES, channels), BF16),
        ],
        [((8, 1024), F32), ((4, 8 * WIN, 128), F32), ((LANES, LANES), BF16)],
        2_000_000_000,
        (image, gain1, qkv_weight, proj_weight, rel_table.T, conv_weight),
    )
    left_part = jnp.concatenate([top[:, cols - SHIFT :], image[:, cols - SHIFT :], bottom[:, cols - SHIFT :]])
    right_part = jnp.concatenate([top[:, :SHIFT], image[:, :SHIFT], bottom[:, :SHIFT]])
    left = from_neighbour(left_part, "col", 1)
    right = from_neighbour(right_part, "col", -1)
    (middle,) = call(
        middle_kernel,
        "middle_columns",
        [((rows, wide, channels), F32)],
        [
            ((2, SHIFT, cols, LANES), F32),
            ((3, rows + 2, wide, LANES), BF16),
            ((rows, wide, LANES), F32),
        ],
        2_000_000_000,
        (image, top, bottom, gain1, gain2, fc1_weight, fc2, bias, normed, q_mid, kv_mid, wkv, wp, wc),
    )
    (out,) = call(
        side_kernel,
        "side_columns",
        [(image.shape, BF16)],
        [
            ((2, tall, 3 * SHIFT, LANES), F32),
            ((2, tall, WIN, 2 * LANES), BF16),
            ((3, 2, rows + 2, SHIFT, LANES), F32),
            ((2, rows, SHIFT, LANES), F32),
        ],
        2_000_000_000,
        (image, top, bottom, left, right, gain1, gain2, fc1_weight, fc2, bias, normed, q_left, q_right,
         wkv, wp, wc, middle),
    )
    return out


def solution(mesh):
    placed = (P("row", "col", None), P(), P(), P(), P(), P(), P(), P(), P())
    return jax.shard_map(
        on_device, mesh=mesh, in_specs=placed, out_specs=P("row", "col", None), check_vma=False
    )
```

time: 35.8 us -> 32.9 us (0.919)
  the two profiles are of different devices: /device:TPU:0 before, /device:TPU:5 now
where the time goes in v2:
time: 32.9 us; the launch traced here: 32.5 us
  starting transfers between devices  12.4 us (38%)
  Pallas kernels  12.3 us (37%)
  local copies, waits for them, and re-layouts  7.46 us (23%)
    ppermute x4, starting transfers between devices, from_neighbour(): return lax.ppermute(block, axis, pairs)  12.4 us
    pallas_call x3, Pallas kernels, call(): pl.pallas_call(kernel, out_shape=[jax.ShapeDtypeStruct(shape, kind) for s...  12.3 us
    unnamed x18, local copies, waits for them, and re-layouts  5.47 us
    slice x1, local copies, waits for them, and re-layouts, on_device(): image[:, :SHIFT]  0.99 us
    slice x1, local copies, waits for them, and re-layouts, on_device(): bottom = from_neighbour(image[:SHIFT], 'row', -1)  0.98 us
  transfers between devices with their start and end apart: 4, of which 0 were waited for; matrix products, arithmetic and copies ran while one was open for 3% of the time, Pallas kernels for 20%

profile of v2, /device:TPU:5, one launch (start us, length us, event | category | flops | bytes accessed | tf_op | source)
XLA Modules:
  0.0 32.5 jit_solution(9581506603876626854)
XLA Ops:
  0.0 1.0 %fusion.1 = (bf16[8,32,180]{2,1,0:T(8,128)(2,1)S(1)}, bf16[8,32,180]{2,1,0:T(8,128)(2,1)S(1)}) fusion(bf16[32,32,180]{2,1,0:T(8,128)(2,1)} %image_ref.5), kind=kLoop, calls=%fused_computation.3 | loop fusion | bytes 368640 | tf_op jit(solution)/shard_map/slice | solution.py:330
  1.0 3.1 %collective-permute-start = (bf16[8,32,180]{2,1,0:T(8,128)(2,1)S(1)}, bf16[8,32,180]{2,1,0:T(8,128)(2,1)S(1)}, u32[]{:S(2)}, u32[]{:S(2)}) collective-permute-start(bf16[8,32,180]{2,1,0:T(8,128)(2,1)S(1)} %get-tuple-element.26), channel_id=1, source_target_pairs={{0,8},{8,16},{16,24},{1,9},{9,17},{17,25},{2,10},{10,18},{18,26},{... | collective-permute-start | bytes 276488 | tf_op jit(solution)/shard_map/ppermute | solution.py:305
  4.1 3.1 %collective-permute-start.1 = (bf16[8,32,180]{2,1,0:T(8,128)(2,1)S(1)}, bf16[8,32,180]{2,1,0:T(8,128)(2,1)S(1)}, u32[]{:S(2)}, u32[]{:S(2)}) collective-permute-start(bf16[8,32,180]{2,1,0:T(8,128)(2,1)S(1)} %get-tuple-element.25), channel_id=1, source_target_pairs={{8,0},{16,8},{24,16},{9,1},{17,9},{25,17},{10,2},{18,10},{26,18},{... | collective-permute-start | bytes 276488 | tf_op jit(solution)/shard_map/ppermute | solution.py:305
  7.2 1.0 %fusion = (bf16[32,8,180]{2,1,0:T(8,128)(2,1)S(1)}, bf16[32,8,180]{2,1,0:T(8,128)(2,1)S(1)}) fusion(bf16[32,32,180]{2,1,0:T(8,128)(2,1)} %image_ref.5), kind=kLoop, calls=%fused_computation.2 | loop fusion | bytes 368640 | tf_op jit(solution)/shard_map/slice | solution.py:350
  8.2 0.0 copy-start
  8.2 1.0 %copy-done = bf16[32,32,180]{2,1,0:T(8,128)(2,1)S(1)} copy-done((bf16[32,32,180]{2,1,0:T(8,128)(2,1)S(1)}, bf16[32,32,180]{2,1,0:T(8,128)(2,1)}, u32[]{:S(2)}) %copy-start) | copy-done | bytes 368664
  9.2 0.0 copy-start.1
  9.2 1.2 %copy-done.1 = bf16[3,3,180,180]{3,2,1,0:T(8,128)(2,1)S(1)} copy-done((bf16[3,3,180,180]{3,2,1,0:T(8,128)(2,1)S(1)}, bf16[3,3,180,180]{3,2,1,0:T(8,128)(2,1)}, u32[]{:S(2)}) %copy-start.1) | copy-done | bytes 583224
  10.4 0.9 %copy-done.2 = bf16[180,540]{1,0:T(8,128)(2,1)S(1)} copy-done((bf16[180,540]{1,0:T(8,128)(2,1)S(1)}, bf16[180,540]{1,0:T(8,128)(2,1)}, u32[]{:S(2)}) %copy-start.2) | copy-done | bytes 194424
  11.3 0.9 %copy-done.5 = bf16[180,180]{1,0:T(8,128)(2,1)S(1)} copy-done((bf16[180,180]{1,0:T(8,128)(2,1)S(1)}, bf16[180,180]{1,0:T(8,128)(2,1)}, u32[]{:S(2)}) %copy-start.5) | copy-done | bytes 64824
  12.2 0.8 %copy-done.6 = f32[961,6]{0,1:T(8,128)S(1)} copy-done((f32[961,6]{0,1:T(8,128)S(1)}, f32[961,6]{0,1:T(8,128)}, u32[]{:S(2)}) %copy-start.6) | copy-done | bytes 23088
  13.0 0.7 %copy-done.7 = f32[180]{0:T(256)S(1)} copy-done((f32[180]{0:T(256)S(1)}, f32[180]{0:T(256)}, u32[]{:S(2)}) %copy-start.7) | copy-done | bytes 744
  13.7 2.0 %own_tile.1 = (f32[6,16,16,256]{3,2,1,0:T(8,128)S(1)}, f32[32,32,256]{2,1,0:T(8,128)S(1)}, f32[32,16,256]{2,1,0:T(8,128)S(1)}, f32[32,8,256]{2,1,0:T(8,128)S(1)}...) custom-call(bf16[32,32,180]{2,1,0:T(8,128)(2,1)S(1)} %copy-done, ...), custom_call_target="tpu_custom_call" | custom-call | flops 2000000000 | bytes 4000000 | tf_op jit(solution)/shard_map/own_tile/pallas_call | solution.py:310
  15.7 0.0 collective-permute-done.top_ref
  15.7 0.0 collective-permute-done.1.bottom_ref
  15.8 3.1 %collective-permute-start.3 = (bf16[48,8,180]{2,1,0:T(8,128)(2,1)S(1)}, bf16[48,8,180]{2,1,0:T(8,128)(2,1)S(1)}, u32[]{:S(2)}, u32[]{:S(2)}) collective-permute-start(bf16[48,8,180]{2,1,0:T(8,128)(2,1)S(1)} %pad_maximum_fusion.1), channel_id=1, source_target_pairs={{1,0},{2,1},{3,2},{4,3},{5,4},{6,5},{7,6},{9,8},{10,9},{11,10},{12... | collective-permute-start | bytes 414728 | tf_op jit(solution)/shard_map/ppermute | solution.py:305
  19.0 3.1 %collective-permute-start.2 = (bf16[48,8,180]{2,1,0:T(8,128)(2,1)S(1)}, bf16[48,8,180]{2,1,0:T(8,128)(2,1)S(1)}, u32[]{:S(2)}, u32[]{:S(2)}) collective-permute-start(bf16[48,8,180]{2,1,0:T(8,128)(2,1)S(1)} %pad_maximum_fusion), channel_id=1, source_target_pairs={{0,1},{1,2},{2,3},{3,4},{4,5},{5,6},{6,7},{8,9},{9,10},{10,11},{11... | collective-permute-start | bytes 414728 | tf_op jit(solution)/shard_map/ppermute | solution.py:305
  22.1 0.0 copy-done.3
  22.1 0.0 copy-done.4
  22.1 0.0 copy-done.8
  22.2 4.4 %middle_columns.1.middle_ref = f32[32,16,180]{2,1,0:T(8,128)S(1)} custom-call(bf16[32,32,180]{2,1,0:T(8,128)(2,1)S(1)} %copy-done, bf16[8,32,180]{2,1,0:T(8,128)(2,1)S(1)} %collective-permute-done.top_ref, bf16[8,32,180]{2,1,0:T(8,128)(2,1)S(1)} %collective-permute-done.1.bottom_ref, f32[1,180]{1,0:T(1,128)S(1)} %bitcast.8, f32[1,180]{1,0:T(1,128)S(1)} %bitcast.10, ...), custom_call_target="tpu_custom_call" | custom-call | flops 2000000000 | bytes 4000000 | tf_op jit(solution)/shard_map/middle_columns/pallas_call | solution.py:310
  26.6 0.0 collective-permute-done.3.right_ref
  26.6 0.0 collective-permute-done.2.left_ref
  26.6 5.9 %side_columns.1 = bf16[32,32,180]{2,1,0:T(8,128)(2,1)} custom-call(bf16[32,32,180]{2,1,0:T(8,128)(2,1)S(1)} %copy-done, bf16[8,32,180]{2,1,0:T(8,128)(2,1)S(1)} %collective-permute-done.top_ref, bf16[8,32,180]{2,1,0:T(8,128)(2,1)S(1)} %collective-permute-done.1.bottom_ref, bf16[48,8,180]{2,1,0:T(8,128)(2,1)S(1)} %collective-permute-done.2.left_ref, ...), custom_call_target="tpu_custom_call" | custom-call | flops 2000000000 | bytes 4000000 | tf_op jit(solution)/shard_map/side_columns/pallas_call | solution.py:310
  (11 shorter events, 0.1 us)
Async XLA Ops:
  1.0 14.7 %collective-permute-start = (bf16[8,32,180]{2,1,0:T(8,128)(2,1)S(1)}, bf16[8,32,180]{2,1,0:T(8,128)(2,1)S(1)}, u32[]{:S(2)}, u32[]{:S(2)}) collective-permute-start(bf16[8,32,180]{2,1,0:T(8,128)(2,1)S(1)} %get-tuple-element.26), channel_id=1, source_target_pairs={{0,8},{8,16},{16,24},{1,9},{9,17},{17,25},{2,10},{10,18},{18,26},{... | collective-permute-start | bytes 276488 | tf_op jit(solution)/shard_map/ppermute | solution.py:305
  4.1 11.6 %collective-permute-start.1 = (bf16[8,32,180]{2,1,0:T(8,128)(2,1)S(1)}, bf16[8,32,180]{2,1,0:T(8,128)(2,1)S(1)}, u32[]{:S(2)}, u32[]{:S(2)}) collective-permute-start(bf16[8,32,180]{2,1,0:T(8,128)(2,1)S(1)} %get-tuple-element.25), channel_id=1, source_target_pairs={{8,0},{16,8},{24,16},{9,1},{17,9},{25,17},{10,2},{18,10},{26,18},{... | collective-permute-start | bytes 276488 | tf_op jit(solution)/shard_map/ppermute | solution.py:305
  8.2 1.0 %copy-start = (bf16[32,32,180]{2,1,0:T(8,128)(2,1)S(1)}, bf16[32,32,180]{2,1,0:T(8,128)(2,1)}, u32[]{:S(2)}) copy-start(bf16[32,32,180]{2,1,0:T(8,128)(2,1)} %image_ref.5) | copy-start | bytes 1105924
  9.2 1.2 %copy-start.1 = (bf16[3,3,180,180]{3,2,1,0:T(8,128)(2,1)S(1)}, bf16[3,3,180,180]{3,2,1,0:T(8,128)(2,1)}, u32[]{:S(2)}) copy-start(bf16[3,3,180,180]{3,2,1,0:T(8,128)(2,1)} %conv_ref.1) | copy-start | bytes 1749604
  10.4 0.9 %copy-start.2 = (bf16[180,540]{1,0:T(8,128)(2,1)S(1)}, bf16[180,540]{1,0:T(8,128)(2,1)}, u32[]{:S(2)}) copy-start(bf16[180,540]{1,0:T(8,128)(2,1)} %qkv_ref.1) | copy-start | bytes 583204
  11.3 0.9 %copy-start.5 = (bf16[180,180]{1,0:T(8,128)(2,1)S(1)}, bf16[180,180]{1,0:T(8,128)(2,1)}, u32[]{:S(2)}) copy-start(bf16[180,180]{1,0:T(8,128)(2,1)} %proj_ref.1) | copy-start | bytes 194404
  12.2 0.8 %copy-start.6 = (f32[961,6]{0,1:T(8,128)S(1)}, f32[961,6]{0,1:T(8,128)}, u32[]{:S(2)}) copy-start(f32[961,6]{0,1:T(8,128)} %param.14) | copy-start | bytes 69196
  13.0 0.7 %copy-start.7 = (f32[180]{0:T(256)S(1)}, f32[180]{0:T(256)}, u32[]{:S(2)}) copy-start(f32[180]{0:T(256)} %param.10) | copy-start | bytes 2164
  13.7 8.5 %copy-start.3 = (bf16[180,360]{1,0:T(8,128)(2,1)S(1)}, bf16[180,360]{1,0:T(8,128)(2,1)}, u32[]{:S(2)}) copy-start(bf16[180,360]{1,0:T(8,128)(2,1)} %fc1_ref.3) | copy-start | bytes 388804
  13.7 8.5 %copy-start.4 = (bf16[360,180]{0,1:T(8,128)(2,1)S(1)}, bf16[360,180]{0,1:T(8,128)(2,1)}, u32[]{:S(2)}) copy-start(bf16[360,180]{0,1:T(8,128)(2,1)} %param.17) | copy-start | bytes 388804
  13.7 8.5 %copy-start.8 = (f32[180]{0:T(256)S(1)}, f32[180]{0:T(256)}, u32[]{:S(2)}) copy-start(f32[180]{0:T(256)} %param.11) | copy-start | bytes 2164
  15.8 10.8 %collective-permute-start.3 = (bf16[48,8,180]{2,1,0:T(8,128)(2,1)S(1)}, bf16[48,8,180]{2,1,0:T(8,128)(2,1)S(1)}, u32[]{:S(2)}, u32[]{:S(2)}) collective-permute-start(bf16[48,8,180]{2,1,0:T(8,128)(2,1)S(1)} %pad_maximum_fusion.1), channel_id=1, source_target_pairs={{1,0},{2,1},{3,2},{4,3},{5,4},{6,5},{7,6},{9,8},{10,9},{11,10},{12... | collective-permute-start | bytes 414728 | tf_op jit(solution)/shard_map/ppermute | solution.py:305
  19.0 7.6 %collective-permute-start.2 = (bf16[48,8,180]{2,1,0:T(8,128)(2,1)S(1)}, bf16[48,8,180]{2,1,0:T(8,128)(2,1)S(1)}, u32[]{:S(2)}, u32[]{:S(2)}) collective-permute-start(bf16[48,8,180]{2,1,0:T(8,128)(2,1)S(1)} %pad_maximum_fusion), channel_id=1, source_target_pairs={{0,1},{1,2},{2,3},{3,4},{4,5},{5,6},{6,7},{8,9},{9,10},{10,11},{11... | collective-permute-start | bytes 414728 | tf_op jit(solution)/shard_map/ppermute | solution.py:305

commit v3 on v2

--- a/solution.py
+++ b/solution.py
@@ -36,6 +36,16 @@
 
 def one_hot(condition):
     return jnp.where(condition, 1.0, 0.0).astype(BF16)
+
+
+def gelu(x):
+    size = jnp.abs(x)
+    t = 1.0 / (1.0 + (0.3275911 * math.sqrt(0.5)) * size)
+    poly = 0.5 * 1.061405429
+    for factor in (-1.453152027, 1.421413741, -0.284496736, 0.254829592):
+        poly = poly * t + 0.5 * factor
+    tail = poly * t * jnp.exp2(size * size * (-0.5 * LOG2E))
+    return jnp.maximum(x, 0.0) - size * tail
 
 
 def lanes_of(width=LANES):
@@ -78,14 +88,28 @@
 
 
 def own_kernel(
-    image_ref, gain1_ref, qkv_ref, proj_ref, table_ref, conv_ref,
-    bias, normed, q_mid, q_left, q_right, kv_mid, wkv, wp, wc,
-    padded, strip, wq,
+    image_hbm, gain1_ref, qkv_hbm, proj_hbm, table_hbm, conv_hbm,
+    bias, normed, q_mid, q_left, q_right, kv_mid, wkv, wp, wc, first_cols, last_cols,
+    padded, strip, wq, table_ref, image_ref, qkv_ref, proj_ref, conv_ref, sems,
 ):
     rows, cols, channels = image_ref.shape
     head_dim = channels // HEADS
     flag_lane, one_lane = channels, channels + 1
+    fetches = [
+        pltpu.make_async_copy(source, target, sems.at[i])
+        for i, (source, target) in enumerate(
+            ((table_hbm, table_ref), (image_hbm, image_ref), (qkv_hbm, qkv_ref),
+             (proj_hbm, proj_ref), (conv_hbm, conv_ref))
+        )
+    ]
+    for fetch in fetches:
+        fetch.start()
+    fetches[0].wait()
     expand_bias(table_ref, padded, strip, bias)
+    for fetch in fetches[1:]:
+        fetch.wait()
+    first_cols[...] = image_ref[...].astype(F32)[:, :SHIFT].astype(BF16)
+    last_cols[...] = image_ref[...].astype(F32)[:, cols - SHIFT :].astype(BF16)
 
     for ref in (wq, wkv, wp, wc):
         ref[...] = jnp.zeros_like(ref)
@@ -104,7 +128,8 @@
     wp[0:channels, :] = proj_ref[...]
     for row_tap in range(3):
         for col_tap in range(3):
-            wc[row_tap, col_tap, 0:channels, :] = conv_ref[row_tap, col_tap]
+            tap = (3 * row_tap + col_tap) * LANES
+            wc[tap : tap + channels, :] = conv_ref[row_tap, col_tap]
 
     mark_lanes(normed, (slice(0, rows), slice(0, cols)), (rows, cols), channels, 0.0)
     gain1 = gain1_ref[...]
@@ -159,15 +184,12 @@
     low = (inverse - high.astype(F32)).astype(BF16)
     heads_out = (raw * (dot(high, spread) + dot(low, spread))).astype(BF16)
     attended = dot(heads_out, wp[...]).astype(BF16).astype(F32)
-    conv_sum = None
-    for row_tap in range(3):
-        for col_tap in range(3):
-            term = dot(pieces(row_tap, col_tap), wc[row_tap, col_tap])
-            conv_sum = term if conv_sum is None else conv_sum + term
+    taps = [pieces(row_tap, col_tap) for row_tap in range(3) for col_tap in range(3)]
+    conv_sum = dot(jnp.concatenate(taps, axis=1), wc[...])
     state1 = image + attended + conv_sum
     normed2 = layer_norm(state1, gain2).astype(BF16)
     hidden = dot(normed2, fc1[...])
-    hidden = (0.5 * hidden * (1.0 + lax.erf(hidden * math.sqrt(0.5)))).astype(BF16)
+    hidden = gelu(hidden).astype(BF16)
     return state1 + dot_nt(hidden, fc2[...])
 
 
@@ -299,20 +321,32 @@
         out_ref[r : r + band] = whole.astype(BF16)
 
 
-def from_neighbour(block, axis, step):
-    count = lax.axis_size(axis)
-    pairs = [(i, i + step) for i in range(count) if 0 <= i + step < count]
-    return lax.ppermute(block, axis, pairs)
-
-
-def call(kernel, name, outs, scratch, flops, operands):
+def swap(low, high, axis):
+    count, place = lax.axis_size(axis), lax.axis_index(axis)
+    even = lax.rem(place, 2) == 0
+
+    def pairs(first):
+        after = {i: i + 1 for i in range(first, count - 1, 2)}
+        before = {j: i for i, j in after.items()}
+        return [(i, after.get(i, before.get(i, i))) for i in range(count)]
+
+    one = lax.ppermute(jnp.where(even, high, low), axis, pairs(0))
+    other = lax.ppermute(jnp.where(even, low, high), axis, pairs(1))
+    zero = jnp.zeros_like(one)
+    before = jnp.where(place == 0, zero, jnp.where(even, other, one))
+    after = jnp.where(place == count - 1, zero, jnp.where(even, one, other))
+    return before, after
+
+
+def call(kernel, name, outs, scratch, flops, operands, in_hbm=()):
     vmem = pl.BlockSpec(memory_space=pltpu.VMEM)
+    hbm = pl.BlockSpec(memory_space=pltpu.HBM)
     return pl.pallas_call(
         kernel,
         out_shape=[jax.ShapeDtypeStruct(shape, kind) for shape, kind in outs],
-        in_specs=[vmem] * len(operands),
+        in_specs=[hbm if i in in_hbm else vmem for i in range(len(operands))],
         out_specs=[vmem] * len(outs),
-        scratch_shapes=[pltpu.VMEM(shape, kind) for shape, kind in scratch],
+        scratch_shapes=[pltpu.VMEM(*s) if isinstance(s, tuple) else s for s in scratch],
         cost_estimate=pl.CostEstimate(flops=flops, bytes_accessed=4_000_000, transcendentals=1_000_000),
         compiler_params=pltpu.CompilerParams(vmem_limit_bytes=24 * 1024 * 1024),
         name=name,
@@ -326,9 +360,8 @@
     rows, cols, channels = image.shape
     tall, wide = rows + 2 * SHIFT, cols - 2 * SHIFT
     gain1, gain2, fc2 = norm1_gain[None], norm2_gain[None], fc2_weight.T
-    top = from_neighbour(image[rows - SHIFT :], "row", 1)
-    bottom = from_neighbour(image[:SHIFT], "row", -1)
-    bias, normed, q_mid, q_left, q_right, kv_mid, wkv, wp, wc = call(
+    top, bottom = swap(image[:SHIFT], image[rows - SHIFT :], "row")
+    bias, normed, q_mid, q_left, q_right, kv_mid, wkv, wp, wc, first_cols, last_cols = call(
         own_kernel,
         "own_tile",
         [
@@ -340,16 +373,22 @@
             ((rows, wide, 2 * LANES), BF16),
             ((LANES, 2 * LANES), BF16),
             ((LANES, channels), BF16),
-            ((3, 3, LANES, channels), BF16),
+            ((9 * LANES, channels), BF16),
+            ((rows, SHIFT, channels), BF16),
+            ((rows, SHIFT, channels), BF16),
         ],
-        [((8, 1024), F32), ((4, 8 * WIN, 128), F32), ((LANES, LANES), BF16)],
+        [
+            ((8, 1024), F32), ((4, 8 * WIN, 128), F32), ((LANES, LANES), BF16),
+            (rel_table.T.shape, F32), (image.shape, BF16), (qkv_weight.shape, BF16),
+            (proj_weight.shape, BF16), (conv_weight.shape, BF16), pltpu.SemaphoreType.DMA((5,)),
+        ],
         2_000_000_000,
         (image, gain1, qkv_weight, proj_weight, rel_table.T, conv_weight),
-    )
-    left_part = jnp.concatenate([top[:, cols - SHIFT :], image[:, cols - SHIFT :], bottom[:, cols - SHIFT :]])
-    right_part = jnp.concatenate([top[:, :SHIFT], image[:, :SHIFT], bottom[:, :SHIFT]])
-    left = from_neighbour(left_part, "col", 1)
-    right = from_neighbour(right_part, "col", -1)
+        (0, 2, 3, 4, 5),
+    )
+    first_part = jnp.concatenate([top[:, :SHIFT], first_cols, bottom[:, :SHIFT]])
+    last_part = jnp.concatenate([top[:, cols - SHIFT :], last_cols, bottom[:, cols - SHIFT :]])
+    left, right = swap(first_part, last_part, "col")
     (middle,) = call(
         middle_kernel,
         "middle_columns",

time: 32.9 us -> 40.7 us (1.24)
  the two profiles are of different devices: /device:TPU:5 before, /device:TPU:0 now
where the time goes in v3:
time: 40.7 us; the launch traced here: 40.1 us
  Pallas kernels  13.6 us (33%)
  local copies, waits for them, and re-layouts  13.3 us (33%)
  starting transfers between devices  10.1 us (25%)
  other arithmetic  2.91 us (7%)
    pallas_call x3, Pallas kernels, call(): pl.pallas_call(kernel, out_shape=[jax.ShapeDtypeStruct(shape, kind) for s...  13.6 us
    unnamed x44, local copies, waits for them, and re-layouts  13.3 us
    ppermute x2, starting transfers between devices, swap(): one = lax.ppermute(jnp.where(even, high, low), axis, pairs(0))  7.26 us
    ppermute x2, starting transfers between devices, swap(): other = lax.ppermute(jnp.where(even, low, high), axis, pairs(1))  2.81 us
    select_n x2, other arithmetic, swap(): one = lax.ppermute(jnp.where(even, high, low), axis, pairs(0))  1.78 us
    select_n x2, other arithmetic, swap(): after = jnp.where(place == count - 1, zero, jnp.where(even, one, other))  1.12 us
  transfers between devices with their start and end apart: 4, of which 0 were waited for; matrix products, arithmetic and copies ran while one was open for 0% of the time, Pallas kernels for 19%

profile of v3, /device:TPU:0, one launch (start us, length us, event | category | flops | bytes accessed | tf_op | source)
XLA Modules:
  0.0 40.1 jit_solution(16477383346721298709)
XLA Ops:
  0.0 1.7 %broadcast_select_fusion.2 = (bf16[8,32,180]{2,1,0:T(8,128)(2,1)}, bf16[8,32,180]{2,1,0:T(8,128)(2,1)}) fusion(pred[]{:T(512)S(6)} %eq.19, bf16[32,32,180]{2,1,0:T(8,128)(2,1)} %image_ref.3), kind=kLoop, calls=%fused_computation.8 | loop fusion | flops 92160 | bytes 368641 | tf_op jit(solution)/shard_map/jit(_where)/select_n | solution.py:333
  1.7 2.1 %collective-permute-start = (bf16[8,32,180]{2,1,0:T(8,128)(2,1)}, bf16[8,32,180]{2,1,0:T(8,128)(2,1)}, u32[]{:S(2)}, u32[]{:S(2)}) collective-permute-start(bf16[8,32,180]{2,1,0:T(8,128)(2,1)} %get-tuple-element.28), channel_id=1, source_target_pairs={{0,0},{8,16},{16,8},{24,24},{1,1},{9,17},{17,9},{25,25},{2,2},{10,... | collective-permute-start | bytes 276488 | tf_op jit(solution)/shard_map/ppermute | solution.py:334
  3.8 4.3 %collective-permute-start.1 = (bf16[8,32,180]{2,1,0:T(8,128)(2,1)}, bf16[8,32,180]{2,1,0:T(8,128)(2,1)}, u32[]{:S(2)}, u32[]{:S(2)}) collective-permute-start(bf16[8,32,180]{2,1,0:T(8,128)(2,1)} %get-tuple-element.27), channel_id=1, source_target_pairs={{0,8},{8,0},{16,24},{24,16},{1,9},{9,1},{17,25},{25,17},{2,10},{10... | collective-permute-start | bytes 276488 | tf_op jit(solution)/shard_map/ppermute | solution.py:333
  8.1 1.0 %copy-done = bf16[32,32,180]{2,1,0:T(8,128)(2,1)S(1)} copy-done((bf16[32,32,180]{2,1,0:T(8,128)(2,1)S(1)}, bf16[32,32,180]{2,1,0:T(8,128)(2,1)}, u32[]{:S(2)}) %copy-start) | copy-done | bytes 368664
  9.1 1.2 %copy-done.2 = bf16[3,3,180,180]{3,2,1,0:T(8,128)(2,1)S(1)} copy-done((bf16[3,3,180,180]{3,2,1,0:T(8,128)(2,1)S(1)}, bf16[3,3,180,180]{3,2,1,0:T(8,128)(2,1)}, u32[]{:S(2)}) %copy-start.2) | copy-done | bytes 583224
  10.3 0.9 %copy-done.3 = bf16[180,540]{1,0:T(8,128)(2,1)S(1)} copy-done((bf16[180,540]{1,0:T(8,128)(2,1)S(1)}, bf16[180,540]{1,0:T(8,128)(2,1)}, u32[]{:S(2)}) %copy-start.3) | copy-done | bytes 194424
  11.2 0.9 %copy-done.6 = bf16[180,180]{1,0:T(8,128)(2,1)S(1)} copy-done((bf16[180,180]{1,0:T(8,128)(2,1)S(1)}, bf16[180,180]{1,0:T(8,128)(2,1)}, u32[]{:S(2)}) %copy-start.6) | copy-done | bytes 64824
  12.1 0.8 %copy-done.7 = f32[961,6]{0,1:T(8,128)S(1)} copy-done((f32[961,6]{0,1:T(8,128)S(1)}, f32[961,6]{0,1:T(8,128)}, u32[]{:S(2)}) %copy-start.7) | copy-done | bytes 23088
  12.9 0.7 %copy-done.8 = f32[180]{0:T(256)S(1)} copy-done((f32[180]{0:T(256)S(1)}, f32[180]{0:T(256)}, u32[]{:S(2)}) %copy-start.8) | copy-done | bytes 744
  13.6 3.0 %own_tile.1 = (f32[6,16,16,256]{3,2,1,0:T(8,128)S(1)}, f32[32,32,256]{2,1,0:T(8,128)S(1)}, f32[32,16,256]{2,1,0:T(8,128)S(1)}, f32[32,8,256]{2,1,0:T(8,128)S(1)}...) custom-call(bf16[32,32,180]{2,1,0:T(8,128)(2,1)S(1)} %copy-done, ...), custom_call_target="tpu_custom_call" | custom-call | flops 2000000000 | bytes 4000000 | tf_op jit(solution)/shard_map/own_tile/pallas_call | solution.py:344
  16.6 1.0 %copy-done.11 = bf16[2304,180]{1,0:T(8,128)(2,1)} copy-done((bf16[2304,180]{1,0:T(8,128)(2,1)}, bf16[2304,180]{1,0:T(8,128)(2,1)S(1)}, u32[]{:S(2)}) %copy-start.11) | copy-done | bytes 829464
  17.6 1.0 %copy-done.14 = f32[32,32,256]{2,1,0:T(8,128)} copy-done((f32[32,32,256]{2,1,0:T(8,128)}, f32[32,32,256]{2,1,0:T(8,128)S(1)}, u32[]{:S(2)}) %copy-start.14) | copy-done | bytes 1048600
  18.6 0.6 %copy-done.16 = bf16[256,180]{1,0:T(8,128)(2,1)} copy-done((bf16[256,180]{1,0:T(8,128)(2,1)}, bf16[256,180]{1,0:T(8,128)(2,1)S(1)}, u32[]{:S(2)}) %copy-start.16) | copy-done | bytes 92184
  19.2 0.8 %copy-done.18 = f32[32,16,256]{2,1,0:T(8,128)} copy-done((f32[32,16,256]{2,1,0:T(8,128)}, f32[32,16,256]{2,1,0:T(8,128)S(1)}, u32[]{:S(2)}) %copy-start.18) | copy-done | bytes 524312
  20.0 0.8 %copy-done.20 = bf16[32,16,512]{2,1,0:T(8,128)(2,1)} copy-done((bf16[32,16,512]{2,1,0:T(8,128)(2,1)}, bf16[32,16,512]{2,1,0:T(8,128)(2,1)S(1)}, u32[]{:S(2)}) %copy-start.20) | copy-done | bytes 524312
  20.9 1.1 %select_select_fusion.2 = (bf16[8,32,180]{2,1,0:T(8,128)(2,1)S(1)}, bf16[8,32,180]{2,1,0:T(8,128)(2,1)S(1)}) fusion(bf16[8,32,180]{2,1,0:T(8,128)(2,1)} %collective-permute-done.1, bf16[8,32,180]{2,1,0:T(8,128)(2,1)} %collective-permute-done, pred[]{:T(512)S(6)} %eq.20, pred[]{:T(512)S(6)} %eq.19, pred[]{:T(512)S(6)} %eq.18), kind=kLoop, calls=%fused_computation.6 | loop fusion | flops 184320 | bytes 368643 | tf_op jit(solution)/shard_map/jit(_where)/select_n | solution.py:337
  22.0 0.1 broadcast_select_fusion
  22.1 0.7 %collective-permute-start.2 = (bf16[48,8,180]{2,1,0:T(8,128)(2,1)S(1)}, bf16[48,8,180]{2,1,0:T(8,128)(2,1)S(1)}, u32[]{:S(2)}, u32[]{:S(2)}) collective-permute-start(bf16[48,8,180]{2,1,0:T(8,128)(2,1)S(1)} %get-tuple-element.32), channel_id=1, source_target_pairs={{0,0},{1,2},{2,1},{3,4},{4,3},{5,6},{6,5},{7,7},{8,8},{9,10},{10,9... | collective-permute-start | bytes 414728 | tf_op jit(solution)/shard_map/ppermute | solution.py:334
  22.8 3.0 %collective-permute-start.3 = (bf16[48,8,180]{2,1,0:T(8,128)(2,1)S(1)}, bf16[48,8,180]{2,1,0:T(8,128)(2,1)S(1)}, u32[]{:S(2)}, u32[]{:S(2)}) collective-permute-start(bf16[48,8,180]{2,1,0:T(8,128)(2,1)S(1)} %get-tuple-element.31), channel_id=1, source_target_pairs={{0,1},{1,0},{2,3},{3,2},{4,5},{5,4},{6,7},{7,6},{8,9},{9,8},{10,11... | collective-permute-start | bytes 414728 | tf_op jit(solution)/shard_map/ppermute | solution.py:333
  25.8 1.3 %copy-done.12 = bf16[2304,180]{1,0:T(8,128)(2,1)S(1)} copy-done((bf16[2304,180]{1,0:T(8,128)(2,1)S(1)}, bf16[2304,180]{1,0:T(8,128)(2,1)}, u32[]{:S(2)}) %copy-start.12) | copy-done | bytes 829464
  27.1 1.2 %copy-done.15 = f32[32,32,256]{2,1,0:T(8,128)S(1)} copy-done((f32[32,32,256]{2,1,0:T(8,128)S(1)}, f32[32,32,256]{2,1,0:T(8,128)}, u32[]{:S(2)}) %copy-start.15) | copy-done | bytes 1048600
  28.3 1.0 %copy-done.21 = bf16[32,16,512]{2,1,0:T(8,128)(2,1)S(1)} copy-done((bf16[32,16,512]{2,1,0:T(8,128)(2,1)S(1)}, bf16[32,16,512]{2,1,0:T(8,128)(2,1)}, u32[]{:S(2)}) %copy-start.21) | copy-done | bytes 524312
  29.4 4.6 %middle_columns.1.middle_ref = f32[32,16,180]{2,1,0:T(8,128)S(1)} custom-call(bf16[32,32,180]{2,1,0:T(8,128)(2,1)S(1)} %copy-done.1, bf16[8,32,180]{2,1,0:T(8,128)(2,1)S(1)} %get-tuple-element.34.top_ref, bf16[8,32,180]{2,1,0:T(8,128)(2,1)S(1)} %get-tuple-element.33.bottom_ref, f32[1,180]{1,0:T(1,128)S(1)} %bitcast.8, f32[1,180]{1,0:T(1,128)S(1)} %bitcast.10, ...), custom_call_target="tpu_custom_call" | custom-call | flops 2000000000 | bytes 4000000 | tf_op jit(solution)/shard_map/middle_columns/pallas_call | solution.py:344
  34.1 6.0 %side_columns.1 = bf16[32,32,180]{2,1,0:T(8,128)(2,1)} custom-call(bf16[32,32,180]{2,1,0:T(8,128)(2,1)S(1)} %copy-done.1, bf16[8,32,180]{2,1,0:T(8,128)(2,1)S(1)} %get-tuple-element.34.top_ref, bf16[8,32,180]{2,1,0:T(8,128)(2,1)S(1)} %get-tuple-element.33.bottom_ref, bf16[48,8,180]{2,1,0:T(8,128)(2,1)S(1)} %get-tuple-element.30.left_ref, ...), custom_call_target="tpu_custom_call" | custom-call | flops 2000000000 | bytes 4000000 | tf_op jit(solution)/shard_map/side_columns/pallas_call | solution.py:344
  (36 shorter events, 0.1 us)
Async XLA Ops:
  1.7 19.2 %collective-permute-start = (bf16[8,32,180]{2,1,0:T(8,128)(2,1)}, bf16[8,32,180]{2,1,0:T(8,128)(2,1)}, u32[]{:S(2)}, u32[]{:S(2)}) collective-permute-start(bf16[8,32,180]{2,1,0:T(8,128)(2,1)} %get-tuple-element.28), channel_id=1, source_target_pairs={{0,0},{8,16},{16,8},{24,24},{1,1},{9,17},{17,9},{25,25},{2,2},{10,... | collective-permute-start | bytes 276488 | tf_op jit(solution)/shard_map/ppermute | solution.py:334
  3.8 17.0 %collective-permute-start.1 = (bf16[8,32,180]{2,1,0:T(8,128)(2,1)}, bf16[8,32,180]{2,1,0:T(8,128)(2,1)}, u32[]{:S(2)}, u32[]{:S(2)}) collective-permute-start(bf16[8,32,180]{2,1,0:T(8,128)(2,1)} %get-tuple-element.27), channel_id=1, source_target_pairs={{0,8},{8,0},{16,24},{24,16},{1,9},{9,1},{17,25},{25,17},{2,10},{10... | collective-permute-start | bytes 276488 | tf_op jit(solution)/shard_map/ppermute | solution.py:333
  8.1 1.0 %copy-start = (bf16[32,32,180]{2,1,0:T(8,128)(2,1)S(1)}, bf16[32,32,180]{2,1,0:T(8,128)(2,1)}, u32[]{:S(2)}) copy-start(bf16[32,32,180]{2,1,0:T(8,128)(2,1)} %image_ref.3) | copy-start | bytes 1105924
  9.1 1.2 %copy-start.2 = (bf16[3,3,180,180]{3,2,1,0:T(8,128)(2,1)S(1)}, bf16[3,3,180,180]{3,2,1,0:T(8,128)(2,1)}, u32[]{:S(2)}) copy-start(bf16[3,3,180,180]{3,2,1,0:T(8,128)(2,1)} %conv_hbm.1) | copy-start | bytes 1749604
  10.3 0.9 %copy-start.3 = (bf16[180,540]{1,0:T(8,128)(2,1)S(1)}, bf16[180,540]{1,0:T(8,128)(2,1)}, u32[]{:S(2)}) copy-start(bf16[180,540]{1,0:T(8,128)(2,1)} %qkv_hbm.1) | copy-start | bytes 583204
  11.2 0.9 %copy-start.6 = (bf16[180,180]{1,0:T(8,128)(2,1)S(1)}, bf16[180,180]{1,0:T(8,128)(2,1)}, u32[]{:S(2)}) copy-start(bf16[180,180]{1,0:T(8,128)(2,1)} %proj_hbm.1) | copy-start | bytes 194404
  12.1 0.8 %copy-start.7 = (f32[961,6]{0,1:T(8,128)S(1)}, f32[961,6]{0,1:T(8,128)}, u32[]{:S(2)}) copy-start(f32[961,6]{0,1:T(8,128)} %param.14) | copy-start | bytes 69196
  16.6 1.0 %copy-start.11 = (bf16[2304,180]{1,0:T(8,128)(2,1)}, bf16[2304,180]{1,0:T(8,128)(2,1)S(1)}, u32[]{:S(2)}) copy-start(bf16[2304,180]{1,0:T(8,128)(2,1)S(1)} %get-tuple-element.24.wc) | copy-start | bytes 2488324
  17.6 1.0 %copy-start.14 = (f32[32,32,256]{2,1,0:T(8,128)}, f32[32,32,256]{2,1,0:T(8,128)S(1)}, u32[]{:S(2)}) copy-start(f32[32,32,256]{2,1,0:T(8,128)S(1)} %get-tuple-element.19.normed) | copy-start | bytes 3145732
  19.2 0.8 %copy-start.18 = (f32[32,16,256]{2,1,0:T(8,128)}, f32[32,16,256]{2,1,0:T(8,128)S(1)}, u32[]{:S(2)}) copy-start(f32[32,16,256]{2,1,0:T(8,128)S(1)} %get-tuple-element.25.q_mid) | copy-start | bytes 1572868
  20.0 0.8 %copy-start.20 = (bf16[32,16,512]{2,1,0:T(8,128)(2,1)}, bf16[32,16,512]{2,1,0:T(8,128)(2,1)S(1)}, u32[]{:S(2)}) copy-start(bf16[32,16,512]{2,1,0:T(8,128)(2,1)S(1)} %get-tuple-element.26.kv_mid) | copy-start | bytes 1572868
  20.8 5.0 %copy-start.1 = (bf16[32,32,180]{2,1,0:T(8,128)(2,1)S(1)}, bf16[32,32,180]{2,1,0:T(8,128)(2,1)}, u32[]{:S(2)}) copy-start(bf16[32,32,180]{2,1,0:T(8,128)(2,1)} %image_ref.3) | copy-start | bytes 1105924
  20.8 5.0 %copy-start.4 = (bf16[180,360]{1,0:T(8,128)(2,1)S(1)}, bf16[180,360]{1,0:T(8,128)(2,1)}, u32[]{:S(2)}) copy-start(bf16[180,360]{1,0:T(8,128)(2,1)} %fc1_ref.3) | copy-start | bytes 388804
  20.8 5.0 %copy-start.5 = (bf16[360,180]{0,1:T(8,128)(2,1)S(1)}, bf16[360,180]{0,1:T(8,128)(2,1)}, u32[]{:S(2)}) copy-start(bf16[360,180]{0,1:T(8,128)(2,1)} %param.17) | copy-start | bytes 388804
  20.8 5.0 %copy-start.9 = (f32[180]{0:T(256)S(1)}, f32[180]{0:T(256)}, u32[]{:S(2)}) copy-start(f32[180]{0:T(256)} %param.10) | copy-start | bytes 2164
  20.8 5.0 %copy-start.10 = (f32[180]{0:T(256)S(1)}, f32[180]{0:T(256)}, u32[]{:S(2)}) copy-start(f32[180]{0:T(256)} %param.11) | copy-start | bytes 2164
  20.8 5.0 %copy-start.17 = (bf16[256,180]{1,0:T(8,128)(2,1)S(1)}, bf16[256,180]{1,0:T(8,128)(2,1)}, u32[]{:S(2)}) copy-start(bf16[256,180]{1,0:T(8,128)(2,1)} %copy-done.16) | copy-start | bytes 276484
  20.9 5.0 %copy-start.19 = (f32[32,16,256]{2,1,0:T(8,128)S(1)}, f32[32,16,256]{2,1,0:T(8,128)}, u32[]{:S(2)}) copy-start(f32[32,16,256]{2,1,0:T(8,128)} %copy-done.18) | copy-start | bytes 1572868
  22.1 11.9 %collective-permute-start.2 = (bf16[48,8,180]{2,1,0:T(8,128)(2,1)S(1)}, bf16[48,8,180]{2,1,0:T(8,128)(2,1)S(1)}, u32[]{:S(2)}, u32[]{:S(2)}) collective-permute-start(bf16[48,8,180]{2,1,0:T(8,128)(2,1)S(1)} %get-tuple-element.32), channel_id=1, source_target_pairs={{0,0},{1,2},{2,1},{3,4},{4,3},{5,6},{6,5},{7,7},{8,8},{9,10},{10,9... | collective-permute-start | bytes 414728 | tf_op jit(solution)/shard_map/ppermute | solution.py:334
  22.8 11.2 %collective-permute-start.3 = (bf16[48,8,180]{2,1,0:T(8,128)(2,1)S(1)}, bf16[48,8,180]{2,1,0:T(8,128)(2,1)S(1)}, u32[]{:S(2)}, u32[]{:S(2)}) collective-permute-start(bf16[48,8,180]{2,1,0:T(8,128)(2,1)S(1)} %get-tuple-element.31), channel_id=1, source_target_pairs={{0,1},{1,0},{2,3},{3,2},{4,5},{5,4},{6,7},{7,6},{8,9},{9,8},{10,11... | collective-permute-start | bytes 414728 | tf_op jit(solution)/shard_map/ppermute | solution.py:333
  25.8 1.3 %copy-start.12 = (bf16[2304,180]{1,0:T(8,128)(2,1)S(1)}, bf16[2304,180]{1,0:T(8,128)(2,1)}, u32[]{:S(2)}) copy-start(bf16[2304,180]{1,0:T(8,128)(2,1)} %copy-done.11) | copy-start | bytes 2488324
  27.1 1.2 %copy-start.15 = (f32[32,32,256]{2,1,0:T(8,128)S(1)}, f32[32,32,256]{2,1,0:T(8,128)}, u32[]{:S(2)}) copy-start(f32[32,32,256]{2,1,0:T(8,128)} %copy-done.14) | copy-start | bytes 3145732
  28.3 1.0 %copy-start.21 = (bf16[32,16,512]{2,1,0:T(8,128)(2,1)S(1)}, bf16[32,16,512]{2,1,0:T(8,128)(2,1)}, u32[]{:S(2)}) copy-start(bf16[32,16,512]{2,1,0:T(8,128)(2,1)} %copy-done.20) | copy-start | bytes 1572868
  29.4 4.7 %copy-start.13 = (bf16[2304,180]{1,0:T(8,128)(2,1)S(1)}, bf16[2304,180]{1,0:T(8,128)(2,1)}, u32[]{:S(2)}) copy-start(bf16[2304,180]{1,0:T(8,128)(2,1)} %copy-done.11) | copy-start | bytes 2488324
  (2 other events, 1.3 us)

commit v4 on v3

--- a/solution.py
+++ b/solution.py
@@ -88,9 +88,9 @@
 
 
 def own_kernel(
-    image_hbm, gain1_ref, qkv_hbm, proj_hbm, table_hbm, conv_hbm,
+    image_hbm, gain1_hbm, qkv_hbm, proj_hbm, table_hbm, conv_hbm,
     bias, normed, q_mid, q_left, q_right, kv_mid, wkv, wp, wc, first_cols, last_cols,
-    padded, strip, wq, table_ref, image_ref, qkv_ref, proj_ref, conv_ref, sems,
+    padded, strip, wq, table_ref, image_ref, gain1_ref, qkv_ref, proj_ref, conv_ref, sems,
 ):
     rows, cols, channels = image_ref.shape
     head_dim = channels // HEADS
@@ -98,7 +98,7 @@
     fetches = [
         pltpu.make_async_copy(source, target, sems.at[i])
         for i, (source, target) in enumerate(
-            ((table_hbm, table_ref), (image_hbm, image_ref), (qkv_hbm, qkv_ref),
+            ((table_hbm, table_ref), (image_hbm, image_ref), (gain1_hbm, gain1_ref), (qkv_hbm, qkv_ref),
              (proj_hbm, proj_ref), (conv_hbm, conv_ref))
         )
     ]
@@ -208,7 +208,8 @@
         mark_lanes(
             bands, (i, slice(0, SHIFT), slice(0, cols)), (SHIFT, cols), channels, (row == edge).astype(F32)
         )
-        bands[i, :, :, 0:channels] = layer_norm(ref[...].astype(F32), gain1)
+        inside = gain1 * (row != edge).astype(F32)
+        bands[i, :, :, 0:channels] = layer_norm(ref[...].astype(F32), inside)
         pixels = bands[i, :, SHIFT : cols - SHIFT].astype(BF16).reshape(-1, LANES)
         kv_band.append(dot(pixels, wkv[...]).astype(BF16))
 
@@ -268,15 +269,22 @@
                    out_col[s])
         mark_lanes(side, (s, slice(SHIFT + rows, tall), slice(halo, halo + SHIFT)), (SHIFT, SHIFT), channels,
                    out_col[s] + out_row[1])
-        for r in range(0, tall, WIN):
-            side[s, r : r + WIN, halo : halo + SHIFT, 0:channels] = layer_norm(
-                ref[r : r + WIN].astype(F32), gain1
+        for r in range(0, tall, SHIFT):
+            inside = gain1 * (1.0 - out_col[s])
+            if r == 0:
+                inside = inside * (1.0 - out_row[0])
+            if r == tall - SHIFT:
+                inside = inside * (1.0 - out_row[1])
+            side[s, r : r + SHIFT, halo : halo + SHIFT, 0:channels] = layer_norm(
+                ref[r : r + SHIFT].astype(F32), inside
             )
         for i, (r0, band_ref) in enumerate(((0, top_ref), (SHIFT + rows, bottom_ref))):
             values = band_ref[...].astype(F32)[:, c0 : c0 + 2 * SHIFT]
             mark_lanes(side, (s, slice(r0, r0 + SHIFT), slice(own, own + 2 * SHIFT)), (SHIFT, 2 * SHIFT),
                        channels, out_row[i])
-            side[s, r0 : r0 + SHIFT, own : own + 2 * SHIFT, 0:channels] = layer_norm(values, gain1)
+            side[s, r0 : r0 + SHIFT, own : own + 2 * SHIFT, 0:channels] = layer_norm(
+                values, gain1 * (1.0 - out_row[i])
+            )
         side[s, SHIFT : SHIFT + rows, own : own + 2 * SHIFT] = normed[:, c0 : c0 + 2 * SHIFT]
 
         k0 = 0 if s == 0 else SHIFT
@@ -321,20 +329,10 @@
         out_ref[r : r + band] = whole.astype(BF16)
 
 
-def swap(low, high, axis):
-    count, place = lax.axis_size(axis), lax.axis_index(axis)
-    even = lax.rem(place, 2) == 0
-
-    def pairs(first):
-        after = {i: i + 1 for i in range(first, count - 1, 2)}
-        before = {j: i for i, j in after.items()}
-        return [(i, after.get(i, before.get(i, i))) for i in range(count)]
-
-    one = lax.ppermute(jnp.where(even, high, low), axis, pairs(0))
-    other = lax.ppermute(jnp.where(even, low, high), axis, pairs(1))
-    zero = jnp.zeros_like(one)
-    before = jnp.where(place == 0, zero, jnp.where(even, other, one))
-    after = jnp.where(place == count - 1, zero, jnp.where(even, one, other))
+def exchange(low, high, axis):
+    count = lax.axis_size(axis)
+    before = lax.ppermute(high, axis, [(i, (i + 1) % count) for i in range(count)])
+    after = lax.ppermute(low, axis, [((i + 1) % count, i) for i in range(count)])
     return before, after
 
 
@@ -343,14 +341,14 @@
     hbm = pl.BlockSpec(memory_space=pltpu.HBM)
     return pl.pallas_call(
         kernel,
-        out_shape=[jax.ShapeDtypeStruct(shape, kind) for shape, kind in outs],
+        out_shape=[out if isinstance(out, jax.ShapeDtypeStruct) else pltpu.VMEM(*out) for out in outs],
         in_specs=[hbm if i in in_hbm else vmem for i in range(len(operands))],
         out_specs=[vmem] * len(outs),
         scratch_shapes=[pltpu.VMEM(*s) if isinstance(s, tuple) else s for s in scratch],
         cost_estimate=pl.CostEstimate(flops=flops, bytes_accessed=4_000_000, transcendentals=1_000_000),
         compiler_params=pltpu.CompilerParams(vmem_limit_bytes=24 * 1024 * 1024),
         name=name,
-    )(*operands)
+    )(*[pltpu.with_memory_space_constraint(x, pltpu.HBM) if i in in_hbm else x for i, x in enumerate(operands)])
 
 
 def on_device(
@@ -360,7 +358,7 @@
     rows, cols, channels = image.shape
     tall, wide = rows + 2 * SHIFT, cols - 2 * SHIFT
     gain1, gain2, fc2 = norm1_gain[None], norm2_gain[None], fc2_weight.T
-    top, bottom = swap(image[:SHIFT], image[rows - SHIFT :], "row")
+    top, bottom = exchange(image[:SHIFT], image[rows - SHIFT :], "row")
     bias, normed, q_mid, q_left, q_right, kv_mid, wkv, wp, wc, first_cols, last_cols = call(
         own_kernel,
         "own_tile",
@@ -379,16 +377,16 @@
         ],
         [
             ((8, 1024), F32), ((4, 8 * WIN, 128), F32), ((LANES, LANES), BF16),
-            (rel_table.T.shape, F32), (image.shape, BF16), (qkv_weight.shape, BF16),
-            (proj_weight.shape, BF16), (conv_weight.shape, BF16), pltpu.SemaphoreType.DMA((5,)),
+            (rel_table.T.shape, F32), (image.shape, BF16), (gain1.shape, F32), (qkv_weight.shape, BF16),
+            (proj_weight.shape, BF16), (conv_weight.shape, BF16), pltpu.SemaphoreType.DMA((6,)),
         ],
         2_000_000_000,
         (image, gain1, qkv_weight, proj_weight, rel_table.T, conv_weight),
-        (0, 2, 3, 4, 5),
+        (0, 1, 2, 3, 4, 5),
     )
     first_part = jnp.concatenate([top[:, :SHIFT], first_cols, bottom[:, :SHIFT]])
     last_part = jnp.concatenate([top[:, cols - SHIFT :], last_cols, bottom[:, cols - SHIFT :]])
-    left, right = swap(first_part, last_part, "col")
+    left, right = exchange(first_part, last_part, "col")
     (middle,) = call(
         middle_kernel,
         "middle_columns",
@@ -404,7 +402,7 @@
     (out,) = call(
         side_kernel,
         "side_columns",
-        [(image.shape, BF16)],
+        [jax.ShapeDtypeStruct(image.shape, BF16)],
         [
             ((2, tall, 3 * SHIFT, LANES), F32),
             ((2, tall, WIN, 2 * LANES), BF16),

time: 40.7 us -> 27.1 us (0.67); the launches traced: 40.1 us -> 27 us
  local copies, waits for them, and re-layouts: 13.3 us -> 1.02 us
  waiting for transfers between devices: 0.01 us -> 5.59 us
  starting transfers between devices: 10.1 us -> 6.29 us
  other arithmetic: 2.91 us -> 0.08 us
    unnamed x44 -> x10, local copies, waits for them, and re-layouts: 13.3 us -> 0.02 us
    ppermute x4, waiting for transfers between devices: 0.01 us -> 5.59 us  [the longest x2 3.36 us: exchange(): lax.ppermute(high, axis, [(i, (i + 1) % count) for i in range(count)])]
    ppermute x4, starting transfers between devices: 10.1 us -> 6.29 us  [the longest x2 3.24 us: exchange(): lax.ppermute(low, axis, [((i + 1) % count, i) for i in range(count)])]
    select_n x4 -> x0, other arithmetic: 2.91 us -> none  [the longest x2 1.78 us: swap(): one = lax.ppermute(jnp.where(even, high, low), axis, pairs(0))]
    slice x0 -> x2, local copies, waits for them, and re-layouts: none -> 0.99 us  [the longest x1 0.98 us: on_device(): top, bottom = exchange(image[:SHIFT], image[rows - SHIFT:], 'row')]
  transfers between devices with their start and end apart: 4 -> 4, of which waited for: 0 -> 3; matrix products, arithmetic and copies ran while one was open for 0% -> 0% of each run, Pallas kernels for 19% -> 29%
where the time goes in v4:
time: 27.1 us; the launch traced here: 27 us
  Pallas kernels  13.9 us (51%)
  starting transfers between devices  6.29 us (23%)
  waiting for transfers between devices  5.59 us (21%)
  local copies, waits for them, and re-layouts  1.02 us (4%)
    pallas_call x3, Pallas kernels, call(): pl.pallas_call(kernel, out_shape=[out if isinstance(out, jax.ShapeDtypeSt...  13.9 us
    ppermute x2, waiting for transfers between devices, exchange(): lax.ppermute(high, axis, [(i, (i + 1) % count) for i in range(count)])  3.36 us
    ppermute x2, starting transfers between devices, exchange(): lax.ppermute(low, axis, [((i + 1) % count, i) for i in range(count)])  3.24 us
    ppermute x2, starting transfers between devices, exchange(): lax.ppermute(high, axis, [(i, (i + 1) % count) for i in range(count)])  3.05 us
    ppermute x2, waiting for transfers between devices, exchange(): lax.ppermute(low, axis, [((i + 1) % count, i) for i in range(count)])  2.23 us
    slice x1, local copies, waits for them, and re-layouts, on_device(): top, bottom = exchange(image[:SHIFT], image[rows - SHIFT:], 'row')  0.98 us
  transfers between devices with their start and end apart: 4, of which 3 were waited for; matrix products, arithmetic and copies ran while one was open for 0% of the time, Pallas kernels for 29%

profile of v4, /device:TPU:0, one launch (start us, length us, event | category | flops | bytes accessed | tf_op | source)
XLA Modules:
  0.0 27.0 jit_solution(10268968657951125195)
XLA Ops:
  0.0 1.0 %fusion = (bf16[8,32,180]{2,1,0:T(8,128)(2,1)S(1)}, bf16[8,32,180]{2,1,0:T(8,128)(2,1)S(1)}) fusion(bf16[32,32,180]{2,1,0:T(8,128)(2,1)} %image_ref.3), kind=kLoop, calls=%fused_computation.2 | loop fusion | bytes 368640 | tf_op jit(solution)/shard_map/slice | solution.py:361
  1.0 3.0 %collective-permute-start = (bf16[8,32,180]{2,1,0:T(8,128)(2,1)S(1)}, bf16[8,32,180]{2,1,0:T(8,128)(2,1)S(1)}, u32[]{:S(2)}, u32[]{:S(2)}) collective-permute-start(bf16[8,32,180]{2,1,0:T(8,128)(2,1)S(1)} %get-tuple-element.28), channel_id=1, source_target_pairs={{0,8},{8,16},{16,24},{24,0},{1,9},{9,17},{17,25},{25,1},{2,10},{10... | collective-permute-start | bytes 276488 | tf_op jit(solution)/shard_map/ppermute | solution.py:334
  4.0 1.0 %collective-permute-start.1 = (bf16[8,32,180]{2,1,0:T(8,128)(2,1)S(1)}, bf16[8,32,180]{2,1,0:T(8,128)(2,1)S(1)}, u32[]{:S(2)}, u32[]{:S(2)}) collective-permute-start(bf16[8,32,180]{2,1,0:T(8,128)(2,1)S(1)} %get-tuple-element.27), channel_id=1, source_target_pairs={{8,0},{16,8},{24,16},{0,24},{9,1},{17,9},{25,17},{1,25},{10,2},{18... | collective-permute-start | bytes 276488 | tf_op jit(solution)/shard_map/ppermute | solution.py:335
  5.0 0.0 copy-start
  5.0 0.0 copy-start.1
  5.0 0.0 copy-start.2
  5.0 0.0 copy-start.3
  5.0 0.0 copy-start.4
  5.0 3.2 %own_tile.1 = (f32[6,16,16,256]{3,2,1,0:T(8,128)S(1)}, f32[32,32,256]{2,1,0:T(8,128)S(1)}, f32[32,16,256]{2,1,0:T(8,128)S(1)}, f32[32,8,256]{2,1,0:T(8,128)S(1)}...) custom-call(bf16[32,32,180]{2,1,0:T(8,128)(2,1)} %image_ref.3, ...), custom_call_target="tpu_custom_call" | custom-call | flops 2000000000 | bytes 4000000 | tf_op jit(solution)/shard_map/own_tile/pallas_call | solution.py:342
  8.3 1.0 %collective-permute-done.top_ref = bf16[8,32,180]{2,1,0:T(8,128)(2,1)S(1)} collective-permute-done((bf16[8,32,180]{2,1,0:T(8,128)(2,1)S(1)}, bf16[8,32,180]{2,1,0:T(8,128)(2,1)S(1)}, u32[]{:S(2)}, u32[]{:S(2)}) %collective-permute-start) | collective-permute-done | bytes 92192 | tf_op jit(solution)/shard_map/ppermute | solution.py:334
  9.3 2.2 %collective-permute-done.1.bottom_ref = bf16[8,32,180]{2,1,0:T(8,128)(2,1)S(1)} collective-permute-done((bf16[8,32,180]{2,1,0:T(8,128)(2,1)S(1)}, bf16[8,32,180]{2,1,0:T(8,128)(2,1)S(1)}, u32[]{:S(2)}, u32[]{:S(2)}) %collective-permute-start.1) | collective-permute-done | bytes 92192 | tf_op jit(solution)/shard_map/ppermute | solution.py:335
  11.5 2.2 %collective-permute-start.3 = (bf16[48,8,180]{2,1,0:T(8,128)(2,1)S(1)}, bf16[48,8,180]{2,1,0:T(8,128)(2,1)S(1)}, u32[]{:S(2)}, u32[]{:S(2)}) collective-permute-start(bf16[48,8,180]{2,1,0:T(8,128)(2,1)S(1)} %pad_maximum_fusion.1), channel_id=1, source_target_pairs={{1,0},{2,1},{3,2},{4,3},{5,4},{6,5},{7,6},{0,7},{9,8},{10,9},{11,1... | collective-permute-start | bytes 414728 | tf_op jit(solution)/shard_map/ppermute | solution.py:335
  13.8 0.1 collective-permute-start.2
  13.9 0.0 copy-done
  13.9 0.0 copy-done.1
  13.9 0.0 copy-done.2
  13.9 0.0 copy-done.3
  13.9 0.0 copy-done.4
  13.9 4.6 %middle_columns.1.middle_ref = f32[32,16,180]{2,1,0:T(8,128)S(1)} custom-call(bf16[32,32,180]{2,1,0:T(8,128)(2,1)S(1)} %copy-done, bf16[8,32,180]{2,1,0:T(8,128)(2,1)S(1)} %collective-permute-done.top_ref, bf16[8,32,180]{2,1,0:T(8,128)(2,1)S(1)} %collective-permute-done.1.bottom_ref, f32[1,180]{1,0:T(1,128)S(1)} %bitcast.7, f32[1,180]{1,0:T(1,128)S(1)} %bitcast.9, ...), custom_call_target="tpu_custom_call" | custom-call | flops 2000000000 | bytes 4000000 | tf_op jit(solution)/shard_map/middle_columns/pallas_call | solution.py:342
  18.6 0.0 collective-permute-done.3.right_ref
  18.6 2.4 %collective-permute-done.2.left_ref = bf16[48,8,180]{2,1,0:T(8,128)(2,1)S(1)} collective-permute-done((bf16[48,8,180]{2,1,0:T(8,128)(2,1)S(1)}, bf16[48,8,180]{2,1,0:T(8,128)(2,1)S(1)}, u32[]{:S(2)}, u32[]{:S(2)}) %collective-permute-start.2) | collective-permute-done | bytes 138272 | tf_op jit(solution)/shard_map/ppermute | solution.py:334
  21.0 6.0 %side_columns.1 = bf16[32,32,180]{2,1,0:T(8,128)(2,1)} custom-call(bf16[32,32,180]{2,1,0:T(8,128)(2,1)S(1)} %copy-done, bf16[8,32,180]{2,1,0:T(8,128)(2,1)S(1)} %collective-permute-done.top_ref, bf16[8,32,180]{2,1,0:T(8,128)(2,1)S(1)} %collective-permute-done.1.bottom_ref, bf16[48,8,180]{2,1,0:T(8,128)(2,1)S(1)} %collective-permute-done.2.left_ref, ...), custom_call_target="tpu_custom_call" | custom-call | flops 2000000000 | bytes 4000000 | tf_op jit(solution)/shard_map/side_columns/pallas_call | solution.py:342
  (4 shorter events, 0.1 us)
Async XLA Ops:
  1.0 8.3 %collective-permute-start = (bf16[8,32,180]{2,1,0:T(8,128)(2,1)S(1)}, bf16[8,32,180]{2,1,0:T(8,128)(2,1)S(1)}, u32[]{:S(2)}, u32[]{:S(2)}) collective-permute-start(bf16[8,32,180]{2,1,0:T(8,128)(2,1)S(1)} %get-tuple-element.28), channel_id=1, source_target_pairs={{0,8},{8,16},{16,24},{24,0},{1,9},{9,17},{17,25},{25,1},{2,10},{10... | collective-permute-start | bytes 276488 | tf_op jit(solution)/shard_map/ppermute | solution.py:334
  4.0 7.5 %collective-permute-start.1 = (bf16[8,32,180]{2,1,0:T(8,128)(2,1)S(1)}, bf16[8,32,180]{2,1,0:T(8,128)(2,1)S(1)}, u32[]{:S(2)}, u32[]{:S(2)}) collective-permute-start(bf16[8,32,180]{2,1,0:T(8,128)(2,1)S(1)} %get-tuple-element.27), channel_id=1, source_target_pairs={{8,0},{16,8},{24,16},{0,24},{9,1},{17,9},{25,17},{1,25},{10,2},{18... | collective-permute-start | bytes 276488 | tf_op jit(solution)/shard_map/ppermute | solution.py:335
  5.0 8.9 %copy-start = (bf16[32,32,180]{2,1,0:T(8,128)(2,1)S(1)}, bf16[32,32,180]{2,1,0:T(8,128)(2,1)}, u32[]{:S(2)}) copy-start(bf16[32,32,180]{2,1,0:T(8,128)(2,1)} %image_ref.3) | copy-start | bytes 1105924
  5.0 8.9 %copy-start.1 = (bf16[180,360]{1,0:T(8,128)(2,1)S(1)}, bf16[180,360]{1,0:T(8,128)(2,1)}, u32[]{:S(2)}) copy-start(bf16[180,360]{1,0:T(8,128)(2,1)} %fc1_ref.3) | copy-start | bytes 388804
  5.0 8.9 %copy-start.2 = (bf16[360,180]{0,1:T(8,128)(2,1)S(1)}, bf16[360,180]{0,1:T(8,128)(2,1)}, u32[]{:S(2)}) copy-start(bf16[360,180]{0,1:T(8,128)(2,1)} %param.17) | copy-start | bytes 388804
  5.0 8.9 %copy-start.3 = (f32[180]{0:T(256)S(1)}, f32[180]{0:T(256)}, u32[]{:S(2)}) copy-start(f32[180]{0:T(256)} %param.10) | copy-start | bytes 2164
  5.0 8.9 %copy-start.4 = (f32[180]{0:T(256)S(1)}, f32[180]{0:T(256)}, u32[]{:S(2)}) copy-start(f32[180]{0:T(256)} %param.11) | copy-start | bytes 2164
  11.5 7.0 %collective-permute-start.3 = (bf16[48,8,180]{2,1,0:T(8,128)(2,1)S(1)}, bf16[48,8,180]{2,1,0:T(8,128)(2,1)S(1)}, u32[]{:S(2)}, u32[]{:S(2)}) collective-permute-start(bf16[48,8,180]{2,1,0:T(8,128)(2,1)S(1)} %pad_maximum_fusion.1), channel_id=1, source_target_pairs={{1,0},{2,1},{3,2},{4,3},{5,4},{6,5},{7,6},{0,7},{9,8},{10,9},{11,1... | collective-permute-start | bytes 414728 | tf_op jit(solution)/shard_map/ppermute | solution.py:335
  13.8 7.1 %collective-permute-start.2 = (bf16[48,8,180]{2,1,0:T(8,128)(2,1)S(1)}, bf16[48,8,180]{2,1,0:T(8,128)(2,1)S(1)}, u32[]{:S(2)}, u32[]{:S(2)}) collective-permute-start(bf16[48,8,180]{2,1,0:T(8,128)(2,1)S(1)} %pad_maximum_fusion), channel_id=1, source_target_pairs={{0,1},{1,2},{2,3},{3,4},{4,5},{5,6},{6,7},{7,0},{8,9},{9,10},{10,1... | collective-permute-start | bytes 414728 | tf_op jit(solution)/shard_map/ppermute | solution.py:334

commit v5 on v4

--- a/solution.py
+++ b/solution.py
@@ -330,9 +330,14 @@
 
 
 def exchange(low, high, axis):
-    count = lax.axis_size(axis)
-    before = lax.ppermute(high, axis, [(i, (i + 1) % count) for i in range(count)])
-    after = lax.ppermute(low, axis, [((i + 1) % count, i) for i in range(count)])
+    count, place = lax.axis_size(axis), lax.axis_index(axis)
+    even = lax.rem(place, 2) == 0
+    inner = [[i, i + 1] for i in range(0, count, 2)]
+    outer = [[i, (i + 1) % count] for i in range(1, count, 2)]
+    one = lax.all_gather(jnp.where(even, high, low), axis, axis_index_groups=inner)
+    other = lax.all_gather(jnp.where(even, low, high), axis, axis_index_groups=outer)
+    before = jnp.where(even, other[0], one[0])
+    after = jnp.where(even, one[1], other[1])
     return before, after
 
 

time: 27.1 us -> 43.3 us (1.60)
  blocking collectives: 0 us -> 24.9 us
  starting transfers between devices: 6.29 us -> 0 us
  waiting for transfers between devices: 5.59 us -> 0 us
  other arithmetic: 0.08 us -> 2.06 us
  local copies, waits for them, and re-layouts: 1.02 us -> 2.09 us
    all_gather x0 -> x4, blocking collectives: none -> 24.9 us  [the longest x2 17.2 us: exchange(): lax.all_gather(jnp.where(even, low, high), axis, axis_index_groups=outer)]
    ppermute x4 -> x0, starting transfers between devices: 6.29 us -> none  [the longest x2 3.24 us: exchange(): lax.ppermute(low, axis, [((i + 1) % count, i) for i in range(count)])]
    ppermute x4 -> x0, waiting for transfers between devices: 5.59 us -> none  [the longest x2 3.36 us: exchange(): lax.ppermute(high, axis, [(i, (i + 1) % count) for i in range(count)])]
    select_n x0 -> x4, other arithmetic: none -> 2.06 us  [the longest x2 1.99 us: exchange(): jnp.where(even, low, high)]
    unnamed x10 -> x34, local copies, waits for them, and re-layouts: 0.02 us -> 1.47 us
    slice x3 -> x0, local copies, waits for them, and re-layouts: 1 us -> none  [the longest x1 0.98 us: on_device(): top, bottom = exchange(image[:SHIFT], image[rows - SHIFT:], 'row')]
    concatenate x0 -> x1, local copies, waits for them, and re-layouts: none -> 0.61 us  [on_device(): jnp.concatenate([top[:, :SHIFT], first_cols, bottom[:, :SHIFT]])]
  transfers between devices with their start and end apart: 4 -> 0, of which waited for: 3 -> 0; matrix products, arithmetic and copies ran while one was open for 0% -> 0% of each run, Pallas kernels for 29% -> 0%
where the time goes in v5:
time: 43.3 us; the launch traced here: 43.2 us
  blocking collectives  24.9 us (58%)
  Pallas kernels  13.8 us (32%)
  local copies, waits for them, and re-layouts  2.09 us (5%)
  other arithmetic  2.06 us (5%)
    all_gather x2, blocking collectives, exchange(): lax.all_gather(jnp.where(even, low, high), axis, axis_index_groups=outer)  17.2 us
    pallas_call x3, Pallas kernels, call(): pl.pallas_call(kernel, out_shape=[out if isinstance(out, jax.ShapeDtypeSt...  13.8 us
    all_gather x2, blocking collectives, exchange(): lax.all_gather(jnp.where(even, high, low), axis, axis_index_groups=inner)  7.71 us
    select_n x2, other arithmetic, exchange(): jnp.where(even, low, high)  1.99 us
    unnamed x34, local copies, waits for them, and re-layouts  1.47 us

profile of v5, /device:TPU:0, one launch (start us, length us, event | category | flops | bytes accessed | tf_op | source)
XLA Modules:
  0.0 43.2 jit_solution(7340864869279490984)
XLA Ops:
  0.0 1.0 %broadcast_select_fusion.3 = (bf16[8,32,180]{2,1,0:T(8,128)(2,1)S(1)}, bf16[8,32,180]{2,1,0:T(8,128)(2,1)S(1)}) fusion(pred[]{:T(512)S(6)} %eq.6, bf16[32,32,180]{2,1,0:T(8,128)(2,1)} %image_ref.3), kind=kLoop, calls=%fused_computation.11 | loop fusion | flops 92160 | bytes 368641 | tf_op jit(solution)/shard_map/jit(_where)/select_n | solution.py:338
  1.0 8.0 %all-gather = bf16[16,32,180]{2,1,0:T(8,128)(2,1)S(1)} all-gather(bf16[8,32,180]{2,1,0:T(8,128)(2,1)S(1)} %get-tuple-element.31), channel_id=2, replica_groups={{8,16},{24,0},{9,17},{25,1},{10,18},{26,2},{11,19},{27,3},{12,20},{28,4..., dimensions={0}, use_global_device_ids=true | all-gather | bytes 276480 | tf_op jit(solution)/shard_map/all_gather | solution.py:338
  9.0 5.6 %all-gather.1 = bf16[16,32,180]{2,1,0:T(8,128)(2,1)S(1)} all-gather(bf16[8,32,180]{2,1,0:T(8,128)(2,1)S(1)} %get-tuple-element.32), channel_id=3, replica_groups={{0,8},{16,24},{1,9},{17,25},{2,10},{18,26},{3,11},{19,27},{4,12},{20,28..., dimensions={0}, use_global_device_ids=true | all-gather | bytes 276480 | tf_op jit(solution)/shard_map/all_gather | solution.py:337
  14.7 0.0 copy-start
  14.7 0.0 copy-start.1
  14.7 0.0 copy-start.2
  14.7 0.0 copy-start.3
  14.8 0.0 copy-start.4
  14.8 3.2 %own_tile.1 = (f32[6,16,16,256]{3,2,1,0:T(8,128)S(1)}, f32[32,32,256]{2,1,0:T(8,128)S(1)}, f32[32,16,256]{2,1,0:T(8,128)S(1)}, f32[32,8,256]{2,1,0:T(8,128)S(1)}...) custom-call(bf16[32,32,180]{2,1,0:T(8,128)(2,1)} %image_ref.3, ...), custom_call_target="tpu_custom_call" | custom-call | flops 2000000000 | bytes 4000000 | tf_op jit(solution)/shard_map/own_tile/pallas_call | solution.py:347
  18.0 0.0 copy-start.9
  18.0 0.7 %copy-done.9 = f32[32,8,256]{2,1,0:T(8,128)} copy-done((f32[32,8,256]{2,1,0:T(8,128)}, f32[32,8,256]{2,1,0:T(8,128)S(1)}, u32[]{:S(2)}) %copy-start.9) | copy-done | bytes 262168
  18.7 0.7 %copy-done.11 = f32[32,8,256]{2,1,0:T(8,128)} copy-done((f32[32,8,256]{2,1,0:T(8,128)}, f32[32,8,256]{2,1,0:T(8,128)S(1)}, u32[]{:S(2)}) %copy-start.11) | copy-done | bytes 262168
  19.4 0.0 copy-done
  19.4 0.0 copy-done.1
  19.4 0.0 copy-done.2
  19.5 0.0 copy-done.3
  19.5 4.6 %middle_columns.1.middle_ref = f32[32,16,180]{2,1,0:T(8,128)S(1)} custom-call(bf16[32,32,180]{2,1,0:T(8,128)(2,1)S(1)} %copy-done, bf16[8,32,180]{2,1,0:T(8,128)(2,1)S(1)} %get-tuple-element.30.top_ref, bf16[8,32,180]{2,1,0:T(8,128)(2,1)S(1)} %get-tuple-element.29.bottom_ref, f32[1,180]{1,0:T(1,128)S(1)} %bitcast.23, f32[1,180]{1,0:T(1,128)S(1)} %bitcast.25, ...), custom_call_target="tpu_custom_call" | custom-call | flops 2000000000 | bytes 4000000 | tf_op jit(solution)/shard_map/middle_columns/pallas_call | solution.py:347
  24.1 0.6 %slice_bitcast_fusion.2 = (bf16[1,8,8,180]{3,2,1,0:T(8,128)(2,1)S(1)}, bf16[1,8,8,180]{3,2,1,0:T(8,128)(2,1)S(1)}, bf16[1,8,8,180]{3,2,1,0:T(8,128)(2,1)S(1)}, bf16[1,8,8,180]{3,2,1,0:T(8,128)(2,1)}) fusion(bf16[8,32,180]{2,1,0:T(8,128)(2,1)S(1)} %get-tuple-element.29.bottom_ref, bf16[8,32,180]{2,1,0:T(8,128)(2,1)S(1)} %get-tuple-element.30.top_ref), kind=kLoop, calls=%fused_computation.14 | loop fusion | bytes 184320 | tf_op jit(solution)/shard_map/concatenate | solution.py:392
  24.8 0.0 copy-start.14
  24.8 0.0 copy-start.16
  24.8 1.0 %broadcast_select_fusion.1 = (bf16[1,48,8,180]{3,2,1,0:T(8,128)(2,1)S(1)}, bf16[1,48,8,180]{3,2,1,0:T(8,128)(2,1)S(1)}) fusion(pred[]{:T(512)S(6)} %eq.7, bf16[1,8,8,180]{3,2,1,0:T(8,128)(2,1)S(1)} %get-tuple-element.38, bf16[1,32,8,180]{3,2,1,0:T(8,128)(2,1)S(1)} %bitcast.19, bf16[1,8,8,180]{3,2,1,0:T(8,128)(2,1)S(1)} %get-tuple-element.39, ...), kind=kLoop, calls=%fused_computation.7 | loop fusion | flops 414720 | bytes 552961 | tf_op jit(solution)/shard_map/jit(_where)/select_n | solution.py:338
  25.8 9.2 %all_gather.24 = bf16[2,48,8,180]{3,2,1,0:T(8,128)(2,1)S(1)} all-gather(bf16[1,48,8,180]{3,2,1,0:T(8,128)(2,1)S(1)} %get-tuple-element.33), channel_id=1, replica_groups={{1,2},{3,4},{5,6},{7,0},{9,10},{11,12},{13,14},{15,8},{17,18},{19,20},{..., dimensions={0}, use_global_device_ids=true | all-gather | bytes 414720 | tf_op jit(solution)/shard_map/all_gather | solution.py:338
  35.0 2.1 %all_gather.25 = bf16[2,48,8,180]{3,2,1,0:T(8,128)(2,1)S(1)} all-gather(bf16[1,48,8,180]{3,2,1,0:T(8,128)(2,1)S(1)} %get-tuple-element.34), channel_id=1, replica_groups={{0,1},{2,3},{4,5},{6,7},{8,9},{10,11},{12,13},{14,15},{16,17},{18,19},{..., dimensions={0}, use_global_device_ids=true | all-gather | bytes 414720 | tf_op jit(solution)/shard_map/all_gather | solution.py:337
  37.2 6.0 %side_columns.1 = bf16[32,32,180]{2,1,0:T(8,128)(2,1)} custom-call(bf16[32,32,180]{2,1,0:T(8,128)(2,1)S(1)} %copy-done, bf16[8,32,180]{2,1,0:T(8,128)(2,1)S(1)} %get-tuple-element.30.top_ref, bf16[8,32,180]{2,1,0:T(8,128)(2,1)S(1)} %get-tuple-element.29.bottom_ref, bf16[48,8,180]{2,1,0:T(8,128)(2,1)S(1)} %get-tuple-element.28.left_ref, ...), custom_call_target="tpu_custom_call" | custom-call | flops 2000000000 | bytes 4000000 | tf_op jit(solution)/shard_map/side_columns/pallas_call | solution.py:347
  (22 shorter events, 0.1 us)
Async XLA Ops:
  14.7 4.7 %copy-start = (bf16[32,32,180]{2,1,0:T(8,128)(2,1)S(1)}, bf16[32,32,180]{2,1,0:T(8,128)(2,1)}, u32[]{:S(2)}) copy-start(bf16[32,32,180]{2,1,0:T(8,128)(2,1)} %image_ref.3) | copy-start | bytes 1105924
  14.7 4.7 %copy-start.1 = (bf16[180,360]{1,0:T(8,128)(2,1)S(1)}, bf16[180,360]{1,0:T(8,128)(2,1)}, u32[]{:S(2)}) copy-start(bf16[180,360]{1,0:T(8,128)(2,1)} %fc1_ref.3) | copy-start | bytes 388804
  14.7 4.7 %copy-start.2 = (bf16[360,180]{0,1:T(8,128)(2,1)S(1)}, bf16[360,180]{0,1:T(8,128)(2,1)}, u32[]{:S(2)}) copy-start(bf16[360,180]{0,1:T(8,128)(2,1)} %param.17) | copy-start | bytes 388804
  14.7 4.7 %copy-start.3 = (f32[180]{0:T(256)S(1)}, f32[180]{0:T(256)}, u32[]{:S(2)}) copy-start(f32[180]{0:T(256)} %param.10) | copy-start | bytes 2164
  14.8 4.7 %copy-start.4 = (f32[180]{0:T(256)S(1)}, f32[180]{0:T(256)}, u32[]{:S(2)}) copy-start(f32[180]{0:T(256)} %param.11) | copy-start | bytes 2164
  18.0 0.7 %copy-start.9 = (f32[32,8,256]{2,1,0:T(8,128)}, f32[32,8,256]{2,1,0:T(8,128)S(1)}, u32[]{:S(2)}) copy-start(f32[32,8,256]{2,1,0:T(8,128)S(1)} %get-tuple-element.20.q_left) | copy-start | bytes 786436
  18.7 0.7 %copy-start.11 = (f32[32,8,256]{2,1,0:T(8,128)}, f32[32,8,256]{2,1,0:T(8,128)S(1)}, u32[]{:S(2)}) copy-start(f32[32,8,256]{2,1,0:T(8,128)S(1)} %get-tuple-element.21.q_right) | copy-start | bytes 786436
  19.4 4.7 %copy-start.5 = (bf16[2304,180]{1,0:T(8,128)(2,1)}, bf16[2304,180]{1,0:T(8,128)(2,1)S(1)}, u32[]{:S(2)}) copy-start(bf16[2304,180]{1,0:T(8,128)(2,1)S(1)} %get-tuple-element.24.wc) | copy-start | bytes 2488324
  19.4 4.7 %copy-start.7 = (f32[32,32,256]{2,1,0:T(8,128)}, f32[32,32,256]{2,1,0:T(8,128)S(1)}, u32[]{:S(2)}) copy-start(f32[32,32,256]{2,1,0:T(8,128)S(1)} %get-tuple-element.19.normed) | copy-start | bytes 3145732
  19.4 4.7 %copy-start.13 = (bf16[256,512]{1,0:T(8,128)(2,1)}, bf16[256,512]{1,0:T(8,128)(2,1)S(1)}, u32[]{:S(2)}) copy-start(bf16[256,512]{1,0:T(8,128)(2,1)S(1)} %get-tuple-element.22.wkv) | copy-start | bytes 786436
  19.4 4.7 %copy-start.15 = (bf16[256,180]{1,0:T(8,128)(2,1)}, bf16[256,180]{1,0:T(8,128)(2,1)S(1)}, u32[]{:S(2)}) copy-start(bf16[256,180]{1,0:T(8,128)(2,1)S(1)} %get-tuple-element.23.wp) | copy-start | bytes 276484
  24.8 12.3 %copy-start.6 = (bf16[2304,180]{1,0:T(8,128)(2,1)S(1)}, bf16[2304,180]{1,0:T(8,128)(2,1)}, u32[]{:S(2)}) copy-start(bf16[2304,180]{1,0:T(8,128)(2,1)} %copy-done.5) | copy-start | bytes 2488324
  24.8 12.4 %copy-start.8 = (f32[32,32,256]{2,1,0:T(8,128)S(1)}, f32[32,32,256]{2,1,0:T(8,128)}, u32[]{:S(2)}) copy-start(f32[32,32,256]{2,1,0:T(8,128)} %copy-done.7) | copy-start | bytes 3145732
  24.8 12.4 %copy-start.10 = (f32[32,8,256]{2,1,0:T(8,128)S(1)}, f32[32,8,256]{2,1,0:T(8,128)}, u32[]{:S(2)}) copy-start(f32[32,8,256]{2,1,0:T(8,128)} %copy-done.9) | copy-start | bytes 786436
  24.8 12.4 %copy-start.12 = (f32[32,8,256]{2,1,0:T(8,128)S(1)}, f32[32,8,256]{2,1,0:T(8,128)}, u32[]{:S(2)}) copy-start(f32[32,8,256]{2,1,0:T(8,128)} %copy-done.11) | copy-start | bytes 786436
  24.8 12.4 %copy-start.14 = (bf16[256,512]{1,0:T(8,128)(2,1)S(1)}, bf16[256,512]{1,0:T(8,128)(2,1)}, u32[]{:S(2)}) copy-start(bf16[256,512]{1,0:T(8,128)(2,1)} %copy-done.13) | copy-start | bytes 786436
  24.8 12.4 %copy-start.16 = (bf16[256,180]{1,0:T(8,128)(2,1)S(1)}, bf16[256,180]{1,0:T(8,128)(2,1)}, u32[]{:S(2)}) copy-start(bf16[256,180]{1,0:T(8,128)(2,1)} %copy-done.15) | copy-start | bytes 276484

commit v6 on v4

v6 whole, which is shorter than its diff:
```python
import math

import jax
import jax.numpy as jnp
from jax import lax
from jax.experimental import pallas as pl
from jax.experimental.pallas import tpu as pltpu
from jax.sharding import PartitionSpec as P

HEADS = 6
WIN = 16
SHIFT = 8
SIDE = 8
AREA = SIDE * SIDE
LANES = 256
HALF = LANES // 2
F32 = jnp.float32
BF16 = jnp.bfloat16
LOG2E = math.log2(math.e)
MASKED = -4.0e9


def layer_norm(values, norm_gain):
    centre = jnp.mean(values, axis=-1, keepdims=True)
    values = values - centre
    spread = jnp.mean(values * values, axis=-1, keepdims=True)
    return values * lax.rsqrt(spread + 1e-05) * norm_gain


def dot(a, b):
    return jnp.dot(a, b, preferred_element_type=F32)


def dot_nt(a, b):
    return lax.dot_general(a, b, (((1,), (1,)), ((), ())), preferred_element_type=F32)


def one_hot(condition):
    return jnp.where(condition, 1.0, 0.0).astype(BF16)


def gelu(x):
    size = jnp.abs(x)
    t = 1.0 / (1.0 + (0.3275911 * math.sqrt(0.5)) * size)
    poly = 0.5 * 1.061405429
    for factor in (-1.453152027, 1.421413741, -0.284496736, 0.254829592):
        poly = poly * t + 0.5 * factor
    tail = poly * t * jnp.exp2(size * size * (-0.5 * LOG2E))
    return jnp.maximum(x, 0.0) - size * tail


def lanes_of(width=LANES):
    return lax.broadcasted_iota(jnp.int32, (1, width), 1)


def marks(channels, outside):
    half = lanes_of()[:, HALF:]
    return jnp.where(half == channels + 1, 1.0, 0.0) + jnp.where(half == channels, outside, 0.0)


def expand_bias(table_ref, padded, strip, bias):
    span = 2 * WIN - 1
    padded[...] = jnp.zeros_like(padded)
    padded[0:HEADS, 0 : span * span] = table_ref[...] * LOG2E
    table = padded[...]
    width = padded.shape[1]
    shifted = jnp.concatenate(
        [table if px == 0 else pltpu.roll(table, width - px, 1) for px in range(WIN)], axis=0
    )
    high = shifted.astype(BF16)
    low = (shifted - high.astype(F32)).astype(BF16)
    entry = lax.broadcasted_iota(jnp.int32, (width, 512), 0)
    place = lax.broadcasted_iota(jnp.int32, (1, 512), 1)
    column = lax.div(place, 256) * SIDE + lax.rem(place, SIDE)
    wanted = (span - 1 - lax.div(lax.rem(place, 256), SIDE)) * span + WIN - 1 - column
    picked = dot(jnp.concatenate([high, low], axis=0), one_hot(entry == wanted))
    half = 8 * WIN
    picked = picked[:half] + picked[half:]
    for tile in range(4):
        strip[tile] = picked[:, 128 * tile : 128 * (tile + 1)]
    for head in range(HEADS):
        for half in range(2):
            rows = jnp.concatenate(
                [strip[2 * half + t, pl.ds(head, WIN, stride=8), :] for t in range(2)], axis=1
            )
            for py in range(WIN):
                start = (WIN - 1 - py) * SIDE
                rolled = (rows if start == 0 else pltpu.roll(rows, 256 - start, 1))[:, 0:128]
                lanes = slice(128 * half, 128 * (half + 1))
                place = slice(py % SIDE * SIDE, (py % SIDE + 1) * SIDE)
                bias[head, py // SIDE, 0, place, lanes] = rolled[:SIDE]
                bias[head, py // SIDE, 1, place, lanes] = rolled[SIDE:]


def scores_of(blocks, keys, head_dim, channels):
    lane = lanes_of()
    part = jnp.concatenate(blocks, axis=0)
    own = [(lane >= h * head_dim) & (lane < (h + 1) * head_dim) for h in range(HEADS)]
    stacked = jnp.concatenate(
        [jnp.where(own[h] | (lane == channels), part, 0.0).astype(BF16) for h in range(HEADS)],
        axis=0,
    )
    return dot_nt(stacked, keys)


def mix(scores, part_bias, values, head_dim, channels):
    lane = lanes_of()
    count = scores.shape[0] // HEADS
    scores = scores.reshape(HEADS, count, WIN * WIN) + part_bias
    scores = scores - jnp.max(scores, axis=-1, keepdims=True)
    soft = jnp.exp2(scores).astype(BF16).reshape(HEADS * count, WIN * WIN)
    mixed = dot(soft, values)
    result = mixed[0:count]
    for h in range(1, HEADS):
        mine = (lane >= h * head_dim) & (lane < (h + 1) * head_dim) | (lane == channels + h)
        result = jnp.where(mine, mixed[h * count : (h + 1) * count], result)
    return result


def attention(units, bias, head_dim, channels):
    def scores_at(unit):
        return scores_of(unit[0], unit[2][:, :LANES], head_dim, channels)

    results = []
    ahead = scores_at(units[0])
    for i, unit in enumerate(units):
        scores, ahead = ahead, scores_at(units[i + 1]) if i + 1 < len(units) else None
        part_bias = jnp.concatenate([bias[:, hy, hx] for hy, hx in unit[1]], axis=1)
        results.append(mix(scores, part_bias, unit[2][:, LANES:], head_dim, channels))
    return results


def spread_matrix(channels):
    head_dim = channels // HEADS
    sum_row = lax.broadcasted_iota(jnp.int32, (HALF, LANES), 0) + HALF - channels
    lane_wide = lax.broadcasted_iota(jnp.int32, (HALF, LANES), 1)
    return one_hot(
        (sum_row >= 0) & (lane_wide >= sum_row * head_dim) & (lane_wide < (sum_row + 1) * head_dim)
        & (lane_wide < channels)
    )


def finish(raw, base, spread, wp, gain2, fc1, fc2, channels):
    half = lanes_of()[:, HALF:]
    is_sum = (half >= channels) & (half < channels + HEADS)
    inverse = jnp.where(is_sum, 1.0 / raw[:, HALF:], 0.0)
    high = inverse.astype(BF16)
    low = (inverse - high.astype(F32)).astype(BF16)
    heads_out = (raw * (dot(high, spread) + dot(low, spread))).astype(BF16)
    state1 = base + dot(heads_out, wp[...]).astype(BF16).astype(F32)
    normed2 = layer_norm(state1, gain2).astype(BF16)
    hidden = gelu(dot(normed2, fc1[...])).astype(BF16)
    return state1 + dot_nt(hidden, fc2[...])


def own_kernel(
    image_hbm, gain1_hbm, gain2_hbm, qkv_hbm, proj_hbm, table_hbm, conv_hbm, fc1_hbm, fc2_hbm,
    bias, query, kv, base, wkv, wp, wc, out_mid,
    padded, strip, wq, normed, shifted,
    table_ref, image_ref, gain1_ref, gain2_ref, qkv_ref, proj_ref, conv_ref, fc1_ref, fc2_ref, sems,
):
    rows, cols, channels = image_ref.shape
    head_dim = channels // HEADS
    flag_lane, one_lane = channels, channels + 1
    blocks_r, blocks_c = rows // SIDE, cols // SIDE
    fetches = [
        pltpu.make_async_copy(source, target, sems.at[i])
        for i, (source, target) in enumerate(
            ((table_hbm, table_ref), (image_hbm, image_ref), (gain1_hbm, gain1_ref), (qkv_hbm, qkv_ref),
             (proj_hbm, proj_ref), (conv_hbm, conv_ref), (gain2_hbm, gain2_ref), (fc1_hbm, fc1_ref),
             (fc2_hbm, fc2_ref))
        )
    ]
    for fetch in fetches:
        fetch.start()

    for ref in (wq, wkv, wp, wc):
        ref[...] = jnp.zeros_like(ref)
    special = lax.broadcasted_iota(jnp.int32, (16, LANES), 0) + 176
    lanes16 = lax.broadcasted_iota(jnp.int32, (16, LANES), 1)
    wq[176:192, :] = one_hot((special == one_lane) & (lanes16 == flag_lane))
    wkv[176:192, 0:LANES] = jnp.where(
        (special == flag_lane) & (lanes16 == flag_lane), MASKED, 0.0
    ).astype(BF16)
    wkv[176:192, LANES:] = one_hot(
        (special == one_lane) & (lanes16 >= channels) & (lanes16 < channels + HEADS)
    )
    normed[...] = jnp.zeros_like(normed)
    normed[1 : 1 + rows, SHIFT : SHIFT + cols, HALF:] = jnp.broadcast_to(
        marks(channels, 0.0)[None], (rows, cols, HALF)
    )

    fetches[0].wait()
    expand_bias(table_ref, padded, strip, bias)
    for fetch in fetches[1:]:
        fetch.wait()
    wq[0:channels, 0:channels] = qkv_ref[:, 0:channels]
    wkv[0:channels, 0:channels] = qkv_ref[:, channels : 2 * channels]
    wkv[0:channels, LANES : LANES + channels] = qkv_ref[:, 2 * channels :]
    wp[0:channels, :] = proj_ref[...]
    for tap in range(9):
        wc[tap * LANES : tap * LANES + channels, :] = conv_ref[tap // 3, tap % 3]

    gain1 = gain1_ref[...]
    scale = head_dim**-0.5 * LOG2E
    for br in range(blocks_r):
        r = br * SIDE
        inner = (slice(1 + r, 1 + r + SIDE), slice(SHIFT, SHIFT + cols))
        normed[(*inner, slice(0, channels))] = layer_norm(image_ref[r : r + SIDE].astype(F32), gain1)
        pixels = normed[inner].astype(BF16).reshape(-1, LANES)
        q = (dot(pixels, wq[...]) * scale).reshape(SIDE, cols, LANES)
        both = dot(pixels, wkv[...]).reshape(SIDE, cols, 2 * LANES)
        for bc in range(blocks_c):
            part = slice(bc * SIDE, (bc + 1) * SIDE)
            query[br, bc] = q[:, part].reshape(AREA, LANES)
            kv[br, bc] = both[:, part].reshape(AREA, 2 * LANES).astype(BF16)

    middle = [(1, 1), (2, 1), (1, 2), (2, 2)]
    pair = jnp.concatenate([kv[at] for at in middle], axis=0)
    units = [
        ([query[1, 1], query[1, 2]], [(0, 0), (0, 1)], pair),
        ([query[2, 1], query[2, 2]], [(1, 0), (1, 1)], pair),
    ]
    mixed = attention(units, bias, head_dim, channels)

    for tap in range(3):
        c0 = SHIFT - 1 + tap
        for r in range(0, rows + 2, SIDE):
            stop = min(r + SIDE, rows + 2)
            shifted[tap, r:stop] = normed[r:stop, c0 : c0 + cols].astype(BF16)
    for br in range(blocks_r):
        r = br * SIDE
        taps = [
            shifted[tap % 3, r + tap // 3 : r + tap // 3 + SIDE].reshape(-1, LANES) for tap in range(9)
        ]
        summed = dot(jnp.concatenate(taps, axis=1), wc[...]).reshape(SIDE, cols, channels)
        summed = summed + image_ref[r : r + SIDE].astype(F32)
        for bc in range(blocks_c):
            base[br, bc] = summed[:, bc * SIDE : (bc + 1) * SIDE].reshape(AREA, channels)

    own_base = jnp.concatenate([base[at] for at in ((1, 1), (1, 2), (2, 1), (2, 2))], axis=0)
    out_mid[...] = finish(
        jnp.concatenate(mixed, axis=0), own_base, spread_matrix(channels), wp, gain2_ref[...], fc1_ref,
        fc2_ref, channels,
    )


def edge_kernel(
    top_ref, bottom_ref, left_ref, right_ref, gain1_ref, gain2_ref, fc1_ref, fc2_ref,
    bias, query, kv, base, wkv, wp, wc,
    kv_edge, fixes, out_edge,
    bands_r, bands_c,
):
    cols, channels = top_ref.shape[1:]
    rows = left_ref.shape[0]
    head_dim = channels // HEADS
    row, last_row = lax.axis_index("row"), lax.axis_size("row") - 1
    col, last_col = lax.axis_index("col"), lax.axis_size("col") - 1
    gain1 = gain1_ref[...]
    outside = [(row == 0).astype(F32), (row == last_row).astype(F32),
               (col == 0).astype(F32), (col == last_col).astype(F32)]

    bands_r[...] = jnp.zeros_like(bands_r)
    bands_c[...] = jnp.zeros_like(bands_c)
    for i, ref in enumerate((top_ref, bottom_ref, left_ref, right_ref)):
        mark = jnp.broadcast_to(marks(channels, outside[i])[None], (*ref.shape[:2], HALF))
        values = layer_norm(ref[...].astype(F32), gain1 * (1.0 - outside[i]))
        if i < 2:
            bands_r[i, :, SHIFT : SHIFT + cols, HALF:] = mark
            bands_r[i, :, SHIFT : SHIFT + cols, 0:channels] = values
            pixels = bands_r[i, :, SHIFT : SHIFT + cols]
            count = cols // SIDE
            blocks = [pixels[:, b * SIDE : (b + 1) * SIDE].reshape(AREA, LANES) for b in range(count)]
        else:
            bands_c[i - 2, 1 : 1 + rows, :, HALF:] = mark
            bands_c[i - 2, 1 : 1 + rows, :, 0:channels] = values
            count = rows // SIDE
            pixels = bands_c[i - 2, 1 : 1 + rows]
            blocks = [pixels.reshape(-1, LANES)]
        both = dot(jnp.concatenate(blocks, axis=0).astype(BF16), wkv[...]).astype(BF16)
        kv_edge[i] = both.reshape(count, AREA, 2 * LANES)

    keys = [
        [kv_edge[0, 1], kv[0, 1], kv_edge[0, 2], kv[0, 2]],
        [kv[3, 1], kv_edge[1, 1], kv[3, 2], kv_edge[1, 2]],
        [kv_edge[2, 1], kv_edge[2, 2], kv[1, 0], kv[2, 0]],
        [kv[1, 3], kv[2, 3], kv_edge[3, 1], kv_edge[3, 2]],
    ]
    places = [((0, 1), (0, 2)), ((3, 1), (3, 2)), ((1, 0), (2, 0)), ((1, 3), (2, 3))]
    quadrants = [((1, 0), (1, 1)), ((0, 0), (0, 1)), ((0, 1), (1, 1)), ((0, 0), (1, 0))]
    units = [
        ([query[at] for at in places[i]], quadrants[i], jnp.concatenate(keys[i], axis=0))
        for i in range(4)
    ]
    mixed = attention(units, bias, head_dim, channels)

    for i, (taps, source) in enumerate((((0, 1, 2), SHIFT - 1), ((6, 7, 8), 0))):
        pieces = [bands_r[i, source, SHIFT - 1 + t : SHIFT - 1 + t + cols] for t in range(3)]
        weights = jnp.concatenate([wc[t * LANES : (t + 1) * LANES] for t in taps], axis=0)
        fixes[i] = dot(jnp.concatenate(pieces, axis=1).astype(BF16), weights)
    for i, (taps, source) in enumerate((((0, 3, 6), SHIFT - 1), ((2, 5, 8), 0))):
        pieces = [bands_c[i, t : t + rows, source] for t in range(3)]
        weights = jnp.concatenate([wc[t * LANES : (t + 1) * LANES] for t in taps], axis=0)
        fixes[2 + i] = dot(jnp.concatenate(pieces, axis=1).astype(BF16), weights)

    gain2, spread = gain2_ref[...], spread_matrix(channels)
    for group in range(2):
        raw = jnp.concatenate([mixed[2 * group], mixed[2 * group + 1]], axis=0)
        parts = [
            corrected(base, fixes, at, channels)
            for at in (*places[2 * group], *places[2 * group + 1])
        ]
        out_edge[group] = finish(
            raw, jnp.concatenate(parts, axis=0), spread, wp, gain2, fc1_ref, fc2_ref, channels
        )


def corrected(base, fixes, at, channels):
    br, bc = at
    block = base[at].reshape(SIDE, SIDE, channels)
    y = lax.broadcasted_iota(jnp.int32, (SIDE, SIDE, 1), 0)
    x = lax.broadcasted_iota(jnp.int32, (SIDE, SIDE, 1), 1)
    if br in (0, 3):
        fix = fixes[0 if br == 0 else 1, bc * SIDE : (bc + 1) * SIDE]
        block = block + jnp.where(y == (0 if br == 0 else SIDE - 1), fix[None], 0.0)
    if bc in (0, 3):
        fix = fixes[2 if bc == 0 else 3, br * SIDE : (br + 1) * SIDE]
        block = block + jnp.where(x == (0 if bc == 0 else SIDE - 1), fix[:, None], 0.0)
    return block.reshape(AREA, channels)


def corner_kernel(
    left_ref, right_ref, gain1_ref, gain2_ref, fc1_ref, fc2_ref,
    bias, query, kv, base, wkv, wp, wc, kv_edge, fixes, out_mid, out_edge,
    out_ref,
    normed,
):
    channels = left_ref.shape[2]
    head_dim = channels // HEADS
    row, last_row = lax.axis_index("row"), lax.axis_size("row") - 1
    col, last_col = lax.axis_index("col"), lax.axis_size("col") - 1
    gain1 = gain1_ref[...]
    out_row = [(row == 0).astype(F32), (row == last_row).astype(F32)]
    out_col = [(col == 0).astype(F32), (col == last_col).astype(F32)]
    for i in range(4):
        ref = (left_ref, right_ref)[i % 2]
        inside = (1.0 - out_row[i // 2]) * (1.0 - out_col[i % 2])
        mark = marks(channels, out_row[i // 2] + out_col[i % 2])
        normed[i, :, HALF:] = jnp.broadcast_to(mark, (AREA, HALF))
        values = ref[i // 2 * SIDE : (i // 2 + 1) * SIDE].astype(F32)
        normed[i, :, 0:channels] = layer_norm(values.reshape(AREA, channels), gain1 * inside)
    corner = dot(normed[...].reshape(-1, LANES).astype(BF16), wkv[...]).astype(BF16)
    corner = [corner[i * AREA : (i + 1) * AREA] for i in range(4)]
    keys = [
        [corner[0], kv_edge[2, 0], kv_edge[0, 0], kv[0, 0]],
        [kv_edge[0, 3], kv[0, 3], corner[1], kv_edge[3, 0]],
        [kv_edge[2, 3], corner[2], kv[3, 0], kv_edge[1, 0]],
        [kv[3, 3], kv_edge[1, 3], kv_edge[3, 3], corner[3]],
    ]
    places = [(0, 0), (0, 3), (3, 0), (3, 3)]
    quadrants = [(1, 1), (1, 0), (0, 1), (0, 0)]
    units = [
        ([query[places[i]]], [quadrants[i]], jnp.concatenate(keys[i], axis=0)) for i in range(4)
    ]
    mixed = attention(units, bias, head_dim, channels)

    parts = []
    for i, (tap, y, x) in enumerate(((0, 7, 7), (2, 7, 0), (6, 0, 7), (8, 0, 0))):
        start = y * SIDE
        term = dot(normed[i, start : start + SIDE].astype(BF16), wc[tap * LANES : (tap + 1) * LANES])
        term = term[x : x + 1]
        pixel = lax.broadcasted_iota(jnp.int32, (AREA, 1), 0)
        at = (SIDE - 1 - y) * SIDE + SIDE - 1 - x
        block = corrected(base, fixes, places[i], channels)
        parts.append(block + jnp.where(pixel == at, term, 0.0))
    out_corner = finish(
        jnp.concatenate(mixed, axis=0), jnp.concatenate(parts, axis=0), spread_matrix(channels), wp,
        gain2_ref[...], fc1_ref, fc2_ref, channels,
    )

    def piece(source, i):
        return source[i * AREA : (i + 1) * AREA].reshape(SIDE, SIDE, channels)

    bands = [
        [piece(out_corner, 0), piece(out_edge.at[0], 0), piece(out_edge.at[0], 1), piece(out_corner, 1)],
        [piece(out_edge.at[1], 0), piece(out_mid, 0), piece(out_mid, 1), piece(out_edge.at[1], 2)],
        [piece(out_edge.at[1], 1), piece(out_mid, 2), piece(out_mid, 3), piece(out_edge.at[1], 3)],
        [piece(out_corner, 2), piece(out_edge.at[0], 2), piece(out_edge.at[0], 3), piece(out_corner, 3)],
    ]
    for br, band in enumerate(bands):
        out_ref[br * SIDE : (br + 1) * SIDE] = jnp.concatenate(band, axis=1).astype(BF16)


def exchange(low, high, axis):
    count = lax.axis_size(axis)
    before = lax.ppermute(high, axis, [(i, (i + 1) % count) for i in range(count)])
    after = lax.ppermute(low, axis, [((i + 1) % count, i) for i in range(count)])
    return before, after


def call(kernel, name, outs, scratch, flops, operands, in_hbm=()):
    vmem = pl.BlockSpec(memory_space=pltpu.VMEM)
    hbm = pl.BlockSpec(memory_space=pltpu.HBM)
    return pl.pallas_call(
        kernel,
        out_shape=[out if isinstance(out, jax.ShapeDtypeStruct) else pltpu.VMEM(*out) for out in outs],
        in_specs=[hbm if i in in_hbm else vmem for i in range(len(operands))],
        out_specs=[vmem] * len(outs),
        scratch_shapes=[pltpu.VMEM(*s) if isinstance(s, tuple) else s for s in scratch],
        cost_estimate=pl.CostEstimate(flops=flops, bytes_accessed=4_000_000, transcendentals=1_000_000),
        compiler_params=pltpu.CompilerParams(vmem_limit_bytes=24 * 1024 * 1024),
        name=name,
    )(*[pltpu.with_memory_space_constraint(x, pltpu.HBM) if i in in_hbm else x for i, x in enumerate(operands)])


def on_device(
    image, norm1_gain, norm2_gain, qkv_weight, proj_weight, rel_table, conv_weight, fc1_weight,
    fc2_weight,
):
    rows, cols, channels = image.shape
    blocks_r, blocks_c = rows // SIDE, cols // SIDE
    gain1, gain2, fc2, table = norm1_gain[None], norm2_gain[None], fc2_weight.T, rel_table.T
    top, bottom = exchange(image[:SHIFT], image[rows - SHIFT :], "row")
    left, right = exchange(image[:, :SHIFT], image[:, cols - SHIFT :], "col")
    fetched = (table, image, gain1, gain2, qkv_weight, proj_weight, conv_weight, fc1_weight, fc2)
    bias, query, kv, base, wkv, wp, wc, out_mid = call(
        own_kernel,
        "own_tile",
        [
            ((HEADS, 2, 2, AREA, WIN * WIN), F32),
            ((blocks_r, blocks_c, AREA, LANES), F32),
            ((blocks_r, blocks_c, AREA, 2 * LANES), BF16),
            ((blocks_r, blocks_c, AREA, channels), F32),
            ((LANES, 2 * LANES), BF16),
            ((LANES, channels), BF16),
            ((9 * LANES, channels), BF16),
            ((4 * AREA, channels), F32),
        ],
        [
            ((8, 1024), F32),
            ((4, 8 * WIN, 128), F32),
            ((LANES, LANES), BF16),
            ((rows + 2, cols + 2 * SHIFT, LANES), F32),
            ((3, rows + 2, cols, LANES), BF16),
            *[(x.shape, x.dtype) for x in fetched],
            pltpu.SemaphoreType.DMA((len(fetched),)),
        ],
        2_000_000_000,
        (image, gain1, gain2, qkv_weight, proj_weight, table, conv_weight, fc1_weight, fc2),
        range(9),
    )
    first = jnp.concatenate([top[:, :SHIFT], bottom[:, :SHIFT]])
    last = jnp.concatenate([top[:, cols - SHIFT :], bottom[:, cols - SHIFT :]])
    left_corner, right_corner = exchange(first, last, "col")
    kv_edge, fixes, out_edge = call(
        edge_kernel,
        "edge_windows",
        [
            ((4, blocks_c, AREA, 2 * LANES), BF16),
            ((4, cols, channels), F32),
            ((2, 4 * AREA, channels), F32),
        ],
        [((2, SHIFT, cols + 2 * SHIFT, LANES), F32), ((2, rows + 2, SHIFT, LANES), F32)],
        2_000_000_000,
        (top, bottom, left, right, gain1, gain2, fc1_weight, fc2, bias, query, kv, base, wkv, wp, wc),
    )
    (out,) = call(
        corner_kernel,
        "corner_windows",
        [jax.ShapeDtypeStruct(image.shape, BF16)],
        [((4, AREA, LANES), F32)],
        1_000_000_000,
        (left_corner, right_corner, gain1, gain2, fc1_weight, fc2, bias, query, kv, base, wkv, wp, wc,
         kv_edge, fixes, out_mid, out_edge),
    )
    return out


def solution(mesh):
    placed = (P("row", "col", None), P(), P(), P(), P(), P(), P(), P(), P())
    return jax.shard_map(
        on_device, mesh=mesh, in_specs=placed, out_specs=P("row", "col", None), check_vma=False
    )
```

time: 27.1 us -> 25.5 us (0.941)
  waiting for transfers between devices: 5.59 us -> 1.62 us
  starting transfers between devices: 6.29 us -> 8.37 us
  local copies, waits for them, and re-layouts: 1.02 us -> 2 us
  Pallas kernels: 13.9 us -> 13.2 us
    ppermute x2 -> x3, waiting for transfers between devices: 2.23 us -> 0.01 us  [exchange(): lax.ppermute(low, axis, [((i + 1) % count, i) for i in range(count)])]
    ppermute x2 -> x3, starting transfers between devices: 3.24 us -> 5.27 us  [exchange(): lax.ppermute(low, axis, [((i + 1) % count, i) for i in range(count)])]
    ppermute x2 -> x3, waiting for transfers between devices: 3.36 us -> 1.61 us  [exchange(): lax.ppermute(high, axis, [(i, (i + 1) % count) for i in range(count)])]
    slice x2 -> x3, local copies, waits for them, and re-layouts: 0.01 us -> 1 us  [the longest x1 0.99 us: on_device(): left, right = exchange(image[:, :SHIFT], image[:, cols - SHIFT:], 'col')]
    pallas_call x3, Pallas kernels: 13.9 us -> 13.2 us  [call(): pl.pallas_call(kernel, out_shape=[out if isinstance(out, jax.ShapeDtypeSt...]
    ppermute x2 -> x3, starting transfers between devices: 3.05 us -> 3.11 us  [exchange(): lax.ppermute(high, axis, [(i, (i + 1) % count) for i in range(count)])]
  transfers between devices with their start and end apart: 4 -> 6, of which waited for: 3 -> 1; matrix products, arithmetic and copies ran while one was open for 0% -> 4% of each run, Pallas kernels for 29% -> 40%
where the time goes in v6:
time: 25.5 us; the launch traced here: 25.4 us
  Pallas kernels  13.2 us (52%)
  starting transfers between devices  8.37 us (33%)
  local copies, waits for them, and re-layouts  2 us (8%)
  waiting for transfers between devices  1.62 us (6%)
    pallas_call x3, Pallas kernels, call(): pl.pallas_call(kernel, out_shape=[out if isinstance(out, jax.ShapeDtypeSt...  13.2 us
    ppermute x3, starting transfers between devices, exchange(): lax.ppermute(low, axis, [((i + 1) % count, i) for i in range(count)])  5.27 us
    ppermute x3, starting transfers between devices, exchange(): lax.ppermute(high, axis, [(i, (i + 1) % count) for i in range(count)])  3.11 us
    ppermute x3, waiting for transfers between devices, exchange(): lax.ppermute(high, axis, [(i, (i + 1) % count) for i in range(count)])  1.61 us
    slice x1, local copies, waits for them, and re-layouts, on_device(): left, right = exchange(image[:, :SHIFT], image[:, cols - SHIFT:], 'col')  0.99 us
    slice x1, local copies, waits for them, and re-layouts, on_device(): top, bottom = exchange(image[:SHIFT], image[rows - SHIFT:], 'row')  0.98 us
  transfers between devices with their start and end apart: 6, of which 1 were waited for; matrix products, arithmetic and copies ran while one was open for 4% of the time, Pallas kernels for 40%

profile of v6, /device:TPU:0, one launch (start us, length us, event | category | flops | bytes accessed | tf_op | source)
XLA Modules:
  0.0 25.4 jit_solution(18147698407457555097)
XLA Ops:
  0.0 1.0 %fusion.1 = (bf16[8,32,180]{2,1,0:T(8,128)(2,1)S(1)}, bf16[8,32,180]{2,1,0:T(8,128)(2,1)S(1)}) fusion(bf16[32,32,180]{2,1,0:T(8,128)(2,1)} %image_hbm.1), kind=kLoop, calls=%fused_computation.3 | loop fusion | bytes 368640 | tf_op jit(solution)/shard_map/slice | solution.py:423
  1.0 3.0 %collective-permute-start = (bf16[8,32,180]{2,1,0:T(8,128)(2,1)S(1)}, bf16[8,32,180]{2,1,0:T(8,128)(2,1)S(1)}, u32[]{:S(2)}, u32[]{:S(2)}) collective-permute-start(bf16[8,32,180]{2,1,0:T(8,128)(2,1)S(1)} %get-tuple-element.29), channel_id=1, source_target_pairs={{0,8},{8,16},{16,24},{24,0},{1,9},{9,17},{17,25},{25,1},{2,10},{10... | collective-permute-start | bytes 276488 | tf_op jit(solution)/shard_map/ppermute | solution.py:396
  4.0 1.0 %collective-permute-start.1 = (bf16[8,32,180]{2,1,0:T(8,128)(2,1)S(1)}, bf16[8,32,180]{2,1,0:T(8,128)(2,1)S(1)}, u32[]{:S(2)}, u32[]{:S(2)}) collective-permute-start(bf16[8,32,180]{2,1,0:T(8,128)(2,1)S(1)} %get-tuple-element.30), channel_id=1, source_target_pairs={{8,0},{16,8},{24,16},{0,24},{9,1},{17,9},{25,17},{1,25},{10,2},{18... | collective-permute-start | bytes 276488 | tf_op jit(solution)/shard_map/ppermute | solution.py:397
  5.0 1.0 %fusion = (bf16[32,8,180]{2,1,0:T(8,128)(2,1)S(1)}, bf16[32,8,180]{2,1,0:T(8,128)(2,1)S(1)}) fusion(bf16[32,32,180]{2,1,0:T(8,128)(2,1)} %image_hbm.1), kind=kLoop, calls=%fused_computation.2 | loop fusion | bytes 368640 | tf_op jit(solution)/shard_map/slice | solution.py:424
  6.0 0.1 collective-permute-start.4
  6.1 3.5 %collective-permute-start.5 = (bf16[32,8,180]{2,1,0:T(8,128)(2,1)S(1)}, bf16[32,8,180]{2,1,0:T(8,128)(2,1)S(1)}, u32[]{:S(2)}, u32[]{:S(2)}) collective-permute-start(bf16[32,8,180]{2,1,0:T(8,128)(2,1)S(1)} %get-tuple-element.27), channel_id=1, source_target_pairs={{1,0},{2,1},{3,2},{4,3},{5,4},{6,5},{7,6},{0,7},{9,8},{10,9},{11,1... | collective-permute-start | bytes 276488 | tf_op jit(solution)/shard_map/ppermute | solution.py:397
  9.6 0.0 copy-start
  9.6 0.0 copy-start.1
  9.6 0.0 copy-start.2
  9.6 6.3 %own_tile.1 = (f32[6,2,2,64,256]{4,3,2,1,0:T(8,128)S(1)}, f32[4,4,64,256]{3,2,1,0:T(8,128)S(1)}, bf16[4,4,64,512]{3,2,1,0:T(8,128)(2,1)S(1)}, f32[4,4,64,180]{3,...) custom-call(bf16[32,32,180]{2,1,0:T(8,128)(2,1)} %image_hbm.1, ...), custom_call_target="tpu_custom_call" | custom-call | flops 2000000000 | bytes 4000000 | tf_op jit(solution)/shard_map/own_tile/pallas_call | solution.py:404
  15.9 0.0 collective-permute-done.top_ref
  15.9 0.0 collective-permute-done.1.bottom_ref
  16.0 0.7 %collective-permute-start.3 = (bf16[16,8,180]{2,1,0:T(8,128)(2,1)S(1)}, bf16[16,8,180]{2,1,0:T(8,128)(2,1)S(1)}, u32[]{:S(2)}, u32[]{:S(2)}) collective-permute-start(bf16[16,8,180]{2,1,0:T(8,128)(2,1)S(1)} %pad_maximum_fusion.1), channel_id=1, source_target_pairs={{1,0},{2,1},{3,2},{4,3},{5,4},{6,5},{7,6},{0,7},{9,8},{10,9},{11,1... | collective-permute-start | bytes 138248 | tf_op jit(solution)/shard_map/ppermute | solution.py:397
  16.7 0.1 collective-permute-start.2
  16.8 0.0 collective-permute-done.4.left_ref
  16.8 0.0 collective-permute-done.5.right_ref
  16.8 0.0 copy-done
  16.8 0.0 copy-done.1
  16.8 0.0 copy-done.2
  16.8 0.0 copy-done.3
  16.8 3.8 %edge_windows.1 = (bf16[4,4,64,512]{3,2,1,0:T(8,128)(2,1)S(1)}, f32[4,32,180]{2,1,0:T(8,128)S(1)}, f32[2,256,180]{2,1,0:T(8,128)S(1)}) custom-call(bf16[8,32,180]{2,1,0:T(8,128)(2,1)S(1)} %collective-permute-done.top_ref, bf16[8,32,180]{2,1,0:T(8,128)(2,1)S(1)} %collective-permute-done.1.bottom_ref, bf16[32,8,180]{2,1,0:T(8,128)(2,1)S(1)} %collective-permute-done.4.left_ref, ...), custom_call_target="tpu_custom_call" | custom-call | flops 2000000000 | bytes 4000000 | tf_op jit(solution)/shard_map/edge_windows/pallas_call | solution.py:404
  20.6 0.0 collective-permute-done.3.right_ref
  20.7 1.6 %collective-permute-done.2.left_ref = bf16[16,8,180]{2,1,0:T(8,128)(2,1)S(1)} collective-permute-done((bf16[16,8,180]{2,1,0:T(8,128)(2,1)S(1)}, bf16[16,8,180]{2,1,0:T(8,128)(2,1)S(1)}, u32[]{:S(2)}, u32[]{:S(2)}) %collective-permute-start.2) | collective-permute-done | bytes 46112 | tf_op jit(solution)/shard_map/ppermute | solution.py:396
  22.3 3.1 %corner_windows.1 = bf16[32,32,180]{2,1,0:T(8,128)(2,1)} custom-call(bf16[16,8,180]{2,1,0:T(8,128)(2,1)S(1)} %collective-permute-done.2.left_ref, bf16[16,8,180]{2,1,0:T(8,128)(2,1)S(1)} %collective-permute-done.3.right_ref, f32[1,180]{1,0:T(1,128)S(1)} %bitcast.9, f32[1,180]{1,0:T(1,128)S(1)} %bitcast.12, bf16[180,360]{1,0:T(8,128)(2,1)S(1)} %copy-done, ...), custom_call_target="tpu_custom_call" | custom-call | flops 1000000000 | bytes 4000000 | tf_op jit(solution)/shard_map/corner_windows/pallas_call | solution.py:404
  (5 shorter events, 0.0 us)
Async XLA Ops:
  1.0 14.9 %collective-permute-start = (bf16[8,32,180]{2,1,0:T(8,128)(2,1)S(1)}, bf16[8,32,180]{2,1,0:T(8,128)(2,1)S(1)}, u32[]{:S(2)}, u32[]{:S(2)}) collective-permute-start(bf16[8,32,180]{2,1,0:T(8,128)(2,1)S(1)} %get-tuple-element.29), channel_id=1, source_target_pairs={{0,8},{8,16},{16,24},{24,0},{1,9},{9,17},{17,25},{25,1},{2,10},{10... | collective-permute-start | bytes 276488 | tf_op jit(solution)/shard_map/ppermute | solution.py:396
  4.0 12.0 %collective-permute-start.1 = (bf16[8,32,180]{2,1,0:T(8,128)(2,1)S(1)}, bf16[8,32,180]{2,1,0:T(8,128)(2,1)S(1)}, u32[]{:S(2)}, u32[]{:S(2)}) collective-permute-start(bf16[8,32,180]{2,1,0:T(8,128)(2,1)S(1)} %get-tuple-element.30), channel_id=1, source_target_pairs={{8,0},{16,8},{24,16},{0,24},{9,1},{17,9},{25,17},{1,25},{10,2},{18... | collective-permute-start | bytes 276488 | tf_op jit(solution)/shard_map/ppermute | solution.py:397
  6.0 10.8 %collective-permute-start.4 = (bf16[32,8,180]{2,1,0:T(8,128)(2,1)S(1)}, bf16[32,8,180]{2,1,0:T(8,128)(2,1)S(1)}, u32[]{:S(2)}, u32[]{:S(2)}) collective-permute-start(bf16[32,8,180]{2,1,0:T(8,128)(2,1)S(1)} %get-tuple-element.28), channel_id=1, source_target_pairs={{0,1},{1,2},{2,3},{3,4},{4,5},{5,6},{6,7},{7,0},{8,9},{9,10},{10,1... | collective-permute-start | bytes 276488 | tf_op jit(solution)/shard_map/ppermute | solution.py:396
  6.1 10.7 %collective-permute-start.5 = (bf16[32,8,180]{2,1,0:T(8,128)(2,1)S(1)}, bf16[32,8,180]{2,1,0:T(8,128)(2,1)S(1)}, u32[]{:S(2)}, u32[]{:S(2)}) collective-permute-start(bf16[32,8,180]{2,1,0:T(8,128)(2,1)S(1)} %get-tuple-element.27), channel_id=1, source_target_pairs={{1,0},{2,1},{3,2},{4,3},{5,4},{6,5},{7,6},{0,7},{9,8},{10,9},{11,1... | collective-permute-start | bytes 276488 | tf_op jit(solution)/shard_map/ppermute | solution.py:397
  9.6 7.2 %copy-start = (bf16[180,360]{1,0:T(8,128)(2,1)S(1)}, bf16[180,360]{1,0:T(8,128)(2,1)}, u32[]{:S(2)}) copy-start(bf16[180,360]{1,0:T(8,128)(2,1)} %fc1_ref.3) | copy-start | bytes 388804
  9.6 7.2 %copy-start.1 = (bf16[360,180]{0,1:T(8,128)(2,1)S(1)}, bf16[360,180]{0,1:T(8,128)(2,1)}, u32[]{:S(2)}) copy-start(bf16[360,180]{0,1:T(8,128)(2,1)} %param.17) | copy-start | bytes 388804
  9.6 7.2 %copy-start.2 = (f32[180]{0:T(256)S(1)}, f32[180]{0:T(256)}, u32[]{:S(2)}) copy-start(f32[180]{0:T(256)} %param.10) | copy-start | bytes 2164
  9.6 7.2 %copy-start.3 = (f32[180]{0:T(256)S(1)}, f32[180]{0:T(256)}, u32[]{:S(2)}) copy-start(f32[180]{0:T(256)} %param.11) | copy-start | bytes 2164
  16.0 4.7 %collective-permute-start.3 = (bf16[16,8,180]{2,1,0:T(8,128)(2,1)S(1)}, bf16[16,8,180]{2,1,0:T(8,128)(2,1)S(1)}, u32[]{:S(2)}, u32[]{:S(2)}) collective-permute-start(bf16[16,8,180]{2,1,0:T(8,128)(2,1)S(1)} %pad_maximum_fusion.1), channel_id=1, source_target_pairs={{1,0},{2,1},{3,2},{4,3},{5,4},{6,5},{7,6},{0,7},{9,8},{10,9},{11,1... | collective-permute-start | bytes 138248 | tf_op jit(solution)/shard_map/ppermute | solution.py:397
  16.7 5.5 %collective-permute-start.2 = (bf16[16,8,180]{2,1,0:T(8,128)(2,1)S(1)}, bf16[16,8,180]{2,1,0:T(8,128)(2,1)S(1)}, u32[]{:S(2)}, u32[]{:S(2)}) collective-permute-start(bf16[16,8,180]{2,1,0:T(8,128)(2,1)S(1)} %pad_maximum_fusion), channel_id=1, source_target_pairs={{0,1},{1,2},{2,3},{3,4},{4,5},{5,6},{6,7},{7,0},{8,9},{9,10},{10,1... | collective-permute-start | bytes 138248 | tf_op jit(solution)/shard_map/ppermute | solution.py:396

commit v7 on v6

--- a/solution.py
+++ b/solution.py
@@ -97,8 +97,7 @@
     part = jnp.concatenate(blocks, axis=0)
     own = [(lane >= h * head_dim) & (lane < (h + 1) * head_dim) for h in range(HEADS)]
     stacked = jnp.concatenate(
-        [jnp.where(own[h] | (lane == channels), part, 0.0).astype(BF16) for h in range(HEADS)],
-        axis=0,
+        [part * one_hot(own[h] | (lane == channels)) for h in range(HEADS)], axis=0
     )
     return dot_nt(stacked, keys)
 
@@ -153,11 +152,24 @@
     return state1 + dot_nt(hidden, fc2[...])
 
 
+def cut_kernel(image_hbm, image_ref, top, bottom, left, right, sem):
+    rows, cols, _ = image_ref.shape
+    fetch = pltpu.make_async_copy(image_hbm, image_ref, sem)
+    fetch.start()
+    fetch.wait()
+    top[...] = image_ref[:SHIFT]
+    bottom[...] = image_ref[rows - SHIFT :]
+    for r in range(0, rows, SIDE):
+        band = image_ref[r : r + SIDE].astype(F32)
+        left[r : r + SIDE] = band[:, :SHIFT].astype(BF16)
+        right[r : r + SIDE] = band[:, cols - SHIFT :].astype(BF16)
+
+
 def own_kernel(
-    image_hbm, gain1_hbm, gain2_hbm, qkv_hbm, proj_hbm, table_hbm, conv_hbm, fc1_hbm, fc2_hbm,
+    image_ref, gain1_hbm, gain2_hbm, qkv_hbm, proj_hbm, table_hbm, conv_hbm, fc1_hbm, fc2_hbm,
     bias, query, kv, base, wkv, wp, wc, out_mid,
     padded, strip, wq, normed, shifted,
-    table_ref, image_ref, gain1_ref, gain2_ref, qkv_ref, proj_ref, conv_ref, fc1_ref, fc2_ref, sems,
+    table_ref, gain1_ref, gain2_ref, qkv_ref, proj_ref, conv_ref, fc1_ref, fc2_ref, sems,
 ):
     rows, cols, channels = image_ref.shape
     head_dim = channels // HEADS
@@ -166,9 +178,8 @@
     fetches = [
         pltpu.make_async_copy(source, target, sems.at[i])
         for i, (source, target) in enumerate(
-            ((table_hbm, table_ref), (image_hbm, image_ref), (gain1_hbm, gain1_ref), (qkv_hbm, qkv_ref),
-             (proj_hbm, proj_ref), (conv_hbm, conv_ref), (gain2_hbm, gain2_ref), (fc1_hbm, fc1_ref),
-             (fc2_hbm, fc2_ref))
+            ((gain1_hbm, gain1_ref), (qkv_hbm, qkv_ref), (table_hbm, table_ref), (proj_hbm, proj_ref),
+             (conv_hbm, conv_ref), (gain2_hbm, gain2_ref), (fc1_hbm, fc1_ref), (fc2_hbm, fc2_ref))
         )
     ]
     for fetch in fetches:
@@ -191,7 +202,11 @@
     )
 
     fetches[0].wait()
-    expand_bias(table_ref, padded, strip, bias)
+    gain1 = gain1_ref[...]
+    for r in range(0, rows, SIDE):
+        inner = (slice(1 + r, 1 + r + SIDE), slice(SHIFT, SHIFT + cols))
+        normed[(*inner, slice(0, channels))] = layer_norm(image_ref[r : r + SIDE].astype(F32), gain1)
+
     for fetch in fetches[1:]:
         fetch.wait()
     wq[0:channels, 0:channels] = qkv_ref[:, 0:channels]
@@ -201,19 +216,18 @@
     for tap in range(9):
         wc[tap * LANES : tap * LANES + channels, :] = conv_ref[tap // 3, tap % 3]
 
-    gain1 = gain1_ref[...]
     scale = head_dim**-0.5 * LOG2E
-    for br in range(blocks_r):
-        r = br * SIDE
-        inner = (slice(1 + r, 1 + r + SIDE), slice(SHIFT, SHIFT + cols))
-        normed[(*inner, slice(0, channels))] = layer_norm(image_ref[r : r + SIDE].astype(F32), gain1)
+    for r in range(0, rows, 2 * SIDE):
+        inner = (slice(1 + r, 1 + r + 2 * SIDE), slice(SHIFT, SHIFT + cols))
         pixels = normed[inner].astype(BF16).reshape(-1, LANES)
-        q = (dot(pixels, wq[...]) * scale).reshape(SIDE, cols, LANES)
-        both = dot(pixels, wkv[...]).reshape(SIDE, cols, 2 * LANES)
-        for bc in range(blocks_c):
-            part = slice(bc * SIDE, (bc + 1) * SIDE)
-            query[br, bc] = q[:, part].reshape(AREA, LANES)
-            kv[br, bc] = both[:, part].reshape(AREA, 2 * LANES).astype(BF16)
+        q = (dot(pixels, wq[...]) * scale).reshape(2 * SIDE, cols, LANES)
+        both = dot(pixels, wkv[...]).reshape(2 * SIDE, cols, 2 * LANES)
+        for i in range(2):
+            for bc in range(blocks_c):
+                part = (slice(i * SIDE, (i + 1) * SIDE), slice(bc * SIDE, (bc + 1) * SIDE))
+                query[r // SIDE + i, bc] = q[part].reshape(AREA, LANES).astype(BF16)
+                kv[r // SIDE + i, bc] = both[part].reshape(AREA, 2 * LANES).astype(BF16)
+    expand_bias(table_ref, padded, strip, bias)
 
     middle = [(1, 1), (2, 1), (1, 2), (2, 2)]
     pair = jnp.concatenate([kv[at] for at in middle], axis=0)
@@ -228,15 +242,17 @@
         for r in range(0, rows + 2, SIDE):
             stop = min(r + SIDE, rows + 2)
             shifted[tap, r:stop] = normed[r:stop, c0 : c0 + cols].astype(BF16)
-    for br in range(blocks_r):
-        r = br * SIDE
+    for r in range(0, rows, 2 * SIDE):
         taps = [
-            shifted[tap % 3, r + tap // 3 : r + tap // 3 + SIDE].reshape(-1, LANES) for tap in range(9)
+            shifted[tap % 3, r + tap // 3 : r + tap // 3 + 2 * SIDE].reshape(-1, LANES)
+            for tap in range(9)
         ]
-        summed = dot(jnp.concatenate(taps, axis=1), wc[...]).reshape(SIDE, cols, channels)
-        summed = summed + image_ref[r : r + SIDE].astype(F32)
-        for bc in range(blocks_c):
-            base[br, bc] = summed[:, bc * SIDE : (bc + 1) * SIDE].reshape(AREA, channels)
+        summed = dot(jnp.concatenate(taps, axis=1), wc[...]).reshape(2 * SIDE, cols, channels)
+        summed = summed + image_ref[r : r + 2 * SIDE].astype(F32)
+        for i in range(2):
+            for bc in range(blocks_c):
+                part = (slice(i * SIDE, (i + 1) * SIDE), slice(bc * SIDE, (bc + 1) * SIDE))
+                base[r // SIDE + i, bc] = summed[part].reshape(AREA, channels)
 
     own_base = jnp.concatenate([base[at] for at in ((1, 1), (1, 2), (2, 1), (2, 2))], axis=0)
     out_mid[...] = finish(
@@ -420,15 +436,25 @@
     rows, cols, channels = image.shape
     blocks_r, blocks_c = rows // SIDE, cols // SIDE
     gain1, gain2, fc2, table = norm1_gain[None], norm2_gain[None], fc2_weight.T, rel_table.T
-    top, bottom = exchange(image[:SHIFT], image[rows - SHIFT :], "row")
-    left, right = exchange(image[:, :SHIFT], image[:, cols - SHIFT :], "col")
-    fetched = (table, image, gain1, gain2, qkv_weight, proj_weight, conv_weight, fc1_weight, fc2)
+    band, column = ((SHIFT, cols, channels), BF16), ((rows, SHIFT, channels), BF16)
+    tile, first_rows, last_rows, first_cols, last_cols = call(
+        cut_kernel,
+        "cut_halo",
+        [(image.shape, BF16), band, band, column, column],
+        [pltpu.SemaphoreType.DMA(())],
+        1_000_000,
+        (image,),
+        (0,),
+    )
+    top, bottom = exchange(first_rows, last_rows, "row")
+    left, right = exchange(first_cols, last_cols, "col")
+    fetched = (table, gain1, gain2, qkv_weight, proj_weight, conv_weight, fc1_weight, fc2)
     bias, query, kv, base, wkv, wp, wc, out_mid = call(
         own_kernel,
         "own_tile",
         [
             ((HEADS, 2, 2, AREA, WIN * WIN), F32),
-            ((blocks_r, blocks_c, AREA, LANES), F32),
+            ((blocks_r, blocks_c, AREA, LANES), BF16),
             ((blocks_r, blocks_c, AREA, 2 * LANES), BF16),
             ((blocks_r, blocks_c, AREA, channels), F32),
             ((LANES, 2 * LANES), BF16),
@@ -446,8 +472,8 @@
             pltpu.SemaphoreType.DMA((len(fetched),)),
         ],
         2_000_000_000,
-        (image, gain1, gain2, qkv_weight, proj_weight, table, conv_weight, fc1_weight, fc2),
-        range(9),
+        (tile, gain1, gain2, qkv_weight, proj_weight, table, conv_weight, fc1_weight, fc2),
+        range(1, 9),
     )
     first = jnp.concatenate([top[:, :SHIFT], bottom[:, :SHIFT]])
     last = jnp.concatenate([top[:, cols - SHIFT :], bottom[:, cols - SHIFT :]])

time: 25.5 us -> 25.4 us (level)
  local copies, waits for them, and re-layouts: 2 us -> 0.03 us
  Pallas kernels: 13.2 us -> 15.1 us
    slice x2 -> x0, local copies, waits for them, and re-layouts: 1.97 us -> none  [the longest x1 0.99 us: on_device(): left, right = exchange(image[:, :SHIFT], image[:, cols - SHIFT:], 'col')]
    pallas_call x3 -> x4, Pallas kernels: 13.2 us -> 15.1 us  [call(): pl.pallas_call(kernel, out_shape=[out if isinstance(out, jax.ShapeDtypeSt...]
  transfers between devices with their start and end apart: 6 -> 6, of which waited for: 1 -> 1; matrix products, arithmetic and copies ran while one was open for 4% -> 0% of each run, Pallas kernels for 40% -> 44%
where the time goes in v7:
time: 25.4 us; the launch traced here: 25.2 us
  Pallas kernels  15.1 us (59%)
  starting transfers between devices  8.25 us (32%)
  waiting for transfers between devices  1.61 us (6%)
    pallas_call x4, Pallas kernels, call(): pl.pallas_call(kernel, out_shape=[out if isinstance(out, jax.ShapeDtypeSt...  15.1 us
    ppermute x3, starting transfers between devices, exchange(): lax.ppermute(low, axis, [((i + 1) % count, i) for i in range(count)])  5.2 us
    ppermute x3, starting transfers between devices, exchange(): lax.ppermute(high, axis, [(i, (i + 1) % count) for i in range(count)])  3.05 us
    ppermute x3, waiting for transfers between devices, exchange(): lax.ppermute(high, axis, [(i, (i + 1) % count) for i in range(count)])  1.61 us
  transfers between devices with their start and end apart: 6, of which 1 were waited for; matrix products, arithmetic and copies ran while one was open for 0% of the time, Pallas kernels for 44%

profile of v7, /device:TPU:0, one launch (start us, length us, event | category | flops | bytes accessed | tf_op | source)
XLA Modules:
  0.0 25.2 jit_solution(8554852403502927933)
XLA Ops:
  0.0 1.1 %cut_halo.1 = (bf16[32,32,180]{2,1,0:T(8,128)(2,1)S(1)}, bf16[8,32,180]{2,1,0:T(8,128)(2,1)S(1)}, bf16[8,32,180]{2,1,0:T(8,128)(2,1)S(1)}, bf16[32,8,180]{2,1,0:T(8,128)(2,1)S(1)}, bf16[32,8,180]{2,1,0:T(8,128)(2,1)S(1)}) custom-call(bf16[32,32,180]{2,1,0:T(8,128)(2,1)} %image_hbm.1), custom_call_target="tpu_custom_call" | custom-call | flops 1000000 | bytes 4000000 | tf_op jit(solution)/shard_map/cut_halo/pallas_call | solution.py:420
  1.1 3.0 %collective-permute-start = (bf16[8,32,180]{2,1,0:T(8,128)(2,1)S(1)}, bf16[8,32,180]{2,1,0:T(8,128)(2,1)S(1)}, u32[]{:S(2)}, u32[]{:S(2)}) collective-permute-start(bf16[8,32,180]{2,1,0:T(8,128)(2,1)S(1)} %get-tuple-element.21), channel_id=1, source_target_pairs={{0,8},{8,16},{16,24},{24,0},{1,9},{9,17},{17,25},{25,1},{2,10},{10... | collective-permute-start | bytes 276488 | tf_op jit(solution)/shard_map/ppermute | solution.py:412
  4.1 1.0 %collective-permute-start.1 = (bf16[8,32,180]{2,1,0:T(8,128)(2,1)S(1)}, bf16[8,32,180]{2,1,0:T(8,128)(2,1)S(1)}, u32[]{:S(2)}, u32[]{:S(2)}) collective-permute-start(bf16[8,32,180]{2,1,0:T(8,128)(2,1)S(1)} %get-tuple-element.22), channel_id=1, source_target_pairs={{8,0},{16,8},{24,16},{0,24},{9,1},{17,9},{25,17},{1,25},{10,2},{18... | collective-permute-start | bytes 276488 | tf_op jit(solution)/shard_map/ppermute | solution.py:413
  5.1 0.0 collective-permute-start.4
  5.1 3.5 %collective-permute-start.5 = (bf16[32,8,180]{2,1,0:T(8,128)(2,1)S(1)}, bf16[32,8,180]{2,1,0:T(8,128)(2,1)S(1)}, u32[]{:S(2)}, u32[]{:S(2)}) collective-permute-start(bf16[32,8,180]{2,1,0:T(8,128)(2,1)S(1)} %get-tuple-element.32), channel_id=1, source_target_pairs={{1,0},{2,1},{3,2},{4,3},{5,4},{6,5},{7,6},{0,7},{9,8},{10,9},{11,1... | collective-permute-start | bytes 276488 | tf_op jit(solution)/shard_map/ppermute | solution.py:413
  8.6 0.0 copy-start
  8.7 0.0 copy-start.1
  8.7 0.0 copy-start.2
  8.7 0.0 copy-start.3
  8.7 7.2 %own_tile.1 = (f32[6,2,2,64,256]{4,3,2,1,0:T(8,128)S(1)}, bf16[4,4,64,256]{3,2,1,0:T(8,128)(2,1)S(1)}, bf16[4,4,64,512]{3,2,1,0:T(8,128)(2,1)S(1)}, f32[4,4,64,1...) custom-call(bf16[32,32,180]{2,1,0:T(8,128)(2,1)S(1)} %get-tuple-elem, ...), custom_call_target="tpu_custom_call" | custom-call | flops 2000000000 | bytes 4000000 | tf_op jit(solution)/shard_map/own_tile/pallas_call | solution.py:420
  15.8 0.0 collective-permute-done.top_ref
  15.9 0.0 collective-permute-done.1.bottom_ref
  15.9 0.6 %collective-permute-start.3 = (bf16[16,8,180]{2,1,0:T(8,128)(2,1)S(1)}, bf16[16,8,180]{2,1,0:T(8,128)(2,1)S(1)}, u32[]{:S(2)}, u32[]{:S(2)}) collective-permute-start(bf16[16,8,180]{2,1,0:T(8,128)(2,1)S(1)} %pad_maximum_fusion.1), channel_id=1, source_target_pairs={{1,0},{2,1},{3,2},{4,3},{5,4},{6,5},{7,6},{0,7},{9,8},{10,9},{11,1... | collective-permute-start | bytes 138248 | tf_op jit(solution)/shard_map/ppermute | solution.py:413
  16.6 0.1 collective-permute-start.2
  16.6 0.0 collective-permute-done.4.left_ref
  16.7 0.0 collective-permute-done.5.right_ref
  16.7 0.0 copy-done
  16.7 0.0 copy-done.1
  16.7 0.0 copy-done.2
  16.7 0.0 copy-done.3
  16.7 3.8 %edge_windows.1 = (bf16[4,4,64,512]{3,2,1,0:T(8,128)(2,1)S(1)}, f32[4,32,180]{2,1,0:T(8,128)S(1)}, f32[2,256,180]{2,1,0:T(8,128)S(1)}) custom-call(bf16[8,32,180]{2,1,0:T(8,128)(2,1)S(1)} %collective-permute-done.top_ref, bf16[8,32,180]{2,1,0:T(8,128)(2,1)S(1)} %collective-permute-done.1.bottom_ref, bf16[32,8,180]{2,1,0:T(8,128)(2,1)S(1)} %collective-permute-done.4.left_ref, ...), custom_call_target="tpu_custom_call" | custom-call | flops 2000000000 | bytes 4000000 | tf_op jit(solution)/shard_map/edge_windows/pallas_call | solution.py:420
  20.5 0.0 collective-permute-done.3.right_ref
  20.5 1.6 %collective-permute-done.2.left_ref = bf16[16,8,180]{2,1,0:T(8,128)(2,1)S(1)} collective-permute-done((bf16[16,8,180]{2,1,0:T(8,128)(2,1)S(1)}, bf16[16,8,180]{2,1,0:T(8,128)(2,1)S(1)}, u32[]{:S(2)}, u32[]{:S(2)}) %collective-permute-start.2) | collective-permute-done | bytes 46112 | tf_op jit(solution)/shard_map/ppermute | solution.py:412
  22.1 3.1 %corner_windows.1 = bf16[32,32,180]{2,1,0:T(8,128)(2,1)} custom-call(bf16[16,8,180]{2,1,0:T(8,128)(2,1)S(1)} %collective-permute-done.2.left_ref, bf16[16,8,180]{2,1,0:T(8,128)(2,1)S(1)} %collective-permute-done.3.right_ref, f32[1,180]{1,0:T(1,128)S(1)} %bitcast.9, f32[1,180]{1,0:T(1,128)S(1)} %bitcast.12, bf16[180,360]{1,0:T(8,128)(2,1)S(1)} %copy-done, ...), custom_call_target="tpu_custom_call" | custom-call | flops 1000000000 | bytes 4000000 | tf_op jit(solution)/shard_map/corner_windows/pallas_call | solution.py:420
  (4 shorter events, 0.0 us)
Async XLA Ops:
  1.1 14.8 %collective-permute-start = (bf16[8,32,180]{2,1,0:T(8,128)(2,1)S(1)}, bf16[8,32,180]{2,1,0:T(8,128)(2,1)S(1)}, u32[]{:S(2)}, u32[]{:S(2)}) collective-permute-start(bf16[8,32,180]{2,1,0:T(8,128)(2,1)S(1)} %get-tuple-element.21), channel_id=1, source_target_pairs={{0,8},{8,16},{16,24},{24,0},{1,9},{9,17},{17,25},{25,1},{2,10},{10... | collective-permute-start | bytes 276488 | tf_op jit(solution)/shard_map/ppermute | solution.py:412
  4.1 11.8 %collective-permute-start.1 = (bf16[8,32,180]{2,1,0:T(8,128)(2,1)S(1)}, bf16[8,32,180]{2,1,0:T(8,128)(2,1)S(1)}, u32[]{:S(2)}, u32[]{:S(2)}) collective-permute-start(bf16[8,32,180]{2,1,0:T(8,128)(2,1)S(1)} %get-tuple-element.22), channel_id=1, source_target_pairs={{8,0},{16,8},{24,16},{0,24},{9,1},{17,9},{25,17},{1,25},{10,2},{18... | collective-permute-start | bytes 276488 | tf_op jit(solution)/shard_map/ppermute | solution.py:413
  5.1 11.5 %collective-permute-start.4 = (bf16[32,8,180]{2,1,0:T(8,128)(2,1)S(1)}, bf16[32,8,180]{2,1,0:T(8,128)(2,1)S(1)}, u32[]{:S(2)}, u32[]{:S(2)}) collective-permute-start(bf16[32,8,180]{2,1,0:T(8,128)(2,1)S(1)} %get-tuple-element.31), channel_id=1, source_target_pairs={{0,1},{1,2},{2,3},{3,4},{4,5},{5,6},{6,7},{7,0},{8,9},{9,10},{10,1... | collective-permute-start | bytes 276488 | tf_op jit(solution)/shard_map/ppermute | solution.py:412
  5.1 11.5 %collective-permute-start.5 = (bf16[32,8,180]{2,1,0:T(8,128)(2,1)S(1)}, bf16[32,8,180]{2,1,0:T(8,128)(2,1)S(1)}, u32[]{:S(2)}, u32[]{:S(2)}) collective-permute-start(bf16[32,8,180]{2,1,0:T(8,128)(2,1)S(1)} %get-tuple-element.32), channel_id=1, source_target_pairs={{1,0},{2,1},{3,2},{4,3},{5,4},{6,5},{7,6},{0,7},{9,8},{10,9},{11,1... | collective-permute-start | bytes 276488 | tf_op jit(solution)/shard_map/ppermute | solution.py:413
  8.6 8.0 %copy-start = (bf16[180,360]{1,0:T(8,128)(2,1)S(1)}, bf16[180,360]{1,0:T(8,128)(2,1)}, u32[]{:S(2)}) copy-start(bf16[180,360]{1,0:T(8,128)(2,1)} %fc1_ref.3) | copy-start | bytes 388804
  8.7 8.0 %copy-start.1 = (bf16[360,180]{0,1:T(8,128)(2,1)S(1)}, bf16[360,180]{0,1:T(8,128)(2,1)}, u32[]{:S(2)}) copy-start(bf16[360,180]{0,1:T(8,128)(2,1)} %param.17) | copy-start | bytes 388804
  8.7 8.0 %copy-start.2 = (f32[180]{0:T(256)S(1)}, f32[180]{0:T(256)}, u32[]{:S(2)}) copy-start(f32[180]{0:T(256)} %param.10) | copy-start | bytes 2164
  8.7 8.0 %copy-start.3 = (f32[180]{0:T(256)S(1)}, f32[180]{0:T(256)}, u32[]{:S(2)}) copy-start(f32[180]{0:T(256)} %param.11) | copy-start | bytes 2164
  15.9 4.6 %collective-permute-start.3 = (bf16[16,8,180]{2,1,0:T(8,128)(2,1)S(1)}, bf16[16,8,180]{2,1,0:T(8,128)(2,1)S(1)}, u32[]{:S(2)}, u32[]{:S(2)}) collective-permute-start(bf16[16,8,180]{2,1,0:T(8,128)(2,1)S(1)} %pad_maximum_fusion.1), channel_id=1, source_target_pairs={{1,0},{2,1},{3,2},{4,3},{5,4},{6,5},{7,6},{0,7},{9,8},{10,9},{11,1... | collective-permute-start | bytes 138248 | tf_op jit(solution)/shard_map/ppermute | solution.py:413
  16.6 5.5 %collective-permute-start.2 = (bf16[16,8,180]{2,1,0:T(8,128)(2,1)S(1)}, bf16[16,8,180]{2,1,0:T(8,128)(2,1)S(1)}, u32[]{:S(2)}, u32[]{:S(2)}) collective-permute-start(bf16[16,8,180]{2,1,0:T(8,128)(2,1)S(1)} %pad_maximum_fusion), channel_id=1, source_target_pairs={{0,1},{1,2},{2,3},{3,4},{4,5},{5,6},{6,7},{7,0},{8,9},{9,10},{10,1... | collective-permute-start | bytes 138248 | tf_op jit(solution)/shard_map/ppermute | solution.py:412

commit v8 on v7

--- a/solution.py
+++ b/solution.py
@@ -120,13 +120,11 @@
     def scores_at(unit):
         return scores_of(unit[0], unit[2][:, :LANES], head_dim, channels)
 
-    results = []
     ahead = scores_at(units[0])
     for i, unit in enumerate(units):
         scores, ahead = ahead, scores_at(units[i + 1]) if i + 1 < len(units) else None
         part_bias = jnp.concatenate([bias[:, hy, hx] for hy, hx in unit[1]], axis=1)
-        results.append(mix(scores, part_bias, unit[2][:, LANES:], head_dim, channels))
-    return results
+        yield mix(scores, part_bias, unit[2][:, LANES:], head_dim, channels)
 
 
 def spread_matrix(channels):
@@ -166,10 +164,10 @@
 
 
 def own_kernel(
-    image_ref, gain1_hbm, gain2_hbm, qkv_hbm, proj_hbm, table_hbm, conv_hbm, fc1_hbm, fc2_hbm,
-    bias, query, kv, base, wkv, wp, wc, out_mid,
+    image_ref, gain1_hbm, qkv_hbm, proj_hbm, table_hbm, conv_hbm,
+    bias, query, kv, base, wkv, wp, wc,
     padded, strip, wq, normed, shifted,
-    table_ref, gain1_ref, gain2_ref, qkv_ref, proj_ref, conv_ref, fc1_ref, fc2_ref, sems,
+    table_ref, gain1_ref, qkv_ref, proj_ref, conv_ref, sems,
 ):
     rows, cols, channels = image_ref.shape
     head_dim = channels // HEADS
@@ -179,7 +177,7 @@
         pltpu.make_async_copy(source, target, sems.at[i])
         for i, (source, target) in enumerate(
             ((gain1_hbm, gain1_ref), (qkv_hbm, qkv_ref), (table_hbm, table_ref), (proj_hbm, proj_ref),
-             (conv_hbm, conv_ref), (gain2_hbm, gain2_ref), (fc1_hbm, fc1_ref), (fc2_hbm, fc2_ref))
+             (conv_hbm, conv_ref))
         )
     ]
     for fetch in fetches:
@@ -217,54 +215,37 @@
         wc[tap * LANES : tap * LANES + channels, :] = conv_ref[tap // 3, tap % 3]
 
     scale = head_dim**-0.5 * LOG2E
-    for r in range(0, rows, 2 * SIDE):
-        inner = (slice(1 + r, 1 + r + 2 * SIDE), slice(SHIFT, SHIFT + cols))
+    for br in range(blocks_r):
+        inner = (slice(1 + br * SIDE, 1 + (br + 1) * SIDE), slice(SHIFT, SHIFT + cols))
         pixels = normed[inner].astype(BF16).reshape(-1, LANES)
-        q = (dot(pixels, wq[...]) * scale).reshape(2 * SIDE, cols, LANES)
-        both = dot(pixels, wkv[...]).reshape(2 * SIDE, cols, 2 * LANES)
-        for i in range(2):
-            for bc in range(blocks_c):
-                part = (slice(i * SIDE, (i + 1) * SIDE), slice(bc * SIDE, (bc + 1) * SIDE))
-                query[r // SIDE + i, bc] = q[part].reshape(AREA, LANES).astype(BF16)
-                kv[r // SIDE + i, bc] = both[part].reshape(AREA, 2 * LANES).astype(BF16)
+        q = (dot(pixels, wq[...]) * scale).reshape(SIDE, cols, LANES)
+        both = dot(pixels, wkv[...]).reshape(SIDE, cols, 2 * LANES)
+        for bc in range(blocks_c):
+            part = slice(bc * SIDE, (bc + 1) * SIDE)
+            query[br, bc] = q[:, part].reshape(AREA, LANES).astype(BF16)
+            kv[br, bc] = both[:, part].reshape(AREA, 2 * LANES).astype(BF16)
     expand_bias(table_ref, padded, strip, bias)
-
-    middle = [(1, 1), (2, 1), (1, 2), (2, 2)]
-    pair = jnp.concatenate([kv[at] for at in middle], axis=0)
-    units = [
-        ([query[1, 1], query[1, 2]], [(0, 0), (0, 1)], pair),
-        ([query[2, 1], query[2, 2]], [(1, 0), (1, 1)], pair),
-    ]
-    mixed = attention(units, bias, head_dim, channels)
 
     for tap in range(3):
         c0 = SHIFT - 1 + tap
         for r in range(0, rows + 2, SIDE):
             stop = min(r + SIDE, rows + 2)
             shifted[tap, r:stop] = normed[r:stop, c0 : c0 + cols].astype(BF16)
-    for r in range(0, rows, 2 * SIDE):
+    for br in range(blocks_r):
+        r = br * SIDE
         taps = [
-            shifted[tap % 3, r + tap // 3 : r + tap // 3 + 2 * SIDE].reshape(-1, LANES)
-            for tap in range(9)
+            shifted[tap % 3, r + tap // 3 : r + tap // 3 + SIDE].reshape(-1, LANES) for tap in range(9)
         ]
-        summed = dot(jnp.concatenate(taps, axis=1), wc[...]).reshape(2 * SIDE, cols, channels)
-        summed = summed + image_ref[r : r + 2 * SIDE].astype(F32)
-        for i in range(2):
-            for bc in range(blocks_c):
-                part = (slice(i * SIDE, (i + 1) * SIDE), slice(bc * SIDE, (bc + 1) * SIDE))
-                base[r // SIDE + i, bc] = summed[part].reshape(AREA, channels)
-
-    own_base = jnp.concatenate([base[at] for at in ((1, 1), (1, 2), (2, 1), (2, 2))], axis=0)
-    out_mid[...] = finish(
-        jnp.concatenate(mixed, axis=0), own_base, spread_matrix(channels), wp, gain2_ref[...], fc1_ref,
-        fc2_ref, channels,
-    )
+        summed = dot(jnp.concatenate(taps, axis=1), wc[...]).reshape(SIDE, cols, channels)
+        summed = summed + image_ref[r : r + SIDE].astype(F32)
+        for bc in range(blocks_c):
+            base[br, bc] = summed[:, bc * SIDE : (bc + 1) * SIDE].reshape(AREA, channels)
 
 
 def edge_kernel(
     top_ref, bottom_ref, left_ref, right_ref, gain1_ref, gain2_ref, fc1_ref, fc2_ref,
     bias, query, kv, base, wkv, wp, wc,
-    kv_edge, fixes, out_edge,
+    kv_edge, fixes, out_edge, out_mid,
     bands_r, bands_c,
 ):
     cols, channels = top_ref.shape[1:]
@@ -304,11 +285,25 @@
     ]
     places = [((0, 1), (0, 2)), ((3, 1), (3, 2)), ((1, 0), (2, 0)), ((1, 3), (2, 3))]
     quadrants = [((1, 0), (1, 1)), ((0, 0), (0, 1)), ((0, 1), (1, 1)), ((0, 0), (1, 0))]
+    middle = jnp.concatenate([kv[at] for at in ((1, 1), (2, 1), (1, 2), (2, 2))], axis=0)
     units = [
+        ([query[1, 1], query[1, 2]], [(0, 0), (0, 1)], middle),
+        ([query[2, 1], query[2, 2]], [(1, 0), (1, 1)], middle),
+    ]
+    units += [
         ([query[at] for at in places[i]], quadrants[i], jnp.concatenate(keys[i], axis=0))
         for i in range(4)
     ]
-    mixed = attention(units, bias, head_dim, channels)
+    gain2, spread = gain2_ref[...], spread_matrix(channels)
+    mixed_mid, mixed = [], []
+    for i, result in enumerate(attention(units, bias, head_dim, channels)):
+        (mixed_mid if i < 2 else mixed).append(result)
+        if i == 2:
+            mid_base = [base[at] for at in ((1, 1), (1, 2), (2, 1), (2, 2))]
+            out_mid[...] = finish(
+                jnp.concatenate(mixed_mid, axis=0), jnp.concatenate(mid_base, axis=0), spread, wp, gain2,
+                fc1_ref, fc2_ref, channels,
+            )
 
     for i, (taps, source) in enumerate((((0, 1, 2), SHIFT - 1), ((6, 7, 8), 0))):
         pieces = [bands_r[i, source, SHIFT - 1 + t : SHIFT - 1 + t + cols] for t in range(3)]
@@ -319,7 +314,6 @@
         weights = jnp.concatenate([wc[t * LANES : (t + 1) * LANES] for t in taps], axis=0)
         fixes[2 + i] = dot(jnp.concatenate(pieces, axis=1).astype(BF16), weights)
 
-    gain2, spread = gain2_ref[...], spread_matrix(channels)
     for group in range(2):
         raw = jnp.concatenate([mixed[2 * group], mixed[2 * group + 1]], axis=0)
         parts = [
@@ -378,7 +372,7 @@
     units = [
         ([query[places[i]]], [quadrants[i]], jnp.concatenate(keys[i], axis=0)) for i in range(4)
     ]
-    mixed = attention(units, bias, head_dim, channels)
+    mixed = list(attention(units, bias, head_dim, channels))
 
     parts = []
     for i, (tap, y, x) in enumerate(((0, 7, 7), (2, 7, 0), (6, 0, 7), (8, 0, 0))):
@@ -448,8 +442,8 @@
     )
     top, bottom = exchange(first_rows, last_rows, "row")
     left, right = exchange(first_cols, last_cols, "col")
-    fetched = (table, gain1, gain2, qkv_weight, proj_weight, conv_weight, fc1_weight, fc2)
-    bias, query, kv, base, wkv, wp, wc, out_mid = call(
+    fetched = (table, gain1, qkv_weight, proj_weight, conv_weight)
+    bias, query, kv, base, wkv, wp, wc = call(
         own_kernel,
         "own_tile",
         [
@@ -460,7 +454,6 @@
             ((LANES, 2 * LANES), BF16),
             ((LANES, channels), BF16),
             ((9 * LANES, channels), BF16),
-            ((4 * AREA, channels), F32),
         ],
         [
             ((8, 1024), F32),
@@ -472,19 +465,20 @@
             pltpu.SemaphoreType.DMA((len(fetched),)),
         ],
         2_000_000_000,
-        (tile, gain1, gain2, qkv_weight, proj_weight, table, conv_weight, fc1_weight, fc2),
-        range(1, 9),
+        (tile, gain1, qkv_weight, proj_weight, table, conv_weight),
+        range(1, 6),
     )
     first = jnp.concatenate([top[:, :SHIFT], bottom[:, :SHIFT]])
     last = jnp.concatenate([top[:, cols - SHIFT :], bottom[:, cols - SHIFT :]])
     left_corner, right_corner = exchange(first, last, "col")
-    kv_edge, fixes, out_edge = call(
+    kv_edge, fixes, out_edge, out_mid = call(
         edge_kernel,
         "edge_windows",
         [
             ((4, blocks_c, AREA, 2 * LANES), BF16),
             ((4, cols, channels), F32),
             ((2, 4 * AREA, channels), F32),
+            ((4 * AREA, channels), F32),
         ],
         [((2, SHIFT, cols + 2 * SHIFT, LANES), F32), ((2, rows + 2, SHIFT, LANES), F32)],
         2_000_000_000,

time: 25.4 us -> 22.7 us (0.89)
  Pallas kernels: 15.1 us -> 13 us
  waiting for transfers between devices: 1.61 us -> 0.26 us
  starting transfers between devices: 8.25 us -> 9.03 us
    pallas_call x4, Pallas kernels: 15.1 us -> 13 us  [call(): pl.pallas_call(kernel, out_shape=[out if isinstance(out, jax.ShapeDtypeSt...]
    ppermute x3, waiting for transfers between devices: 1.61 us -> 0.25 us  [exchange(): lax.ppermute(high, axis, [(i, (i + 1) % count) for i in range(count)])]
    ppermute x3, starting transfers between devices: 5.2 us -> 5.98 us  [exchange(): lax.ppermute(low, axis, [((i + 1) % count, i) for i in range(count)])]
  transfers between devices with their start and end apart: 6 -> 6, of which waited for: 1 -> 1; matrix products, arithmetic and copies ran while one was open for 0% -> 0% of each run, Pallas kernels for 44% -> 39%
where the time goes in v8:
time: 22.7 us; the launch traced here: 22.5 us
  Pallas kernels  13 us (57%)
  starting transfers between devices  9.03 us (40%)
  waiting for transfers between devices  0.26 us (1%)
    pallas_call x4, Pallas kernels, call(): pl.pallas_call(kernel, out_shape=[out if isinstance(out, jax.ShapeDtypeSt...  13 us
    ppermute x3, starting transfers between devices, exchange(): lax.ppermute(low, axis, [((i + 1) % count, i) for i in range(count)])  5.98 us
    ppermute x3, starting transfers between devices, exchange(): lax.ppermute(high, axis, [(i, (i + 1) % count) for i in range(count)])  3.05 us
  transfers between devices with their start and end apart: 6, of which 1 were waited for; matrix products, arithmetic and copies ran while one was open for 0% of the time, Pallas kernels for 39%

profile of v8, /device:TPU:0, one launch (start us, length us, event | category | flops | bytes accessed | tf_op | source)
XLA Modules:
  0.0 22.5 jit_solution(8978360871869592827)
XLA Ops:
  0.0 1.1 %cut_halo.1 = (bf16[32,32,180]{2,1,0:T(8,128)(2,1)S(1)}, bf16[8,32,180]{2,1,0:T(8,128)(2,1)S(1)}, bf16[8,32,180]{2,1,0:T(8,128)(2,1)S(1)}, bf16[32,8,180]{2,1,0:T(8,128)(2,1)S(1)}, bf16[32,8,180]{2,1,0:T(8,128)(2,1)S(1)}) custom-call(bf16[32,32,180]{2,1,0:T(8,128)(2,1)} %image_hbm.1), custom_call_target="tpu_custom_call" | custom-call | flops 1000000 | bytes 4000000 | tf_op jit(solution)/shard_map/cut_halo/pallas_call | solution.py:414
  1.1 3.0 %collective-permute-start = (bf16[8,32,180]{2,1,0:T(8,128)(2,1)S(1)}, bf16[8,32,180]{2,1,0:T(8,128)(2,1)S(1)}, u32[]{:S(2)}, u32[]{:S(2)}) collective-permute-start(bf16[8,32,180]{2,1,0:T(8,128)(2,1)S(1)} %get-tuple-element.21), channel_id=1, source_target_pairs={{0,8},{8,16},{16,24},{24,0},{1,9},{9,17},{17,25},{25,1},{2,10},{10... | collective-permute-start | bytes 276488 | tf_op jit(solution)/shard_map/ppermute | solution.py:406
  4.1 1.0 %collective-permute-start.1 = (bf16[8,32,180]{2,1,0:T(8,128)(2,1)S(1)}, bf16[8,32,180]{2,1,0:T(8,128)(2,1)S(1)}, u32[]{:S(2)}, u32[]{:S(2)}) collective-permute-start(bf16[8,32,180]{2,1,0:T(8,128)(2,1)S(1)} %get-tuple-element.22), channel_id=1, source_target_pairs={{8,0},{16,8},{24,16},{0,24},{9,1},{17,9},{25,17},{1,25},{10,2},{18... | collective-permute-start | bytes 276488 | tf_op jit(solution)/shard_map/ppermute | solution.py:407
  5.1 0.0 collective-permute-start.4
  5.1 3.5 %collective-permute-start.5 = (bf16[32,8,180]{2,1,0:T(8,128)(2,1)S(1)}, bf16[32,8,180]{2,1,0:T(8,128)(2,1)S(1)}, u32[]{:S(2)}, u32[]{:S(2)}) collective-permute-start(bf16[32,8,180]{2,1,0:T(8,128)(2,1)S(1)} %get-tuple-element.32), channel_id=1, source_target_pairs={{1,0},{2,1},{3,2},{4,3},{5,4},{6,5},{7,6},{0,7},{9,8},{10,9},{11,1... | collective-permute-start | bytes 276488 | tf_op jit(solution)/shard_map/ppermute | solution.py:407
  8.6 0.0 copy-start
  8.7 0.0 copy-start.1
  8.7 0.0 copy-start.2
  8.7 0.0 copy-start.3
  8.7 3.7 %own_tile.1 = (f32[6,2,2,64,256]{4,3,2,1,0:T(8,128)S(1)}, bf16[4,4,64,256]{3,2,1,0:T(8,128)(2,1)S(1)}, bf16[4,4,64,512]{3,2,1,0:T(8,128)(2,1)S(1)}, f32[4,4,64,1...) custom-call(bf16[32,32,180]{2,1,0:T(8,128)(2,1)S(1)} %get-tuple-elem, ...), custom_call_target="tpu_custom_call" | custom-call | flops 2000000000 | bytes 4000000 | tf_op jit(solution)/shard_map/own_tile/pallas_call | solution.py:414
  12.4 0.0 collective-permute-done.top_ref
  12.4 0.0 collective-permute-done.1.bottom_ref
  12.4 1.4 %collective-permute-start.3 = (bf16[16,8,180]{2,1,0:T(8,128)(2,1)S(1)}, bf16[16,8,180]{2,1,0:T(8,128)(2,1)S(1)}, u32[]{:S(2)}, u32[]{:S(2)}) collective-permute-start(bf16[16,8,180]{2,1,0:T(8,128)(2,1)S(1)} %pad_maximum_fusion.1), channel_id=1, source_target_pairs={{1,0},{2,1},{3,2},{4,3},{5,4},{6,5},{7,6},{0,7},{9,8},{10,9},{11,1... | collective-permute-start | bytes 138248 | tf_op jit(solution)/shard_map/ppermute | solution.py:407
  13.9 0.1 collective-permute-start.2
  13.9 0.0 collective-permute-done.4.left_ref
  13.9 0.0 collective-permute-done.5.right_ref
  13.9 0.0 copy-done
  14.0 0.0 copy-done.1
  14.0 0.0 copy-done.2
  14.0 0.0 copy-done.3
  14.0 5.1 %edge_windows.1 = (bf16[4,4,64,512]{3,2,1,0:T(8,128)(2,1)S(1)}, f32[4,32,180]{2,1,0:T(8,128)S(1)}, f32[2,256,180]{2,1,0:T(8,128)S(1)}, f32[256,180]{1,0:T(8,128)S(1)}) custom-call(bf16[8,32,180]{2,1,0:T(8,128)(2,1)S(1)} %collective-permute-done.top_ref, bf16[8,32,180]{2,1,0:T(8,128)(2,1)S(1)} %collective-permute-done.1.bottom_ref, ...), custom_call_target="tpu_custom_call" | custom-call | flops 2000000000 | bytes 4000000 | tf_op jit(solution)/shard_map/edge_windows/pallas_call | solution.py:414
  19.1 0.0 collective-permute-done.3.right_ref
  19.2 0.2 %collective-permute-done.2.left_ref = bf16[16,8,180]{2,1,0:T(8,128)(2,1)S(1)} collective-permute-done((bf16[16,8,180]{2,1,0:T(8,128)(2,1)S(1)}, bf16[16,8,180]{2,1,0:T(8,128)(2,1)S(1)}, u32[]{:S(2)}, u32[]{:S(2)}) %collective-permute-start.2) | collective-permute-done | bytes 46112 | tf_op jit(solution)/shard_map/ppermute | solution.py:406
  19.4 3.1 %corner_windows.1 = bf16[32,32,180]{2,1,0:T(8,128)(2,1)} custom-call(bf16[16,8,180]{2,1,0:T(8,128)(2,1)S(1)} %collective-permute-done.2.left_ref, bf16[16,8,180]{2,1,0:T(8,128)(2,1)S(1)} %collective-permute-done.3.right_ref, f32[1,180]{1,0:T(1,128)S(1)} %bitcast.8, f32[1,180]{1,0:T(1,128)S(1)} %bitcast.10, bf16[180,360]{1,0:T(8,128)(2,1)S(1)} %copy-done, ...), custom_call_target="tpu_custom_call" | custom-call | flops 1000000000 | bytes 4000000 | tf_op jit(solution)/shard_map/corner_windows/pallas_call | solution.py:414
  (4 shorter events, 0.0 us)
Async XLA Ops:
  1.1 11.3 %collective-permute-start = (bf16[8,32,180]{2,1,0:T(8,128)(2,1)S(1)}, bf16[8,32,180]{2,1,0:T(8,128)(2,1)S(1)}, u32[]{:S(2)}, u32[]{:S(2)}) collective-permute-start(bf16[8,32,180]{2,1,0:T(8,128)(2,1)S(1)} %get-tuple-element.21), channel_id=1, source_target_pairs={{0,8},{8,16},{16,24},{24,0},{1,9},{9,17},{17,25},{25,1},{2,10},{10... | collective-permute-start | bytes 276488 | tf_op jit(solution)/shard_map/ppermute | solution.py:406
  4.1 8.3 %collective-permute-start.1 = (bf16[8,32,180]{2,1,0:T(8,128)(2,1)S(1)}, bf16[8,32,180]{2,1,0:T(8,128)(2,1)S(1)}, u32[]{:S(2)}, u32[]{:S(2)}) collective-permute-start(bf16[8,32,180]{2,1,0:T(8,128)(2,1)S(1)} %get-tuple-element.22), channel_id=1, source_target_pairs={{8,0},{16,8},{24,16},{0,24},{9,1},{17,9},{25,17},{1,25},{10,2},{18... | collective-permute-start | bytes 276488 | tf_op jit(solution)/shard_map/ppermute | solution.py:407
  5.1 8.8 %collective-permute-start.4 = (bf16[32,8,180]{2,1,0:T(8,128)(2,1)S(1)}, bf16[32,8,180]{2,1,0:T(8,128)(2,1)S(1)}, u32[]{:S(2)}, u32[]{:S(2)}) collective-permute-start(bf16[32,8,180]{2,1,0:T(8,128)(2,1)S(1)} %get-tuple-element.31), channel_id=1, source_target_pairs={{0,1},{1,2},{2,3},{3,4},{4,5},{5,6},{6,7},{7,0},{8,9},{9,10},{10,1... | collective-permute-start | bytes 276488 | tf_op jit(solution)/shard_map/ppermute | solution.py:406
  5.1 8.8 %collective-permute-start.5 = (bf16[32,8,180]{2,1,0:T(8,128)(2,1)S(1)}, bf16[32,8,180]{2,1,0:T(8,128)(2,1)S(1)}, u32[]{:S(2)}, u32[]{:S(2)}) collective-permute-start(bf16[32,8,180]{2,1,0:T(8,128)(2,1)S(1)} %get-tuple-element.32), channel_id=1, source_target_pairs={{1,0},{2,1},{3,2},{4,3},{5,4},{6,5},{7,6},{0,7},{9,8},{10,9},{11,1... | collective-permute-start | bytes 276488 | tf_op jit(solution)/shard_map/ppermute | solution.py:407
  8.6 5.3 %copy-start = (bf16[180,360]{1,0:T(8,128)(2,1)S(1)}, bf16[180,360]{1,0:T(8,128)(2,1)}, u32[]{:S(2)}) copy-start(bf16[180,360]{1,0:T(8,128)(2,1)} %fc1_ref.3) | copy-start | bytes 388804
  8.7 5.3 %copy-start.1 = (bf16[360,180]{0,1:T(8,128)(2,1)S(1)}, bf16[360,180]{0,1:T(8,128)(2,1)}, u32[]{:S(2)}) copy-start(bf16[360,180]{0,1:T(8,128)(2,1)} %param.17) | copy-start | bytes 388804
  8.7 5.3 %copy-start.2 = (f32[180]{0:T(256)S(1)}, f32[180]{0:T(256)}, u32[]{:S(2)}) copy-start(f32[180]{0:T(256)} %param.10) | copy-start | bytes 2164
  8.7 5.3 %copy-start.3 = (f32[180]{0:T(256)S(1)}, f32[180]{0:T(256)}, u32[]{:S(2)}) copy-start(f32[180]{0:T(256)} %param.11) | copy-start | bytes 2164
  12.4 6.7 %collective-permute-start.3 = (bf16[16,8,180]{2,1,0:T(8,128)(2,1)S(1)}, bf16[16,8,180]{2,1,0:T(8,128)(2,1)S(1)}, u32[]{:S(2)}, u32[]{:S(2)}) collective-permute-start(bf16[16,8,180]{2,1,0:T(8,128)(2,1)S(1)} %pad_maximum_fusion.1), channel_id=1, source_target_pairs={{1,0},{2,1},{3,2},{4,3},{5,4},{6,5},{7,6},{0,7},{9,8},{10,9},{11,1... | collective-permute-start | bytes 138248 | tf_op jit(solution)/shard_map/ppermute | solution.py:407
  13.9 5.5 %collective-permute-start.2 = (bf16[16,8,180]{2,1,0:T(8,128)(2,1)S(1)}, bf16[16,8,180]{2,1,0:T(8,128)(2,1)S(1)}, u32[]{:S(2)}, u32[]{:S(2)}) collective-permute-start(bf16[16,8,180]{2,1,0:T(8,128)(2,1)S(1)} %pad_maximum_fusion), channel_id=1, source_target_pairs={{0,1},{1,2},{2,3},{3,4},{4,5},{5,6},{6,7},{7,0},{8,9},{9,10},{10,1... | collective-permute-start | bytes 138248 | tf_op jit(solution)/shard_map/ppermute | solution.py:406

commit v9 on v8

--- a/solution.py
+++ b/solution.py
@@ -107,13 +107,15 @@
     count = scores.shape[0] // HEADS
     scores = scores.reshape(HEADS, count, WIN * WIN) + part_bias
     scores = scores - jnp.max(scores, axis=-1, keepdims=True)
-    soft = jnp.exp2(scores).astype(BF16).reshape(HEADS * count, WIN * WIN)
-    mixed = dot(soft, values)
-    result = mixed[0:count]
+    weights = jnp.exp2(scores)
+    total = jnp.sum(weights, axis=-1, keepdims=True)
+    mixed = dot(weights.astype(BF16).reshape(HEADS * count, WIN * WIN), values)
+    result, divisor = mixed[0:count], jnp.broadcast_to(total[0], (count, LANES))
     for h in range(1, HEADS):
-        mine = (lane >= h * head_dim) & (lane < (h + 1) * head_dim) | (lane == channels + h)
+        mine = (lane >= h * head_dim) & (lane < (h + 1) * head_dim)
         result = jnp.where(mine, mixed[h * count : (h + 1) * count], result)
-    return result
+        divisor = jnp.where(mine, total[h], divisor)
+    return (result / divisor).astype(BF16)
 
 
 def attention(units, bias, head_dim, channels):
@@ -127,23 +129,7 @@
         yield mix(scores, part_bias, unit[2][:, LANES:], head_dim, channels)
 
 
-def spread_matrix(channels):
-    head_dim = channels // HEADS
-    sum_row = lax.broadcasted_iota(jnp.int32, (HALF, LANES), 0) + HALF - channels
-    lane_wide = lax.broadcasted_iota(jnp.int32, (HALF, LANES), 1)
-    return one_hot(
-        (sum_row >= 0) & (lane_wide >= sum_row * head_dim) & (lane_wide < (sum_row + 1) * head_dim)
-        & (lane_wide < channels)
-    )
-
-
-def finish(raw, base, spread, wp, gain2, fc1, fc2, channels):
-    half = lanes_of()[:, HALF:]
-    is_sum = (half >= channels) & (half < channels + HEADS)
-    inverse = jnp.where(is_sum, 1.0 / raw[:, HALF:], 0.0)
-    high = inverse.astype(BF16)
-    low = (inverse - high.astype(F32)).astype(BF16)
-    heads_out = (raw * (dot(high, spread) + dot(low, spread))).astype(BF16)
+def finish(heads_out, base, wp, gain2, fc1, fc2, channels):
     state1 = base + dot(heads_out, wp[...]).astype(BF16).astype(F32)
     normed2 = layer_norm(state1, gain2).astype(BF16)
     hidden = gelu(dot(normed2, fc1[...])).astype(BF16)
@@ -191,9 +177,6 @@
     wkv[176:192, 0:LANES] = jnp.where(
         (special == flag_lane) & (lanes16 == flag_lane), MASKED, 0.0
     ).astype(BF16)
-    wkv[176:192, LANES:] = one_hot(
-        (special == one_lane) & (lanes16 >= channels) & (lanes16 < channels + HEADS)
-    )
     normed[...] = jnp.zeros_like(normed)
     normed[1 : 1 + rows, SHIFT : SHIFT + cols, HALF:] = jnp.broadcast_to(
         marks(channels, 0.0)[None], (rows, cols, HALF)
@@ -245,8 +228,8 @@
 def edge_kernel(
     top_ref, bottom_ref, left_ref, right_ref, gain1_ref, gain2_ref, fc1_ref, fc2_ref,
     bias, query, kv, base, wkv, wp, wc,
-    kv_edge, fixes, out_edge, out_mid,
-    bands_r, bands_c,
+    kv_edge, corner_base, out_edge, out_mid,
+    bands_r, bands_c, fixes,
 ):
     cols, channels = top_ref.shape[1:]
     rows = left_ref.shape[0]
@@ -294,14 +277,14 @@
         ([query[at] for at in places[i]], quadrants[i], jnp.concatenate(keys[i], axis=0))
         for i in range(4)
     ]
-    gain2, spread = gain2_ref[...], spread_matrix(channels)
+    gain2 = gain2_ref[...]
     mixed_mid, mixed = [], []
     for i, result in enumerate(attention(units, bias, head_dim, channels)):
         (mixed_mid if i < 2 else mixed).append(result)
         if i == 2:
             mid_base = [base[at] for at in ((1, 1), (1, 2), (2, 1), (2, 2))]
             out_mid[...] = finish(
-                jnp.concatenate(mixed_mid, axis=0), jnp.concatenate(mid_base, axis=0), spread, wp, gain2,
+                jnp.concatenate(mixed_mid, axis=0), jnp.concatenate(mid_base, axis=0), wp, gain2,
                 fc1_ref, fc2_ref, channels,
             )
 
@@ -314,6 +297,8 @@
         weights = jnp.concatenate([wc[t * LANES : (t + 1) * LANES] for t in taps], axis=0)
         fixes[2 + i] = dot(jnp.concatenate(pieces, axis=1).astype(BF16), weights)
 
+    for i, at in enumerate(((0, 0), (0, 3), (3, 0), (3, 3))):
+        corner_base[i] = corrected(base, fixes, at, channels)
     for group in range(2):
         raw = jnp.concatenate([mixed[2 * group], mixed[2 * group + 1]], axis=0)
         parts = [
@@ -321,7 +306,7 @@
             for at in (*places[2 * group], *places[2 * group + 1])
         ]
         out_edge[group] = finish(
-            raw, jnp.concatenate(parts, axis=0), spread, wp, gain2, fc1_ref, fc2_ref, channels
+            raw, jnp.concatenate(parts, axis=0), wp, gain2, fc1_ref, fc2_ref, channels
         )
 
 
@@ -341,12 +326,32 @@
 
 def corner_kernel(
     left_ref, right_ref, gain1_ref, gain2_ref, fc1_ref, fc2_ref,
-    bias, query, kv, base, wkv, wp, wc, kv_edge, fixes, out_mid, out_edge,
-    out_ref,
-    normed,
+    bias, query, kv, wkv, wp, wc, kv_edge, corner_base, out_mid, out_edge,
+    out_hbm,
+    normed, out_ref, sems,
 ):
-    channels = left_ref.shape[2]
+    rows, _, channels = out_ref.shape
     head_dim = channels // HEADS
+
+    def finish_bands(which, corners):
+        def piece(source, i):
+            return source[i * AREA : (i + 1) * AREA]
+
+        for br in which:
+            if br in (0, 3):
+                i = 0 if br == 0 else 2
+                band = [corners[i], piece(out_edge.at[0], i), piece(out_edge.at[0], i + 1), corners[i + 1]]
+            else:
+                i = br - 1
+                band = [piece(out_edge.at[1], i), piece(out_mid, 2 * i), piece(out_mid, 2 * i + 1),
+                        piece(out_edge.at[1], i + 2)]
+            band = [part.reshape(SIDE, SIDE, channels) for part in band]
+            out_ref[br * SIDE : (br + 1) * SIDE] = jnp.concatenate(band, axis=1).astype(BF16)
+
+    finish_bands((1, 2), None)
+    inner = slice(SIDE, rows - SIDE)
+    writes = [pltpu.make_async_copy(out_ref.at[inner], out_hbm.at[inner], sems.at[0])]
+    writes[0].start()
     row, last_row = lax.axis_index("row"), lax.axis_size("row") - 1
     col, last_col = lax.axis_index("col"), lax.axis_size("col") - 1
     gain1 = gain1_ref[...]
@@ -381,24 +386,20 @@
         term = term[x : x + 1]
         pixel = lax.broadcasted_iota(jnp.int32, (AREA, 1), 0)
         at = (SIDE - 1 - y) * SIDE + SIDE - 1 - x
-        block = corrected(base, fixes, places[i], channels)
-        parts.append(block + jnp.where(pixel == at, term, 0.0))
+        parts.append(corner_base[i] + jnp.where(pixel == at, term, 0.0))
     out_corner = finish(
-        jnp.concatenate(mixed, axis=0), jnp.concatenate(parts, axis=0), spread_matrix(channels), wp,
-        gain2_ref[...], fc1_ref, fc2_ref, channels,
-    )
-
-    def piece(source, i):
-        return source[i * AREA : (i + 1) * AREA].reshape(SIDE, SIDE, channels)
-
-    bands = [
-        [piece(out_corner, 0), piece(out_edge.at[0], 0), piece(out_edge.at[0], 1), piece(out_corner, 1)],
-        [piece(out_edge.at[1], 0), piece(out_mid, 0), piece(out_mid, 1), piece(out_edge.at[1], 2)],
-        [piece(out_edge.at[1], 1), piece(out_mid, 2), piece(out_mid, 3), piece(out_edge.at[1], 3)],
-        [piece(out_corner, 2), piece(out_edge.at[0], 2), piece(out_edge.at[0], 3), piece(out_corner, 3)],
-    ]
-    for br, band in enumerate(bands):
-        out_ref[br * SIDE : (br + 1) * SIDE] = jnp.concatenate(band, axis=1).astype(BF16)
+        jnp.concatenate(mixed, axis=0), jnp.concatenate(parts, axis=0), wp, gain2_ref[...], fc1_ref, fc2_ref, channels,
+    )
+
+    finish_bands((0, 3), [out_corner[i * AREA : (i + 1) * AREA] for i in range(4)])
+    writes[0].wait()
+    for r in (0, rows - SIDE):
+        at = slice(r, r + SIDE)
+        write = pltpu.make_async_copy(out_ref.at[at], out_hbm.at[at], sems.at[1 if r == 0 else 2])
+        write.start()
+        writes.append(write)
+    writes[1].wait()
+    writes[2].wait()
 
 
 def exchange(low, high, axis):
@@ -415,7 +416,7 @@
         kernel,
         out_shape=[out if isinstance(out, jax.ShapeDtypeStruct) else pltpu.VMEM(*out) for out in outs],
         in_specs=[hbm if i in in_hbm else vmem for i in range(len(operands))],
-        out_specs=[vmem] * len(outs),
+        out_specs=[hbm if isinstance(out, jax.ShapeDtypeStruct) else vmem for out in outs],
         scratch_shapes=[pltpu.VMEM(*s) if isinstance(s, tuple) else s for s in scratch],
         cost_estimate=pl.CostEstimate(flops=flops, bytes_accessed=4_000_000, transcendentals=1_000_000),
         compiler_params=pltpu.CompilerParams(vmem_limit_bytes=24 * 1024 * 1024),
@@ -471,16 +472,20 @@
     first = jnp.concatenate([top[:, :SHIFT], bottom[:, :SHIFT]])
     last = jnp.concatenate([top[:, cols - SHIFT :], bottom[:, cols - SHIFT :]])
     left_corner, right_corner = exchange(first, last, "col")
-    kv_edge, fixes, out_edge, out_mid = call(
+    kv_edge, corner_base, out_edge, out_mid = call(
         edge_kernel,
         "edge_windows",
         [
             ((4, blocks_c, AREA, 2 * LANES), BF16),
-            ((4, cols, channels), F32),
+            ((4, AREA, channels), F32),
             ((2, 4 * AREA, channels), F32),
             ((4 * AREA, channels), F32),
         ],
-        [((2, SHIFT, cols + 2 * SHIFT, LANES), F32), ((2, rows + 2, SHIFT, LANES), F32)],
+        [
+            ((2, SHIFT, cols + 2 * SHIFT, LANES), F32),
+            ((2, rows + 2, SHIFT, LANES), F32),
+            ((4, cols, channels), F32),
+        ],
         2_000_000_000,
         (top, bottom, left, right, gain1, gain2, fc1_weight, fc2, bias, query, kv, base, wkv, wp, wc),
     )
@@ -488,10 +493,10 @@
         corner_kernel,
         "corner_windows",
         [jax.ShapeDtypeStruct(image.shape, BF16)],
-        [((4, AREA, LANES), F32)],
+        [((4, AREA, LANES), F32), (image.shape, BF16), pltpu.SemaphoreType.DMA((3,))],
         1_000_000_000,
-        (left_corner, right_corner, gain1, gain2, fc1_weight, fc2, bias, query, kv, base, wkv, wp, wc,
-         kv_edge, fixes, out_mid, out_edge),
+        (left_corner, right_corner, gain1, gain2, fc1_weight, fc2, bias, query, kv, wkv, wp, wc,
+         kv_edge, corner_base, out_mid, out_edge),
     )
     return out
 

time: 22.7 us -> 22.8 us (level)
  waiting for transfers between devices: 0.26 us -> 0.81 us
  Pallas kernels: 13 us -> 12.5 us
    ppermute x3, waiting for transfers between devices: 0.25 us -> 0.8 us  [exchange(): lax.ppermute(high, axis, [(i, (i + 1) % count) for i in range(count)])]
    pallas_call x4, Pallas kernels: 13 us -> 12.5 us  [call(): pl.pallas_call(kernel, out_shape=[out if isinstance(out, jax.ShapeDtypeSt...]
  transfers between devices with their start and end apart: 6 -> 6, of which waited for: 1 -> 1; matrix products, arithmetic and copies ran while one was open for 0% -> 0% of each run, Pallas kernels for 39% -> 37%
where the time goes in v9:
time: 22.8 us; the launch traced here: 22.6 us
  Pallas kernels  12.5 us (55%)
  starting transfers between devices  9.03 us (40%)
  waiting for transfers between devices  0.81 us (4%)
    pallas_call x4, Pallas kernels, call(): pl.pallas_call(kernel, out_shape=[out if isinstance(out, jax.ShapeDtypeSt...  12.5 us
    ppermute x3, starting transfers between devices, exchange(): lax.ppermute(low, axis, [((i + 1) % count, i) for i in range(count)])  5.98 us
    ppermute x3, starting transfers between devices, exchange(): lax.ppermute(high, axis, [(i, (i + 1) % count) for i in range(count)])  3.05 us
    ppermute x3, waiting for transfers between devices, exchange(): lax.ppermute(high, axis, [(i, (i + 1) % count) for i in range(count)])  0.8 us
  transfers between devices with their start and end apart: 6, of which 1 were waited for; matrix products, arithmetic and copies ran while one was open for 0% of the time, Pallas kernels for 37%

profile of v9, /device:TPU:0, one launch (start us, length us, event | category | flops | bytes accessed | tf_op | source)
XLA Modules:
  0.0 22.6 jit_solution(1885541244256296360)
XLA Ops:
  0.0 1.1 %cut_halo.1 = (bf16[32,32,180]{2,1,0:T(8,128)(2,1)S(1)}, bf16[8,32,180]{2,1,0:T(8,128)(2,1)S(1)}, bf16[8,32,180]{2,1,0:T(8,128)(2,1)S(1)}, bf16[32,8,180]{2,1,0:T(8,128)(2,1)S(1)}, bf16[32,8,180]{2,1,0:T(8,128)(2,1)S(1)}) custom-call(bf16[32,32,180]{2,1,0:T(8,128)(2,1)} %image_hbm.1), custom_call_target="tpu_custom_call" | custom-call | flops 1000000 | bytes 4000000 | tf_op jit(solution)/shard_map/cut_halo/pallas_call | solution.py:415
  1.1 3.0 %collective-permute-start = (bf16[8,32,180]{2,1,0:T(8,128)(2,1)S(1)}, bf16[8,32,180]{2,1,0:T(8,128)(2,1)S(1)}, u32[]{:S(2)}, u32[]{:S(2)}) collective-permute-start(bf16[8,32,180]{2,1,0:T(8,128)(2,1)S(1)} %get-tuple-element.21), channel_id=1, source_target_pairs={{0,8},{8,16},{16,24},{24,0},{1,9},{9,17},{17,25},{25,1},{2,10},{10... | collective-permute-start | bytes 276488 | tf_op jit(solution)/shard_map/ppermute | solution.py:407
  4.1 1.0 %collective-permute-start.1 = (bf16[8,32,180]{2,1,0:T(8,128)(2,1)S(1)}, bf16[8,32,180]{2,1,0:T(8,128)(2,1)S(1)}, u32[]{:S(2)}, u32[]{:S(2)}) collective-permute-start(bf16[8,32,180]{2,1,0:T(8,128)(2,1)S(1)} %get-tuple-element.22), channel_id=1, source_target_pairs={{8,0},{16,8},{24,16},{0,24},{9,1},{17,9},{25,17},{1,25},{10,2},{18... | collective-permute-start | bytes 276488 | tf_op jit(solution)/shard_map/ppermute | solution.py:408
  5.1 0.0 collective-permute-start.4
  5.1 3.5 %collective-permute-start.5 = (bf16[32,8,180]{2,1,0:T(8,128)(2,1)S(1)}, bf16[32,8,180]{2,1,0:T(8,128)(2,1)S(1)}, u32[]{:S(2)}, u32[]{:S(2)}) collective-permute-start(bf16[32,8,180]{2,1,0:T(8,128)(2,1)S(1)} %get-tuple-element.31), channel_id=1, source_target_pairs={{1,0},{2,1},{3,2},{4,3},{5,4},{6,5},{7,6},{0,7},{9,8},{10,9},{11,1... | collective-permute-start | bytes 276488 | tf_op jit(solution)/shard_map/ppermute | solution.py:408
  8.6 0.0 copy-start
  8.7 0.0 copy-start.1
  8.7 0.0 copy-start.2
  8.7 0.0 copy-start.3
  8.7 3.7 %own_tile.1 = (f32[6,2,2,64,256]{4,3,2,1,0:T(8,128)S(1)}, bf16[4,4,64,256]{3,2,1,0:T(8,128)(2,1)S(1)}, bf16[4,4,64,512]{3,2,1,0:T(8,128)(2,1)S(1)}, f32[4,4,64,1...) custom-call(bf16[32,32,180]{2,1,0:T(8,128)(2,1)S(1)} %get-tuple-elem, ...), custom_call_target="tpu_custom_call" | custom-call | flops 2000000000 | bytes 4000000 | tf_op jit(solution)/shard_map/own_tile/pallas_call | solution.py:415
  12.4 0.0 collective-permute-done.top_ref
  12.4 0.0 collective-permute-done.1.bottom_ref
  12.4 1.4 %collective-permute-start.3 = (bf16[16,8,180]{2,1,0:T(8,128)(2,1)S(1)}, bf16[16,8,180]{2,1,0:T(8,128)(2,1)S(1)}, u32[]{:S(2)}, u32[]{:S(2)}) collective-permute-start(bf16[16,8,180]{2,1,0:T(8,128)(2,1)S(1)} %pad_maximum_fusion.1), channel_id=1, source_target_pairs={{1,0},{2,1},{3,2},{4,3},{5,4},{6,5},{7,6},{0,7},{9,8},{10,9},{11,1... | collective-permute-start | bytes 138248 | tf_op jit(solution)/shard_map/ppermute | solution.py:408
  13.9 0.1 collective-permute-start.2
  13.9 0.0 collective-permute-done.4.left_ref
  13.9 0.0 collective-permute-done.5.right_ref
  13.9 0.0 copy-done
  14.0 0.0 copy-done.1
  14.0 0.0 copy-done.2
  14.0 0.0 copy-done.3
  14.0 4.6 %edge_windows.1 = (bf16[4,4,64,512]{3,2,1,0:T(8,128)(2,1)S(1)}, f32[4,64,180]{2,1,0:T(8,128)S(1)}, f32[2,256,180]{2,1,0:T(8,128)S(1)}, f32[256,180]{1,0:T(8,128)S(1)}) custom-call(bf16[8,32,180]{2,1,0:T(8,128)(2,1)S(1)} %collective-permute-done.top_ref, bf16[8,32,180]{2,1,0:T(8,128)(2,1)S(1)} %collective-permute-done.1.bottom_ref, ...), custom_call_target="tpu_custom_call" | custom-call | flops 2000000000 | bytes 4000000 | tf_op jit(solution)/shard_map/edge_windows/pallas_call | solution.py:415
  18.6 0.0 collective-permute-done.3.right_ref
  18.6 0.8 %collective-permute-done.2.left_ref = bf16[16,8,180]{2,1,0:T(8,128)(2,1)S(1)} collective-permute-done((bf16[16,8,180]{2,1,0:T(8,128)(2,1)S(1)}, bf16[16,8,180]{2,1,0:T(8,128)(2,1)S(1)}, u32[]{:S(2)}, u32[]{:S(2)}) %collective-permute-start.2) | collective-permute-done | bytes 46112 | tf_op jit(solution)/shard_map/ppermute | solution.py:407
  19.4 3.2 %corner_windows.1 = bf16[32,32,180]{2,1,0:T(8,128)(2,1)} custom-call(bf16[16,8,180]{2,1,0:T(8,128)(2,1)S(1)} %collective-permute-done.2.left_ref, bf16[16,8,180]{2,1,0:T(8,128)(2,1)S(1)} %collective-permute-done.3.right_ref, f32[1,180]{1,0:T(1,128)S(1)} %bitcast.8, f32[1,180]{1,0:T(1,128)S(1)} %bitcast.10, bf16[180,360]{1,0:T(8,128)(2,1)S(1)} %copy-done, ...), custom_call_target="tpu_custom_call" | custom-call | flops 1000000000 | bytes 4000000 | tf_op jit(solution)/shard_map/corner_windows/pallas_call | solution.py:415
  (4 shorter events, 0.0 us)
Async XLA Ops:
  1.1 11.3 %collective-permute-start = (bf16[8,32,180]{2,1,0:T(8,128)(2,1)S(1)}, bf16[8,32,180]{2,1,0:T(8,128)(2,1)S(1)}, u32[]{:S(2)}, u32[]{:S(2)}) collective-permute-start(bf16[8,32,180]{2,1,0:T(8,128)(2,1)S(1)} %get-tuple-element.21), channel_id=1, source_target_pairs={{0,8},{8,16},{16,24},{24,0},{1,9},{9,17},{17,25},{25,1},{2,10},{10... | collective-permute-start | bytes 276488 | tf_op jit(solution)/shard_map/ppermute | solution.py:407
  4.1 8.3 %collective-permute-start.1 = (bf16[8,32,180]{2,1,0:T(8,128)(2,1)S(1)}, bf16[8,32,180]{2,1,0:T(8,128)(2,1)S(1)}, u32[]{:S(2)}, u32[]{:S(2)}) collective-permute-start(bf16[8,32,180]{2,1,0:T(8,128)(2,1)S(1)} %get-tuple-element.22), channel_id=1, source_target_pairs={{8,0},{16,8},{24,16},{0,24},{9,1},{17,9},{25,17},{1,25},{10,2},{18... | collective-permute-start | bytes 276488 | tf_op jit(solution)/shard_map/ppermute | solution.py:408
  5.1 8.8 %collective-permute-start.4 = (bf16[32,8,180]{2,1,0:T(8,128)(2,1)S(1)}, bf16[32,8,180]{2,1,0:T(8,128)(2,1)S(1)}, u32[]{:S(2)}, u32[]{:S(2)}) collective-permute-start(bf16[32,8,180]{2,1,0:T(8,128)(2,1)S(1)} %get-tuple-element.30), channel_id=1, source_target_pairs={{0,1},{1,2},{2,3},{3,4},{4,5},{5,6},{6,7},{7,0},{8,9},{9,10},{10,1... | collective-permute-start | bytes 276488 | tf_op jit(solution)/shard_map/ppermute | solution.py:407
  5.1 8.8 %collective-permute-start.5 = (bf16[32,8,180]{2,1,0:T(8,128)(2,1)S(1)}, bf16[32,8,180]{2,1,0:T(8,128)(2,1)S(1)}, u32[]{:S(2)}, u32[]{:S(2)}) collective-permute-start(bf16[32,8,180]{2,1,0:T(8,128)(2,1)S(1)} %get-tuple-element.31), channel_id=1, source_target_pairs={{1,0},{2,1},{3,2},{4,3},{5,4},{6,5},{7,6},{0,7},{9,8},{10,9},{11,1... | collective-permute-start | bytes 276488 | tf_op jit(solution)/shard_map/ppermute | solution.py:408
  8.6 5.3 %copy-start = (bf16[180,360]{1,0:T(8,128)(2,1)S(1)}, bf16[180,360]{1,0:T(8,128)(2,1)}, u32[]{:S(2)}) copy-start(bf16[180,360]{1,0:T(8,128)(2,1)} %fc1_ref.3) | copy-start | bytes 388804
  8.7 5.3 %copy-start.1 = (bf16[360,180]{0,1:T(8,128)(2,1)S(1)}, bf16[360,180]{0,1:T(8,128)(2,1)}, u32[]{:S(2)}) copy-start(bf16[360,180]{0,1:T(8,128)(2,1)} %param.17) | copy-start | bytes 388804
  8.7 5.3 %copy-start.2 = (f32[180]{0:T(256)S(1)}, f32[180]{0:T(256)}, u32[]{:S(2)}) copy-start(f32[180]{0:T(256)} %param.10) | copy-start | bytes 2164
  8.7 5.3 %copy-start.3 = (f32[180]{0:T(256)S(1)}, f32[180]{0:T(256)}, u32[]{:S(2)}) copy-start(f32[180]{0:T(256)} %param.11) | copy-start | bytes 2164
  12.4 6.2 %collective-permute-start.3 = (bf16[16,8,180]{2,1,0:T(8,128)(2,1)S(1)}, bf16[16,8,180]{2,1,0:T(8,128)(2,1)S(1)}, u32[]{:S(2)}, u32[]{:S(2)}) collective-permute-start(bf16[16,8,180]{2,1,0:T(8,128)(2,1)S(1)} %pad_maximum_fusion.1), channel_id=1, source_target_pairs={{1,0},{2,1},{3,2},{4,3},{5,4},{6,5},{7,6},{0,7},{9,8},{10,9},{11,1... | collective-permute-start | bytes 138248 | tf_op jit(solution)/shard_map/ppermute | solution.py:408
  13.9 5.5 %collective-permute-start.2 = (bf16[16,8,180]{2,1,0:T(8,128)(2,1)S(1)}, bf16[16,8,180]{2,1,0:T(8,128)(2,1)S(1)}, u32[]{:S(2)}, u32[]{:S(2)}) collective-permute-start(bf16[16,8,180]{2,1,0:T(8,128)(2,1)S(1)} %pad_maximum_fusion), channel_id=1, source_target_pairs={{0,1},{1,2},{2,3},{3,4},{4,5},{5,6},{6,7},{7,0},{8,9},{9,10},{10,1... | collective-permute-start | bytes 138248 | tf_op jit(solution)/shard_map/ppermute | solution.py:407

commit v10 on v9

--- a/solution.py
+++ b/solution.py
@@ -24,6 +24,13 @@
     centre = jnp.mean(values, axis=-1, keepdims=True)
     values = values - centre
     spread = jnp.mean(values * values, axis=-1, keepdims=True)
+    return values * lax.rsqrt(spread + 1e-05) * norm_gain
+
+
+def layer_norm_padded(values, norm_gain, channels):
+    centre = jnp.sum(values, axis=-1, keepdims=True) * (1.0 / channels)
+    values = jnp.where(lanes_of() < channels, values - centre, 0.0)
+    spread = jnp.sum(values * values, axis=-1, keepdims=True) * (1.0 / channels)
     return values * lax.rsqrt(spread + 1e-05) * norm_gain
 
 
@@ -129,11 +136,11 @@
         yield mix(scores, part_bias, unit[2][:, LANES:], head_dim, channels)
 
 
-def finish(heads_out, base, wp, gain2, fc1, fc2, channels):
+def finish(heads_out, base, wp, gain2, w1, w2, channels):
     state1 = base + dot(heads_out, wp[...]).astype(BF16).astype(F32)
-    normed2 = layer_norm(state1, gain2).astype(BF16)
-    hidden = gelu(dot(normed2, fc1[...])).astype(BF16)
-    return state1 + dot_nt(hidden, fc2[...])
+    normed2 = layer_norm_padded(state1, gain2, channels).astype(BF16)
+    hidden = gelu(dot(normed2, w1[...])).astype(BF16)
+    return state1 + dot(hidden, w2[...])
 
 
 def cut_kernel(image_hbm, image_ref, top, bottom, left, right, sem):
@@ -150,10 +157,10 @@
 
 
 def own_kernel(
-    image_ref, gain1_hbm, qkv_hbm, proj_hbm, table_hbm, conv_hbm,
-    bias, query, kv, base, wkv, wp, wc,
+    image_ref, gain1_hbm, gain2_hbm, qkv_hbm, proj_hbm, table_hbm, conv_hbm, fc1_hbm, fc2_hbm,
+    bias, query, kv, base, wkv, wp, wc, w1, w2, g2,
     padded, strip, wq, normed, shifted,
-    table_ref, gain1_ref, qkv_ref, proj_ref, conv_ref, sems,
+    table_ref, gain1_ref, gain2_ref, qkv_ref, proj_ref, conv_ref, fc1_ref, fc2_ref, sems,
 ):
     rows, cols, channels = image_ref.shape
     head_dim = channels // HEADS
@@ -163,13 +170,13 @@
         pltpu.make_async_copy(source, target, sems.at[i])
         for i, (source, target) in enumerate(
             ((gain1_hbm, gain1_ref), (qkv_hbm, qkv_ref), (table_hbm, table_ref), (proj_hbm, proj_ref),
-             (conv_hbm, conv_ref))
+             (conv_hbm, conv_ref), (gain2_hbm, gain2_ref), (fc1_hbm, fc1_ref), (fc2_hbm, fc2_ref))
         )
     ]
     for fetch in fetches:
         fetch.start()
 
-    for ref in (wq, wkv, wp, wc):
+    for ref in (wq, wkv, wp, wc, w1, w2, g2):
         ref[...] = jnp.zeros_like(ref)
     special = lax.broadcasted_iota(jnp.int32, (16, LANES), 0) + 176
     lanes16 = lax.broadcasted_iota(jnp.int32, (16, LANES), 1)
@@ -193,9 +200,12 @@
     wq[0:channels, 0:channels] = qkv_ref[:, 0:channels]
     wkv[0:channels, 0:channels] = qkv_ref[:, channels : 2 * channels]
     wkv[0:channels, LANES : LANES + channels] = qkv_ref[:, 2 * channels :]
-    wp[0:channels, :] = proj_ref[...]
+    wp[0:channels, 0:channels] = proj_ref[...]
+    w1[0:channels, 0 : fc1_ref.shape[1]] = fc1_ref[...]
+    w2[0 : fc2_ref.shape[1], 0:channels] = fc2_ref[...].astype(F32).T.astype(BF16)
+    g2[:, 0:channels] = gain2_ref[...]
     for tap in range(9):
-        wc[tap * LANES : tap * LANES + channels, :] = conv_ref[tap // 3, tap % 3]
+        wc[tap * LANES : tap * LANES + channels, 0:channels] = conv_ref[tap // 3, tap % 3]
 
     scale = head_dim**-0.5 * LOG2E
     for br in range(blocks_r):
@@ -219,15 +229,16 @@
         taps = [
             shifted[tap % 3, r + tap // 3 : r + tap // 3 + SIDE].reshape(-1, LANES) for tap in range(9)
         ]
-        summed = dot(jnp.concatenate(taps, axis=1), wc[...]).reshape(SIDE, cols, channels)
+        summed = dot(jnp.concatenate(taps, axis=1), wc[...])[:, :channels].reshape(SIDE, cols, channels)
         summed = summed + image_ref[r : r + SIDE].astype(F32)
         for bc in range(blocks_c):
-            base[br, bc] = summed[:, bc * SIDE : (bc + 1) * SIDE].reshape(AREA, channels)
+            base[br, bc, :, HALF:] = jnp.zeros((AREA, HALF), F32)
+            base[br, bc, :, 0:channels] = summed[:, bc * SIDE : (bc + 1) * SIDE].reshape(AREA, channels)
 
 
 def edge_kernel(
-    top_ref, bottom_ref, left_ref, right_ref, gain1_ref, gain2_ref, fc1_ref, fc2_ref,
-    bias, query, kv, base, wkv, wp, wc,
+    top_ref, bottom_ref, left_ref, right_ref, gain1_ref,
+    bias, query, kv, base, wkv, wp, wc, w1, w2, g2,
     kv_edge, corner_base, out_edge, out_mid,
     bands_r, bands_c, fixes,
 ):
@@ -277,17 +288,6 @@
         ([query[at] for at in places[i]], quadrants[i], jnp.concatenate(keys[i], axis=0))
         for i in range(4)
     ]
-    gain2 = gain2_ref[...]
-    mixed_mid, mixed = [], []
-    for i, result in enumerate(attention(units, bias, head_dim, channels)):
-        (mixed_mid if i < 2 else mixed).append(result)
-        if i == 2:
-            mid_base = [base[at] for at in ((1, 1), (1, 2), (2, 1), (2, 2))]
-            out_mid[...] = finish(
-                jnp.concatenate(mixed_mid, axis=0), jnp.concatenate(mid_base, axis=0), wp, gain2,
-                fc1_ref, fc2_ref, channels,
-            )
-
     for i, (taps, source) in enumerate((((0, 1, 2), SHIFT - 1), ((6, 7, 8), 0))):
         pieces = [bands_r[i, source, SHIFT - 1 + t : SHIFT - 1 + t + cols] for t in range(3)]
         weights = jnp.concatenate([wc[t * LANES : (t + 1) * LANES] for t in taps], axis=0)
@@ -297,22 +297,29 @@
         weights = jnp.concatenate([wc[t * LANES : (t + 1) * LANES] for t in taps], axis=0)
         fixes[2 + i] = dot(jnp.concatenate(pieces, axis=1).astype(BF16), weights)
 
+    gain2, done = g2[...], []
+    for i, result in enumerate(attention(units, bias, head_dim, channels)):
+        done.append(result)
+        if i % 2 == 0:
+            continue
+        if i == 1:
+            parts = [base[at] for at in ((1, 1), (1, 2), (2, 1), (2, 2))]
+        else:
+            parts = [corrected(base, fixes, at) for at in (*places[i - 3], *places[i - 2])]
+        out = finish(
+            jnp.concatenate(done[-2:], axis=0), jnp.concatenate(parts, axis=0), wp, gain2, w1, w2, channels
+        )
+        if i == 1:
+            out_mid[...] = out
+        else:
+            out_edge[i // 2 - 1] = out
     for i, at in enumerate(((0, 0), (0, 3), (3, 0), (3, 3))):
-        corner_base[i] = corrected(base, fixes, at, channels)
-    for group in range(2):
-        raw = jnp.concatenate([mixed[2 * group], mixed[2 * group + 1]], axis=0)
-        parts = [
-            corrected(base, fixes, at, channels)
-            for at in (*places[2 * group], *places[2 * group + 1])
-        ]
-        out_edge[group] = finish(
-            raw, jnp.concatenate(parts, axis=0), wp, gain2, fc1_ref, fc2_ref, channels
-        )
-
-
-def corrected(base, fixes, at, channels):
+        corner_base[i] = corrected(base, fixes, at)
+
+
+def corrected(base, fixes, at):
     br, bc = at
-    block = base[at].reshape(SIDE, SIDE, channels)
+    block = base[at].reshape(SIDE, SIDE, LANES)
     y = lax.broadcasted_iota(jnp.int32, (SIDE, SIDE, 1), 0)
     x = lax.broadcasted_iota(jnp.int32, (SIDE, SIDE, 1), 1)
     if br in (0, 3):
@@ -321,12 +328,12 @@
     if bc in (0, 3):
         fix = fixes[2 if bc == 0 else 3, br * SIDE : (br + 1) * SIDE]
         block = block + jnp.where(x == (0 if bc == 0 else SIDE - 1), fix[:, None], 0.0)
-    return block.reshape(AREA, channels)
+    return block.reshape(AREA, LANES)
 
 
 def corner_kernel(
-    left_ref, right_ref, gain1_ref, gain2_ref, fc1_ref, fc2_ref,
-    bias, query, kv, wkv, wp, wc, kv_edge, corner_base, out_mid, out_edge,
+    left_ref, right_ref, gain1_ref,
+    bias, query, kv, wkv, wp, wc, w1, w2, g2, kv_edge, corner_base, out_mid, out_edge,
     out_hbm,
     normed, out_ref, sems,
 ):
@@ -340,12 +347,12 @@
         for br in which:
             if br in (0, 3):
                 i = 0 if br == 0 else 2
-                band = [corners[i], piece(out_edge.at[0], i), piece(out_edge.at[0], i + 1), corners[i + 1]]
+                band = [corners[0], piece(out_edge.at[0], i), piece(out_edge.at[0], i + 1), corners[1]]
             else:
                 i = br - 1
                 band = [piece(out_edge.at[1], i), piece(out_mid, 2 * i), piece(out_mid, 2 * i + 1),
                         piece(out_edge.at[1], i + 2)]
-            band = [part.reshape(SIDE, SIDE, channels) for part in band]
+            band = [part[:, :channels].reshape(SIDE, SIDE, channels) for part in band]
             out_ref[br * SIDE : (br + 1) * SIDE] = jnp.concatenate(band, axis=1).astype(BF16)
 
     finish_bands((1, 2), None)
@@ -377,8 +384,6 @@
     units = [
         ([query[places[i]]], [quadrants[i]], jnp.concatenate(keys[i], axis=0)) for i in range(4)
     ]
-    mixed = list(attention(units, bias, head_dim, channels))
-
     parts = []
     for i, (tap, y, x) in enumerate(((0, 7, 7), (2, 7, 0), (6, 0, 7), (8, 0, 0))):
         start = y * SIDE
@@ -387,11 +392,16 @@
         pixel = lax.broadcasted_iota(jnp.int32, (AREA, 1), 0)
         at = (SIDE - 1 - y) * SIDE + SIDE - 1 - x
         parts.append(corner_base[i] + jnp.where(pixel == at, term, 0.0))
-    out_corner = finish(
-        jnp.concatenate(mixed, axis=0), jnp.concatenate(parts, axis=0), wp, gain2_ref[...], fc1_ref, fc2_ref, channels,
-    )
-
-    finish_bands((0, 3), [out_corner[i * AREA : (i + 1) * AREA] for i in range(4)])
+    done = []
+    for i, result in enumerate(attention(units, bias, head_dim, channels)):
+        done.append(result)
+        if i % 2 == 0:
+            continue
+        out = finish(
+            jnp.concatenate(done[-2:], axis=0), jnp.concatenate(parts[i - 1 : i + 1], axis=0), wp, g2[...],
+            w1, w2, channels,
+        )
+        finish_bands((0,) if i == 1 else (3,), [out[:AREA], out[AREA:]])
     writes[0].wait()
     for r in (0, rows - SIDE):
         at = slice(r, r + SIDE)
@@ -443,18 +453,22 @@
     )
     top, bottom = exchange(first_rows, last_rows, "row")
     left, right = exchange(first_cols, last_cols, "col")
-    fetched = (table, gain1, qkv_weight, proj_weight, conv_weight)
-    bias, query, kv, base, wkv, wp, wc = call(
+    fetched = (table, gain1, gain2, qkv_weight, proj_weight, conv_weight, fc1_weight, fc2)
+    hidden = -(-fc1_weight.shape[1] // 128) * 128
+    bias, query, kv, base, wkv, wp, wc, w1, w2, g2 = call(
         own_kernel,
         "own_tile",
         [
             ((HEADS, 2, 2, AREA, WIN * WIN), F32),
             ((blocks_r, blocks_c, AREA, LANES), BF16),
             ((blocks_r, blocks_c, AREA, 2 * LANES), BF16),
-            ((blocks_r, blocks_c, AREA, channels), F32),
+            ((blocks_r, blocks_c, AREA, LANES), F32),
             ((LANES, 2 * LANES), BF16),
-            ((LANES, channels), BF16),
-            ((9 * LANES, channels), BF16),
+            ((LANES, LANES), BF16),
+            ((9 * LANES, LANES), BF16),
+            ((LANES, hidden), BF16),
+            ((hidden, LANES), BF16),
+            ((1, LANES), F32),
         ],
         [
             ((8, 1024), F32),
@@ -466,8 +480,8 @@
             pltpu.SemaphoreType.DMA((len(fetched),)),
         ],
         2_000_000_000,
-        (tile, gain1, qkv_weight, proj_weight, table, conv_weight),
-        range(1, 6),
+        (tile, gain1, gain2, qkv_weight, proj_weight, table, conv_weight, fc1_weight, fc2),
+        range(1, 9),
     )
     first = jnp.concatenate([top[:, :SHIFT], bottom[:, :SHIFT]])
     last = jnp.concatenate([top[:, cols - SHIFT :], bottom[:, cols - SHIFT :]])
@@ -477,17 +491,17 @@
         "edge_windows",
         [
             ((4, blocks_c, AREA, 2 * LANES), BF16),
-            ((4, AREA, channels), F32),
-            ((2, 4 * AREA, channels), F32),
-            ((4 * AREA, channels), F32),
+            ((4, AREA, LANES), F32),
+            ((2, 4 * AREA, LANES), F32),
+            ((4 * AREA, LANES), F32),
         ],
         [
             ((2, SHIFT, cols + 2 * SHIFT, LANES), F32),
             ((2, rows + 2, SHIFT, LANES), F32),
-            ((4, cols, channels), F32),
+            ((4, cols, LANES), F32),
         ],
         2_000_000_000,
-        (top, bottom, left, right, gain1, gain2, fc1_weight, fc2, bias, query, kv, base, wkv, wp, wc),
+        (top, bottom, left, right, gain1, bias, query, kv, base, wkv, wp, wc, w1, w2, g2),
     )
     (out,) = call(
         corner_kernel,
@@ -495,7 +509,7 @@
         [jax.ShapeDtypeStruct(image.shape, BF16)],
         [((4, AREA, LANES), F32), (image.shape, BF16), pltpu.SemaphoreType.DMA((3,))],
         1_000_000_000,
-        (left_corner, right_corner, gain1, gain2, fc1_weight, fc2, bias, query, kv, wkv, wp, wc,
+        (left_corner, right_corner, gain1, bias, query, kv, wkv, wp, wc, w1, w2, g2,
          kv_edge, corner_base, out_mid, out_edge),
     )
     return out

time: 22.8 us -> 22.9 us (level)
  Pallas kernels: 12.5 us -> 13.5 us
  waiting for transfers between devices: 0.81 us -> 0.16 us
    pallas_call x4, Pallas kernels: 12.5 us -> 13.5 us  [call(): pl.pallas_call(kernel, out_shape=[out if isinstance(out, jax.ShapeDtypeSt...]
    ppermute x3, waiting for transfers between devices: 0.8 us -> 0.15 us  [exchange(): lax.ppermute(high, axis, [(i, (i + 1) % count) for i in range(count)])]
  transfers between devices with their start and end apart: 6 -> 6, of which waited for: 1 -> 1; matrix products, arithmetic and copies ran while one was open for 0% -> 0% of each run, Pallas kernels for 37% -> 40%
where the time goes in v10:
time: 22.9 us; the launch traced here: 22.7 us
  Pallas kernels  13.5 us (59%)
  starting transfers between devices  8.82 us (39%)
    pallas_call x4, Pallas kernels, call(): pl.pallas_call(kernel, out_shape=[out if isinstance(out, jax.ShapeDtypeSt...  13.5 us
    ppermute x3, starting transfers between devices, exchange(): lax.ppermute(low, axis, [((i + 1) % count, i) for i in range(count)])  5.77 us
    ppermute x3, starting transfers between devices, exchange(): lax.ppermute(high, axis, [(i, (i + 1) % count) for i in range(count)])  3.05 us
  transfers between devices with their start and end apart: 6, of which 1 were waited for; matrix products, arithmetic and copies ran while one was open for 0% of the time, Pallas kernels for 40%

profile of v10, /device:TPU:0, one launch (start us, length us, event | category | flops | bytes accessed | tf_op | source)
XLA Modules:
  0.0 22.7 jit_solution(7343600015970955826)
XLA Ops:
  0.0 1.1 %cut_halo.1 = (bf16[32,32,180]{2,1,0:T(8,128)(2,1)S(1)}, bf16[8,32,180]{2,1,0:T(8,128)(2,1)S(1)}, bf16[8,32,180]{2,1,0:T(8,128)(2,1)S(1)}, bf16[32,8,180]{2,1,0:T(8,128)(2,1)S(1)}, bf16[32,8,180]{2,1,0:T(8,128)(2,1)S(1)}) custom-call(bf16[32,32,180]{2,1,0:T(8,128)(2,1)} %image_hbm.1), custom_call_target="tpu_custom_call" | custom-call | flops 1000000 | bytes 4000000 | tf_op jit(solution)/shard_map/cut_halo/pallas_call | solution.py:425
  1.1 3.0 %collective-permute-start = (bf16[8,32,180]{2,1,0:T(8,128)(2,1)S(1)}, bf16[8,32,180]{2,1,0:T(8,128)(2,1)S(1)}, u32[]{:S(2)}, u32[]{:S(2)}) collective-permute-start(bf16[8,32,180]{2,1,0:T(8,128)(2,1)S(1)} %get-tuple-element.24), channel_id=1, source_target_pairs={{0,8},{8,16},{16,24},{24,0},{1,9},{9,17},{17,25},{25,1},{2,10},{10... | collective-permute-start | bytes 276488 | tf_op jit(solution)/shard_map/ppermute | solution.py:417
  4.1 1.0 %collective-permute-start.1 = (bf16[8,32,180]{2,1,0:T(8,128)(2,1)S(1)}, bf16[8,32,180]{2,1,0:T(8,128)(2,1)S(1)}, u32[]{:S(2)}, u32[]{:S(2)}) collective-permute-start(bf16[8,32,180]{2,1,0:T(8,128)(2,1)S(1)} %get-tuple-element.25), channel_id=1, source_target_pairs={{8,0},{16,8},{24,16},{0,24},{9,1},{17,9},{25,17},{1,25},{10,2},{18... | collective-permute-start | bytes 276488 | tf_op jit(solution)/shard_map/ppermute | solution.py:418
  5.1 0.0 collective-permute-start.4
  5.1 3.5 %collective-permute-start.5 = (bf16[32,8,180]{2,1,0:T(8,128)(2,1)S(1)}, bf16[32,8,180]{2,1,0:T(8,128)(2,1)S(1)}, u32[]{:S(2)}, u32[]{:S(2)}) collective-permute-start(bf16[32,8,180]{2,1,0:T(8,128)(2,1)S(1)} %get-tuple-element.37), channel_id=1, source_target_pairs={{1,0},{2,1},{3,2},{4,3},{5,4},{6,5},{7,6},{0,7},{9,8},{10,9},{11,1... | collective-permute-start | bytes 276488 | tf_op jit(solution)/shard_map/ppermute | solution.py:418
  8.6 0.0 copy-start
  8.7 3.9 %own_tile.1 = (f32[6,2,2,64,256]{4,3,2,1,0:T(8,128)S(1)}, bf16[4,4,64,256]{3,2,1,0:T(8,128)(2,1)S(1)}, bf16[4,4,64,512]{3,2,1,0:T(8,128)(2,1)S(1)}, f32[4,4,64,2...) custom-call(bf16[32,32,180]{2,1,0:T(8,128)(2,1)S(1)} %get-tuple-elem, ...), custom_call_target="tpu_custom_call" | custom-call | flops 2000000000 | bytes 4000000 | tf_op jit(solution)/shard_map/own_tile/pallas_call | solution.py:425
  12.6 0.0 collective-permute-done.top_ref
  12.6 0.0 collective-permute-done.1.bottom_ref
  12.6 1.2 %collective-permute-start.3 = (bf16[16,8,180]{2,1,0:T(8,128)(2,1)S(1)}, bf16[16,8,180]{2,1,0:T(8,128)(2,1)S(1)}, u32[]{:S(2)}, u32[]{:S(2)}) collective-permute-start(bf16[16,8,180]{2,1,0:T(8,128)(2,1)S(1)} %pad_maximum_fusion.1), channel_id=1, source_target_pairs={{1,0},{2,1},{3,2},{4,3},{5,4},{6,5},{7,6},{0,7},{9,8},{10,9},{11,1... | collective-permute-start | bytes 138248 | tf_op jit(solution)/shard_map/ppermute | solution.py:418
  13.9 0.1 collective-permute-start.2
  13.9 0.0 collective-permute-done.4.left_ref
  13.9 0.0 collective-permute-done.5.right_ref
  13.9 0.0 copy-done
  14.0 5.3 %edge_windows.1 = (bf16[4,4,64,512]{3,2,1,0:T(8,128)(2,1)S(1)}, f32[4,64,256]{2,1,0:T(8,128)S(1)}, f32[2,256,256]{2,1,0:T(8,128)S(1)}, f32[256,256]{1,0:T(8,128)S(1)}) custom-call(bf16[8,32,180]{2,1,0:T(8,128)(2,1)S(1)} %collective-permute-done.top_ref, bf16[8,32,180]{2,1,0:T(8,128)(2,1)S(1)} %collective-permute-done.1.bottom_ref, ...), custom_call_target="tpu_custom_call" | custom-call | flops 2000000000 | bytes 4000000 | tf_op jit(solution)/shard_map/edge_windows/pallas_call | solution.py:425
  19.2 0.0 collective-permute-done.3.right_ref
  19.3 0.1 collective-permute-done.2.left_ref
  19.4 3.3 %corner_windows.1 = bf16[32,32,180]{2,1,0:T(8,128)(2,1)} custom-call(bf16[16,8,180]{2,1,0:T(8,128)(2,1)S(1)} %collective-permute-done.2.left_ref, bf16[16,8,180]{2,1,0:T(8,128)(2,1)S(1)} %collective-permute-done.3.right_ref, f32[1,180]{1,0:T(1,128)S(1)} %bitcast.6, f32[6,2,2,64,256]{4,3,2,1,0:T(8,128)S(1)} %get-tuple-element.27.bias, ...), custom_call_target="tpu_custom_call" | custom-call | flops 1000000000 | bytes 4000000 | tf_op jit(solution)/shard_map/corner_windows/pallas_call | solution.py:425
  (4 shorter events, 0.0 us)
Async XLA Ops:
  1.1 11.5 %collective-permute-start = (bf16[8,32,180]{2,1,0:T(8,128)(2,1)S(1)}, bf16[8,32,180]{2,1,0:T(8,128)(2,1)S(1)}, u32[]{:S(2)}, u32[]{:S(2)}) collective-permute-start(bf16[8,32,180]{2,1,0:T(8,128)(2,1)S(1)} %get-tuple-element.24), channel_id=1, source_target_pairs={{0,8},{8,16},{16,24},{24,0},{1,9},{9,17},{17,25},{25,1},{2,10},{10... | collective-permute-start | bytes 276488 | tf_op jit(solution)/shard_map/ppermute | solution.py:417
  4.1 8.5 %collective-permute-start.1 = (bf16[8,32,180]{2,1,0:T(8,128)(2,1)S(1)}, bf16[8,32,180]{2,1,0:T(8,128)(2,1)S(1)}, u32[]{:S(2)}, u32[]{:S(2)}) collective-permute-start(bf16[8,32,180]{2,1,0:T(8,128)(2,1)S(1)} %get-tuple-element.25), channel_id=1, source_target_pairs={{8,0},{16,8},{24,16},{0,24},{9,1},{17,9},{25,17},{1,25},{10,2},{18... | collective-permute-start | bytes 276488 | tf_op jit(solution)/shard_map/ppermute | solution.py:418
  5.1 8.8 %collective-permute-start.4 = (bf16[32,8,180]{2,1,0:T(8,128)(2,1)S(1)}, bf16[32,8,180]{2,1,0:T(8,128)(2,1)S(1)}, u32[]{:S(2)}, u32[]{:S(2)}) collective-permute-start(bf16[32,8,180]{2,1,0:T(8,128)(2,1)S(1)} %get-tuple-element.36), channel_id=1, source_target_pairs={{0,1},{1,2},{2,3},{3,4},{4,5},{5,6},{6,7},{7,0},{8,9},{9,10},{10,1... | collective-permute-start | bytes 276488 | tf_op jit(solution)/shard_map/ppermute | solution.py:417
  5.1 8.8 %collective-permute-start.5 = (bf16[32,8,180]{2,1,0:T(8,128)(2,1)S(1)}, bf16[32,8,180]{2,1,0:T(8,128)(2,1)S(1)}, u32[]{:S(2)}, u32[]{:S(2)}) collective-permute-start(bf16[32,8,180]{2,1,0:T(8,128)(2,1)S(1)} %get-tuple-element.37), channel_id=1, source_target_pairs={{1,0},{2,1},{3,2},{4,3},{5,4},{6,5},{7,6},{0,7},{9,8},{10,9},{11,1... | collective-permute-start | bytes 276488 | tf_op jit(solution)/shard_map/ppermute | solution.py:418
  8.6 5.3 %copy-start = (f32[180]{0:T(256)S(1)}, f32[180]{0:T(256)}, u32[]{:S(2)}) copy-start(f32[180]{0:T(256)} %param.10) | copy-start | bytes 2164
  12.6 6.6 %collective-permute-start.3 = (bf16[16,8,180]{2,1,0:T(8,128)(2,1)S(1)}, bf16[16,8,180]{2,1,0:T(8,128)(2,1)S(1)}, u32[]{:S(2)}, u32[]{:S(2)}) collective-permute-start(bf16[16,8,180]{2,1,0:T(8,128)(2,1)S(1)} %pad_maximum_fusion.1), channel_id=1, source_target_pairs={{1,0},{2,1},{3,2},{4,3},{5,4},{6,5},{7,6},{0,7},{9,8},{10,9},{11,1... | collective-permute-start | bytes 138248 | tf_op jit(solution)/shard_map/ppermute | solution.py:418
  13.9 5.5 %collective-permute-start.2 = (bf16[16,8,180]{2,1,0:T(8,128)(2,1)S(1)}, bf16[16,8,180]{2,1,0:T(8,128)(2,1)S(1)}, u32[]{:S(2)}, u32[]{:S(2)}) collective-permute-start(bf16[16,8,180]{2,1,0:T(8,128)(2,1)S(1)} %pad_maximum_fusion), channel_id=1, source_target_pairs={{0,1},{1,2},{2,3},{3,4},{4,5},{5,6},{6,7},{7,0},{8,9},{9,10},{10,1... | collective-permute-start | bytes 138248 | tf_op jit(solution)/shard_map/ppermute | solution.py:417

commit v11 on v10

--- a/solution.py
+++ b/solution.py
@@ -20,6 +20,18 @@
 MASKED = -4.0e9
 
 
+def weave(tasks, width):
+    waiting, active = list(tasks), []
+    while waiting or active:
+        while waiting and len(active) < width:
+            active.append(waiting.pop(0))
+        for task in list(active):
+            try:
+                next(task)
+            except StopIteration:
+                active.remove(task)
+
+
 def layer_norm(values, norm_gain):
     centre = jnp.mean(values, axis=-1, keepdims=True)
     values = values - centre
@@ -76,16 +88,19 @@
     )
     high = shifted.astype(BF16)
     low = (shifted - high.astype(F32)).astype(BF16)
+    yield
     entry = lax.broadcasted_iota(jnp.int32, (width, 512), 0)
     place = lax.broadcasted_iota(jnp.int32, (1, 512), 1)
     column = lax.div(place, 256) * SIDE + lax.rem(place, SIDE)
     wanted = (span - 1 - lax.div(lax.rem(place, 256), SIDE)) * span + WIN - 1 - column
     picked = dot(jnp.concatenate([high, low], axis=0), one_hot(entry == wanted))
+    yield
     half = 8 * WIN
     picked = picked[:half] + picked[half:]
     for tile in range(4):
         strip[tile] = picked[:, 128 * tile : 128 * (tile + 1)]
     for head in range(HEADS):
+        yield
         for half in range(2):
             rows = jnp.concatenate(
                 [strip[2 * half + t, pl.ds(head, WIN, stride=8), :] for t in range(2)], axis=1
@@ -109,38 +124,47 @@
     return dot_nt(stacked, keys)
 
 
-def mix(scores, part_bias, values, head_dim, channels):
+def attend(unit, bias, head_dim, channels, put):
     lane = lanes_of()
+    blocks, quadrants, pair = unit
+    pair = pair()
+    scores = scores_of(blocks, pair[:, :LANES], head_dim, channels)
     count = scores.shape[0] // HEADS
+    yield
+    part_bias = jnp.concatenate([bias[:, hy, hx] for hy, hx in quadrants], axis=1)
     scores = scores.reshape(HEADS, count, WIN * WIN) + part_bias
     scores = scores - jnp.max(scores, axis=-1, keepdims=True)
     weights = jnp.exp2(scores)
     total = jnp.sum(weights, axis=-1, keepdims=True)
-    mixed = dot(weights.astype(BF16).reshape(HEADS * count, WIN * WIN), values)
+    weights = weights.astype(BF16).reshape(HEADS * count, WIN * WIN)
+    yield
+    mixed = dot(weights, pair[:, LANES:])
+    yield
     result, divisor = mixed[0:count], jnp.broadcast_to(total[0], (count, LANES))
     for h in range(1, HEADS):
         mine = (lane >= h * head_dim) & (lane < (h + 1) * head_dim)
         result = jnp.where(mine, mixed[h * count : (h + 1) * count], result)
         divisor = jnp.where(mine, total[h], divisor)
-    return (result / divisor).astype(BF16)
-
-
-def attention(units, bias, head_dim, channels):
-    def scores_at(unit):
-        return scores_of(unit[0], unit[2][:, :LANES], head_dim, channels)
-
-    ahead = scores_at(units[0])
-    for i, unit in enumerate(units):
-        scores, ahead = ahead, scores_at(units[i + 1]) if i + 1 < len(units) else None
-        part_bias = jnp.concatenate([bias[:, hy, hx] for hy, hx in unit[1]], axis=1)
-        yield mix(scores, part_bias, unit[2][:, LANES:], head_dim, channels)
-
-
-def finish(heads_out, base, wp, gain2, w1, w2, channels):
-    state1 = base + dot(heads_out, wp[...]).astype(BF16).astype(F32)
+    put((result / divisor).astype(BF16))
+
+
+def finish(heads_out, base, wp, gain2, w1, w2, channels, put):
+    attended = dot(heads_out, wp[...])
+    yield
+    state1 = base() + attended.astype(BF16).astype(F32)
     normed2 = layer_norm_padded(state1, gain2, channels).astype(BF16)
-    hidden = gelu(dot(normed2, w1[...])).astype(BF16)
-    return state1 + dot(hidden, w2[...])
+    yield
+    hidden = dot(normed2, w1[...])
+    yield
+    hidden = gelu(hidden).astype(BF16)
+    yield
+    put(state1 + dot(hidden, w2[...]))
+
+
+def after(ready, make):
+    while not ready():
+        yield
+    yield from make()
 
 
 def cut_kernel(image_hbm, image_ref, top, bottom, left, right, sem):
@@ -191,49 +215,66 @@
 
     fetches[0].wait()
     gain1 = gain1_ref[...]
-    for r in range(0, rows, SIDE):
+    scale = head_dim**-0.5 * LOG2E
+
+    def weights():
+        for fetch in fetches[1:]:
+            fetch.wait()
+        wq[0:channels, 0:channels] = qkv_ref[:, 0:channels]
+        wkv[0:channels, 0:channels] = qkv_ref[:, channels : 2 * channels]
+        wkv[0:channels, LANES : LANES + channels] = qkv_ref[:, 2 * channels :]
+        wp[0:channels, 0:channels] = proj_ref[...]
+        w1[0:channels, 0 : fc1_ref.shape[1]] = fc1_ref[...]
+        w2[0 : fc2_ref.shape[1], 0:channels] = fc2_ref[...].astype(F32).T.astype(BF16)
+        g2[:, 0:channels] = gain2_ref[...]
+        for tap in range(9):
+            wc[tap * LANES : tap * LANES + channels, 0:channels] = conv_ref[tap // 3, tap % 3]
+
+    def norm(br):
+        r = br * SIDE
         inner = (slice(1 + r, 1 + r + SIDE), slice(SHIFT, SHIFT + cols))
         normed[(*inner, slice(0, channels))] = layer_norm(image_ref[r : r + SIDE].astype(F32), gain1)
 
-    for fetch in fetches[1:]:
-        fetch.wait()
-    wq[0:channels, 0:channels] = qkv_ref[:, 0:channels]
-    wkv[0:channels, 0:channels] = qkv_ref[:, channels : 2 * channels]
-    wkv[0:channels, LANES : LANES + channels] = qkv_ref[:, 2 * channels :]
-    wp[0:channels, 0:channels] = proj_ref[...]
-    w1[0:channels, 0 : fc1_ref.shape[1]] = fc1_ref[...]
-    w2[0 : fc2_ref.shape[1], 0:channels] = fc2_ref[...].astype(F32).T.astype(BF16)
-    g2[:, 0:channels] = gain2_ref[...]
-    for tap in range(9):
-        wc[tap * LANES : tap * LANES + channels, 0:channels] = conv_ref[tap // 3, tap % 3]
-
-    scale = head_dim**-0.5 * LOG2E
-    for br in range(blocks_r):
+    def project(br):
         inner = (slice(1 + br * SIDE, 1 + (br + 1) * SIDE), slice(SHIFT, SHIFT + cols))
         pixels = normed[inner].astype(BF16).reshape(-1, LANES)
-        q = (dot(pixels, wq[...]) * scale).reshape(SIDE, cols, LANES)
+        q = dot(pixels, wq[...])
+        yield
         both = dot(pixels, wkv[...]).reshape(SIDE, cols, 2 * LANES)
+        q = (q * scale).reshape(SIDE, cols, LANES)
         for bc in range(blocks_c):
             part = slice(bc * SIDE, (bc + 1) * SIDE)
             query[br, bc] = q[:, part].reshape(AREA, LANES).astype(BF16)
+        yield
+        for bc in range(blocks_c):
+            part = slice(bc * SIDE, (bc + 1) * SIDE)
             kv[br, bc] = both[:, part].reshape(AREA, 2 * LANES).astype(BF16)
-    expand_bias(table_ref, padded, strip, bias)
-
-    for tap in range(3):
-        c0 = SHIFT - 1 + tap
-        for r in range(0, rows + 2, SIDE):
-            stop = min(r + SIDE, rows + 2)
-            shifted[tap, r:stop] = normed[r:stop, c0 : c0 + cols].astype(BF16)
-    for br in range(blocks_r):
+
+    def convolve(br):
         r = br * SIDE
+        for tap in range(3):
+            c0 = SHIFT - 1 + tap
+            start = 0 if br == 0 else r + 2
+            shifted[tap, start : r + SIDE + 2] = normed[start : r + SIDE + 2, c0 : c0 + cols].astype(BF16)
+        yield
         taps = [
             shifted[tap % 3, r + tap // 3 : r + tap // 3 + SIDE].reshape(-1, LANES) for tap in range(9)
         ]
-        summed = dot(jnp.concatenate(taps, axis=1), wc[...])[:, :channels].reshape(SIDE, cols, channels)
+        summed = dot(jnp.concatenate(taps, axis=1), wc[...])
+        yield
+        summed = summed[:, :channels].reshape(SIDE, cols, channels)
         summed = summed + image_ref[r : r + SIDE].astype(F32)
         for bc in range(blocks_c):
             base[br, bc, :, HALF:] = jnp.zeros((AREA, HALF), F32)
             base[br, bc, :, 0:channels] = summed[:, bc * SIDE : (bc + 1) * SIDE].reshape(AREA, channels)
+
+    for br in range(blocks_r):
+        norm(br)
+    weights()
+    tasks = [expand_bias(table_ref, padded, strip, bias)]
+    for br in range(blocks_r):
+        tasks += [project(br), convolve(br)]
+    weave(tasks, 3)
 
 
 def edge_kernel(
@@ -253,7 +294,10 @@
 
     bands_r[...] = jnp.zeros_like(bands_r)
     bands_c[...] = jnp.zeros_like(bands_c)
-    for i, ref in enumerate((top_ref, bottom_ref, left_ref, right_ref)):
+    sides = []
+
+    def band(i):
+        ref = (top_ref, bottom_ref, left_ref, right_ref)[i]
         mark = jnp.broadcast_to(marks(channels, outside[i])[None], (*ref.shape[:2], HALF))
         values = layer_norm(ref[...].astype(F32), gain1 * (1.0 - outside[i]))
         if i < 2:
@@ -266,55 +310,76 @@
             bands_c[i - 2, 1 : 1 + rows, :, HALF:] = mark
             bands_c[i - 2, 1 : 1 + rows, :, 0:channels] = values
             count = rows // SIDE
-            pixels = bands_c[i - 2, 1 : 1 + rows]
-            blocks = [pixels.reshape(-1, LANES)]
-        both = dot(jnp.concatenate(blocks, axis=0).astype(BF16), wkv[...]).astype(BF16)
-        kv_edge[i] = both.reshape(count, AREA, 2 * LANES)
+            blocks = [bands_c[i - 2, 1 : 1 + rows].reshape(-1, LANES)]
+        pixels = jnp.concatenate(blocks, axis=0).astype(BF16)
+        yield
+        both = dot(pixels, wkv[...])
+        yield
+        kv_edge[i] = both.astype(BF16).reshape(count, AREA, 2 * LANES)
+        sides.append(i)
 
     keys = [
-        [kv_edge[0, 1], kv[0, 1], kv_edge[0, 2], kv[0, 2]],
-        [kv[3, 1], kv_edge[1, 1], kv[3, 2], kv_edge[1, 2]],
-        [kv_edge[2, 1], kv_edge[2, 2], kv[1, 0], kv[2, 0]],
-        [kv[1, 3], kv[2, 3], kv_edge[3, 1], kv_edge[3, 2]],
+        lambda: [kv_edge[0, 1], kv[0, 1], kv_edge[0, 2], kv[0, 2]],
+        lambda: [kv[3, 1], kv_edge[1, 1], kv[3, 2], kv_edge[1, 2]],
+        lambda: [kv_edge[2, 1], kv_edge[2, 2], kv[1, 0], kv[2, 0]],
+        lambda: [kv[1, 3], kv[2, 3], kv_edge[3, 1], kv_edge[3, 2]],
+        lambda: [kv[1, 1], kv[2, 1], kv[1, 2], kv[2, 2]],
     ]
     places = [((0, 1), (0, 2)), ((3, 1), (3, 2)), ((1, 0), (2, 0)), ((1, 3), (2, 3))]
+    places += [((1, 1), (1, 2)), ((2, 1), (2, 2))]
     quadrants = [((1, 0), (1, 1)), ((0, 0), (0, 1)), ((0, 1), (1, 1)), ((0, 0), (1, 0))]
-    middle = jnp.concatenate([kv[at] for at in ((1, 1), (2, 1), (1, 2), (2, 2))], axis=0)
-    units = [
-        ([query[1, 1], query[1, 2]], [(0, 0), (0, 1)], middle),
-        ([query[2, 1], query[2, 2]], [(1, 0), (1, 1)], middle),
-    ]
-    units += [
-        ([query[at] for at in places[i]], quadrants[i], jnp.concatenate(keys[i], axis=0))
-        for i in range(4)
-    ]
-    for i, (taps, source) in enumerate((((0, 1, 2), SHIFT - 1), ((6, 7, 8), 0))):
-        pieces = [bands_r[i, source, SHIFT - 1 + t : SHIFT - 1 + t + cols] for t in range(3)]
+    quadrants += [((0, 0), (0, 1)), ((1, 0), (1, 1))]
+    done = {}
+
+    def unit(i):
+        def put(result):
+            done[i] = result
+
+        window = keys[min(i, 4)]
+        parts = ([query[at] for at in places[i]], quadrants[i], lambda: jnp.concatenate(window(), axis=0))
+        make = lambda: attend(parts, bias, head_dim, channels, put)
+        return after(lambda: i >= 4 or i in sides, make)
+
+    def tail(i):
+        def put(out):
+            if i == 4:
+                out_mid[...] = out
+            else:
+                out_edge[i // 2] = out
+
+        def part(at):
+            return base[at] if i == 4 else corrected(base, fixes, at)
+
+        def make():
+            return finish(
+                jnp.concatenate([done[i], done[i + 1]], axis=0),
+                lambda: jnp.concatenate([part(at) for at in (*places[i], *places[i + 1])], axis=0),
+                wp, g2[...], w1, w2, channels, put,
+            )
+
+        return after(lambda: i in done and i + 1 in done, make)
+
+    def fix(i):
+        taps = ((0, 1, 2), (6, 7, 8), (0, 3, 6), (2, 5, 8))[i]
+        source = (SHIFT - 1, 0)[i % 2]
+        if i < 2:
+            pieces = [bands_r[i, source, SHIFT - 1 + t : SHIFT - 1 + t + cols] for t in range(3)]
+        else:
+            pieces = [bands_c[i - 2, t : t + rows, source] for t in range(3)]
         weights = jnp.concatenate([wc[t * LANES : (t + 1) * LANES] for t in taps], axis=0)
         fixes[i] = dot(jnp.concatenate(pieces, axis=1).astype(BF16), weights)
-    for i, (taps, source) in enumerate((((0, 3, 6), SHIFT - 1), ((2, 5, 8), 0))):
-        pieces = [bands_c[i, t : t + rows, source] for t in range(3)]
-        weights = jnp.concatenate([wc[t * LANES : (t + 1) * LANES] for t in taps], axis=0)
-        fixes[2 + i] = dot(jnp.concatenate(pieces, axis=1).astype(BF16), weights)
-
-    gain2, done = g2[...], []
-    for i, result in enumerate(attention(units, bias, head_dim, channels)):
-        done.append(result)
-        if i % 2 == 0:
-            continue
-        if i == 1:
-            parts = [base[at] for at in ((1, 1), (1, 2), (2, 1), (2, 2))]
-        else:
-            parts = [corrected(base, fixes, at) for at in (*places[i - 3], *places[i - 2])]
-        out = finish(
-            jnp.concatenate(done[-2:], axis=0), jnp.concatenate(parts, axis=0), wp, gain2, w1, w2, channels
-        )
-        if i == 1:
-            out_mid[...] = out
-        else:
-            out_edge[i // 2 - 1] = out
-    for i, at in enumerate(((0, 0), (0, 3), (3, 0), (3, 3))):
-        corner_base[i] = corrected(base, fixes, at)
+        yield
+
+    def corners():
+        for i, at in enumerate(((0, 0), (0, 3), (3, 0), (3, 3))):
+            corner_base[i] = corrected(base, fixes, at)
+            yield
+
+    weave(
+        [unit(4), band(0), band(1), unit(5), band(2), band(3), unit(0), fix(0), unit(1), fix(1), tail(4),
+         unit(2), fix(2), unit(3), fix(3), tail(0), corners(), tail(2)],
+        3,
+    )
 
 
 def corrected(base, fixes, at):
@@ -364,44 +429,61 @@
     gain1 = gain1_ref[...]
     out_row = [(row == 0).astype(F32), (row == last_row).astype(F32)]
     out_col = [(col == 0).astype(F32), (col == last_col).astype(F32)]
-    for i in range(4):
-        ref = (left_ref, right_ref)[i % 2]
-        inside = (1.0 - out_row[i // 2]) * (1.0 - out_col[i % 2])
-        mark = marks(channels, out_row[i // 2] + out_col[i % 2])
-        normed[i, :, HALF:] = jnp.broadcast_to(mark, (AREA, HALF))
-        values = ref[i // 2 * SIDE : (i // 2 + 1) * SIDE].astype(F32)
-        normed[i, :, 0:channels] = layer_norm(values.reshape(AREA, channels), gain1 * inside)
-    corner = dot(normed[...].reshape(-1, LANES).astype(BF16), wkv[...]).astype(BF16)
-    corner = [corner[i * AREA : (i + 1) * AREA] for i in range(4)]
+    corner, done = {}, {}
+
+    def project(pair):
+        for i in (2 * pair, 2 * pair + 1):
+            ref = (left_ref, right_ref)[i % 2]
+            inside = (1.0 - out_row[i // 2]) * (1.0 - out_col[i % 2])
+            mark = marks(channels, out_row[i // 2] + out_col[i % 2])
+            normed[i, :, HALF:] = jnp.broadcast_to(mark, (AREA, HALF))
+            values = ref[i // 2 * SIDE : (i // 2 + 1) * SIDE].astype(F32)
+            normed[i, :, 0:channels] = layer_norm(values.reshape(AREA, channels), gain1 * inside)
+        yield
+        both = dot(normed[2 * pair : 2 * pair + 2].reshape(-1, LANES).astype(BF16), wkv[...])
+        yield
+        both = both.astype(BF16)
+        corner[2 * pair], corner[2 * pair + 1] = both[:AREA], both[AREA:]
+
     keys = [
-        [corner[0], kv_edge[2, 0], kv_edge[0, 0], kv[0, 0]],
-        [kv_edge[0, 3], kv[0, 3], corner[1], kv_edge[3, 0]],
-        [kv_edge[2, 3], corner[2], kv[3, 0], kv_edge[1, 0]],
-        [kv[3, 3], kv_edge[1, 3], kv_edge[3, 3], corner[3]],
+        lambda: [corner[0], kv_edge[2, 0], kv_edge[0, 0], kv[0, 0]],
+        lambda: [kv_edge[0, 3], kv[0, 3], corner[1], kv_edge[3, 0]],
+        lambda: [kv_edge[2, 3], corner[2], kv[3, 0], kv_edge[1, 0]],
+        lambda: [kv[3, 3], kv_edge[1, 3], kv_edge[3, 3], corner[3]],
     ]
     places = [(0, 0), (0, 3), (3, 0), (3, 3)]
     quadrants = [(1, 1), (1, 0), (0, 1), (0, 0)]
-    units = [
-        ([query[places[i]]], [quadrants[i]], jnp.concatenate(keys[i], axis=0)) for i in range(4)
-    ]
-    parts = []
-    for i, (tap, y, x) in enumerate(((0, 7, 7), (2, 7, 0), (6, 0, 7), (8, 0, 0))):
+
+    def unit(i):
+        def put(result):
+            done[i] = result
+
+        parts = ([query[places[i]]], [quadrants[i]], lambda: jnp.concatenate(keys[i](), axis=0))
+        return after(lambda: i in corner, lambda: attend(parts, bias, head_dim, channels, put))
+
+    def whole(i):
+        tap, y, x = ((0, 7, 7), (2, 7, 0), (6, 0, 7), (8, 0, 0))[i]
         start = y * SIDE
         term = dot(normed[i, start : start + SIDE].astype(BF16), wc[tap * LANES : (tap + 1) * LANES])
         term = term[x : x + 1]
         pixel = lax.broadcasted_iota(jnp.int32, (AREA, 1), 0)
         at = (SIDE - 1 - y) * SIDE + SIDE - 1 - x
-        parts.append(corner_base[i] + jnp.where(pixel == at, term, 0.0))
-    done = []
-    for i, result in enumerate(attention(units, bias, head_dim, channels)):
-        done.append(result)
-        if i % 2 == 0:
-            continue
-        out = finish(
-            jnp.concatenate(done[-2:], axis=0), jnp.concatenate(parts[i - 1 : i + 1], axis=0), wp, g2[...],
-            w1, w2, channels,
-        )
-        finish_bands((0,) if i == 1 else (3,), [out[:AREA], out[AREA:]])
+        return corner_base[i] + jnp.where(pixel == at, term, 0.0)
+
+    def tail(i):
+        def put(out):
+            finish_bands((0,) if i == 0 else (3,), [out[:AREA], out[AREA:]])
+
+        def make():
+            return finish(
+                jnp.concatenate([done[i], done[i + 1]], axis=0),
+                lambda: jnp.concatenate([whole(i), whole(i + 1)], axis=0),
+                wp, g2[...], w1, w2, channels, put,
+            )
+
+        return after(lambda: i in done and i + 1 in done, make)
+
+    weave([project(0), project(1), unit(0), unit(1), unit(2), unit(3), tail(0), tail(2)], 4)
     writes[0].wait()
     for r in (0, rows - SIDE):
         at = slice(r, r + SIDE)

time: 22.9 us -> 22.9 us (level)
  waiting for transfers between devices: 0.16 us -> 0.84 us
  Pallas kernels: 13.5 us -> 12.9 us
    ppermute x3, waiting for transfers between devices: 0.15 us -> 0.84 us  [exchange(): lax.ppermute(high, axis, [(i, (i + 1) % count) for i in range(count)])]
    pallas_call x4, Pallas kernels: 13.5 us -> 12.9 us  [call(): pl.pallas_call(kernel, out_shape=[out if isinstance(out, jax.ShapeDtypeSt...]
  transfers between devices with their start and end apart: 6 -> 6, of which waited for: 1 -> 1; matrix products, arithmetic and copies ran while one was open for 0% -> 0% of each run, Pallas kernels for 40% -> 37%
where the time goes in v11:
time: 22.9 us; the launch traced here: 22.8 us
  Pallas kernels  12.9 us (56%)
  starting transfers between devices  8.88 us (39%)
  waiting for transfers between devices  0.84 us (4%)
    pallas_call x4, Pallas kernels, call(): pl.pallas_call(kernel, out_shape=[out if isinstance(out, jax.ShapeDtypeSt...  12.9 us
    ppermute x3, starting transfers between devices, exchange(): lax.ppermute(low, axis, [((i + 1) % count, i) for i in range(count)])  5.83 us
    ppermute x3, starting transfers between devices, exchange(): lax.ppermute(high, axis, [(i, (i + 1) % count) for i in range(count)])  3.05 us
    ppermute x3, waiting for transfers between devices, exchange(): lax.ppermute(high, axis, [(i, (i + 1) % count) for i in range(count)])  0.84 us
  transfers between devices with their start and end apart: 6, of which 1 were waited for; matrix products, arithmetic and copies ran while one was open for 0% of the time, Pallas kernels for 37%

profile of v11, /device:TPU:0, one launch (start us, length us, event | category | flops | bytes accessed | tf_op | source)
XLA Modules:
  0.0 22.8 jit_solution(17525272064280665337)
XLA Ops:
  0.0 1.1 %cut_halo.1 = (bf16[32,32,180]{2,1,0:T(8,128)(2,1)S(1)}, bf16[8,32,180]{2,1,0:T(8,128)(2,1)S(1)}, bf16[8,32,180]{2,1,0:T(8,128)(2,1)S(1)}, bf16[32,8,180]{2,1,0:T(8,128)(2,1)S(1)}, bf16[32,8,180]{2,1,0:T(8,128)(2,1)S(1)}) custom-call(bf16[32,32,180]{2,1,0:T(8,128)(2,1)} %image_hbm.1), custom_call_target="tpu_custom_call" | custom-call | flops 1000000 | bytes 4000000 | tf_op jit(solution)/shard_map/cut_halo/pallas_call | solution.py:507
  1.1 3.0 %collective-permute-start = (bf16[8,32,180]{2,1,0:T(8,128)(2,1)S(1)}, bf16[8,32,180]{2,1,0:T(8,128)(2,1)S(1)}, u32[]{:S(2)}, u32[]{:S(2)}) collective-permute-start(bf16[8,32,180]{2,1,0:T(8,128)(2,1)S(1)} %get-tuple-element.24), channel_id=1, source_target_pairs={{0,8},{8,16},{16,24},{24,0},{1,9},{9,17},{17,25},{25,1},{2,10},{10... | collective-permute-start | bytes 276488 | tf_op jit(solution)/shard_map/ppermute | solution.py:499
  4.1 1.0 %collective-permute-start.1 = (bf16[8,32,180]{2,1,0:T(8,128)(2,1)S(1)}, bf16[8,32,180]{2,1,0:T(8,128)(2,1)S(1)}, u32[]{:S(2)}, u32[]{:S(2)}) collective-permute-start(bf16[8,32,180]{2,1,0:T(8,128)(2,1)S(1)} %get-tuple-element.25), channel_id=1, source_target_pairs={{8,0},{16,8},{24,16},{0,24},{9,1},{17,9},{25,17},{1,25},{10,2},{18... | collective-permute-start | bytes 276488 | tf_op jit(solution)/shard_map/ppermute | solution.py:500
  5.1 0.0 collective-permute-start.4
  5.1 3.5 %collective-permute-start.5 = (bf16[32,8,180]{2,1,0:T(8,128)(2,1)S(1)}, bf16[32,8,180]{2,1,0:T(8,128)(2,1)S(1)}, u32[]{:S(2)}, u32[]{:S(2)}) collective-permute-start(bf16[32,8,180]{2,1,0:T(8,128)(2,1)S(1)} %get-tuple-element.37), channel_id=1, source_target_pairs={{1,0},{2,1},{3,2},{4,3},{5,4},{6,5},{7,6},{0,7},{9,8},{10,9},{11,1... | collective-permute-start | bytes 276488 | tf_op jit(solution)/shard_map/ppermute | solution.py:500
  8.6 0.0 copy-start
  8.7 3.8 %own_tile.1 = (f32[6,2,2,64,256]{4,3,2,1,0:T(8,128)S(1)}, bf16[4,4,64,256]{3,2,1,0:T(8,128)(2,1)S(1)}, bf16[4,4,64,512]{3,2,1,0:T(8,128)(2,1)S(1)}, f32[4,4,64,2...) custom-call(bf16[32,32,180]{2,1,0:T(8,128)(2,1)S(1)} %get-tuple-elem, ...), custom_call_target="tpu_custom_call" | custom-call | flops 2000000000 | bytes 4000000 | tf_op jit(solution)/shard_map/own_tile/pallas_call | solution.py:507
  12.5 0.0 collective-permute-done.top_ref
  12.5 0.0 collective-permute-done.1.bottom_ref
  12.6 1.3 %collective-permute-start.3 = (bf16[16,8,180]{2,1,0:T(8,128)(2,1)S(1)}, bf16[16,8,180]{2,1,0:T(8,128)(2,1)S(1)}, u32[]{:S(2)}, u32[]{:S(2)}) collective-permute-start(bf16[16,8,180]{2,1,0:T(8,128)(2,1)S(1)} %pad_maximum_fusion.1), channel_id=1, source_target_pairs={{1,0},{2,1},{3,2},{4,3},{5,4},{6,5},{7,6},{0,7},{9,8},{10,9},{11,1... | collective-permute-start | bytes 138248 | tf_op jit(solution)/shard_map/ppermute | solution.py:500
  13.9 0.1 collective-permute-start.2
  13.9 0.0 collective-permute-done.4.left_ref
  13.9 0.0 collective-permute-done.5.right_ref
  13.9 0.0 copy-done
  14.0 4.6 %edge_windows.1 = (bf16[4,4,64,512]{3,2,1,0:T(8,128)(2,1)S(1)}, f32[4,64,256]{2,1,0:T(8,128)S(1)}, f32[2,256,256]{2,1,0:T(8,128)S(1)}, f32[256,256]{1,0:T(8,128)S(1)}) custom-call(bf16[8,32,180]{2,1,0:T(8,128)(2,1)S(1)} %collective-permute-done.top_ref, bf16[8,32,180]{2,1,0:T(8,128)(2,1)S(1)} %collective-permute-done.1.bottom_ref, ...), custom_call_target="tpu_custom_call" | custom-call | flops 2000000000 | bytes 4000000 | tf_op jit(solution)/shard_map/edge_windows/pallas_call | solution.py:507
  18.6 0.0 collective-permute-done.3.right_ref
  18.6 0.8 %collective-permute-done.2.left_ref = bf16[16,8,180]{2,1,0:T(8,128)(2,1)S(1)} collective-permute-done((bf16[16,8,180]{2,1,0:T(8,128)(2,1)S(1)}, bf16[16,8,180]{2,1,0:T(8,128)(2,1)S(1)}, u32[]{:S(2)}, u32[]{:S(2)}) %collective-permute-start.2) | collective-permute-done | bytes 46112 | tf_op jit(solution)/shard_map/ppermute | solution.py:499
  19.4 3.4 %corner_windows.1 = bf16[32,32,180]{2,1,0:T(8,128)(2,1)} custom-call(bf16[16,8,180]{2,1,0:T(8,128)(2,1)S(1)} %collective-permute-done.2.left_ref, bf16[16,8,180]{2,1,0:T(8,128)(2,1)S(1)} %collective-permute-done.3.right_ref, f32[1,180]{1,0:T(1,128)S(1)} %bitcast.6, f32[6,2,2,64,256]{4,3,2,1,0:T(8,128)S(1)} %get-tuple-element.27.bias, ...), custom_call_target="tpu_custom_call" | custom-call | flops 1000000000 | bytes 4000000 | tf_op jit(solution)/shard_map/corner_windows/pallas_call | solution.py:507
  (4 shorter events, 0.0 us)
Async XLA Ops:
  1.1 11.4 %collective-permute-start = (bf16[8,32,180]{2,1,0:T(8,128)(2,1)S(1)}, bf16[8,32,180]{2,1,0:T(8,128)(2,1)S(1)}, u32[]{:S(2)}, u32[]{:S(2)}) collective-permute-start(bf16[8,32,180]{2,1,0:T(8,128)(2,1)S(1)} %get-tuple-element.24), channel_id=1, source_target_pairs={{0,8},{8,16},{16,24},{24,0},{1,9},{9,17},{17,25},{25,1},{2,10},{10... | collective-permute-start | bytes 276488 | tf_op jit(solution)/shard_map/ppermute | solution.py:499
  4.1 8.4 %collective-permute-start.1 = (bf16[8,32,180]{2,1,0:T(8,128)(2,1)S(1)}, bf16[8,32,180]{2,1,0:T(8,128)(2,1)S(1)}, u32[]{:S(2)}, u32[]{:S(2)}) collective-permute-start(bf16[8,32,180]{2,1,0:T(8,128)(2,1)S(1)} %get-tuple-element.25), channel_id=1, source_target_pairs={{8,0},{16,8},{24,16},{0,24},{9,1},{17,9},{25,17},{1,25},{10,2},{18... | collective-permute-start | bytes 276488 | tf_op jit(solution)/shard_map/ppermute | solution.py:500
  5.1 8.8 %collective-permute-start.4 = (bf16[32,8,180]{2,1,0:T(8,128)(2,1)S(1)}, bf16[32,8,180]{2,1,0:T(8,128)(2,1)S(1)}, u32[]{:S(2)}, u32[]{:S(2)}) collective-permute-start(bf16[32,8,180]{2,1,0:T(8,128)(2,1)S(1)} %get-tuple-element.36), channel_id=1, source_target_pairs={{0,1},{1,2},{2,3},{3,4},{4,5},{5,6},{6,7},{7,0},{8,9},{9,10},{10,1... | collective-permute-start | bytes 276488 | tf_op jit(solution)/shard_map/ppermute | solution.py:499
  5.1 8.8 %collective-permute-start.5 = (bf16[32,8,180]{2,1,0:T(8,128)(2,1)S(1)}, bf16[32,8,180]{2,1,0:T(8,128)(2,1)S(1)}, u32[]{:S(2)}, u32[]{:S(2)}) collective-permute-start(bf16[32,8,180]{2,1,0:T(8,128)(2,1)S(1)} %get-tuple-element.37), channel_id=1, source_target_pairs={{1,0},{2,1},{3,2},{4,3},{5,4},{6,5},{7,6},{0,7},{9,8},{10,9},{11,1... | collective-permute-start | bytes 276488 | tf_op jit(solution)/shard_map/ppermute | solution.py:500
  8.6 5.3 %copy-start = (f32[180]{0:T(256)S(1)}, f32[180]{0:T(256)}, u32[]{:S(2)}) copy-start(f32[180]{0:T(256)} %param.10) | copy-start | bytes 2164
  12.6 6.0 %collective-permute-start.3 = (bf16[16,8,180]{2,1,0:T(8,128)(2,1)S(1)}, bf16[16,8,180]{2,1,0:T(8,128)(2,1)S(1)}, u32[]{:S(2)}, u32[]{:S(2)}) collective-permute-start(bf16[16,8,180]{2,1,0:T(8,128)(2,1)S(1)} %pad_maximum_fusion.1), channel_id=1, source_target_pairs={{1,0},{2,1},{3,2},{4,3},{5,4},{6,5},{7,6},{0,7},{9,8},{10,9},{11,1... | collective-permute-start | bytes 138248 | tf_op jit(solution)/shard_map/ppermute | solution.py:500
  13.9 5.5 %collective-permute-start.2 = (bf16[16,8,180]{2,1,0:T(8,128)(2,1)S(1)}, bf16[16,8,180]{2,1,0:T(8,128)(2,1)S(1)}, u32[]{:S(2)}, u32[]{:S(2)}) collective-permute-start(bf16[16,8,180]{2,1,0:T(8,128)(2,1)S(1)} %pad_maximum_fusion), channel_id=1, source_target_pairs={{0,1},{1,2},{2,3},{3,4},{4,5},{5,6},{6,7},{7,0},{8,9},{9,10},{10,1... | collective-permute-start | bytes 138248 | tf_op jit(solution)/shard_map/ppermute | solution.py:499

commit v12 on v11

--- a/solution.py
+++ b/solution.py
@@ -59,13 +59,13 @@
 
 
 def gelu(x):
-    size = jnp.abs(x)
-    t = 1.0 / (1.0 + (0.3275911 * math.sqrt(0.5)) * size)
-    poly = 0.5 * 1.061405429
-    for factor in (-1.453152027, 1.421413741, -0.284496736, 0.254829592):
-        poly = poly * t + 0.5 * factor
-    tail = poly * t * jnp.exp2(size * size * (-0.5 * LOG2E))
-    return jnp.maximum(x, 0.0) - size * tail
+    square = jnp.minimum(x * x, 25.0)
+    poly = -5.58203231240273e-08
+    for factor in (2.777085437695777e-06, -4.707012890217347e-05, -5.859274357446709e-05,
+                   0.036366718434813275, 0.7978721905787034):
+        poly = poly * square + factor
+    half = 0.5 * x
+    return half + half * jnp.tanh(x * poly)
 
 
 def lanes_of(width=LANES):
@@ -182,8 +182,8 @@
 
 def own_kernel(
     image_ref, gain1_hbm, gain2_hbm, qkv_hbm, proj_hbm, table_hbm, conv_hbm, fc1_hbm, fc2_hbm,
-    bias, query, kv, base, wkv, wp, wc, w1, w2, g2,
-    padded, strip, wq, normed, shifted,
+    bias, query, kv, normed, wkv, wp, wc, w1, w2, g2,
+    padded, strip, wq,
     table_ref, gain1_ref, gain2_ref, qkv_ref, proj_ref, conv_ref, fc1_ref, fc2_ref, sems,
 ):
     rows, cols, channels = image_ref.shape
@@ -208,10 +208,7 @@
     wkv[176:192, 0:LANES] = jnp.where(
         (special == flag_lane) & (lanes16 == flag_lane), MASKED, 0.0
     ).astype(BF16)
-    normed[...] = jnp.zeros_like(normed)
-    normed[1 : 1 + rows, SHIFT : SHIFT + cols, HALF:] = jnp.broadcast_to(
-        marks(channels, 0.0)[None], (rows, cols, HALF)
-    )
+    normed[:, :, HALF:] = jnp.broadcast_to(marks(channels, 0.0)[None], (rows, cols, HALF))
 
     fetches[0].wait()
     gain1 = gain1_ref[...]
@@ -231,13 +228,11 @@
             wc[tap * LANES : tap * LANES + channels, 0:channels] = conv_ref[tap // 3, tap % 3]
 
     def norm(br):
-        r = br * SIDE
-        inner = (slice(1 + r, 1 + r + SIDE), slice(SHIFT, SHIFT + cols))
-        normed[(*inner, slice(0, channels))] = layer_norm(image_ref[r : r + SIDE].astype(F32), gain1)
+        at = slice(br * SIDE, (br + 1) * SIDE)
+        normed[at, :, 0:channels] = layer_norm(image_ref[at].astype(F32), gain1)
 
     def project(br):
-        inner = (slice(1 + br * SIDE, 1 + (br + 1) * SIDE), slice(SHIFT, SHIFT + cols))
-        pixels = normed[inner].astype(BF16).reshape(-1, LANES)
+        pixels = normed[br * SIDE : (br + 1) * SIDE].astype(BF16).reshape(-1, LANES)
         q = dot(pixels, wq[...])
         yield
         both = dot(pixels, wkv[...]).reshape(SIDE, cols, 2 * LANES)
@@ -250,38 +245,20 @@
             part = slice(bc * SIDE, (bc + 1) * SIDE)
             kv[br, bc] = both[:, part].reshape(AREA, 2 * LANES).astype(BF16)
 
-    def convolve(br):
-        r = br * SIDE
-        for tap in range(3):
-            c0 = SHIFT - 1 + tap
-            start = 0 if br == 0 else r + 2
-            shifted[tap, start : r + SIDE + 2] = normed[start : r + SIDE + 2, c0 : c0 + cols].astype(BF16)
-        yield
-        taps = [
-            shifted[tap % 3, r + tap // 3 : r + tap // 3 + SIDE].reshape(-1, LANES) for tap in range(9)
-        ]
-        summed = dot(jnp.concatenate(taps, axis=1), wc[...])
-        yield
-        summed = summed[:, :channels].reshape(SIDE, cols, channels)
-        summed = summed + image_ref[r : r + SIDE].astype(F32)
-        for bc in range(blocks_c):
-            base[br, bc, :, HALF:] = jnp.zeros((AREA, HALF), F32)
-            base[br, bc, :, 0:channels] = summed[:, bc * SIDE : (bc + 1) * SIDE].reshape(AREA, channels)
-
     for br in range(blocks_r):
         norm(br)
     weights()
     tasks = [expand_bias(table_ref, padded, strip, bias)]
     for br in range(blocks_r):
-        tasks += [project(br), convolve(br)]
+        tasks.append(project(br))
     weave(tasks, 3)
 
 
 def edge_kernel(
-    top_ref, bottom_ref, left_ref, right_ref, gain1_ref,
-    bias, query, kv, base, wkv, wp, wc, w1, w2, g2,
+    image_ref, top_ref, bottom_ref, left_ref, right_ref, gain1_ref,
+    bias, query, kv, normed, wkv, wp, wc, w1, w2, g2,
     kv_edge, corner_base, out_edge, out_mid,
-    bands_r, bands_c, fixes,
+    halo, base, shifted,
 ):
     cols, channels = top_ref.shape[1:]
     rows = left_ref.shape[0]
@@ -292,32 +269,63 @@
     outside = [(row == 0).astype(F32), (row == last_row).astype(F32),
                (col == 0).astype(F32), (col == last_col).astype(F32)]
 
-    bands_r[...] = jnp.zeros_like(bands_r)
-    bands_c[...] = jnp.zeros_like(bands_c)
+    for r in (0, SHIFT + rows):
+        for c in (0, SHIFT + cols):
+            halo[r : r + SHIFT, c : c + SHIFT] = jnp.zeros((SHIFT, SHIFT, LANES), F32)
     sides = []
 
     def band(i):
         ref = (top_ref, bottom_ref, left_ref, right_ref)[i]
+        start = (0, SHIFT + (rows if i < 2 else cols))[i % 2]
+        inner = slice(SHIFT, SHIFT + (cols if i < 2 else rows))
+        outer = slice(start, start + SHIFT)
+        place = (outer, inner) if i < 2 else (inner, outer)
         mark = jnp.broadcast_to(marks(channels, outside[i])[None], (*ref.shape[:2], HALF))
-        values = layer_norm(ref[...].astype(F32), gain1 * (1.0 - outside[i]))
+        halo[(*place, slice(HALF, LANES))] = mark
+        halo[(*place, slice(0, channels))] = layer_norm(ref[...].astype(F32), gain1 * (1.0 - outside[i]))
+        pixels = halo[place]
         if i < 2:
-            bands_r[i, :, SHIFT : SHIFT + cols, HALF:] = mark
-            bands_r[i, :, SHIFT : SHIFT + cols, 0:channels] = values
-            pixels = bands_r[i, :, SHIFT : SHIFT + cols]
-            count = cols // SIDE
-            blocks = [pixels[:, b * SIDE : (b + 1) * SIDE].reshape(AREA, LANES) for b in range(count)]
+            blocks = [pixels[:, b * SIDE : (b + 1) * SIDE].reshape(AREA, LANES) for b in range(cols // SIDE)]
         else:
-            bands_c[i - 2, 1 : 1 + rows, :, HALF:] = mark
-            bands_c[i - 2, 1 : 1 + rows, :, 0:channels] = values
-            count = rows // SIDE
-            blocks = [bands_c[i - 2, 1 : 1 + rows].reshape(-1, LANES)]
+            blocks = [pixels.reshape(-1, LANES)]
         pixels = jnp.concatenate(blocks, axis=0).astype(BF16)
         yield
         both = dot(pixels, wkv[...])
         yield
-        kv_edge[i] = both.astype(BF16).reshape(count, AREA, 2 * LANES)
+        kv_edge[i] = both.astype(BF16).reshape(-1, AREA, 2 * LANES)
         sides.append(i)
 
+    def tile():
+        for r in range(0, rows, SIDE):
+            halo[SHIFT + r : SHIFT + r + SIDE, SHIFT : SHIFT + cols] = normed[r : r + SIDE]
+            yield
+
+    def convolve(br):
+        r = br * SIDE
+        for tap in range(3):
+            c0 = SHIFT - 1 + tap
+            start, stop = 0 if br == 0 else r + 2, r + SIDE + 2
+            shifted[tap, start:stop] = halo[
+                SHIFT - 1 + start : SHIFT - 1 + stop, c0 : c0 + cols
+            ].astype(BF16)
+        yield
+        taps = [
+            shifted[tap % 3, r + tap // 3 : r + tap // 3 + SIDE].reshape(-1, LANES) for tap in range(9)
+        ]
+        summed = dot(jnp.concatenate(taps, axis=1), wc[...])
+        yield
+        summed = summed[:, :channels].reshape(SIDE, cols, channels)
+        summed = summed + image_ref[r : r + SIDE].astype(F32)
+        for bc in range(cols // SIDE):
+            part = summed[:, bc * SIDE : (bc + 1) * SIDE].reshape(AREA, channels)
+            if (br, bc) in corners:
+                ref = corner_base.at[corners.index((br, bc))]
+            else:
+                ref = base.at[br, bc]
+            ref[:, HALF:] = jnp.zeros((AREA, HALF), F32)
+            ref[:, 0:channels] = part
+
+    corners = [(0, 0), (0, 3), (3, 0), (3, 3)]
     keys = [
         lambda: [kv_edge[0, 1], kv[0, 1], kv_edge[0, 2], kv[0, 2]],
         lambda: [kv[3, 1], kv_edge[1, 1], kv[3, 2], kv_edge[1, 2]],
@@ -347,53 +355,20 @@
             else:
                 out_edge[i // 2] = out
 
-        def part(at):
-            return base[at] if i == 4 else corrected(base, fixes, at)
-
         def make():
             return finish(
                 jnp.concatenate([done[i], done[i + 1]], axis=0),
-                lambda: jnp.concatenate([part(at) for at in (*places[i], *places[i + 1])], axis=0),
+                lambda: jnp.concatenate([base[at] for at in (*places[i], *places[i + 1])], axis=0),
                 wp, g2[...], w1, w2, channels, put,
             )
 
         return after(lambda: i in done and i + 1 in done, make)
 
-    def fix(i):
-        taps = ((0, 1, 2), (6, 7, 8), (0, 3, 6), (2, 5, 8))[i]
-        source = (SHIFT - 1, 0)[i % 2]
-        if i < 2:
-            pieces = [bands_r[i, source, SHIFT - 1 + t : SHIFT - 1 + t + cols] for t in range(3)]
-        else:
-            pieces = [bands_c[i - 2, t : t + rows, source] for t in range(3)]
-        weights = jnp.concatenate([wc[t * LANES : (t + 1) * LANES] for t in taps], axis=0)
-        fixes[i] = dot(jnp.concatenate(pieces, axis=1).astype(BF16), weights)
-        yield
-
-    def corners():
-        for i, at in enumerate(((0, 0), (0, 3), (3, 0), (3, 3))):
-            corner_base[i] = corrected(base, fixes, at)
-            yield
-
     weave(
-        [unit(4), band(0), band(1), unit(5), band(2), band(3), unit(0), fix(0), unit(1), fix(1), tail(4),
-         unit(2), fix(2), unit(3), fix(3), tail(0), corners(), tail(2)],
+        [unit(4), band(0), band(1), unit(5), band(2), band(3), tile(), unit(0), convolve(0), unit(1),
+         convolve(1), unit(2), convolve(2), unit(3), convolve(3), tail(4), tail(0), tail(2)],
         3,
     )
-
-
-def corrected(base, fixes, at):
-    br, bc = at
-    block = base[at].reshape(SIDE, SIDE, LANES)
-    y = lax.broadcasted_iota(jnp.int32, (SIDE, SIDE, 1), 0)
-    x = lax.broadcasted_iota(jnp.int32, (SIDE, SIDE, 1), 1)
-    if br in (0, 3):
-        fix = fixes[0 if br == 0 else 1, bc * SIDE : (bc + 1) * SIDE]
-        block = block + jnp.where(y == (0 if br == 0 else SIDE - 1), fix[None], 0.0)
-    if bc in (0, 3):
-        fix = fixes[2 if bc == 0 else 3, br * SIDE : (br + 1) * SIDE]
-        block = block + jnp.where(x == (0 if bc == 0 else SIDE - 1), fix[:, None], 0.0)
-    return block.reshape(AREA, LANES)
 
 
 def corner_kernel(
@@ -537,14 +512,14 @@
     left, right = exchange(first_cols, last_cols, "col")
     fetched = (table, gain1, gain2, qkv_weight, proj_weight, conv_weight, fc1_weight, fc2)
     hidden = -(-fc1_weight.shape[1] // 128) * 128
-    bias, query, kv, base, wkv, wp, wc, w1, w2, g2 = call(
+    bias, query, kv, normed, wkv, wp, wc, w1, w2, g2 = call(
         own_kernel,
         "own_tile",
         [
             ((HEADS, 2, 2, AREA, WIN * WIN), F32),
             ((blocks_r, blocks_c, AREA, LANES), BF16),
             ((blocks_r, blocks_c, AREA, 2 * LANES), BF16),
-            ((blocks_r, blocks_c, AREA, LANES), F32),
+            ((rows, cols, LANES), F32),
             ((LANES, 2 * LANES), BF16),
             ((LANES, LANES), BF16),
             ((9 * LANES, LANES), BF16),
@@ -556,8 +531,6 @@
             ((8, 1024), F32),
             ((4, 8 * WIN, 128), F32),
             ((LANES, LANES), BF16),
-            ((rows + 2, cols + 2 * SHIFT, LANES), F32),
-            ((3, rows + 2, cols, LANES), BF16),
             *[(x.shape, x.dtype) for x in fetched],
             pltpu.SemaphoreType.DMA((len(fetched),)),
         ],
@@ -578,12 +551,12 @@
             ((4 * AREA, LANES), F32),
         ],
         [
-            ((2, SHIFT, cols + 2 * SHIFT, LANES), F32),
-            ((2, rows + 2, SHIFT, LANES), F32),
-            ((4, cols, LANES), F32),
+            ((rows + 2 * SHIFT, cols + 2 * SHIFT, LANES), F32),
+            ((blocks_r, blocks_c, AREA, LANES), F32),
+            ((3, rows + 2, cols, LANES), BF16),
         ],
         2_000_000_000,
-        (top, bottom, left, right, gain1, bias, query, kv, base, wkv, wp, wc, w1, w2, g2),
+        (tile, top, bottom, left, right, gain1, bias, query, kv, normed, wkv, wp, wc, w1, w2, g2),
     )
     (out,) = call(
         corner_kernel,

time: 22.9 us -> 22.9 us (level)
  waiting for transfers between devices: 0.84 us -> 0.1 us
  starting transfers between devices: 8.88 us -> 9.5 us
    ppermute x3, waiting for transfers between devices: 0.84 us -> 0.1 us  [exchange(): lax.ppermute(high, axis, [(i, (i + 1) % count) for i in range(count)])]
    ppermute x3, starting transfers between devices: 5.83 us -> 6.45 us  [exchange(): lax.ppermute(low, axis, [((i + 1) % count, i) for i in range(count)])]
  transfers between devices with their start and end apart: 6 -> 6, of which waited for: 1 -> 1; matrix products, arithmetic and copies ran while one was open for 0% -> 0% of each run, Pallas kernels for 37% -> 38%
where the time goes in v12:
time: 22.9 us; the launch traced here: 22.7 us
  Pallas kernels  13 us (57%)
  starting transfers between devices  9.5 us (41%)
    pallas_call x4, Pallas kernels, call(): pl.pallas_call(kernel, out_shape=[out if isinstance(out, jax.ShapeDtypeSt...  13 us
    ppermute x3, starting transfers between devices, exchange(): lax.ppermute(low, axis, [((i + 1) % count, i) for i in range(count)])  6.45 us
    ppermute x3, starting transfers between devices, exchange(): lax.ppermute(high, axis, [(i, (i + 1) % count) for i in range(count)])  3.05 us
  transfers between devices with their start and end apart: 6, of which 1 were waited for; matrix products, arithmetic and copies ran while one was open for 0% of the time, Pallas kernels for 38%

profile of v12, /device:TPU:0, one launch (start us, length us, event | category | flops | bytes accessed | tf_op | source)
XLA Modules:
  0.0 22.7 jit_solution(17596835728294859645)
XLA Ops:
  0.0 1.1 %cut_halo.1 = (bf16[32,32,180]{2,1,0:T(8,128)(2,1)S(1)}, bf16[8,32,180]{2,1,0:T(8,128)(2,1)S(1)}, bf16[8,32,180]{2,1,0:T(8,128)(2,1)S(1)}, bf16[32,8,180]{2,1,0:T(8,128)(2,1)S(1)}, bf16[32,8,180]{2,1,0:T(8,128)(2,1)S(1)}) custom-call(bf16[32,32,180]{2,1,0:T(8,128)(2,1)} %image_hbm.1), custom_call_target="tpu_custom_call" | custom-call | flops 1000000 | bytes 4000000 | tf_op jit(solution)/shard_map/cut_halo/pallas_call | solution.py:482
  1.1 3.0 %collective-permute-start = (bf16[8,32,180]{2,1,0:T(8,128)(2,1)S(1)}, bf16[8,32,180]{2,1,0:T(8,128)(2,1)S(1)}, u32[]{:S(2)}, u32[]{:S(2)}) collective-permute-start(bf16[8,32,180]{2,1,0:T(8,128)(2,1)S(1)} %get-tuple-element.24), channel_id=1, source_target_pairs={{0,8},{8,16},{16,24},{24,0},{1,9},{9,17},{17,25},{25,1},{2,10},{10... | collective-permute-start | bytes 276488 | tf_op jit(solution)/shard_map/ppermute | solution.py:474
  4.1 1.0 %collective-permute-start.1 = (bf16[8,32,180]{2,1,0:T(8,128)(2,1)S(1)}, bf16[8,32,180]{2,1,0:T(8,128)(2,1)S(1)}, u32[]{:S(2)}, u32[]{:S(2)}) collective-permute-start(bf16[8,32,180]{2,1,0:T(8,128)(2,1)S(1)} %get-tuple-element.25), channel_id=1, source_target_pairs={{8,0},{16,8},{24,16},{0,24},{9,1},{17,9},{25,17},{1,25},{10,2},{18... | collective-permute-start | bytes 276488 | tf_op jit(solution)/shard_map/ppermute | solution.py:475
  5.1 0.0 collective-permute-start.4
  5.1 3.5 %collective-permute-start.5 = (bf16[32,8,180]{2,1,0:T(8,128)(2,1)S(1)}, bf16[32,8,180]{2,1,0:T(8,128)(2,1)S(1)}, u32[]{:S(2)}, u32[]{:S(2)}) collective-permute-start(bf16[32,8,180]{2,1,0:T(8,128)(2,1)S(1)} %get-tuple-element.37), channel_id=1, source_target_pairs={{1,0},{2,1},{3,2},{4,3},{5,4},{6,5},{7,6},{0,7},{9,8},{10,9},{11,1... | collective-permute-start | bytes 276488 | tf_op jit(solution)/shard_map/ppermute | solution.py:475
  8.6 0.0 copy-start
  8.7 3.2 %own_tile.1 = (f32[6,2,2,64,256]{4,3,2,1,0:T(8,128)S(1)}, bf16[4,4,64,256]{3,2,1,0:T(8,128)(2,1)S(1)}, bf16[4,4,64,512]{3,2,1,0:T(8,128)(2,1)S(1)}, f32[32,32,25...) custom-call(bf16[32,32,180]{2,1,0:T(8,128)(2,1)S(1)} %get-tuple-elem, ...), custom_call_target="tpu_custom_call" | custom-call | flops 2000000000 | bytes 4000000 | tf_op jit(solution)/shard_map/own_tile/pallas_call | solution.py:482
  11.9 0.0 collective-permute-done.top_ref
  11.9 0.0 collective-permute-done.1.bottom_ref
  12.0 1.9 %collective-permute-start.3 = (bf16[16,8,180]{2,1,0:T(8,128)(2,1)S(1)}, bf16[16,8,180]{2,1,0:T(8,128)(2,1)S(1)}, u32[]{:S(2)}, u32[]{:S(2)}) collective-permute-start(bf16[16,8,180]{2,1,0:T(8,128)(2,1)S(1)} %pad_maximum_fusion.1), channel_id=1, source_target_pairs={{1,0},{2,1},{3,2},{4,3},{5,4},{6,5},{7,6},{0,7},{9,8},{10,9},{11,1... | collective-permute-start | bytes 138248 | tf_op jit(solution)/shard_map/ppermute | solution.py:475
  13.9 0.1 collective-permute-start.2
  13.9 0.0 collective-permute-done.4.left_ref
  13.9 0.0 collective-permute-done.5.right_ref
  13.9 0.0 copy-done
  14.0 5.3 %edge_windows.1 = (bf16[4,4,64,512]{3,2,1,0:T(8,128)(2,1)S(1)}, f32[4,64,256]{2,1,0:T(8,128)S(1)}, f32[2,256,256]{2,1,0:T(8,128)S(1)}, f32[256,256]{1,0:T(8,128)S(1)}) custom-call(bf16[32,32,180]{2,1,0:T(8,128)(2,1)S(1)} %get-tuple-element.26.image_ref, bf16[8,32,180]{2,1,0:T(8,128)(2,1)S(1)} %collective-permute-done.top_ref, ...), custom_call_target="tpu_custom_call" | custom-call | flops 2000000000 | bytes 4000000 | tf_op jit(solution)/shard_map/edge_windows/pallas_call | solution.py:482
  19.3 0.0 collective-permute-done.3.right_ref
  19.3 0.1 collective-permute-done.2.left_ref
  19.4 3.3 %corner_windows.1 = bf16[32,32,180]{2,1,0:T(8,128)(2,1)} custom-call(bf16[16,8,180]{2,1,0:T(8,128)(2,1)S(1)} %collective-permute-done.2.left_ref, bf16[16,8,180]{2,1,0:T(8,128)(2,1)S(1)} %collective-permute-done.3.right_ref, f32[1,180]{1,0:T(1,128)S(1)} %bitcast.6, f32[6,2,2,64,256]{4,3,2,1,0:T(8,128)S(1)} %get-tuple-element.27.bias, ...), custom_call_target="tpu_custom_call" | custom-call | flops 1000000000 | bytes 4000000 | tf_op jit(solution)/shard_map/corner_windows/pallas_call | solution.py:482
  (4 shorter events, 0.0 us)
Async XLA Ops:
  1.1 10.8 %collective-permute-start = (bf16[8,32,180]{2,1,0:T(8,128)(2,1)S(1)}, bf16[8,32,180]{2,1,0:T(8,128)(2,1)S(1)}, u32[]{:S(2)}, u32[]{:S(2)}) collective-permute-start(bf16[8,32,180]{2,1,0:T(8,128)(2,1)S(1)} %get-tuple-element.24), channel_id=1, source_target_pairs={{0,8},{8,16},{16,24},{24,0},{1,9},{9,17},{17,25},{25,1},{2,10},{10... | collective-permute-start | bytes 276488 | tf_op jit(solution)/shard_map/ppermute | solution.py:474
  4.1 7.8 %collective-permute-start.1 = (bf16[8,32,180]{2,1,0:T(8,128)(2,1)S(1)}, bf16[8,32,180]{2,1,0:T(8,128)(2,1)S(1)}, u32[]{:S(2)}, u32[]{:S(2)}) collective-permute-start(bf16[8,32,180]{2,1,0:T(8,128)(2,1)S(1)} %get-tuple-element.25), channel_id=1, source_target_pairs={{8,0},{16,8},{24,16},{0,24},{9,1},{17,9},{25,17},{1,25},{10,2},{18... | collective-permute-start | bytes 276488 | tf_op jit(solution)/shard_map/ppermute | solution.py:475
  5.1 8.8 %collective-permute-start.4 = (bf16[32,8,180]{2,1,0:T(8,128)(2,1)S(1)}, bf16[32,8,180]{2,1,0:T(8,128)(2,1)S(1)}, u32[]{:S(2)}, u32[]{:S(2)}) collective-permute-start(bf16[32,8,180]{2,1,0:T(8,128)(2,1)S(1)} %get-tuple-element.36), channel_id=1, source_target_pairs={{0,1},{1,2},{2,3},{3,4},{4,5},{5,6},{6,7},{7,0},{8,9},{9,10},{10,1... | collective-permute-start | bytes 276488 | tf_op jit(solution)/shard_map/ppermute | solution.py:474
  5.1 8.8 %collective-permute-start.5 = (bf16[32,8,180]{2,1,0:T(8,128)(2,1)S(1)}, bf16[32,8,180]{2,1,0:T(8,128)(2,1)S(1)}, u32[]{:S(2)}, u32[]{:S(2)}) collective-permute-start(bf16[32,8,180]{2,1,0:T(8,128)(2,1)S(1)} %get-tuple-element.37), channel_id=1, source_target_pairs={{1,0},{2,1},{3,2},{4,3},{5,4},{6,5},{7,6},{0,7},{9,8},{10,9},{11,1... | collective-permute-start | bytes 276488 | tf_op jit(solution)/shard_map/ppermute | solution.py:475
  8.6 5.3 %copy-start = (f32[180]{0:T(256)S(1)}, f32[180]{0:T(256)}, u32[]{:S(2)}) copy-start(f32[180]{0:T(256)} %param.10) | copy-start | bytes 2164
  12.0 7.3 %collective-permute-start.3 = (bf16[16,8,180]{2,1,0:T(8,128)(2,1)S(1)}, bf16[16,8,180]{2,1,0:T(8,128)(2,1)S(1)}, u32[]{:S(2)}, u32[]{:S(2)}) collective-permute-start(bf16[16,8,180]{2,1,0:T(8,128)(2,1)S(1)} %pad_maximum_fusion.1), channel_id=1, source_target_pairs={{1,0},{2,1},{3,2},{4,3},{5,4},{6,5},{7,6},{0,7},{9,8},{10,9},{11,1... | collective-permute-start | bytes 138248 | tf_op jit(solution)/shard_map/ppermute | solution.py:475
  13.9 5.5 %collective-permute-start.2 = (bf16[16,8,180]{2,1,0:T(8,128)(2,1)S(1)}, bf16[16,8,180]{2,1,0:T(8,128)(2,1)S(1)}, u32[]{:S(2)}, u32[]{:S(2)}) collective-permute-start(bf16[16,8,180]{2,1,0:T(8,128)(2,1)S(1)} %pad_maximum_fusion), channel_id=1, source_target_pairs={{0,1},{1,2},{2,3},{3,4},{4,5},{5,6},{6,7},{7,0},{8,9},{9,10},{10,1... | collective-permute-start | bytes 138248 | tf_op jit(solution)/shard_map/ppermute | solution.py:474

commit v13 on v11

--- a/solution.py
+++ b/solution.py
@@ -59,13 +59,13 @@
 
 
 def gelu(x):
-    size = jnp.abs(x)
-    t = 1.0 / (1.0 + (0.3275911 * math.sqrt(0.5)) * size)
-    poly = 0.5 * 1.061405429
-    for factor in (-1.453152027, 1.421413741, -0.284496736, 0.254829592):
-        poly = poly * t + 0.5 * factor
-    tail = poly * t * jnp.exp2(size * size * (-0.5 * LOG2E))
-    return jnp.maximum(x, 0.0) - size * tail
+    square = jnp.minimum(x * x, 25.0)
+    poly = -5.58203231240273e-08
+    for factor in (2.777085437695777e-06, -4.707012890217347e-05, -5.859274357446709e-05,
+                   0.036366718434813275, 0.7978721905787034):
+        poly = poly * square + factor
+    half = 0.5 * x
+    return half + half * jnp.tanh(x * poly)
 
 
 def lanes_of(width=LANES):
@@ -134,18 +134,21 @@
     part_bias = jnp.concatenate([bias[:, hy, hx] for hy, hx in quadrants], axis=1)
     scores = scores.reshape(HEADS, count, WIN * WIN) + part_bias
     scores = scores - jnp.max(scores, axis=-1, keepdims=True)
-    weights = jnp.exp2(scores)
-    total = jnp.sum(weights, axis=-1, keepdims=True)
-    weights = weights.astype(BF16).reshape(HEADS * count, WIN * WIN)
+    weights = jnp.exp2(scores).astype(BF16).reshape(HEADS * count, WIN * WIN)
     yield
     mixed = dot(weights, pair[:, LANES:])
-    yield
-    result, divisor = mixed[0:count], jnp.broadcast_to(total[0], (count, LANES))
+    total = dot(weights, jnp.ones((WIN * WIN, HALF), BF16))
+    yield
+    result, low, high = mixed[0:count], total[0:count], total[0:count]
     for h in range(1, HEADS):
+        rows = slice(h * count, (h + 1) * count)
         mine = (lane >= h * head_dim) & (lane < (h + 1) * head_dim)
-        result = jnp.where(mine, mixed[h * count : (h + 1) * count], result)
-        divisor = jnp.where(mine, total[h], divisor)
-    put((result / divisor).astype(BF16))
+        result = jnp.where(mine, mixed[rows], result)
+        if h * head_dim < HALF:
+            low = jnp.where(mine[:, :HALF], total[rows], low)
+        if (h + 1) * head_dim > HALF:
+            high = jnp.where(mine[:, HALF:], total[rows], high)
+    put((result / jnp.concatenate([low, high], axis=1)).astype(BF16))
 
 
 def finish(heads_out, base, wp, gain2, w1, w2, channels, put):

time: 22.9 us -> 22.9 us (level)
  no operation moved by 1% of the time
where the time goes in v13:
time: 22.9 us; the launch traced here: 22.7 us
  Pallas kernels  12.8 us (56%)
  starting transfers between devices  8.88 us (39%)
  waiting for transfers between devices  0.83 us (4%)
    pallas_call x4, Pallas kernels, call(): pl.pallas_call(kernel, out_shape=[out if isinstance(out, jax.ShapeDtypeSt...  12.8 us
    ppermute x3, starting transfers between devices, exchange(): lax.ppermute(low, axis, [((i + 1) % count, i) for i in range(count)])  5.83 us
    ppermute x3, starting transfers between devices, exchange(): lax.ppermute(high, axis, [(i, (i + 1) % count) for i in range(count)])  3.05 us
    ppermute x3, waiting for transfers between devices, exchange(): lax.ppermute(high, axis, [(i, (i + 1) % count) for i in range(count)])  0.82 us
  transfers between devices with their start and end apart: 6, of which 1 were waited for; matrix products, arithmetic and copies ran while one was open for 0% of the time, Pallas kernels for 37%

profile of v13, /device:TPU:0, one launch (start us, length us, event | category | flops | bytes accessed | tf_op | source)
XLA Modules:
  0.0 22.7 jit_solution(18237181842016851722)
XLA Ops:
  0.0 1.1 %cut_halo.1 = (bf16[32,32,180]{2,1,0:T(8,128)(2,1)S(1)}, bf16[8,32,180]{2,1,0:T(8,128)(2,1)S(1)}, bf16[8,32,180]{2,1,0:T(8,128)(2,1)S(1)}, bf16[32,8,180]{2,1,0:T(8,128)(2,1)S(1)}, bf16[32,8,180]{2,1,0:T(8,128)(2,1)S(1)}) custom-call(bf16[32,32,180]{2,1,0:T(8,128)(2,1)} %image_hbm.1), custom_call_target="tpu_custom_call" | custom-call | flops 1000000 | bytes 4000000 | tf_op jit(solution)/shard_map/cut_halo/pallas_call | solution.py:510
  1.1 3.0 %collective-permute-start = (bf16[8,32,180]{2,1,0:T(8,128)(2,1)S(1)}, bf16[8,32,180]{2,1,0:T(8,128)(2,1)S(1)}, u32[]{:S(2)}, u32[]{:S(2)}) collective-permute-start(bf16[8,32,180]{2,1,0:T(8,128)(2,1)S(1)} %get-tuple-element.24), channel_id=1, source_target_pairs={{0,8},{8,16},{16,24},{24,0},{1,9},{9,17},{17,25},{25,1},{2,10},{10... | collective-permute-start | bytes 276488 | tf_op jit(solution)/shard_map/ppermute | solution.py:502
  4.1 1.0 %collective-permute-start.1 = (bf16[8,32,180]{2,1,0:T(8,128)(2,1)S(1)}, bf16[8,32,180]{2,1,0:T(8,128)(2,1)S(1)}, u32[]{:S(2)}, u32[]{:S(2)}) collective-permute-start(bf16[8,32,180]{2,1,0:T(8,128)(2,1)S(1)} %get-tuple-element.25), channel_id=1, source_target_pairs={{8,0},{16,8},{24,16},{0,24},{9,1},{17,9},{25,17},{1,25},{10,2},{18... | collective-permute-start | bytes 276488 | tf_op jit(solution)/shard_map/ppermute | solution.py:503
  5.1 0.0 collective-permute-start.4
  5.1 3.5 %collective-permute-start.5 = (bf16[32,8,180]{2,1,0:T(8,128)(2,1)S(1)}, bf16[32,8,180]{2,1,0:T(8,128)(2,1)S(1)}, u32[]{:S(2)}, u32[]{:S(2)}) collective-permute-start(bf16[32,8,180]{2,1,0:T(8,128)(2,1)S(1)} %get-tuple-element.37), channel_id=1, source_target_pairs={{1,0},{2,1},{3,2},{4,3},{5,4},{6,5},{7,6},{0,7},{9,8},{10,9},{11,1... | collective-permute-start | bytes 276488 | tf_op jit(solution)/shard_map/ppermute | solution.py:503
  8.6 0.0 copy-start
  8.7 3.8 %own_tile.1 = (f32[6,2,2,64,256]{4,3,2,1,0:T(8,128)S(1)}, bf16[4,4,64,256]{3,2,1,0:T(8,128)(2,1)S(1)}, bf16[4,4,64,512]{3,2,1,0:T(8,128)(2,1)S(1)}, f32[4,4,64,2...) custom-call(bf16[32,32,180]{2,1,0:T(8,128)(2,1)S(1)} %get-tuple-elem, ...), custom_call_target="tpu_custom_call" | custom-call | flops 2000000000 | bytes 4000000 | tf_op jit(solution)/shard_map/own_tile/pallas_call | solution.py:510
  12.5 0.0 collective-permute-done.top_ref
  12.5 0.0 collective-permute-done.1.bottom_ref
  12.6 1.3 %collective-permute-start.3 = (bf16[16,8,180]{2,1,0:T(8,128)(2,1)S(1)}, bf16[16,8,180]{2,1,0:T(8,128)(2,1)S(1)}, u32[]{:S(2)}, u32[]{:S(2)}) collective-permute-start(bf16[16,8,180]{2,1,0:T(8,128)(2,1)S(1)} %pad_maximum_fusion.1), channel_id=1, source_target_pairs={{1,0},{2,1},{3,2},{4,3},{5,4},{6,5},{7,6},{0,7},{9,8},{10,9},{11,1... | collective-permute-start | bytes 138248 | tf_op jit(solution)/shard_map/ppermute | solution.py:503
  13.9 0.1 collective-permute-start.2
  13.9 0.0 collective-permute-done.4.left_ref
  13.9 0.0 collective-permute-done.5.right_ref
  13.9 0.0 copy-done
  14.0 4.6 %edge_windows.1 = (bf16[4,4,64,512]{3,2,1,0:T(8,128)(2,1)S(1)}, f32[4,64,256]{2,1,0:T(8,128)S(1)}, f32[2,256,256]{2,1,0:T(8,128)S(1)}, f32[256,256]{1,0:T(8,128)S(1)}) custom-call(bf16[8,32,180]{2,1,0:T(8,128)(2,1)S(1)} %collective-permute-done.top_ref, bf16[8,32,180]{2,1,0:T(8,128)(2,1)S(1)} %collective-permute-done.1.bottom_ref, ...), custom_call_target="tpu_custom_call" | custom-call | flops 2000000000 | bytes 4000000 | tf_op jit(solution)/shard_map/edge_windows/pallas_call | solution.py:510
  18.6 0.0 collective-permute-done.3.right_ref
  18.6 0.8 %collective-permute-done.2.left_ref = bf16[16,8,180]{2,1,0:T(8,128)(2,1)S(1)} collective-permute-done((bf16[16,8,180]{2,1,0:T(8,128)(2,1)S(1)}, bf16[16,8,180]{2,1,0:T(8,128)(2,1)S(1)}, u32[]{:S(2)}, u32[]{:S(2)}) %collective-permute-start.2) | collective-permute-done | bytes 46112 | tf_op jit(solution)/shard_map/ppermute | solution.py:502
  19.4 3.3 %corner_windows.1 = bf16[32,32,180]{2,1,0:T(8,128)(2,1)} custom-call(bf16[16,8,180]{2,1,0:T(8,128)(2,1)S(1)} %collective-permute-done.2.left_ref, bf16[16,8,180]{2,1,0:T(8,128)(2,1)S(1)} %collective-permute-done.3.right_ref, f32[1,180]{1,0:T(1,128)S(1)} %bitcast.6, f32[6,2,2,64,256]{4,3,2,1,0:T(8,128)S(1)} %get-tuple-element.27.bias, ...), custom_call_target="tpu_custom_call" | custom-call | flops 1000000000 | bytes 4000000 | tf_op jit(solution)/shard_map/corner_windows/pallas_call | solution.py:510
  (4 shorter events, 0.0 us)
Async XLA Ops:
  1.1 11.4 %collective-permute-start = (bf16[8,32,180]{2,1,0:T(8,128)(2,1)S(1)}, bf16[8,32,180]{2,1,0:T(8,128)(2,1)S(1)}, u32[]{:S(2)}, u32[]{:S(2)}) collective-permute-start(bf16[8,32,180]{2,1,0:T(8,128)(2,1)S(1)} %get-tuple-element.24), channel_id=1, source_target_pairs={{0,8},{8,16},{16,24},{24,0},{1,9},{9,17},{17,25},{25,1},{2,10},{10... | collective-permute-start | bytes 276488 | tf_op jit(solution)/shard_map/ppermute | solution.py:502
  4.1 8.4 %collective-permute-start.1 = (bf16[8,32,180]{2,1,0:T(8,128)(2,1)S(1)}, bf16[8,32,180]{2,1,0:T(8,128)(2,1)S(1)}, u32[]{:S(2)}, u32[]{:S(2)}) collective-permute-start(bf16[8,32,180]{2,1,0:T(8,128)(2,1)S(1)} %get-tuple-element.25), channel_id=1, source_target_pairs={{8,0},{16,8},{24,16},{0,24},{9,1},{17,9},{25,17},{1,25},{10,2},{18... | collective-permute-start | bytes 276488 | tf_op jit(solution)/shard_map/ppermute | solution.py:503
  5.1 8.8 %collective-permute-start.4 = (bf16[32,8,180]{2,1,0:T(8,128)(2,1)S(1)}, bf16[32,8,180]{2,1,0:T(8,128)(2,1)S(1)}, u32[]{:S(2)}, u32[]{:S(2)}) collective-permute-start(bf16[32,8,180]{2,1,0:T(8,128)(2,1)S(1)} %get-tuple-element.36), channel_id=1, source_target_pairs={{0,1},{1,2},{2,3},{3,4},{4,5},{5,6},{6,7},{7,0},{8,9},{9,10},{10,1... | collective-permute-start | bytes 276488 | tf_op jit(solution)/shard_map/ppermute | solution.py:502
  5.1 8.8 %collective-permute-start.5 = (bf16[32,8,180]{2,1,0:T(8,128)(2,1)S(1)}, bf16[32,8,180]{2,1,0:T(8,128)(2,1)S(1)}, u32[]{:S(2)}, u32[]{:S(2)}) collective-permute-start(bf16[32,8,180]{2,1,0:T(8,128)(2,1)S(1)} %get-tuple-element.37), channel_id=1, source_target_pairs={{1,0},{2,1},{3,2},{4,3},{5,4},{6,5},{7,6},{0,7},{9,8},{10,9},{11,1... | collective-permute-start | bytes 276488 | tf_op jit(solution)/shard_map/ppermute | solution.py:503
  8.6 5.3 %copy-start = (f32[180]{0:T(256)S(1)}, f32[180]{0:T(256)}, u32[]{:S(2)}) copy-start(f32[180]{0:T(256)} %param.10) | copy-start | bytes 2164
  12.6 6.0 %collective-permute-start.3 = (bf16[16,8,180]{2,1,0:T(8,128)(2,1)S(1)}, bf16[16,8,180]{2,1,0:T(8,128)(2,1)S(1)}, u32[]{:S(2)}, u32[]{:S(2)}) collective-permute-start(bf16[16,8,180]{2,1,0:T(8,128)(2,1)S(1)} %pad_maximum_fusion.1), channel_id=1, source_target_pairs={{1,0},{2,1},{3,2},{4,3},{5,4},{6,5},{7,6},{0,7},{9,8},{10,9},{11,1... | collective-permute-start | bytes 138248 | tf_op jit(solution)/shard_map/ppermute | solution.py:503
  13.9 5.5 %collective-permute-start.2 = (bf16[16,8,180]{2,1,0:T(8,128)(2,1)S(1)}, bf16[16,8,180]{2,1,0:T(8,128)(2,1)S(1)}, u32[]{:S(2)}, u32[]{:S(2)}) collective-permute-start(bf16[16,8,180]{2,1,0:T(8,128)(2,1)S(1)} %pad_maximum_fusion), channel_id=1, source_target_pairs={{0,1},{1,2},{2,3},{3,4},{4,5},{5,6},{6,7},{7,0},{8,9},{9,10},{10,1... | collective-permute-start | bytes 138248 | tf_op jit(solution)/shard_map/ppermute | solution.py:502

commit v14 on v13

--- a/solution.py
+++ b/solution.py
@@ -114,41 +114,39 @@
                 bias[head, py // SIDE, 1, place, lanes] = rolled[SIDE:]
 
 
-def scores_of(blocks, keys, head_dim, channels):
+def by_head(part, head_dim, flag):
     lane = lanes_of()
-    part = jnp.concatenate(blocks, axis=0)
     own = [(lane >= h * head_dim) & (lane < (h + 1) * head_dim) for h in range(HEADS)]
-    stacked = jnp.concatenate(
-        [part * one_hot(own[h] | (lane == channels)) for h in range(HEADS)], axis=0
-    )
-    return dot_nt(stacked, keys)
+    return jnp.concatenate([part * one_hot(own[h] | (lane == flag)) for h in range(HEADS)], axis=0)
+
+
+def softmax(scores, part_bias):
+    scores = scores + part_bias
+    scores = scores - jnp.max(scores, axis=-1, keepdims=True)
+    weights = jnp.exp2(scores)
+    return weights.astype(BF16), jnp.sum(weights, axis=-1, keepdims=True)
 
 
 def attend(unit, bias, head_dim, channels, put):
     lane = lanes_of()
     blocks, quadrants, pair = unit
     pair = pair()
-    scores = scores_of(blocks, pair[:, :LANES], head_dim, channels)
-    count = scores.shape[0] // HEADS
+    part = jnp.concatenate(blocks, axis=0)
+    count = part.shape[0]
+    scores = dot_nt(by_head(part, head_dim, channels), pair[:, :LANES])
     yield
     part_bias = jnp.concatenate([bias[:, hy, hx] for hy, hx in quadrants], axis=1)
-    scores = scores.reshape(HEADS, count, WIN * WIN) + part_bias
-    scores = scores - jnp.max(scores, axis=-1, keepdims=True)
-    weights = jnp.exp2(scores).astype(BF16).reshape(HEADS * count, WIN * WIN)
+    weights, total = softmax(scores.reshape(HEADS, count, WIN * WIN), part_bias)
+    weights = weights.reshape(HEADS * count, WIN * WIN)
     yield
     mixed = dot(weights, pair[:, LANES:])
-    total = dot(weights, jnp.ones((WIN * WIN, HALF), BF16))
-    yield
-    result, low, high = mixed[0:count], total[0:count], total[0:count]
+    yield
+    result, divisor = mixed[0:count], jnp.broadcast_to(total[0], (count, LANES))
     for h in range(1, HEADS):
-        rows = slice(h * count, (h + 1) * count)
         mine = (lane >= h * head_dim) & (lane < (h + 1) * head_dim)
-        result = jnp.where(mine, mixed[rows], result)
-        if h * head_dim < HALF:
-            low = jnp.where(mine[:, :HALF], total[rows], low)
-        if (h + 1) * head_dim > HALF:
-            high = jnp.where(mine[:, HALF:], total[rows], high)
-    put((result / jnp.concatenate([low, high], axis=1)).astype(BF16))
+        result = jnp.where(mine, mixed[h * count : (h + 1) * count], result)
+        divisor = jnp.where(mine, total[h], divisor)
+    put((result / divisor).astype(BF16))
 
 
 def finish(heads_out, base, wp, gain2, w1, w2, channels, put):
@@ -170,11 +168,21 @@
     yield from make()
 
 
-def cut_kernel(image_hbm, image_ref, top, bottom, left, right, sem):
+def cut_kernel(
+    image_hbm, gain1_hbm, table_hbm, qkv_hbm, image_ref, gain1_ref, table_ref, qkv_ref,
+    top, bottom, left, right, sems,
+):
     rows, cols, _ = image_ref.shape
-    fetch = pltpu.make_async_copy(image_hbm, image_ref, sem)
-    fetch.start()
-    fetch.wait()
+    fetches = [
+        pltpu.make_async_copy(source, target, sems.at[i])
+        for i, (source, target) in enumerate(
+            ((image_hbm, image_ref), (gain1_hbm, gain1_ref), (table_hbm, table_ref), (qkv_hbm, qkv_ref))
+        )
+    ]
+    for fetch in fetches:
+        fetch.start()
+    for fetch in fetches:
+        fetch.wait()
     top[...] = image_ref[:SHIFT]
     bottom[...] = image_ref[rows - SHIFT :]
     for r in range(0, rows, SIDE):
@@ -184,10 +192,10 @@
 
 
 def own_kernel(
-    image_ref, gain1_hbm, gain2_hbm, qkv_hbm, proj_hbm, table_hbm, conv_hbm, fc1_hbm, fc2_hbm,
-    bias, query, kv, base, wkv, wp, wc, w1, w2, g2,
+    image_ref, gain1_ref, table_ref, qkv_ref, gain2_hbm, proj_hbm, conv_hbm, fc1_hbm, fc2_hbm,
+    bias, query, kv, base, own_x, wkv, wp, wc, w1, w2, g2,
     padded, strip, wq, normed, shifted,
-    table_ref, gain1_ref, gain2_ref, qkv_ref, proj_ref, conv_ref, fc1_ref, fc2_ref, sems,
+    gain2_ref, proj_ref, conv_ref, fc1_ref, fc2_ref, sems,
 ):
     rows, cols, channels = image_ref.shape
     head_dim = channels // HEADS
@@ -196,8 +204,8 @@
     fetches = [
         pltpu.make_async_copy(source, target, sems.at[i])
         for i, (source, target) in enumerate(
-            ((gain1_hbm, gain1_ref), (qkv_hbm, qkv_ref), (table_hbm, table_ref), (proj_hbm, proj_ref),
-             (conv_hbm, conv_ref), (gain2_hbm, gain2_ref), (fc1_hbm, fc1_ref), (fc2_hbm, fc2_ref))
+            ((conv_hbm, conv_ref), (proj_hbm, proj_ref), (gain2_hbm, gain2_ref), (fc1_hbm, fc1_ref),
+             (fc2_hbm, fc2_ref))
         )
     ]
     for fetch in fetches:
@@ -216,22 +224,23 @@
         marks(channels, 0.0)[None], (rows, cols, HALF)
     )
 
-    fetches[0].wait()
     gain1 = gain1_ref[...]
     scale = head_dim**-0.5 * LOG2E
 
+    wq[0:channels, 0:channels] = qkv_ref[:, 0:channels]
+    wkv[0:channels, 0:channels] = qkv_ref[:, channels : 2 * channels]
+    wkv[0:channels, LANES : LANES + channels] = qkv_ref[:, 2 * channels :]
+
     def weights():
-        for fetch in fetches[1:]:
+        for fetch in fetches:
             fetch.wait()
-        wq[0:channels, 0:channels] = qkv_ref[:, 0:channels]
-        wkv[0:channels, 0:channels] = qkv_ref[:, channels : 2 * channels]
-        wkv[0:channels, LANES : LANES + channels] = qkv_ref[:, 2 * channels :]
         wp[0:channels, 0:channels] = proj_ref[...]
         w1[0:channels, 0 : fc1_ref.shape[1]] = fc1_ref[...]
         w2[0 : fc2_ref.shape[1], 0:channels] = fc2_ref[...].astype(F32).T.astype(BF16)
         g2[:, 0:channels] = gain2_ref[...]
         for tap in range(9):
             wc[tap * LANES : tap * LANES + channels, 0:channels] = conv_ref[tap // 3, tap % 3]
+        yield
 
     def norm(br):
         r = br * SIDE
@@ -273,18 +282,19 @@
 
     for br in range(blocks_r):
         norm(br)
-    weights()
-    tasks = [expand_bias(table_ref, padded, strip, bias)]
-    for br in range(blocks_r):
-        tasks += [project(br), convolve(br)]
+    for i, (br, bc) in enumerate(((0, 0), (0, 3), (3, 0), (3, 3))):
+        at = (slice(1 + br * SIDE, 1 + (br + 1) * SIDE), slice(SHIFT + bc * SIDE, SHIFT + (bc + 1) * SIDE))
+        own_x[i] = normed[at].reshape(AREA, LANES).astype(BF16)
+    tasks = [expand_bias(table_ref, padded, strip, bias), *[project(br) for br in range(blocks_r)]]
+    tasks += [weights(), *[convolve(br) for br in range(blocks_r)]]
     weave(tasks, 3)
 
 
 def edge_kernel(
     top_ref, bottom_ref, left_ref, right_ref, gain1_ref,
-    bias, query, kv, base, wkv, wp, wc, w1, w2, g2,
-    kv_edge, corner_base, out_edge, out_mid,
-    bands_r, bands_c, fixes,
+    bias, query, kv, base, own_x, wkv, wp, wc, w1, w2, g2,
+    corner_base, corner_x, corner_q, folded, out_edge, out_mid,
+    bands_r, bands_c, fixes, kv_edge,
 ):
     cols, channels = top_ref.shape[1:]
     rows = left_ref.shape[0]
@@ -374,8 +384,21 @@
         yield
 
     def corners():
+        tops = [bands_r[i, :, SHIFT + c : SHIFT + c + SIDE] for i in range(2) for c in (0, cols - SIDE)]
+        lefts = [bands_c[i, 1 + r : 1 + r + SIDE] for r in (0, rows - SIDE) for i in range(2)]
         for i, at in enumerate(((0, 0), (0, 3), (3, 0), (3, 3))):
             corner_base[i] = corrected(base, fixes, at)
+            slots = ((1, 2, 3), (3, 0, 1), (0, 3, 2), (2, 1, 0))[i]
+            corner_x[i, slots[0]] = lefts[i].reshape(AREA, LANES).astype(BF16)
+            corner_x[i, slots[1]] = tops[i].reshape(AREA, LANES).astype(BF16)
+            corner_x[i, slots[2]] = own_x[i]
+            yield
+            corner_q[i] = dot_nt(by_head(query[at], head_dim, channels), wkv[:, :LANES]).astype(BF16)
+            yield
+        lane = lanes_of()
+        for h in range(HEADS):
+            mine = one_hot((lane >= h * head_dim) & (lane < (h + 1) * head_dim))
+            folded[h * LANES : (h + 1) * LANES] = dot(wkv[:, LANES:] * mine, wp[...]).astype(BF16)
             yield
 
     weave(
@@ -401,7 +424,7 @@
 
 def corner_kernel(
     left_ref, right_ref, gain1_ref,
-    bias, query, kv, wkv, wp, wc, w1, w2, g2, kv_edge, corner_base, out_mid, out_edge,
+    bias, corner_x, corner_q, folded, wc, w1, w2, g2, corner_base, out_mid, out_edge,
     out_hbm,
     normed, out_ref, sems,
 ):
@@ -434,35 +457,29 @@
     out_col = [(col == 0).astype(F32), (col == last_col).astype(F32)]
     corner, done = {}, {}
 
-    def project(pair):
-        for i in (2 * pair, 2 * pair + 1):
-            ref = (left_ref, right_ref)[i % 2]
-            inside = (1.0 - out_row[i // 2]) * (1.0 - out_col[i % 2])
-            mark = marks(channels, out_row[i // 2] + out_col[i % 2])
-            normed[i, :, HALF:] = jnp.broadcast_to(mark, (AREA, HALF))
-            values = ref[i // 2 * SIDE : (i // 2 + 1) * SIDE].astype(F32)
-            normed[i, :, 0:channels] = layer_norm(values.reshape(AREA, channels), gain1 * inside)
-        yield
-        both = dot(normed[2 * pair : 2 * pair + 2].reshape(-1, LANES).astype(BF16), wkv[...])
-        yield
-        both = both.astype(BF16)
-        corner[2 * pair], corner[2 * pair + 1] = both[:AREA], both[AREA:]
-
-    keys = [
-        lambda: [corner[0], kv_edge[2, 0], kv_edge[0, 0], kv[0, 0]],
-        lambda: [kv_edge[0, 3], kv[0, 3], corner[1], kv_edge[3, 0]],
-        lambda: [kv_edge[2, 3], corner[2], kv[3, 0], kv_edge[1, 0]],
-        lambda: [kv[3, 3], kv_edge[1, 3], kv_edge[3, 3], corner[3]],
-    ]
-    places = [(0, 0), (0, 3), (3, 0), (3, 3)]
-    quadrants = [(1, 1), (1, 0), (0, 1), (0, 0)]
+    def norm(i):
+        ref = (left_ref, right_ref)[i % 2]
+        inside = (1.0 - out_row[i // 2]) * (1.0 - out_col[i % 2])
+        mark = marks(channels, out_row[i // 2] + out_col[i % 2])
+        normed[i, :, HALF:] = jnp.broadcast_to(mark, (AREA, HALF))
+        values = ref[i // 2 * SIDE : (i // 2 + 1) * SIDE].astype(F32)
+        normed[i, :, 0:channels] = layer_norm(values.reshape(AREA, channels), gain1 * inside)
+        corner[i] = normed[i].astype(BF16)
 
     def unit(i):
-        def put(result):
-            done[i] = result
-
-        parts = ([query[places[i]]], [quadrants[i]], lambda: jnp.concatenate(keys[i](), axis=0))
-        return after(lambda: i in corner, lambda: attend(parts, bias, head_dim, channels, put))
+        norm(i)
+        yield
+        slot = (0, 2, 1, 3)[i]
+        blocks = [corner[i] if b == slot else corner_x[i, b] for b in range(4)]
+        pixels = jnp.concatenate(blocks, axis=0)
+        scores = dot_nt(corner_q[i], pixels).reshape(HEADS, AREA, WIN * WIN)
+        yield
+        weights, total = softmax(scores, bias[:, 1 - i // 2, 1 - i % 2])
+        yield
+        mixed = dot(weights.reshape(HEADS * AREA, WIN * WIN), pixels).reshape(HEADS, AREA, LANES)
+        yield
+        mixed = (mixed / total).astype(BF16)
+        done[i] = jnp.concatenate([mixed[h] for h in range(HEADS)], axis=1)
 
     def whole(i):
         tap, y, x = ((0, 7, 7), (2, 7, 0), (6, 0, 7), (8, 0, 0))[i]
@@ -481,12 +498,12 @@
             return finish(
                 jnp.concatenate([done[i], done[i + 1]], axis=0),
                 lambda: jnp.concatenate([whole(i), whole(i + 1)], axis=0),
-                wp, g2[...], w1, w2, channels, put,
+                folded, g2[...], w1, w2, channels, put,
             )
 
         return after(lambda: i in done and i + 1 in done, make)
 
-    weave([project(0), project(1), unit(0), unit(1), unit(2), unit(3), tail(0), tail(2)], 4)
+    weave([unit(0), unit(1), unit(2), unit(3), tail(0), tail(2)], 4)
     writes[0].wait()
     for r in (0, rows - SIDE):
         at = slice(r, r + SIDE)
@@ -527,20 +544,21 @@
     blocks_r, blocks_c = rows // SIDE, cols // SIDE
     gain1, gain2, fc2, table = norm1_gain[None], norm2_gain[None], fc2_weight.T, rel_table.T
     band, column = ((SHIFT, cols, channels), BF16), ((rows, SHIFT, channels), BF16)
-    tile, first_rows, last_rows, first_cols, last_cols = call(
+    tile, gain1, table, qkv_weight, first_rows, last_rows, first_cols, last_cols = call(
         cut_kernel,
         "cut_halo",
-        [(image.shape, BF16), band, band, column, column],
-        [pltpu.SemaphoreType.DMA(())],
+        [(image.shape, BF16), (gain1.shape, F32), (table.shape, F32), (qkv_weight.shape, BF16),
+         band, band, column, column],
+        [pltpu.SemaphoreType.DMA((4,))],
         1_000_000,
-        (image,),
-        (0,),
+        (image, gain1, table, qkv_weight),
+        range(4),
     )
     top, bottom = exchange(first_rows, last_rows, "row")
     left, right = exchange(first_cols, last_cols, "col")
-    fetched = (table, gain1, gain2, qkv_weight, proj_weight, conv_weight, fc1_weight, fc2)
+    fetched = (gain2, proj_weight, conv_weight, fc1_weight, fc2)
     hidden = -(-fc1_weight.shape[1] // 128) * 128
-    bias, query, kv, base, wkv, wp, wc, w1, w2, g2 = call(
+    bias, query, kv, base, own_x, wkv, wp, wc, w1, w2, g2 = call(
         own_kernel,
         "own_tile",
         [
@@ -548,6 +566,7 @@
             ((blocks_r, blocks_c, AREA, LANES), BF16),
             ((blocks_r, blocks_c, AREA, 2 * LANES), BF16),
             ((blocks_r, blocks_c, AREA, LANES), F32),
+            ((4, AREA, LANES), BF16),
             ((LANES, 2 * LANES), BF16),
             ((LANES, LANES), BF16),
             ((9 * LANES, LANES), BF16),
@@ -565,18 +584,20 @@
             pltpu.SemaphoreType.DMA((len(fetched),)),
         ],
         2_000_000_000,
-        (tile, gain1, gain2, qkv_weight, proj_weight, table, conv_weight, fc1_weight, fc2),
-        range(1, 9),
+        (tile, gain1, table, qkv_weight, gain2, proj_weight, conv_weight, fc1_weight, fc2),
+        range(4, 9),
     )
     first = jnp.concatenate([top[:, :SHIFT], bottom[:, :SHIFT]])
     last = jnp.concatenate([top[:, cols - SHIFT :], bottom[:, cols - SHIFT :]])
     left_corner, right_corner = exchange(first, last, "col")
-    kv_edge, corner_base, out_edge, out_mid = call(
+    corner_base, corner_x, corner_q, folded, out_edge, out_mid = call(
         edge_kernel,
         "edge_windows",
         [
-            ((4, blocks_c, AREA, 2 * LANES), BF16),
             ((4, AREA, LANES), F32),
+            ((4, 4, AREA, LANES), BF16),
+            ((4, HEADS * AREA, LANES), BF16),
+            ((HEADS * LANES, LANES), BF16),
             ((2, 4 * AREA, LANES), F32),
             ((4 * AREA, LANES), F32),
         ],
@@ -584,9 +605,10 @@
             ((2, SHIFT, cols + 2 * SHIFT, LANES), F32),
             ((2, rows + 2, SHIFT, LANES), F32),
             ((4, cols, LANES), F32),
+            ((4, blocks_c, AREA, 2 * LANES), BF16),
         ],
         2_000_000_000,
-        (top, bottom, left, right, gain1, bias, query, kv, base, wkv, wp, wc, w1, w2, g2),
+        (top, bottom, left, right, gain1, bias, query, kv, base, own_x, wkv, wp, wc, w1, w2, g2),
     )
     (out,) = call(
         corner_kernel,
@@ -594,8 +616,8 @@
         [jax.ShapeDtypeStruct(image.shape, BF16)],
         [((4, AREA, LANES), F32), (image.shape, BF16), pltpu.SemaphoreType.DMA((3,))],
         1_000_000_000,
-        (left_corner, right_corner, gain1, bias, query, kv, wkv, wp, wc, w1, w2, g2,
-         kv_edge, corner_base, out_mid, out_edge),
+        (left_corner, right_corner, gain1, bias, corner_x, corner_q, folded, wc, w1, w2, g2,
+         corner_base, out_mid, out_edge),
     )
     return out
 

time: 22.9 us -> 22.9 us (level)
  Pallas kernels: 12.8 us -> 13.8 us
  starting transfers between devices: 8.88 us -> 8.28 us
  waiting for transfers between devices: 0.83 us -> 0.54 us
    pallas_call x4, Pallas kernels: 12.8 us -> 13.8 us  [call(): pl.pallas_call(kernel, out_shape=[out if isinstance(out, jax.ShapeDtypeSt...]
    ppermute x3, starting transfers between devices: 5.83 us -> 5.23 us  [exchange(): lax.ppermute(low, axis, [((i + 1) % count, i) for i in range(count)])]
    ppermute x3, waiting for transfers between devices: 0.82 us -> 0.53 us  [exchange(): lax.ppermute(high, axis, [(i, (i + 1) % count) for i in range(count)])]
  transfers between devices with their start and end apart: 6 -> 6, of which waited for: 1 -> 1; matrix products, arithmetic and copies ran while one was open for 0% -> 0% of each run, Pallas kernels for 37% -> 41%
where the time goes in v14:
time: 22.9 us; the launch traced here: 22.8 us
  Pallas kernels  13.8 us (60%)
  starting transfers between devices  8.28 us (36%)
  waiting for transfers between devices  0.54 us (2%)
    pallas_call x4, Pallas kernels, call(): pl.pallas_call(kernel, out_shape=[out if isinstance(out, jax.ShapeDtypeSt...  13.8 us
    ppermute x3, starting transfers between devices, exchange(): lax.ppermute(low, axis, [((i + 1) % count, i) for i in range(count)])  5.23 us
    ppermute x3, starting transfers between devices, exchange(): lax.ppermute(high, axis, [(i, (i + 1) % count) for i in range(count)])  3.05 us
    ppermute x3, waiting for transfers between devices, exchange(): lax.ppermute(high, axis, [(i, (i + 1) % count) for i in range(count)])  0.53 us
  transfers between devices with their start and end apart: 6, of which 1 were waited for; matrix products, arithmetic and copies ran while one was open for 0% of the time, Pallas kernels for 41%

profile of v14, /device:TPU:0, one launch (start us, length us, event | category | flops | bytes accessed | tf_op | source)
XLA Modules:
  0.0 22.8 jit_solution(14625877932221111332)
XLA Ops:
  0.0 1.2 %cut_halo.1 = (bf16[32,32,180]{2,1,0:T(8,128)(2,1)S(1)}, f32[1,180]{1,0:T(1,128)S(1)}, f32[6,961]{1,0:T(8,128)S(1)}, bf16[180,540]{1,0:T(8,128)(2,1)S(1)}, bf16[...) custom-call(bf16[32,32,180]{2,1,0:T(8,128)(2,1)} %image_hbm.1, ...), custom_call_target="tpu_custom_call" | custom-call | flops 1000000 | bytes 4000000 | tf_op jit(solution)/shard_map/cut_halo/pallas_call | solution.py:527
  1.2 3.0 %collective-permute-start = (bf16[8,32,180]{2,1,0:T(8,128)(2,1)S(1)}, bf16[8,32,180]{2,1,0:T(8,128)(2,1)S(1)}, u32[]{:S(2)}, u32[]{:S(2)}) collective-permute-start(bf16[8,32,180]{2,1,0:T(8,128)(2,1)S(1)} %get-tuple-element.30), channel_id=1, source_target_pairs={{0,8},{8,16},{16,24},{24,0},{1,9},{9,17},{17,25},{25,1},{2,10},{10... | collective-permute-start | bytes 276488 | tf_op jit(solution)/shard_map/ppermute | solution.py:519
  4.2 1.0 %collective-permute-start.1 = (bf16[8,32,180]{2,1,0:T(8,128)(2,1)S(1)}, bf16[8,32,180]{2,1,0:T(8,128)(2,1)S(1)}, u32[]{:S(2)}, u32[]{:S(2)}) collective-permute-start(bf16[8,32,180]{2,1,0:T(8,128)(2,1)S(1)} %get-tuple-element.31), channel_id=1, source_target_pairs={{8,0},{16,8},{24,16},{0,24},{9,1},{17,9},{25,17},{1,25},{10,2},{18... | collective-permute-start | bytes 276488 | tf_op jit(solution)/shard_map/ppermute | solution.py:520
  5.2 0.0 collective-permute-start.4
  5.2 3.5 %collective-permute-start.5 = (bf16[32,8,180]{2,1,0:T(8,128)(2,1)S(1)}, bf16[32,8,180]{2,1,0:T(8,128)(2,1)S(1)}, u32[]{:S(2)}, u32[]{:S(2)}) collective-permute-start(bf16[32,8,180]{2,1,0:T(8,128)(2,1)S(1)} %get-tuple-element.38), channel_id=1, source_target_pairs={{1,0},{2,1},{3,2},{4,3},{5,4},{6,5},{7,6},{0,7},{9,8},{10,9},{11,1... | collective-permute-start | bytes 276488 | tf_op jit(solution)/shard_map/ppermute | solution.py:520
  8.8 4.4 %own_tile.1 = (f32[6,2,2,64,256]{4,3,2,1,0:T(8,128)S(1)}, bf16[4,4,64,256]{3,2,1,0:T(8,128)(2,1)S(1)}, bf16[4,4,64,512]{3,2,1,0:T(8,128)(2,1)S(1)}, f32[4,4,64,2...) custom-call(bf16[32,32,180]{2,1,0:T(8,128)(2,1)S(1)} %get-tuple-elem, ...), custom_call_target="tpu_custom_call" | custom-call | flops 2000000000 | bytes 4000000 | tf_op jit(solution)/shard_map/own_tile/pallas_call | solution.py:527
  13.2 0.0 collective-permute-done.top_ref
  13.2 0.0 collective-permute-done.1.bottom_ref
  13.3 0.7 %collective-permute-start.3 = (bf16[16,8,180]{2,1,0:T(8,128)(2,1)S(1)}, bf16[16,8,180]{2,1,0:T(8,128)(2,1)S(1)}, u32[]{:S(2)}, u32[]{:S(2)}) collective-permute-start(bf16[16,8,180]{2,1,0:T(8,128)(2,1)S(1)} %pad_maximum_fusion.1), channel_id=1, source_target_pairs={{1,0},{2,1},{3,2},{4,3},{5,4},{6,5},{7,6},{0,7},{9,8},{10,9},{11,1... | collective-permute-start | bytes 138248 | tf_op jit(solution)/shard_map/ppermute | solution.py:520
  14.0 0.1 collective-permute-start.2
  14.0 0.0 collective-permute-done.4.left_ref
  14.1 0.0 collective-permute-done.5.right_ref
  14.1 4.9 %edge_windows.1 = (f32[4,64,256]{2,1,0:T(8,128)S(1)}, bf16[4,4,64,256]{3,2,1,0:T(8,128)(2,1)S(1)}, bf16[4,384,256]{2,1,0:T(8,128)(2,1)S(1)}, bf16[1536,256]{1,0:...) custom-call(bf16[8,32,180]{2,1,0:T(8,128)(2,1)S(1)} %collective-permute-done.top_ref, ...), custom_call_target="tpu_custom_call" | custom-call | flops 2000000000 | bytes 4000000 | tf_op jit(solution)/shard_map/edge_windows/pallas_call | solution.py:527
  19.0 0.0 collective-permute-done.3.right_ref
  19.0 0.5 %collective-permute-done.2.left_ref = bf16[16,8,180]{2,1,0:T(8,128)(2,1)S(1)} collective-permute-done((bf16[16,8,180]{2,1,0:T(8,128)(2,1)S(1)}, bf16[16,8,180]{2,1,0:T(8,128)(2,1)S(1)}, u32[]{:S(2)}, u32[]{:S(2)}) %collective-permute-start.2) | collective-permute-done | bytes 46112 | tf_op jit(solution)/shard_map/ppermute | solution.py:519
  19.5 3.3 %corner_windows.1 = bf16[32,32,180]{2,1,0:T(8,128)(2,1)} custom-call(bf16[16,8,180]{2,1,0:T(8,128)(2,1)S(1)} %collective-permute-done.2.left_ref, bf16[16,8,180]{2,1,0:T(8,128)(2,1)S(1)} %collective-permute-done.3.right_ref, f32[1,180]{1,0:T(1,128)S(1)} %get-tuple-element.32.gain1_ref, f32[6,2,2,64,256]{4,3,2,1,0:T(8,128)S(1)} %get-tuple-element.36.bias, ...), custom_call_target="tpu_custom_call" | custom-call | flops 1000000000 | bytes 4000000 | tf_op jit(solution)/shard_map/corner_windows/pallas_call | solution.py:527
  (4 shorter events, 0.0 us)
Async XLA Ops:
  1.2 12.0 %collective-permute-start = (bf16[8,32,180]{2,1,0:T(8,128)(2,1)S(1)}, bf16[8,32,180]{2,1,0:T(8,128)(2,1)S(1)}, u32[]{:S(2)}, u32[]{:S(2)}) collective-permute-start(bf16[8,32,180]{2,1,0:T(8,128)(2,1)S(1)} %get-tuple-element.30), channel_id=1, source_target_pairs={{0,8},{8,16},{16,24},{24,0},{1,9},{9,17},{17,25},{25,1},{2,10},{10... | collective-permute-start | bytes 276488 | tf_op jit(solution)/shard_map/ppermute | solution.py:519
  4.2 9.0 %collective-permute-start.1 = (bf16[8,32,180]{2,1,0:T(8,128)(2,1)S(1)}, bf16[8,32,180]{2,1,0:T(8,128)(2,1)S(1)}, u32[]{:S(2)}, u32[]{:S(2)}) collective-permute-start(bf16[8,32,180]{2,1,0:T(8,128)(2,1)S(1)} %get-tuple-element.31), channel_id=1, source_target_pairs={{8,0},{16,8},{24,16},{0,24},{9,1},{17,9},{25,17},{1,25},{10,2},{18... | collective-permute-start | bytes 276488 | tf_op jit(solution)/shard_map/ppermute | solution.py:520
  5.2 8.8 %collective-permute-start.4 = (bf16[32,8,180]{2,1,0:T(8,128)(2,1)S(1)}, bf16[32,8,180]{2,1,0:T(8,128)(2,1)S(1)}, u32[]{:S(2)}, u32[]{:S(2)}) collective-permute-start(bf16[32,8,180]{2,1,0:T(8,128)(2,1)S(1)} %get-tuple-element.37), channel_id=1, source_target_pairs={{0,1},{1,2},{2,3},{3,4},{4,5},{5,6},{6,7},{7,0},{8,9},{9,10},{10,1... | collective-permute-start | bytes 276488 | tf_op jit(solution)/shard_map/ppermute | solution.py:519
  5.2 8.8 %collective-permute-start.5 = (bf16[32,8,180]{2,1,0:T(8,128)(2,1)S(1)}, bf16[32,8,180]{2,1,0:T(8,128)(2,1)S(1)}, u32[]{:S(2)}, u32[]{:S(2)}) collective-permute-start(bf16[32,8,180]{2,1,0:T(8,128)(2,1)S(1)} %get-tuple-element.38), channel_id=1, source_target_pairs={{1,0},{2,1},{3,2},{4,3},{5,4},{6,5},{7,6},{0,7},{9,8},{10,9},{11,1... | collective-permute-start | bytes 276488 | tf_op jit(solution)/shard_map/ppermute | solution.py:520
  13.3 5.7 %collective-permute-start.3 = (bf16[16,8,180]{2,1,0:T(8,128)(2,1)S(1)}, bf16[16,8,180]{2,1,0:T(8,128)(2,1)S(1)}, u32[]{:S(2)}, u32[]{:S(2)}) collective-permute-start(bf16[16,8,180]{2,1,0:T(8,128)(2,1)S(1)} %pad_maximum_fusion.1), channel_id=1, source_target_pairs={{1,0},{2,1},{3,2},{4,3},{5,4},{6,5},{7,6},{0,7},{9,8},{10,9},{11,1... | collective-permute-start | bytes 138248 | tf_op jit(solution)/shard_map/ppermute | solution.py:520
  14.0 5.5 %collective-permute-start.2 = (bf16[16,8,180]{2,1,0:T(8,128)(2,1)S(1)}, bf16[16,8,180]{2,1,0:T(8,128)(2,1)S(1)}, u32[]{:S(2)}, u32[]{:S(2)}) collective-permute-start(bf16[16,8,180]{2,1,0:T(8,128)(2,1)S(1)} %pad_maximum_fusion), channel_id=1, source_target_pairs={{0,1},{1,2},{2,3},{3,4},{4,5},{5,6},{6,7},{7,0},{8,9},{9,10},{10,1... | collective-permute-start | bytes 138248 | tf_op jit(solution)/shard_map/ppermute | solution.py:519

commit v15 on v12

--- a/solution.py
+++ b/solution.py
@@ -167,13 +167,39 @@
     yield from make()
 
 
-def cut_kernel(image_hbm, image_ref, top, bottom, left, right, sem):
+def pack(pixels, spare):
+    rows, cols, channels = pixels.shape
+    spare[...] = jnp.zeros_like(spare)
+    spare[:, :, 0:channels] = pixels
+    rest = spare[:, :, HALF:]
+    second = pltpu.roll(rest[:, cols // 2 :].reshape(-1, HALF), HALF // 2, 1)
+    both = rest[:, : cols // 2] + second.reshape(rows, cols // 2, HALF)
+    return jnp.concatenate([spare[:, :, :HALF], both], axis=1).astype(BF16)
+
+
+def unpack(main, rest, turned, channels):
+    if turned:
+        rest = pltpu.roll(rest.reshape(-1, HALF), HALF // 2, 1).reshape(rest.shape)
+    return jnp.concatenate([main, rest], axis=2)[:, :, :channels]
+
+
+def cut_kernel(
+    image_hbm, gain1_hbm, table_hbm, qkv_hbm, image_ref, gain1_ref, table_ref, qkv_ref,
+    top, bottom, left, right, spare, sems,
+):
     rows, cols, _ = image_ref.shape
-    fetch = pltpu.make_async_copy(image_hbm, image_ref, sem)
-    fetch.start()
-    fetch.wait()
-    top[...] = image_ref[:SHIFT]
-    bottom[...] = image_ref[rows - SHIFT :]
+    fetches = [
+        pltpu.make_async_copy(source, target, sems.at[i])
+        for i, (source, target) in enumerate(
+            ((image_hbm, image_ref), (gain1_hbm, gain1_ref), (table_hbm, table_ref), (qkv_hbm, qkv_ref))
+        )
+    ]
+    for fetch in fetches:
+        fetch.start()
+    for fetch in fetches:
+        fetch.wait()
+    top[...] = pack(image_ref[:SHIFT].astype(F32), spare.at[0])
+    bottom[...] = pack(image_ref[rows - SHIFT :].astype(F32), spare.at[1])
     for r in range(0, rows, SIDE):
         band = image_ref[r : r + SIDE].astype(F32)
         left[r : r + SIDE] = band[:, :SHIFT].astype(BF16)
@@ -181,10 +207,10 @@
 
 
 def own_kernel(
-    image_ref, gain1_hbm, gain2_hbm, qkv_hbm, proj_hbm, table_hbm, conv_hbm, fc1_hbm, fc2_hbm,
+    image_ref, gain1_ref, table_ref, qkv_ref, gain2_hbm, proj_hbm, conv_hbm, fc1_hbm, fc2_hbm,
     bias, query, kv, normed, wkv, wp, wc, w1, w2, g2,
     padded, strip, wq,
-    table_ref, gain1_ref, gain2_ref, qkv_ref, proj_ref, conv_ref, fc1_ref, fc2_ref, sems,
+    gain2_ref, proj_ref, conv_ref, fc1_ref, fc2_ref, sems,
 ):
     rows, cols, channels = image_ref.shape
     head_dim = channels // HEADS
@@ -193,8 +219,8 @@
     fetches = [
         pltpu.make_async_copy(source, target, sems.at[i])
         for i, (source, target) in enumerate(
-            ((gain1_hbm, gain1_ref), (qkv_hbm, qkv_ref), (table_hbm, table_ref), (proj_hbm, proj_ref),
-             (conv_hbm, conv_ref), (gain2_hbm, gain2_ref), (fc1_hbm, fc1_ref), (fc2_hbm, fc2_ref))
+            ((conv_hbm, conv_ref), (proj_hbm, proj_ref), (gain2_hbm, gain2_ref), (fc1_hbm, fc1_ref),
+             (fc2_hbm, fc2_ref))
         )
     ]
     for fetch in fetches:
@@ -210,16 +236,16 @@
     ).astype(BF16)
     normed[:, :, HALF:] = jnp.broadcast_to(marks(channels, 0.0)[None], (rows, cols, HALF))
 
-    fetches[0].wait()
     gain1 = gain1_ref[...]
     scale = head_dim**-0.5 * LOG2E
 
+    wq[0:channels, 0:channels] = qkv_ref[:, 0:channels]
+    wkv[0:channels, 0:channels] = qkv_ref[:, channels : 2 * channels]
+    wkv[0:channels, LANES : LANES + channels] = qkv_ref[:, 2 * channels :]
+
     def weights():
-        for fetch in fetches[1:]:
+        for fetch in fetches:
             fetch.wait()
-        wq[0:channels, 0:channels] = qkv_ref[:, 0:channels]
-        wkv[0:channels, 0:channels] = qkv_ref[:, channels : 2 * channels]
-        wkv[0:channels, LANES : LANES + channels] = qkv_ref[:, 2 * channels :]
         wp[0:channels, 0:channels] = proj_ref[...]
         w1[0:channels, 0 : fc1_ref.shape[1]] = fc1_ref[...]
         w2[0 : fc2_ref.shape[1], 0:channels] = fc2_ref[...].astype(F32).T.astype(BF16)
@@ -247,11 +273,8 @@
 
     for br in range(blocks_r):
         norm(br)
+    weave([expand_bias(table_ref, padded, strip, bias), *[project(br) for br in range(blocks_r)]], 3)
     weights()
-    tasks = [expand_bias(table_ref, padded, strip, bias)]
-    for br in range(blocks_r):
-        tasks.append(project(br))
-    weave(tasks, 3)
 
 
 def edge_kernel(
@@ -260,8 +283,7 @@
     kv_edge, corner_base, out_edge, out_mid,
     halo, base, shifted,
 ):
-    cols, channels = top_ref.shape[1:]
-    rows = left_ref.shape[0]
+    rows, cols, channels = image_ref.shape
     head_dim = channels // HEADS
     row, last_row = lax.axis_index("row"), lax.axis_size("row") - 1
     col, last_col = lax.axis_index("col"), lax.axis_size("col") - 1
@@ -280,9 +302,16 @@
         inner = slice(SHIFT, SHIFT + (cols if i < 2 else rows))
         outer = slice(start, start + SHIFT)
         place = (outer, inner) if i < 2 else (inner, outer)
-        mark = jnp.broadcast_to(marks(channels, outside[i])[None], (*ref.shape[:2], HALF))
+        values = ref[...].astype(F32)
+        if i < 2:
+            rest, half = values[:, cols:], cols // 2
+            values = jnp.concatenate(
+                [unpack(values[:, :half], rest, False, channels),
+                 unpack(values[:, half:cols], rest, True, channels)], axis=1
+            )
+        mark = jnp.broadcast_to(marks(channels, outside[i])[None], (*values.shape[:2], HALF))
         halo[(*place, slice(HALF, LANES))] = mark
-        halo[(*place, slice(0, channels))] = layer_norm(ref[...].astype(F32), gain1 * (1.0 - outside[i]))
+        halo[(*place, slice(0, channels))] = layer_norm(values, gain1 * (1.0 - outside[i]))
         pixels = halo[place]
         if i < 2:
             blocks = [pixels[:, b * SIDE : (b + 1) * SIDE].reshape(AREA, LANES) for b in range(cols // SIDE)]
@@ -413,6 +442,7 @@
             mark = marks(channels, out_row[i // 2] + out_col[i % 2])
             normed[i, :, HALF:] = jnp.broadcast_to(mark, (AREA, HALF))
             values = ref[i // 2 * SIDE : (i // 2 + 1) * SIDE].astype(F32)
+            values = unpack(values[:, :SIDE], values[:, SIDE:], i % 2 == 0, channels)
             normed[i, :, 0:channels] = layer_norm(values.reshape(AREA, channels), gain1 * inside)
         yield
         both = dot(normed[2 * pair : 2 * pair + 2].reshape(-1, LANES).astype(BF16), wkv[...])
@@ -498,19 +528,20 @@
     rows, cols, channels = image.shape
     blocks_r, blocks_c = rows // SIDE, cols // SIDE
     gain1, gain2, fc2, table = norm1_gain[None], norm2_gain[None], fc2_weight.T, rel_table.T
-    band, column = ((SHIFT, cols, channels), BF16), ((rows, SHIFT, channels), BF16)
-    tile, first_rows, last_rows, first_cols, last_cols = call(
+    band, column = ((SHIFT, cols * 3 // 2, HALF), BF16), ((rows, SHIFT, channels), BF16)
+    tile, gain1, table, qkv_weight, first_rows, last_rows, first_cols, last_cols = call(
         cut_kernel,
         "cut_halo",
-        [(image.shape, BF16), band, band, column, column],
-        [pltpu.SemaphoreType.DMA(())],
+        [(image.shape, BF16), (gain1.shape, F32), (table.shape, F32), (qkv_weight.shape, BF16),
+         band, band, column, column],
+        [((2, SHIFT, cols, LANES), F32), pltpu.SemaphoreType.DMA((4,))],
         1_000_000,
-        (image,),
-        (0,),
+        (image, gain1, table, qkv_weight),
+        range(4),
     )
     top, bottom = exchange(first_rows, last_rows, "row")
     left, right = exchange(first_cols, last_cols, "col")
-    fetched = (table, gain1, gain2, qkv_weight, proj_weight, conv_weight, fc1_weight, fc2)
+    fetched = (gain2, proj_weight, conv_weight, fc1_weight, fc2)
     hidden = -(-fc1_weight.shape[1] // 128) * 128
     bias, query, kv, normed, wkv, wp, wc, w1, w2, g2 = call(
         own_kernel,
@@ -535,11 +566,16 @@
             pltpu.SemaphoreType.DMA((len(fetched),)),
         ],
         2_000_000_000,
-        (tile, gain1, gain2, qkv_weight, proj_weight, table, conv_weight, fc1_weight, fc2),
-        range(1, 9),
-    )
-    first = jnp.concatenate([top[:, :SHIFT], bottom[:, :SHIFT]])
-    last = jnp.concatenate([top[:, cols - SHIFT :], bottom[:, cols - SHIFT :]])
+        (tile, gain1, table, qkv_weight, gain2, proj_weight, conv_weight, fc1_weight, fc2),
+        range(4, 9),
+    )
+    def ends(start, rest):
+        parts = [(start, start + SHIFT), (cols + rest, cols + rest + SHIFT)]
+        return jnp.concatenate(
+            [jnp.concatenate([x[:, a:b] for a, b in parts], axis=1) for x in (top, bottom)]
+        )
+
+    first, last = ends(0, 0), ends(cols - SHIFT, cols // 2 - SHIFT)
     left_corner, right_corner = exchange(first, last, "col")
     kv_edge, corner_base, out_edge, out_mid = call(
         edge_kernel,

time: 22.9 us -> 22.3 us (0.974)
  starting transfers between devices: 9.5 us -> 8.26 us
  Pallas kernels: 13 us -> 13.7 us
    ppermute x3, starting transfers between devices: 6.45 us -> 5.2 us  [exchange(): lax.ppermute(low, axis, [((i + 1) % count, i) for i in range(count)])]
    pallas_call x4, Pallas kernels: 13 us -> 13.7 us  [call(): pl.pallas_call(kernel, out_shape=[out if isinstance(out, jax.ShapeDtypeSt...]
  transfers between devices with their start and end apart: 6 -> 6, of which waited for: 1 -> 0; matrix products, arithmetic and copies ran while one was open for 0% -> 0% of each run, Pallas kernels for 38% -> 40%
where the time goes in v15:
time: 22.3 us; the launch traced here: 22.2 us
  Pallas kernels  13.7 us (61%)
  starting transfers between devices  8.26 us (37%)
    pallas_call x4, Pallas kernels, call(): pl.pallas_call(kernel, out_shape=[out if isinstance(out, jax.ShapeDtypeSt...  13.7 us
    ppermute x3, starting transfers between devices, exchange(): lax.ppermute(low, axis, [((i + 1) % count, i) for i in range(count)])  5.2 us
    ppermute x3, starting transfers between devices, exchange(): lax.ppermute(high, axis, [(i, (i + 1) % count) for i in range(count)])  3.05 us
  transfers between devices with their start and end apart: 6, of which 0 were waited for; matrix products, arithmetic and copies ran while one was open for 0% of the time, Pallas kernels for 40%

profile of v15, /device:TPU:0, one launch (start us, length us, event | category | flops | bytes accessed | tf_op | source)
XLA Modules:
  0.0 22.2 jit_solution(9171034206744777308)
XLA Ops:
  0.0 1.3 %cut_halo.1 = (bf16[32,32,180]{2,1,0:T(8,128)(2,1)S(1)}, f32[1,180]{1,0:T(1,128)S(1)}, f32[6,961]{1,0:T(8,128)S(1)}, bf16[180,540]{1,0:T(8,128)(2,1)S(1)}, bf16[...) custom-call(bf16[32,32,180]{2,1,0:T(8,128)(2,1)} %image_hbm.1, ...), custom_call_target="tpu_custom_call" | custom-call | flops 1000000 | bytes 4000000 | tf_op jit(solution)/shard_map/cut_halo/pallas_call | solution.py:512
  1.3 3.0 %collective-permute-start = (bf16[8,48,128]{2,1,0:T(8,128)(2,1)S(1)}, bf16[8,48,128]{2,1,0:T(8,128)(2,1)S(1)}, u32[]{:S(2)}, u32[]{:S(2)}) collective-permute-start(bf16[8,48,128]{2,1,0:T(8,128)(2,1)S(1)} %get-tuple-element.27), channel_id=1, source_target_pairs={{0,8},{8,16},{16,24},{24,0},{1,9},{9,17},{17,25},{25,1},{2,10},{10... | collective-permute-start | bytes 294920 | tf_op jit(solution)/shard_map/ppermute | solution.py:504
  4.3 1.0 %collective-permute-start.1 = (bf16[8,48,128]{2,1,0:T(8,128)(2,1)S(1)}, bf16[8,48,128]{2,1,0:T(8,128)(2,1)S(1)}, u32[]{:S(2)}, u32[]{:S(2)}) collective-permute-start(bf16[8,48,128]{2,1,0:T(8,128)(2,1)S(1)} %get-tuple-element.28), channel_id=1, source_target_pairs={{8,0},{16,8},{24,16},{0,24},{9,1},{17,9},{25,17},{1,25},{10,2},{18... | collective-permute-start | bytes 294920 | tf_op jit(solution)/shard_map/ppermute | solution.py:505
  5.3 0.0 collective-permute-start.4
  5.3 3.5 %collective-permute-start.5 = (bf16[32,8,180]{2,1,0:T(8,128)(2,1)S(1)}, bf16[32,8,180]{2,1,0:T(8,128)(2,1)S(1)}, u32[]{:S(2)}, u32[]{:S(2)}) collective-permute-start(bf16[32,8,180]{2,1,0:T(8,128)(2,1)S(1)} %get-tuple-element.43), channel_id=1, source_target_pairs={{1,0},{2,1},{3,2},{4,3},{5,4},{6,5},{7,6},{0,7},{9,8},{10,9},{11,1... | collective-permute-start | bytes 276488 | tf_op jit(solution)/shard_map/ppermute | solution.py:505
  8.9 3.4 %own_tile.1 = (f32[6,2,2,64,256]{4,3,2,1,0:T(8,128)S(1)}, bf16[4,4,64,256]{3,2,1,0:T(8,128)(2,1)S(1)}, bf16[4,4,64,512]{3,2,1,0:T(8,128)(2,1)S(1)}, f32[32,32,25...) custom-call(bf16[32,32,180]{2,1,0:T(8,128)(2,1)S(1)} %get-tuple-elem, ...), custom_call_target="tpu_custom_call" | custom-call | flops 2000000000 | bytes 4000000 | tf_op jit(solution)/shard_map/own_tile/pallas_call | solution.py:512
  12.3 0.0 collective-permute-done.top_ref
  12.3 0.0 collective-permute-done.1.bottom_ref
  12.4 0.6 %collective-permute-start.3 = (bf16[16,16,128]{2,1,0:T(8,128)(2,1)S(1)}, bf16[16,16,128]{2,1,0:T(8,128)(2,1)S(1)}, u32[]{:S(2)}, u32[]{:S(2)}) collective-permute-start(bf16[16,16,128]{2,1,0:T(8,128)(2,1)S(1)} %maximum_maximum_fusion.1), channel_id=1, source_target_pairs={{1,0},{2,1},{3,2},{4,3},{5,4},{6,5},{7,6},{0,7},{9,8},{10,9},{11,1... | collective-permute-start | bytes 196616 | tf_op jit(solution)/shard_map/ppermute | solution.py:505
  13.1 0.1 collective-permute-start.2
  13.1 0.0 collective-permute-done.4.left_ref
  13.1 0.0 collective-permute-done.5.right_ref
  13.1 5.5 %edge_windows.1 = (bf16[4,4,64,512]{3,2,1,0:T(8,128)(2,1)S(1)}, f32[4,64,256]{2,1,0:T(8,128)S(1)}, f32[2,256,256]{2,1,0:T(8,128)S(1)}, f32[256,256]{1,0:T(8,128)S(1)}) custom-call(bf16[32,32,180]{2,1,0:T(8,128)(2,1)S(1)} %get-tuple-element.30.image_ref, bf16[8,48,128]{2,1,0:T(8,128)(2,1)S(1)} %collective-permute-done.top_ref, ...), custom_call_target="tpu_custom_call" | custom-call | flops 2000000000 | bytes 4000000 | tf_op jit(solution)/shard_map/edge_windows/pallas_call | solution.py:512
  18.7 0.0 collective-permute-done.3.right_ref
  18.7 0.0 collective-permute-done.2.left_ref
  18.7 3.5 %corner_windows.1 = bf16[32,32,180]{2,1,0:T(8,128)(2,1)} custom-call(bf16[16,16,128]{2,1,0:T(8,128)(2,1)S(1)} %collective-permute-done.2.left_ref, bf16[16,16,128]{2,1,0:T(8,128)(2,1)S(1)} %collective-permute-done.3.right_ref, f32[1,180]{1,0:T(1,128)S(1)} %get-tuple-element.29.gain1_ref, f32[6,2,2,64,256]{4,3,2,1,0:T(8,128)S(1)} %get-tuple-element.33.bias, ...), custom_call_target="tpu_custom_call" | custom-call | flops 1000000000 | bytes 4000000 | tf_op jit(solution)/shard_map/corner_windows/pallas_call | solution.py:512
  (4 shorter events, 0.1 us)
Async XLA Ops:
  1.3 11.0 %collective-permute-start = (bf16[8,48,128]{2,1,0:T(8,128)(2,1)S(1)}, bf16[8,48,128]{2,1,0:T(8,128)(2,1)S(1)}, u32[]{:S(2)}, u32[]{:S(2)}) collective-permute-start(bf16[8,48,128]{2,1,0:T(8,128)(2,1)S(1)} %get-tuple-element.27), channel_id=1, source_target_pairs={{0,8},{8,16},{16,24},{24,0},{1,9},{9,17},{17,25},{25,1},{2,10},{10... | collective-permute-start | bytes 294920 | tf_op jit(solution)/shard_map/ppermute | solution.py:504
  4.3 8.0 %collective-permute-start.1 = (bf16[8,48,128]{2,1,0:T(8,128)(2,1)S(1)}, bf16[8,48,128]{2,1,0:T(8,128)(2,1)S(1)}, u32[]{:S(2)}, u32[]{:S(2)}) collective-permute-start(bf16[8,48,128]{2,1,0:T(8,128)(2,1)S(1)} %get-tuple-element.28), channel_id=1, source_target_pairs={{8,0},{16,8},{24,16},{0,24},{9,1},{17,9},{25,17},{1,25},{10,2},{18... | collective-permute-start | bytes 294920 | tf_op jit(solution)/shard_map/ppermute | solution.py:505
  5.3 7.8 %collective-permute-start.4 = (bf16[32,8,180]{2,1,0:T(8,128)(2,1)S(1)}, bf16[32,8,180]{2,1,0:T(8,128)(2,1)S(1)}, u32[]{:S(2)}, u32[]{:S(2)}) collective-permute-start(bf16[32,8,180]{2,1,0:T(8,128)(2,1)S(1)} %get-tuple-element.42), channel_id=1, source_target_pairs={{0,1},{1,2},{2,3},{3,4},{4,5},{5,6},{6,7},{7,0},{8,9},{9,10},{10,1... | collective-permute-start | bytes 276488 | tf_op jit(solution)/shard_map/ppermute | solution.py:504
  5.3 7.8 %collective-permute-start.5 = (bf16[32,8,180]{2,1,0:T(8,128)(2,1)S(1)}, bf16[32,8,180]{2,1,0:T(8,128)(2,1)S(1)}, u32[]{:S(2)}, u32[]{:S(2)}) collective-permute-start(bf16[32,8,180]{2,1,0:T(8,128)(2,1)S(1)} %get-tuple-element.43), channel_id=1, source_target_pairs={{1,0},{2,1},{3,2},{4,3},{5,4},{6,5},{7,6},{0,7},{9,8},{10,9},{11,1... | collective-permute-start | bytes 276488 | tf_op jit(solution)/shard_map/ppermute | solution.py:505
  12.4 6.3 %collective-permute-start.3 = (bf16[16,16,128]{2,1,0:T(8,128)(2,1)S(1)}, bf16[16,16,128]{2,1,0:T(8,128)(2,1)S(1)}, u32[]{:S(2)}, u32[]{:S(2)}) collective-permute-start(bf16[16,16,128]{2,1,0:T(8,128)(2,1)S(1)} %maximum_maximum_fusion.1), channel_id=1, source_target_pairs={{1,0},{2,1},{3,2},{4,3},{5,4},{6,5},{7,6},{0,7},{9,8},{10,9},{11,1... | collective-permute-start | bytes 196616 | tf_op jit(solution)/shard_map/ppermute | solution.py:505
  13.1 5.6 %collective-permute-start.2 = (bf16[16,16,128]{2,1,0:T(8,128)(2,1)S(1)}, bf16[16,16,128]{2,1,0:T(8,128)(2,1)S(1)}, u32[]{:S(2)}, u32[]{:S(2)}) collective-permute-start(bf16[16,16,128]{2,1,0:T(8,128)(2,1)S(1)} %maximum_maximum_fusion), channel_id=1, source_target_pairs={{0,1},{1,2},{2,3},{3,4},{4,5},{5,6},{6,7},{7,0},{8,9},{9,10},{10,1... | collective-permute-start | bytes 196616 | tf_op jit(solution)/shard_map/ppermute | solution.py:504

commit v16 on v15

--- a/solution.py
+++ b/solution.py
@@ -18,6 +18,7 @@
 BF16 = jnp.bfloat16
 LOG2E = math.log2(math.e)
 MASKED = -4.0e9
+CORNERS = [(0, 0), (0, 3), (3, 0), (3, 3)]
 
 
 def weave(tasks, width):
@@ -105,13 +106,16 @@
             rows = jnp.concatenate(
                 [strip[2 * half + t, pl.ds(head, WIN, stride=8), :] for t in range(2)], axis=1
             )
-            for py in range(WIN):
+            for py in range(0, WIN, 2):
                 start = (WIN - 1 - py) * SIDE
-                rolled = (rows if start == 0 else pltpu.roll(rows, 256 - start, 1))[:, 0:128]
+                pair = [pltpu.roll(rows, 256 - start, 1)[:, 0:128]]
+                start -= SIDE
+                pair.append((rows if start == 0 else pltpu.roll(rows, 256 - start, 1))[:, 0:128])
                 lanes = slice(128 * half, 128 * (half + 1))
-                place = slice(py % SIDE * SIDE, (py % SIDE + 1) * SIDE)
-                bias[head, py // SIDE, 0, place, lanes] = rolled[:SIDE]
-                bias[head, py // SIDE, 1, place, lanes] = rolled[SIDE:]
+                place = slice(py % SIDE * SIDE, (py % SIDE + 2) * SIDE)
+                for hx in range(2):
+                    part = [rolled[hx * SIDE : (hx + 1) * SIDE] for rolled in pair]
+                    bias[head, py // SIDE, hx, place, lanes] = jnp.concatenate(part, axis=0).astype(BF16)
 
 
 def scores_of(blocks, keys, head_dim, channels):
@@ -131,7 +135,7 @@
     scores = scores_of(blocks, pair[:, :LANES], head_dim, channels)
     count = scores.shape[0] // HEADS
     yield
-    part_bias = jnp.concatenate([bias[:, hy, hx] for hy, hx in quadrants], axis=1)
+    part_bias = jnp.concatenate([bias[:, hy, hx] for hy, hx in quadrants], axis=1).astype(F32)
     scores = scores.reshape(HEADS, count, WIN * WIN) + part_bias
     scores = scores - jnp.max(scores, axis=-1, keepdims=True)
     weights = jnp.exp2(scores)
@@ -208,8 +212,8 @@
 
 def own_kernel(
     image_ref, gain1_ref, table_ref, qkv_ref, gain2_hbm, proj_hbm, conv_hbm, fc1_hbm, fc2_hbm,
-    bias, query, kv, normed, wkv, wp, wc, w1, w2, g2,
-    padded, strip, wq,
+    bias, query, kv, normed, q_corner, kv_corner, wkv, wp, wc, w1, w2, g2,
+    padded, strip, wq, normed32,
     gain2_ref, proj_ref, conv_ref, fc1_ref, fc2_ref, sems,
 ):
     rows, cols, channels = image_ref.shape
@@ -234,7 +238,7 @@
     wkv[176:192, 0:LANES] = jnp.where(
         (special == flag_lane) & (lanes16 == flag_lane), MASKED, 0.0
     ).astype(BF16)
-    normed[:, :, HALF:] = jnp.broadcast_to(marks(channels, 0.0)[None], (rows, cols, HALF))
+    normed32[:, :, HALF:] = jnp.broadcast_to(marks(channels, 0.0)[None], (rows, cols, HALF))
 
     gain1 = gain1_ref[...]
     scale = head_dim**-0.5 * LOG2E
@@ -255,21 +259,24 @@
 
     def norm(br):
         at = slice(br * SIDE, (br + 1) * SIDE)
-        normed[at, :, 0:channels] = layer_norm(image_ref[at].astype(F32), gain1)
+        normed32[at, :, 0:channels] = layer_norm(image_ref[at].astype(F32), gain1)
+        normed[at] = normed32[at].astype(BF16)
 
     def project(br):
-        pixels = normed[br * SIDE : (br + 1) * SIDE].astype(BF16).reshape(-1, LANES)
+        pixels = normed[br * SIDE : (br + 1) * SIDE].reshape(-1, LANES)
         q = dot(pixels, wq[...])
         yield
         both = dot(pixels, wkv[...]).reshape(SIDE, cols, 2 * LANES)
         q = (q * scale).reshape(SIDE, cols, LANES)
         for bc in range(blocks_c):
             part = slice(bc * SIDE, (bc + 1) * SIDE)
-            query[br, bc] = q[:, part].reshape(AREA, LANES).astype(BF16)
+            ref = q_corner.at[CORNERS.index((br, bc))] if (br, bc) in CORNERS else query.at[br, bc]
+            ref[...] = q[:, part].reshape(AREA, LANES).astype(BF16)
         yield
         for bc in range(blocks_c):
             part = slice(bc * SIDE, (bc + 1) * SIDE)
-            kv[br, bc] = both[:, part].reshape(AREA, 2 * LANES).astype(BF16)
+            ref = kv_corner.at[CORNERS.index((br, bc))] if (br, bc) in CORNERS else kv.at[br, bc]
+            ref[...] = both[:, part].reshape(AREA, 2 * LANES).astype(BF16)
 
     for br in range(blocks_r):
         norm(br)
@@ -280,8 +287,8 @@
 def edge_kernel(
     image_ref, top_ref, bottom_ref, left_ref, right_ref, gain1_ref,
     bias, query, kv, normed, wkv, wp, wc, w1, w2, g2,
-    kv_edge, corner_base, out_edge, out_mid,
-    halo, base, shifted,
+    kv_ends, corner_base, out_edge, out_mid,
+    halo, base, shifted, kv_edge,
 ):
     rows, cols, channels = image_ref.shape
     head_dim = channels // HEADS
@@ -321,12 +328,14 @@
         yield
         both = dot(pixels, wkv[...])
         yield
-        kv_edge[i] = both.astype(BF16).reshape(-1, AREA, 2 * LANES)
+        both = both.astype(BF16).reshape(-1, AREA, 2 * LANES)
+        kv_edge[i] = both
+        kv_ends[i, 0], kv_ends[i, 1] = both[0], both[-1]
         sides.append(i)
 
     def tile():
         for r in range(0, rows, SIDE):
-            halo[SHIFT + r : SHIFT + r + SIDE, SHIFT : SHIFT + cols] = normed[r : r + SIDE]
+            halo[SHIFT + r : SHIFT + r + SIDE, SHIFT : SHIFT + cols] = normed[r : r + SIDE].astype(F32)
             yield
 
     def convolve(br):
@@ -347,14 +356,13 @@
         summed = summed + image_ref[r : r + SIDE].astype(F32)
         for bc in range(cols // SIDE):
             part = summed[:, bc * SIDE : (bc + 1) * SIDE].reshape(AREA, channels)
-            if (br, bc) in corners:
-                ref = corner_base.at[corners.index((br, bc))]
+            if (br, bc) in CORNERS:
+                ref = corner_base.at[CORNERS.index((br, bc))]
             else:
                 ref = base.at[br, bc]
             ref[:, HALF:] = jnp.zeros((AREA, HALF), F32)
             ref[:, 0:channels] = part
 
-    corners = [(0, 0), (0, 3), (3, 0), (3, 3)]
     keys = [
         lambda: [kv_edge[0, 1], kv[0, 1], kv_edge[0, 2], kv[0, 2]],
         lambda: [kv[3, 1], kv_edge[1, 1], kv[3, 2], kv_edge[1, 2]],
@@ -380,9 +388,9 @@
     def tail(i):
         def put(out):
             if i == 4:
-                out_mid[...] = out
+                out_mid[...] = out.astype(BF16)
             else:
-                out_edge[i // 2] = out
+                out_edge[i // 2] = out.astype(BF16)
 
         def make():
             return finish(
@@ -402,9 +410,9 @@
 
 def corner_kernel(
     left_ref, right_ref, gain1_ref,
-    bias, query, kv, wkv, wp, wc, w1, w2, g2, kv_edge, corner_base, out_mid, out_edge,
+    conv_hbm, bias, query, kv, wkv, wp, w1, w2, g2, kv_edge, corner_base, out_mid, out_edge,
     out_hbm,
-    normed, out_ref, sems,
+    normed, out_ref, taps, sems,
 ):
     rows, _, channels = out_ref.shape
     head_dim = channels // HEADS
@@ -421,9 +429,15 @@
                 i = br - 1
                 band = [piece(out_edge.at[1], i), piece(out_mid, 2 * i), piece(out_mid, 2 * i + 1),
                         piece(out_edge.at[1], i + 2)]
-            band = [part[:, :channels].reshape(SIDE, SIDE, channels) for part in band]
+            band = [part[:, :channels].astype(F32).reshape(SIDE, SIDE, channels) for part in band]
             out_ref[br * SIDE : (br + 1) * SIDE] = jnp.concatenate(band, axis=1).astype(BF16)
 
+    fetches = [
+        pltpu.make_async_copy(conv_hbm.at[2 * (i // 2), 2 * (i % 2)], taps.at[i], sems.at[3 + i])
+        for i in range(4)
+    ]
+    for fetch in fetches:
+        fetch.start()
     finish_bands((1, 2), None)
     inner = slice(SIDE, rows - SIDE)
     writes = [pltpu.make_async_copy(out_ref.at[inner], out_hbm.at[inner], sems.at[0])]
@@ -451,25 +465,27 @@
         corner[2 * pair], corner[2 * pair + 1] = both[:AREA], both[AREA:]
 
     keys = [
-        lambda: [corner[0], kv_edge[2, 0], kv_edge[0, 0], kv[0, 0]],
-        lambda: [kv_edge[0, 3], kv[0, 3], corner[1], kv_edge[3, 0]],
-        lambda: [kv_edge[2, 3], corner[2], kv[3, 0], kv_edge[1, 0]],
-        lambda: [kv[3, 3], kv_edge[1, 3], kv_edge[3, 3], corner[3]],
+        lambda: [corner[0], kv_edge[2, 0], kv_edge[0, 0], kv[0]],
+        lambda: [kv_edge[0, 1], kv[1], corner[1], kv_edge[3, 0]],
+        lambda: [kv_edge[2, 1], corner[2], kv[2], kv_edge[1, 0]],
+        lambda: [kv[3], kv_edge[1, 1], kv_edge[3, 1], corner[3]],
     ]
-    places = [(0, 0), (0, 3), (3, 0), (3, 3)]
     quadrants = [(1, 1), (1, 0), (0, 1), (0, 0)]
 
     def unit(i):
         def put(result):
             done[i] = result
 
-        parts = ([query[places[i]]], [quadrants[i]], lambda: jnp.concatenate(keys[i](), axis=0))
+        parts = ([query[i]], [quadrants[i]], lambda: jnp.concatenate(keys[i](), axis=0))
         return after(lambda: i in corner, lambda: attend(parts, bias, head_dim, channels, put))
 
     def whole(i):
-        tap, y, x = ((0, 7, 7), (2, 7, 0), (6, 0, 7), (8, 0, 0))[i]
-        start = y * SIDE
-        term = dot(normed[i, start : start + SIDE].astype(BF16), wc[tap * LANES : (tap + 1) * LANES])
+        y, x = ((7, 7), (7, 0), (0, 7), (0, 0))[i]
+        if i == 0:
+            for fetch in fetches:
+                fetch.wait()
+        pixels = normed[i, y * SIDE : (y + 1) * SIDE][:, :channels].astype(BF16)
+        term = jnp.pad(dot(pixels, taps[i]), ((0, 0), (0, LANES - channels)))
         term = term[x : x + 1]
         pixel = lax.broadcasted_iota(jnp.int32, (AREA, 1), 0)
         at = (SIDE - 1 - y) * SIDE + SIDE - 1 - x
@@ -543,14 +559,16 @@
     left, right = exchange(first_cols, last_cols, "col")
     fetched = (gain2, proj_weight, conv_weight, fc1_weight, fc2)
     hidden = -(-fc1_weight.shape[1] // 128) * 128
-    bias, query, kv, normed, wkv, wp, wc, w1, w2, g2 = call(
+    bias, query, kv, normed, q_corner, kv_corner, wkv, wp, wc, w1, w2, g2 = call(
         own_kernel,
         "own_tile",
         [
-            ((HEADS, 2, 2, AREA, WIN * WIN), F32),
+            ((HEADS, 2, 2, AREA, WIN * WIN), BF16),
             ((blocks_r, blocks_c, AREA, LANES), BF16),
             ((blocks_r, blocks_c, AREA, 2 * LANES), BF16),
-            ((rows, cols, LANES), F32),
+            ((rows, cols, LANES), BF16),
+            ((4, AREA, LANES), BF16),
+            ((4, AREA, 2 * LANES), BF16),
             ((LANES, 2 * LANES), BF16),
             ((LANES, LANES), BF16),
             ((9 * LANES, LANES), BF16),
@@ -562,6 +580,7 @@
             ((8, 1024), F32),
             ((4, 8 * WIN, 128), F32),
             ((LANES, LANES), BF16),
+            ((rows, cols, LANES), F32),
             *[(x.shape, x.dtype) for x in fetched],
             pltpu.SemaphoreType.DMA((len(fetched),)),
         ],
@@ -577,19 +596,20 @@
 
     first, last = ends(0, 0), ends(cols - SHIFT, cols // 2 - SHIFT)
     left_corner, right_corner = exchange(first, last, "col")
-    kv_edge, corner_base, out_edge, out_mid = call(
+    kv_ends, corner_base, out_edge, out_mid = call(
         edge_kernel,
         "edge_windows",
         [
-            ((4, blocks_c, AREA, 2 * LANES), BF16),
+            ((4, 2, AREA, 2 * LANES), BF16),
             ((4, AREA, LANES), F32),
-            ((2, 4 * AREA, LANES), F32),
-            ((4 * AREA, LANES), F32),
+            ((2, 4 * AREA, LANES), BF16),
+            ((4 * AREA, LANES), BF16),
         ],
         [
             ((rows + 2 * SHIFT, cols + 2 * SHIFT, LANES), F32),
             ((blocks_r, blocks_c, AREA, LANES), F32),
             ((3, rows + 2, cols, LANES), BF16),
+            ((4, blocks_c, AREA, 2 * LANES), BF16),
         ],
         2_000_000_000,
         (tile, top, bottom, left, right, gain1, bias, query, kv, normed, wkv, wp, wc, w1, w2, g2),
@@ -598,10 +618,12 @@
         corner_kernel,
         "corner_windows",
         [jax.ShapeDtypeStruct(image.shape, BF16)],
-        [((4, AREA, LANES), F32), (image.shape, BF16), pltpu.SemaphoreType.DMA((3,))],
+        [((4, AREA, LANES), F32), (image.shape, BF16), ((4, channels, channels), BF16),
+         pltpu.SemaphoreType.DMA((7,))],
         1_000_000_000,
-        (left_corner, right_corner, gain1, bias, query, kv, wkv, wp, wc, w1, w2, g2,
-         kv_edge, corner_base, out_mid, out_edge),
+        (left_corner, right_corner, gain1, conv_weight, bias, q_corner, kv_corner, wkv, wp, w1, w2, g2,
+         kv_ends, corner_base, out_mid, out_edge),
+        (3,),
     )
     return out
 

time: 22.3 us -> 22.3 us (level)
  transfers between devices with their start and end apart: 6 -> 6, of which waited for: 0 -> 0; matrix products, arithmetic and copies ran while one was open for 0% -> 0% of each run, Pallas kernels for 40% -> 39%
where the time goes in v16:
time: 22.3 us; the launch traced here: 22.1 us
  Pallas kernels  13.6 us (61%)
  starting transfers between devices  8.25 us (37%)
    pallas_call x4, Pallas kernels, call(): pl.pallas_call(kernel, out_shape=[out if isinstance(out, jax.ShapeDtypeSt...  13.6 us
    ppermute x3, starting transfers between devices, exchange(): lax.ppermute(low, axis, [((i + 1) % count, i) for i in range(count)])  5.2 us
    ppermute x3, starting transfers between devices, exchange(): lax.ppermute(high, axis, [(i, (i + 1) % count) for i in range(count)])  3.05 us
  transfers between devices with their start and end apart: 6, of which 0 were waited for; matrix products, arithmetic and copies ran while one was open for 0% of the time, Pallas kernels for 39%

profile of v16, /device:TPU:0, one launch (start us, length us, event | category | flops | bytes accessed | tf_op | source)
XLA Modules:
  0.0 22.1 jit_solution(9897908662580176855)
XLA Ops:
  0.0 1.3 %cut_halo.1 = (bf16[32,32,180]{2,1,0:T(8,128)(2,1)S(1)}, f32[1,180]{1,0:T(1,128)S(1)}, f32[6,961]{1,0:T(8,128)S(1)}, bf16[180,540]{1,0:T(8,128)(2,1)S(1)}, bf16[...) custom-call(bf16[32,32,180]{2,1,0:T(8,128)(2,1)} %image_hbm.1, ...), custom_call_target="tpu_custom_call" | custom-call | flops 1000000 | bytes 4000000 | tf_op jit(solution)/shard_map/cut_halo/pallas_call | solution.py:528
  1.3 3.0 %collective-permute-start = (bf16[8,48,128]{2,1,0:T(8,128)(2,1)S(1)}, bf16[8,48,128]{2,1,0:T(8,128)(2,1)S(1)}, u32[]{:S(2)}, u32[]{:S(2)}) collective-permute-start(bf16[8,48,128]{2,1,0:T(8,128)(2,1)S(1)} %get-tuple-element.29), channel_id=1, source_target_pairs={{0,8},{8,16},{16,24},{24,0},{1,9},{9,17},{17,25},{25,1},{2,10},{10... | collective-permute-start | bytes 294920 | tf_op jit(solution)/shard_map/ppermute | solution.py:520
  4.3 1.0 %collective-permute-start.1 = (bf16[8,48,128]{2,1,0:T(8,128)(2,1)S(1)}, bf16[8,48,128]{2,1,0:T(8,128)(2,1)S(1)}, u32[]{:S(2)}, u32[]{:S(2)}) collective-permute-start(bf16[8,48,128]{2,1,0:T(8,128)(2,1)S(1)} %get-tuple-element.30), channel_id=1, source_target_pairs={{8,0},{16,8},{24,16},{0,24},{9,1},{17,9},{25,17},{1,25},{10,2},{18... | collective-permute-start | bytes 294920 | tf_op jit(solution)/shard_map/ppermute | solution.py:521
  5.3 0.0 collective-permute-start.4
  5.3 3.5 %collective-permute-start.5 = (bf16[32,8,180]{2,1,0:T(8,128)(2,1)S(1)}, bf16[32,8,180]{2,1,0:T(8,128)(2,1)S(1)}, u32[]{:S(2)}, u32[]{:S(2)}) collective-permute-start(bf16[32,8,180]{2,1,0:T(8,128)(2,1)S(1)} %get-tuple-element.44), channel_id=1, source_target_pairs={{1,0},{2,1},{3,2},{4,3},{5,4},{6,5},{7,6},{0,7},{9,8},{10,9},{11,1... | collective-permute-start | bytes 276488 | tf_op jit(solution)/shard_map/ppermute | solution.py:521
  8.9 3.1 %own_tile.1 = (bf16[6,2,2,64,256]{4,3,2,1,0:T(8,128)(2,1)S(1)}, bf16[4,4,64,256]{3,2,1,0:T(8,128)(2,1)S(1)}, bf16[4,4,64,512]{3,2,1,0:T(8,128)(2,1)S(1)}, bf16[3...) custom-call(bf16[32,32,180]{2,1,0:T(8,128)(2,1)S(1)} %get-tuple-elem, ...), custom_call_target="tpu_custom_call" | custom-call | flops 2000000000 | bytes 4000000 | tf_op jit(solution)/shard_map/own_tile/pallas_call | solution.py:528
  12.0 0.0 collective-permute-done.top_ref
  12.0 0.0 collective-permute-done.1.bottom_ref
  12.1 0.6 %collective-permute-start.3 = (bf16[16,16,128]{2,1,0:T(8,128)(2,1)S(1)}, bf16[16,16,128]{2,1,0:T(8,128)(2,1)S(1)}, u32[]{:S(2)}, u32[]{:S(2)}) collective-permute-start(bf16[16,16,128]{2,1,0:T(8,128)(2,1)S(1)} %maximum_maximum_fusion.1), channel_id=1, source_target_pairs={{1,0},{2,1},{3,2},{4,3},{5,4},{6,5},{7,6},{0,7},{9,8},{10,9},{11,1... | collective-permute-start | bytes 196616 | tf_op jit(solution)/shard_map/ppermute | solution.py:521
  12.7 0.1 collective-permute-start.2
  12.8 0.0 collective-permute-done.4.left_ref
  12.8 0.0 collective-permute-done.5.right_ref
  12.8 5.4 %edge_windows.1 = (bf16[4,2,64,512]{3,2,1,0:T(8,128)(2,1)S(1)}, f32[4,64,256]{2,1,0:T(8,128)S(1)}, bf16[2,256,256]{2,1,0:T(8,128)(2,1)S(1)}, bf16[256,256]{1,0:T(8,128)(2,1)S(1)}) custom-call(bf16[32,32,180]{2,1,0:T(8,128)(2,1)S(1)} %get-tuple-element.32.image_ref, bf16[8,48,128]{2,1,0:T(8,128)(2,1)S(1)} %collective-permute-done.top_ref, ...), custom_call_target="tpu_custom_call" | custom-call | flops 2000000000 | bytes 4000000 | tf_op jit(solution)/shard_map/edge_windows/pallas_call | solution.py:528
  18.2 0.0 collective-permute-done.3.right_ref
  18.3 0.0 collective-permute-done.2.left_ref
  18.3 3.8 %corner_windows.1 = bf16[32,32,180]{2,1,0:T(8,128)(2,1)} custom-call(bf16[16,16,128]{2,1,0:T(8,128)(2,1)S(1)} %collective-permute-done.2.left_ref, bf16[16,16,128]{2,1,0:T(8,128)(2,1)S(1)} %collective-permute-done.3.right_ref, f32[1,180]{1,0:T(1,128)S(1)} %get-tuple-element.31.gain1_ref, bf16[3,3,180,180]{3,2,1,0:T(8,128)(2,1)} %conv_hbm.3, ...), custom_call_target="tpu_custom_call" | custom-call | flops 1000000000 | bytes 4000000 | tf_op jit(solution)/shard_map/corner_windows/pallas_call | solution.py:528
  (4 shorter events, 0.1 us)
Async XLA Ops:
  1.3 10.6 %collective-permute-start = (bf16[8,48,128]{2,1,0:T(8,128)(2,1)S(1)}, bf16[8,48,128]{2,1,0:T(8,128)(2,1)S(1)}, u32[]{:S(2)}, u32[]{:S(2)}) collective-permute-start(bf16[8,48,128]{2,1,0:T(8,128)(2,1)S(1)} %get-tuple-element.29), channel_id=1, source_target_pairs={{0,8},{8,16},{16,24},{24,0},{1,9},{9,17},{17,25},{25,1},{2,10},{10... | collective-permute-start | bytes 294920 | tf_op jit(solution)/shard_map/ppermute | solution.py:520
  4.3 7.7 %collective-permute-start.1 = (bf16[8,48,128]{2,1,0:T(8,128)(2,1)S(1)}, bf16[8,48,128]{2,1,0:T(8,128)(2,1)S(1)}, u32[]{:S(2)}, u32[]{:S(2)}) collective-permute-start(bf16[8,48,128]{2,1,0:T(8,128)(2,1)S(1)} %get-tuple-element.30), channel_id=1, source_target_pairs={{8,0},{16,8},{24,16},{0,24},{9,1},{17,9},{25,17},{1,25},{10,2},{18... | collective-permute-start | bytes 294920 | tf_op jit(solution)/shard_map/ppermute | solution.py:521
  5.3 7.4 %collective-permute-start.4 = (bf16[32,8,180]{2,1,0:T(8,128)(2,1)S(1)}, bf16[32,8,180]{2,1,0:T(8,128)(2,1)S(1)}, u32[]{:S(2)}, u32[]{:S(2)}) collective-permute-start(bf16[32,8,180]{2,1,0:T(8,128)(2,1)S(1)} %get-tuple-element.43), channel_id=1, source_target_pairs={{0,1},{1,2},{2,3},{3,4},{4,5},{5,6},{6,7},{7,0},{8,9},{9,10},{10,1... | collective-permute-start | bytes 276488 | tf_op jit(solution)/shard_map/ppermute | solution.py:520
  5.3 7.5 %collective-permute-start.5 = (bf16[32,8,180]{2,1,0:T(8,128)(2,1)S(1)}, bf16[32,8,180]{2,1,0:T(8,128)(2,1)S(1)}, u32[]{:S(2)}, u32[]{:S(2)}) collective-permute-start(bf16[32,8,180]{2,1,0:T(8,128)(2,1)S(1)} %get-tuple-element.44), channel_id=1, source_target_pairs={{1,0},{2,1},{3,2},{4,3},{5,4},{6,5},{7,6},{0,7},{9,8},{10,9},{11,1... | collective-permute-start | bytes 276488 | tf_op jit(solution)/shard_map/ppermute | solution.py:521
  12.1 6.2 %collective-permute-start.3 = (bf16[16,16,128]{2,1,0:T(8,128)(2,1)S(1)}, bf16[16,16,128]{2,1,0:T(8,128)(2,1)S(1)}, u32[]{:S(2)}, u32[]{:S(2)}) collective-permute-start(bf16[16,16,128]{2,1,0:T(8,128)(2,1)S(1)} %maximum_maximum_fusion.1), channel_id=1, source_target_pairs={{1,0},{2,1},{3,2},{4,3},{5,4},{6,5},{7,6},{0,7},{9,8},{10,9},{11,1... | collective-permute-start | bytes 196616 | tf_op jit(solution)/shard_map/ppermute | solution.py:521
  12.7 5.5 %collective-permute-start.2 = (bf16[16,16,128]{2,1,0:T(8,128)(2,1)S(1)}, bf16[16,16,128]{2,1,0:T(8,128)(2,1)S(1)}, u32[]{:S(2)}, u32[]{:S(2)}) collective-permute-start(bf16[16,16,128]{2,1,0:T(8,128)(2,1)S(1)} %maximum_maximum_fusion), channel_id=1, source_target_pairs={{0,1},{1,2},{2,3},{3,4},{4,5},{5,6},{6,7},{7,0},{8,9},{9,10},{10,1... | collective-permute-start | bytes 196616 | tf_op jit(solution)/shard_map/ppermute | solution.py:520

commit v17 on v15

--- a/solution.py
+++ b/solution.py
@@ -68,6 +68,13 @@
     return half + half * jnp.tanh(x * poly)
 
 
+def pick(index, values):
+    result = jnp.int32(values[-1])
+    for i in range(len(values) - 2, -1, -1):
+        result = jnp.where(index == i, jnp.int32(values[i]), result)
+    return result
+
+
 def lanes_of(width=LANES):
     return lax.broadcasted_iota(jnp.int32, (1, width), 1)
 
@@ -88,30 +95,29 @@
     )
     high = shifted.astype(BF16)
     low = (shifted - high.astype(F32)).astype(BF16)
-    yield
     entry = lax.broadcasted_iota(jnp.int32, (width, 512), 0)
     place = lax.broadcasted_iota(jnp.int32, (1, 512), 1)
     column = lax.div(place, 256) * SIDE + lax.rem(place, SIDE)
     wanted = (span - 1 - lax.div(lax.rem(place, 256), SIDE)) * span + WIN - 1 - column
     picked = dot(jnp.concatenate([high, low], axis=0), one_hot(entry == wanted))
-    yield
     half = 8 * WIN
     picked = picked[:half] + picked[half:]
     for tile in range(4):
         strip[tile] = picked[:, 128 * tile : 128 * (tile + 1)]
-    for head in range(HEADS):
-        yield
+
+    @pl.loop(0, HEADS)
+    def _(head):
         for half in range(2):
             rows = jnp.concatenate(
                 [strip[2 * half + t, pl.ds(head, WIN, stride=8), :] for t in range(2)], axis=1
             )
+            lanes = slice(128 * half, 128 * (half + 1))
             for py in range(WIN):
                 start = (WIN - 1 - py) * SIDE
                 rolled = (rows if start == 0 else pltpu.roll(rows, 256 - start, 1))[:, 0:128]
-                lanes = slice(128 * half, 128 * (half + 1))
                 place = slice(py % SIDE * SIDE, (py % SIDE + 1) * SIDE)
-                bias[head, py // SIDE, 0, place, lanes] = rolled[:SIDE]
-                bias[head, py // SIDE, 1, place, lanes] = rolled[SIDE:]
+                bias[head, py // SIDE * 2, place, lanes] = rolled[:SIDE]
+                bias[head, py // SIDE * 2 + 1, place, lanes] = rolled[SIDE:]
 
 
 def scores_of(blocks, keys, head_dim, channels):
@@ -131,7 +137,7 @@
     scores = scores_of(blocks, pair[:, :LANES], head_dim, channels)
     count = scores.shape[0] // HEADS
     yield
-    part_bias = jnp.concatenate([bias[:, hy, hx] for hy, hx in quadrants], axis=1)
+    part_bias = jnp.concatenate([bias[:, quadrant] for quadrant in quadrants], axis=1)
     scores = scores.reshape(HEADS, count, WIN * WIN) + part_bias
     scores = scores - jnp.max(scores, axis=-1, keepdims=True)
     weights = jnp.exp2(scores)
@@ -253,35 +259,27 @@
         for tap in range(9):
             wc[tap * LANES : tap * LANES + channels, 0:channels] = conv_ref[tap // 3, tap % 3]
 
-    def norm(br):
-        at = slice(br * SIDE, (br + 1) * SIDE)
+    @pl.loop(0, blocks_r)
+    def _(br):
+        at = pl.ds(br * SIDE, SIDE)
         normed[at, :, 0:channels] = layer_norm(image_ref[at].astype(F32), gain1)
-
-    def project(br):
-        pixels = normed[br * SIDE : (br + 1) * SIDE].astype(BF16).reshape(-1, LANES)
-        q = dot(pixels, wq[...])
-        yield
+        pixels = normed[at].astype(BF16).reshape(-1, LANES)
+        q = (dot(pixels, wq[...]) * scale).reshape(SIDE, cols, LANES)
         both = dot(pixels, wkv[...]).reshape(SIDE, cols, 2 * LANES)
-        q = (q * scale).reshape(SIDE, cols, LANES)
         for bc in range(blocks_c):
             part = slice(bc * SIDE, (bc + 1) * SIDE)
-            query[br, bc] = q[:, part].reshape(AREA, LANES).astype(BF16)
-        yield
-        for bc in range(blocks_c):
-            part = slice(bc * SIDE, (bc + 1) * SIDE)
-            kv[br, bc] = both[:, part].reshape(AREA, 2 * LANES).astype(BF16)
-
-    for br in range(blocks_r):
-        norm(br)
-    weave([expand_bias(table_ref, padded, strip, bias), *[project(br) for br in range(blocks_r)]], 3)
+            query[br * blocks_c + bc] = q[:, part].reshape(AREA, LANES).astype(BF16)
+            kv[br * blocks_c + bc] = both[:, part].reshape(AREA, 2 * LANES).astype(BF16)
+
+    expand_bias(table_ref, padded, strip, bias)
     weights()
 
 
 def edge_kernel(
     image_ref, top_ref, bottom_ref, left_ref, right_ref, gain1_ref,
     bias, query, kv, normed, wkv, wp, wc, w1, w2, g2,
-    kv_edge, corner_base, out_edge, out_mid,
-    halo, base, shifted,
+    blocks, base, out,
+    halo, shifted, heads,
 ):
     rows, cols, channels = image_ref.shape
     head_dim = channels // HEADS
@@ -294,8 +292,6 @@
     for r in (0, SHIFT + rows):
         for c in (0, SHIFT + cols):
             halo[r : r + SHIFT, c : c + SHIFT] = jnp.zeros((SHIFT, SHIFT, LANES), F32)
-    sides = []
-
     def band(i):
         ref = (top_ref, bottom_ref, left_ref, right_ref)[i]
         start = (0, SHIFT + (rows if i < 2 else cols))[i % 2]
@@ -314,95 +310,72 @@
         halo[(*place, slice(0, channels))] = layer_norm(values, gain1 * (1.0 - outside[i]))
         pixels = halo[place]
         if i < 2:
-            blocks = [pixels[:, b * SIDE : (b + 1) * SIDE].reshape(AREA, LANES) for b in range(cols // SIDE)]
+            parts = [pixels[:, b * SIDE : (b + 1) * SIDE].reshape(AREA, LANES) for b in range(cols // SIDE)]
         else:
-            blocks = [pixels.reshape(-1, LANES)]
-        pixels = jnp.concatenate(blocks, axis=0).astype(BF16)
+            parts = [pixels.reshape(-1, LANES)]
+        pixels = jnp.concatenate(parts, axis=0).astype(BF16)
         yield
         both = dot(pixels, wkv[...])
         yield
-        kv_edge[i] = both.astype(BF16).reshape(-1, AREA, 2 * LANES)
-        sides.append(i)
-
-    def tile():
-        for r in range(0, rows, SIDE):
-            halo[SHIFT + r : SHIFT + r + SIDE, SHIFT : SHIFT + cols] = normed[r : r + SIDE]
-            yield
+        blocks[16 + 4 * i : 20 + 4 * i] = both.astype(BF16).reshape(-1, AREA, 2 * LANES)
+
+    weave([band(i) for i in range(4)], 4)
+
+    @pl.loop(0, rows // SIDE)
+    def _(br):
+        halo[pl.ds(SHIFT + br * SIDE, SIDE), SHIFT : SHIFT + cols] = normed[pl.ds(br * SIDE, SIDE)]
+        blocks[pl.ds(br * 4, 4)] = kv[pl.ds(br * 4, 4)]
+
+    @pl.loop(0, (rows + 2) // 2)
+    def _(i):
+        for tap in range(3):
+            c0 = SHIFT - 1 + tap
+            piece = halo[pl.ds(SHIFT - 1 + 2 * i, 2), c0 : c0 + cols]
+            shifted[tap, pl.ds(2 * i, 2)] = piece.astype(BF16)
+
+    slots = [[17, 13, 25, 7, 5, 5], [1, 21, 26, 11, 9, 9], [18, 14, 4, 29, 6, 6], [2, 22, 8, 30, 10, 10]]
+    places = [[1, 13, 4, 7, 5, 9], [2, 14, 8, 11, 6, 10]]
+    quadrants = [[2, 0, 1, 0, 0, 2], [3, 1, 3, 2, 1, 3]]
+
+    def unit(i):
+        def put(result):
+            heads[i] = result
+
+        parts = [query[pick(i, place)] for place in places]
+        pair = lambda: jnp.concatenate([blocks[pick(i, slot)] for slot in slots], axis=0)
+        return attend((parts, [pick(i, q) for q in quadrants], pair), bias, head_dim, channels, put)
 
     def convolve(br):
         r = br * SIDE
-        for tap in range(3):
-            c0 = SHIFT - 1 + tap
-            start, stop = 0 if br == 0 else r + 2, r + SIDE + 2
-            shifted[tap, start:stop] = halo[
-                SHIFT - 1 + start : SHIFT - 1 + stop, c0 : c0 + cols
-            ].astype(BF16)
-        yield
         taps = [
-            shifted[tap % 3, r + tap // 3 : r + tap // 3 + SIDE].reshape(-1, LANES) for tap in range(9)
+            shifted[tap % 3, pl.ds(r + tap // 3, SIDE)].reshape(-1, LANES) for tap in range(9)
         ]
         summed = dot(jnp.concatenate(taps, axis=1), wc[...])
         yield
         summed = summed[:, :channels].reshape(SIDE, cols, channels)
-        summed = summed + image_ref[r : r + SIDE].astype(F32)
+        summed = summed + image_ref[pl.ds(r, SIDE)].astype(F32)
         for bc in range(cols // SIDE):
+            base[br * 4 + bc, :, HALF:] = jnp.zeros((AREA, HALF), F32)
             part = summed[:, bc * SIDE : (bc + 1) * SIDE].reshape(AREA, channels)
-            if (br, bc) in corners:
-                ref = corner_base.at[corners.index((br, bc))]
-            else:
-                ref = base.at[br, bc]
-            ref[:, HALF:] = jnp.zeros((AREA, HALF), F32)
-            ref[:, 0:channels] = part
-
-    corners = [(0, 0), (0, 3), (3, 0), (3, 3)]
-    keys = [
-        lambda: [kv_edge[0, 1], kv[0, 1], kv_edge[0, 2], kv[0, 2]],
-        lambda: [kv[3, 1], kv_edge[1, 1], kv[3, 2], kv_edge[1, 2]],
-        lambda: [kv_edge[2, 1], kv_edge[2, 2], kv[1, 0], kv[2, 0]],
-        lambda: [kv[1, 3], kv[2, 3], kv_edge[3, 1], kv_edge[3, 2]],
-        lambda: [kv[1, 1], kv[2, 1], kv[1, 2], kv[2, 2]],
-    ]
-    places = [((0, 1), (0, 2)), ((3, 1), (3, 2)), ((1, 0), (2, 0)), ((1, 3), (2, 3))]
-    places += [((1, 1), (1, 2)), ((2, 1), (2, 2))]
-    quadrants = [((1, 0), (1, 1)), ((0, 0), (0, 1)), ((0, 1), (1, 1)), ((0, 0), (1, 0))]
-    quadrants += [((0, 0), (0, 1)), ((1, 0), (1, 1))]
-    done = {}
-
-    def unit(i):
+            base[br * 4 + bc, :, 0:channels] = part
+
+    @pl.loop(0, 2)
+    def _(i):
+        weave([unit(i), convolve(2 * i), unit(i + 2), convolve(2 * i + 1), unit(i + 4)], 5)
+
+    @pl.loop(0, 3)
+    def _(i):
         def put(result):
-            done[i] = result
-
-        window = keys[min(i, 4)]
-        parts = ([query[at] for at in places[i]], quadrants[i], lambda: jnp.concatenate(window(), axis=0))
-        make = lambda: attend(parts, bias, head_dim, channels, put)
-        return after(lambda: i >= 4 or i in sides, make)
-
-    def tail(i):
-        def put(out):
-            if i == 4:
-                out_mid[...] = out
-            else:
-                out_edge[i // 2] = out
-
-        def make():
-            return finish(
-                jnp.concatenate([done[i], done[i + 1]], axis=0),
-                lambda: jnp.concatenate([base[at] for at in (*places[i], *places[i + 1])], axis=0),
-                wp, g2[...], w1, w2, channels, put,
-            )
-
-        return after(lambda: i in done and i + 1 in done, make)
-
-    weave(
-        [unit(4), band(0), band(1), unit(5), band(2), band(3), tile(), unit(0), convolve(0), unit(1),
-         convolve(1), unit(2), convolve(2), unit(3), convolve(3), tail(4), tail(0), tail(2)],
-        3,
-    )
+            out[i] = result
+
+        parts = [base[pick(2 * i + j, place)] for j in range(2) for place in places]
+        raw = heads[pl.ds(2 * i, 2)].reshape(-1, LANES)
+        weave([finish(raw, lambda: jnp.concatenate(parts, axis=0), wp, g2[...], w1, w2, channels, put)], 1)
 
 
 def corner_kernel(
     left_ref, right_ref, gain1_ref,
-    bias, query, kv, wkv, wp, wc, w1, w2, g2, kv_edge, corner_base, out_mid, out_edge,
+    bias, query, wkv, wp, wc, w1, w2, g2, blocks, base, out_inner,
     out_hbm,
     normed, out_ref, sems,
 ):
@@ -416,11 +389,11 @@
         for br in which:
             if br in (0, 3):
                 i = 0 if br == 0 else 2
-                band = [corners[0], piece(out_edge.at[0], i), piece(out_edge.at[0], i + 1), corners[1]]
+                band = [corners[0], piece(out_inner.at[0], i), piece(out_inner.at[0], i + 1), corners[1]]
             else:
                 i = br - 1
-                band = [piece(out_edge.at[1], i), piece(out_mid, 2 * i), piece(out_mid, 2 * i + 1),
-                        piece(out_edge.at[1], i + 2)]
+                band = [piece(out_inner.at[1], i), piece(out_inner.at[2], 2 * i),
+                        piece(out_inner.at[2], 2 * i + 1), piece(out_inner.at[1], i + 2)]
             band = [part[:, :channels].reshape(SIDE, SIDE, channels) for part in band]
             out_ref[br * SIDE : (br + 1) * SIDE] = jnp.concatenate(band, axis=1).astype(BF16)
 
@@ -451,13 +424,13 @@
         corner[2 * pair], corner[2 * pair + 1] = both[:AREA], both[AREA:]
 
     keys = [
-        lambda: [corner[0], kv_edge[2, 0], kv_edge[0, 0], kv[0, 0]],
-        lambda: [kv_edge[0, 3], kv[0, 3], corner[1], kv_edge[3, 0]],
-        lambda: [kv_edge[2, 3], corner[2], kv[3, 0], kv_edge[1, 0]],
-        lambda: [kv[3, 3], kv_edge[1, 3], kv_edge[3, 3], corner[3]],
+        lambda: [corner[0], blocks[24], blocks[16], blocks[0]],
+        lambda: [blocks[19], blocks[3], corner[1], blocks[28]],
+        lambda: [blocks[27], corner[2], blocks[12], blocks[20]],
+        lambda: [blocks[15], blocks[23], blocks[31], corner[3]],
     ]
-    places = [(0, 0), (0, 3), (3, 0), (3, 3)]
-    quadrants = [(1, 1), (1, 0), (0, 1), (0, 0)]
+    places = [0, 3, 12, 15]
+    quadrants = [3, 2, 1, 0]
 
     def unit(i):
         def put(result):
@@ -473,7 +446,7 @@
         term = term[x : x + 1]
         pixel = lax.broadcasted_iota(jnp.int32, (AREA, 1), 0)
         at = (SIDE - 1 - y) * SIDE + SIDE - 1 - x
-        return corner_base[i] + jnp.where(pixel == at, term, 0.0)
+        return base[places[i]] + jnp.where(pixel == at, term, 0.0)
 
     def tail(i):
         def put(out):
@@ -547,9 +520,9 @@
         own_kernel,
         "own_tile",
         [
-            ((HEADS, 2, 2, AREA, WIN * WIN), F32),
-            ((blocks_r, blocks_c, AREA, LANES), BF16),
-            ((blocks_r, blocks_c, AREA, 2 * LANES), BF16),
+            ((HEADS, 4, AREA, WIN * WIN), F32),
+            ((blocks_r * blocks_c, AREA, LANES), BF16),
+            ((blocks_r * blocks_c, AREA, 2 * LANES), BF16),
             ((rows, cols, LANES), F32),
             ((LANES, 2 * LANES), BF16),
             ((LANES, LANES), BF16),
@@ -577,19 +550,18 @@
 
     first, last = ends(0, 0), ends(cols - SHIFT, cols // 2 - SHIFT)
     left_corner, right_corner = exchange(first, last, "col")
-    kv_edge, corner_base, out_edge, out_mid = call(
+    blocks, base, out_inner = call(
         edge_kernel,
         "edge_windows",
         [
-            ((4, blocks_c, AREA, 2 * LANES), BF16),
-            ((4, AREA, LANES), F32),
-            ((2, 4 * AREA, LANES), F32),
-            ((4 * AREA, LANES), F32),
+            ((2 * blocks_r * blocks_c, AREA, 2 * LANES), BF16),
+            ((blocks_r * blocks_c, AREA, LANES), F32),
+            ((3, 4 * AREA, LANES), F32),
         ],
         [
             ((rows + 2 * SHIFT, cols + 2 * SHIFT, LANES), F32),
-            ((blocks_r, blocks_c, AREA, LANES), F32),
             ((3, rows + 2, cols, LANES), BF16),
+            ((HEADS, 2 * AREA, LANES), BF16),
         ],
         2_000_000_000,
         (tile, top, bottom, left, right, gain1, bias, query, kv, normed, wkv, wp, wc, w1, w2, g2),
@@ -600,8 +572,7 @@
         [jax.ShapeDtypeStruct(image.shape, BF16)],
         [((4, AREA, LANES), F32), (image.shape, BF16), pltpu.SemaphoreType.DMA((3,))],
         1_000_000_000,
-        (left_corner, right_corner, gain1, bias, query, kv, wkv, wp, wc, w1, w2, g2,
-         kv_edge, corner_base, out_mid, out_edge),
+        (left_corner, right_corner, gain1, bias, query, wkv, wp, wc, w1, w2, g2, blocks, base, out_inner),
     )
     return out
 

time: 22.3 us -> 24.7 us (1.11)
  Pallas kernels: 13.7 us -> 16.1 us
    pallas_call x4, Pallas kernels: 13.7 us -> 16.1 us  [call(): pl.pallas_call(kernel, out_shape=[out if isinstance(out, jax.ShapeDtypeSt...]
  transfers between devices with their start and end apart: 6 -> 6, of which waited for: 0 -> 0; matrix products, arithmetic and copies ran while one was open for 0% -> 0% of each run, Pallas kernels for 40% -> 46%
where the time goes in v17:
time: 24.7 us; the launch traced here: 24.5 us
  Pallas kernels  16.1 us (65%)
  starting transfers between devices  8.25 us (33%)
    pallas_call x4, Pallas kernels, call(): pl.pallas_call(kernel, out_shape=[out if isinstance(out, jax.ShapeDtypeSt...  16.1 us
    ppermute x3, starting transfers between devices, exchange(): lax.ppermute(low, axis, [((i + 1) % count, i) for i in range(count)])  5.2 us
    ppermute x3, starting transfers between devices, exchange(): lax.ppermute(high, axis, [(i, (i + 1) % count) for i in range(count)])  3.05 us
  transfers between devices with their start and end apart: 6, of which 0 were waited for; matrix products, arithmetic and copies ran while one was open for 0% of the time, Pallas kernels for 46%

profile of v17, /device:TPU:0, one launch (start us, length us, event | category | flops | bytes accessed | tf_op | source)
XLA Modules:
  0.0 24.5 jit_solution(1587064653928338792)
XLA Ops:
  0.0 1.3 %cut_halo.1 = (bf16[32,32,180]{2,1,0:T(8,128)(2,1)S(1)}, f32[1,180]{1,0:T(1,128)S(1)}, f32[6,961]{1,0:T(8,128)S(1)}, bf16[180,540]{1,0:T(8,128)(2,1)S(1)}, bf16[...) custom-call(bf16[32,32,180]{2,1,0:T(8,128)(2,1)} %image_hbm.1, ...), custom_call_target="tpu_custom_call" | custom-call | flops 1000000 | bytes 4000000 | tf_op jit(solution)/shard_map/cut_halo/pallas_call | solution.py:485
  1.3 3.0 %collective-permute-start = (bf16[8,48,128]{2,1,0:T(8,128)(2,1)S(1)}, bf16[8,48,128]{2,1,0:T(8,128)(2,1)S(1)}, u32[]{:S(2)}, u32[]{:S(2)}) collective-permute-start(bf16[8,48,128]{2,1,0:T(8,128)(2,1)S(1)} %get-tuple-element.26), channel_id=1, source_target_pairs={{0,8},{8,16},{16,24},{24,0},{1,9},{9,17},{17,25},{25,1},{2,10},{10... | collective-permute-start | bytes 294920 | tf_op jit(solution)/shard_map/ppermute | solution.py:477
  4.3 1.0 %collective-permute-start.1 = (bf16[8,48,128]{2,1,0:T(8,128)(2,1)S(1)}, bf16[8,48,128]{2,1,0:T(8,128)(2,1)S(1)}, u32[]{:S(2)}, u32[]{:S(2)}) collective-permute-start(bf16[8,48,128]{2,1,0:T(8,128)(2,1)S(1)} %get-tuple-element.27), channel_id=1, source_target_pairs={{8,0},{16,8},{24,16},{0,24},{9,1},{17,9},{25,17},{1,25},{10,2},{18... | collective-permute-start | bytes 294920 | tf_op jit(solution)/shard_map/ppermute | solution.py:478
  5.3 0.0 collective-permute-start.4
  5.3 3.5 %collective-permute-start.5 = (bf16[32,8,180]{2,1,0:T(8,128)(2,1)S(1)}, bf16[32,8,180]{2,1,0:T(8,128)(2,1)S(1)}, u32[]{:S(2)}, u32[]{:S(2)}) collective-permute-start(bf16[32,8,180]{2,1,0:T(8,128)(2,1)S(1)} %get-tuple-element.41), channel_id=1, source_target_pairs={{1,0},{2,1},{3,2},{4,3},{5,4},{6,5},{7,6},{0,7},{9,8},{10,9},{11,1... | collective-permute-start | bytes 276488 | tf_op jit(solution)/shard_map/ppermute | solution.py:478
  8.9 3.9 %own_tile.1 = (f32[6,4,64,256]{3,2,1,0:T(8,128)S(1)}, bf16[16,64,256]{2,1,0:T(8,128)(2,1)S(1)}, bf16[16,64,512]{2,1,0:T(8,128)(2,1)S(1)}, f32[32,32,256]{2,1,0:T...) custom-call(bf16[32,32,180]{2,1,0:T(8,128)(2,1)S(1)} %get-tuple-elem, ...), custom_call_target="tpu_custom_call" | custom-call | flops 2000000000 | bytes 4000000 | tf_op jit(solution)/shard_map/own_tile/pallas_call | solution.py:485
  12.8 0.0 collective-permute-done.top_ref
  12.8 0.0 collective-permute-done.1.bottom_ref
  12.9 0.6 %collective-permute-start.3 = (bf16[16,16,128]{2,1,0:T(8,128)(2,1)S(1)}, bf16[16,16,128]{2,1,0:T(8,128)(2,1)S(1)}, u32[]{:S(2)}, u32[]{:S(2)}) collective-permute-start(bf16[16,16,128]{2,1,0:T(8,128)(2,1)S(1)} %maximum_maximum_fusion.1), channel_id=1, source_target_pairs={{1,0},{2,1},{3,2},{4,3},{5,4},{6,5},{7,6},{0,7},{9,8},{10,9},{11,1... | collective-permute-start | bytes 196616 | tf_op jit(solution)/shard_map/ppermute | solution.py:478
  13.6 0.1 collective-permute-start.2
  13.6 0.0 collective-permute-done.4.left_ref
  13.6 0.0 collective-permute-done.5.right_ref
  13.6 7.4 %edge_windows.1 = (bf16[32,64,512]{2,1,0:T(8,128)(2,1)S(1)}, f32[16,64,256]{2,1,0:T(8,128)S(1)}, f32[3,256,256]{2,1,0:T(8,128)S(1)}) custom-call(bf16[32,32,180]{2,1,0:T(8,128)(2,1)S(1)} %get-tuple-element.29.image_ref, bf16[8,48,128]{2,1,0:T(8,128)(2,1)S(1)} %collective-permute-done.top_ref, bf16[8,48,128]{2,1,0:T(8,128)(2,1)S(1)} %collective-permute-done.1.bottom_ref, ...), custom_call_target="tpu_custom_call" | custom-call | flops 2000000000 | bytes 4000000 | tf_op jit(solution)/shard_map/edge_windows/pallas_call | solution.py:485
  21.1 0.0 collective-permute-done.3.right_ref
  21.1 0.0 collective-permute-done.2.left_ref
  21.1 3.4 %corner_windows.1 = bf16[32,32,180]{2,1,0:T(8,128)(2,1)} custom-call(bf16[16,16,128]{2,1,0:T(8,128)(2,1)S(1)} %collective-permute-done.2.left_ref, bf16[16,16,128]{2,1,0:T(8,128)(2,1)S(1)} %collective-permute-done.3.right_ref, f32[1,180]{1,0:T(1,128)S(1)} %get-tuple-element.28.gain1_ref, f32[6,4,64,256]{3,2,1,0:T(8,128)S(1)} %get-tuple-element.32.bias, ...), custom_call_target="tpu_custom_call" | custom-call | flops 1000000000 | bytes 4000000 | tf_op jit(solution)/shard_map/corner_windows/pallas_call | solution.py:485
  (4 shorter events, 0.1 us)
Async XLA Ops:
  1.3 11.5 %collective-permute-start = (bf16[8,48,128]{2,1,0:T(8,128)(2,1)S(1)}, bf16[8,48,128]{2,1,0:T(8,128)(2,1)S(1)}, u32[]{:S(2)}, u32[]{:S(2)}) collective-permute-start(bf16[8,48,128]{2,1,0:T(8,128)(2,1)S(1)} %get-tuple-element.26), channel_id=1, source_target_pairs={{0,8},{8,16},{16,24},{24,0},{1,9},{9,17},{17,25},{25,1},{2,10},{10... | collective-permute-start | bytes 294920 | tf_op jit(solution)/shard_map/ppermute | solution.py:477
  4.3 8.5 %collective-permute-start.1 = (bf16[8,48,128]{2,1,0:T(8,128)(2,1)S(1)}, bf16[8,48,128]{2,1,0:T(8,128)(2,1)S(1)}, u32[]{:S(2)}, u32[]{:S(2)}) collective-permute-start(bf16[8,48,128]{2,1,0:T(8,128)(2,1)S(1)} %get-tuple-element.27), channel_id=1, source_target_pairs={{8,0},{16,8},{24,16},{0,24},{9,1},{17,9},{25,17},{1,25},{10,2},{18... | collective-permute-start | bytes 294920 | tf_op jit(solution)/shard_map/ppermute | solution.py:478
  5.3 8.3 %collective-permute-start.4 = (bf16[32,8,180]{2,1,0:T(8,128)(2,1)S(1)}, bf16[32,8,180]{2,1,0:T(8,128)(2,1)S(1)}, u32[]{:S(2)}, u32[]{:S(2)}) collective-permute-start(bf16[32,8,180]{2,1,0:T(8,128)(2,1)S(1)} %get-tuple-element.40), channel_id=1, source_target_pairs={{0,1},{1,2},{2,3},{3,4},{4,5},{5,6},{6,7},{7,0},{8,9},{9,10},{10,1... | collective-permute-start | bytes 276488 | tf_op jit(solution)/shard_map/ppermute | solution.py:477
  5.3 8.3 %collective-permute-start.5 = (bf16[32,8,180]{2,1,0:T(8,128)(2,1)S(1)}, bf16[32,8,180]{2,1,0:T(8,128)(2,1)S(1)}, u32[]{:S(2)}, u32[]{:S(2)}) collective-permute-start(bf16[32,8,180]{2,1,0:T(8,128)(2,1)S(1)} %get-tuple-element.41), channel_id=1, source_target_pairs={{1,0},{2,1},{3,2},{4,3},{5,4},{6,5},{7,6},{0,7},{9,8},{10,9},{11,1... | collective-permute-start | bytes 276488 | tf_op jit(solution)/shard_map/ppermute | solution.py:478
  12.9 8.2 %collective-permute-start.3 = (bf16[16,16,128]{2,1,0:T(8,128)(2,1)S(1)}, bf16[16,16,128]{2,1,0:T(8,128)(2,1)S(1)}, u32[]{:S(2)}, u32[]{:S(2)}) collective-permute-start(bf16[16,16,128]{2,1,0:T(8,128)(2,1)S(1)} %maximum_maximum_fusion.1), channel_id=1, source_target_pairs={{1,0},{2,1},{3,2},{4,3},{5,4},{6,5},{7,6},{0,7},{9,8},{10,9},{11,1... | collective-permute-start | bytes 196616 | tf_op jit(solution)/shard_map/ppermute | solution.py:478
  13.6 7.5 %collective-permute-start.2 = (bf16[16,16,128]{2,1,0:T(8,128)(2,1)S(1)}, bf16[16,16,128]{2,1,0:T(8,128)(2,1)S(1)}, u32[]{:S(2)}, u32[]{:S(2)}) collective-permute-start(bf16[16,16,128]{2,1,0:T(8,128)(2,1)S(1)} %maximum_maximum_fusion), channel_id=1, source_target_pairs={{0,1},{1,2},{2,3},{3,4},{4,5},{5,6},{6,7},{7,0},{8,9},{9,10},{10,1... | collective-permute-start | bytes 196616 | tf_op jit(solution)/shard_map/ppermute | solution.py:477

commit v18 on v15

--- a/solution.py
+++ b/solution.py
@@ -252,6 +252,8 @@
         g2[:, 0:channels] = gain2_ref[...]
         for tap in range(9):
             wc[tap * LANES : tap * LANES + channels, 0:channels] = conv_ref[tap // 3, tap % 3]
+            if tap % 3 == 2:
+                yield
 
     def norm(br):
         at = slice(br * SIDE, (br + 1) * SIDE)
@@ -273,8 +275,8 @@
 
     for br in range(blocks_r):
         norm(br)
-    weave([expand_bias(table_ref, padded, strip, bias), *[project(br) for br in range(blocks_r)]], 3)
-    weights()
+    tasks = [expand_bias(table_ref, padded, strip, bias), *[project(br) for br in range(blocks_r)]]
+    weave([*tasks, weights()], 3)
 
 
 def edge_kernel(
@@ -416,7 +418,7 @@
         for br in which:
             if br in (0, 3):
                 i = 0 if br == 0 else 2
-                band = [corners[0], piece(out_edge.at[0], i), piece(out_edge.at[0], i + 1), corners[1]]
+                band = [corners[i], piece(out_edge.at[0], i), piece(out_edge.at[0], i + 1), corners[i + 1]]
             else:
                 i = br - 1
                 band = [piece(out_edge.at[1], i), piece(out_mid, 2 * i), piece(out_mid, 2 * i + 1),
@@ -435,8 +437,8 @@
     out_col = [(col == 0).astype(F32), (col == last_col).astype(F32)]
     corner, done = {}, {}
 
-    def project(pair):
-        for i in (2 * pair, 2 * pair + 1):
+    def project():
+        for i in range(4):
             ref = (left_ref, right_ref)[i % 2]
             inside = (1.0 - out_row[i // 2]) * (1.0 - out_col[i % 2])
             mark = marks(channels, out_row[i // 2] + out_col[i % 2])
@@ -444,11 +446,10 @@
             values = ref[i // 2 * SIDE : (i // 2 + 1) * SIDE].astype(F32)
             values = unpack(values[:, :SIDE], values[:, SIDE:], i % 2 == 0, channels)
             normed[i, :, 0:channels] = layer_norm(values.reshape(AREA, channels), gain1 * inside)
-        yield
-        both = dot(normed[2 * pair : 2 * pair + 2].reshape(-1, LANES).astype(BF16), wkv[...])
-        yield
+        both = dot(normed[...].reshape(-1, LANES).astype(BF16), wkv[...])
         both = both.astype(BF16)
-        corner[2 * pair], corner[2 * pair + 1] = both[:AREA], both[AREA:]
+        for i in range(4):
+            corner[i] = both[i * AREA : (i + 1) * AREA]
 
     keys = [
         lambda: [corner[0], kv_edge[2, 0], kv_edge[0, 0], kv[0, 0]],
@@ -475,20 +476,21 @@
         at = (SIDE - 1 - y) * SIDE + SIDE - 1 - x
         return corner_base[i] + jnp.where(pixel == at, term, 0.0)
 
-    def tail(i):
+    def tail():
         def put(out):
-            finish_bands((0,) if i == 0 else (3,), [out[:AREA], out[AREA:]])
+            finish_bands((0, 3), [out[i * AREA : (i + 1) * AREA] for i in range(4)])
 
         def make():
             return finish(
-                jnp.concatenate([done[i], done[i + 1]], axis=0),
-                lambda: jnp.concatenate([whole(i), whole(i + 1)], axis=0),
+                jnp.concatenate([done[i] for i in range(4)], axis=0),
+                lambda: jnp.concatenate([whole(i) for i in range(4)], axis=0),
                 wp, g2[...], w1, w2, channels, put,
             )
 
-        return after(lambda: i in done and i + 1 in done, make)
-
-    weave([project(0), project(1), unit(0), unit(1), unit(2), unit(3), tail(0), tail(2)], 4)
+        return after(lambda: len(done) == 4, make)
+
+    project()
+    weave([unit(0), unit(1), unit(2), unit(3), tail()], 2)
     writes[0].wait()
     for r in (0, rows - SIDE):
         at = slice(r, r + SIDE)

time: 22.3 us -> 22.2 us (level)
  no operation moved by 1% of the time
where the time goes in v18:
time: 22.2 us; the launch traced here: 22 us
  Pallas kernels  13.6 us (61%)
  starting transfers between devices  8.26 us (37%)
    pallas_call x4, Pallas kernels, call(): pl.pallas_call(kernel, out_shape=[out if isinstance(out, jax.ShapeDtypeSt...  13.6 us
    ppermute x3, starting transfers between devices, exchange(): lax.ppermute(low, axis, [((i + 1) % count, i) for i in range(count)])  5.21 us
    ppermute x3, starting transfers between devices, exchange(): lax.ppermute(high, axis, [(i, (i + 1) % count) for i in range(count)])  3.05 us
  transfers between devices with their start and end apart: 6, of which 0 were waited for; matrix products, arithmetic and copies ran while one was open for 0% of the time, Pallas kernels for 40%

profile of v18, /device:TPU:0, one launch (start us, length us, event | category | flops | bytes accessed | tf_op | source)
XLA Modules:
  0.0 22.0 jit_solution(11407819554412447266)
XLA Ops:
  0.0 1.3 %cut_halo.1 = (bf16[32,32,180]{2,1,0:T(8,128)(2,1)S(1)}, f32[1,180]{1,0:T(1,128)S(1)}, f32[6,961]{1,0:T(8,128)S(1)}, bf16[180,540]{1,0:T(8,128)(2,1)S(1)}, bf16[...) custom-call(bf16[32,32,180]{2,1,0:T(8,128)(2,1)} %image_hbm.1, ...), custom_call_target="tpu_custom_call" | custom-call | flops 1000000 | bytes 4000000 | tf_op jit(solution)/shard_map/cut_halo/pallas_call | solution.py:514
  1.3 3.0 %collective-permute-start = (bf16[8,48,128]{2,1,0:T(8,128)(2,1)S(1)}, bf16[8,48,128]{2,1,0:T(8,128)(2,1)S(1)}, u32[]{:S(2)}, u32[]{:S(2)}) collective-permute-start(bf16[8,48,128]{2,1,0:T(8,128)(2,1)S(1)} %get-tuple-element.27), channel_id=1, source_target_pairs={{0,8},{8,16},{16,24},{24,0},{1,9},{9,17},{17,25},{25,1},{2,10},{10... | collective-permute-start | bytes 294920 | tf_op jit(solution)/shard_map/ppermute | solution.py:506
  4.3 1.0 %collective-permute-start.1 = (bf16[8,48,128]{2,1,0:T(8,128)(2,1)S(1)}, bf16[8,48,128]{2,1,0:T(8,128)(2,1)S(1)}, u32[]{:S(2)}, u32[]{:S(2)}) collective-permute-start(bf16[8,48,128]{2,1,0:T(8,128)(2,1)S(1)} %get-tuple-element.28), channel_id=1, source_target_pairs={{8,0},{16,8},{24,16},{0,24},{9,1},{17,9},{25,17},{1,25},{10,2},{18... | collective-permute-start | bytes 294920 | tf_op jit(solution)/shard_map/ppermute | solution.py:507
  5.3 0.0 collective-permute-start.4
  5.3 3.5 %collective-permute-start.5 = (bf16[32,8,180]{2,1,0:T(8,128)(2,1)S(1)}, bf16[32,8,180]{2,1,0:T(8,128)(2,1)S(1)}, u32[]{:S(2)}, u32[]{:S(2)}) collective-permute-start(bf16[32,8,180]{2,1,0:T(8,128)(2,1)S(1)} %get-tuple-element.43), channel_id=1, source_target_pairs={{1,0},{2,1},{3,2},{4,3},{5,4},{6,5},{7,6},{0,7},{9,8},{10,9},{11,1... | collective-permute-start | bytes 276488 | tf_op jit(solution)/shard_map/ppermute | solution.py:507
  8.9 3.2 %own_tile.1 = (f32[6,2,2,64,256]{4,3,2,1,0:T(8,128)S(1)}, bf16[4,4,64,256]{3,2,1,0:T(8,128)(2,1)S(1)}, bf16[4,4,64,512]{3,2,1,0:T(8,128)(2,1)S(1)}, f32[32,32,25...) custom-call(bf16[32,32,180]{2,1,0:T(8,128)(2,1)S(1)} %get-tuple-elem, ...), custom_call_target="tpu_custom_call" | custom-call | flops 2000000000 | bytes 4000000 | tf_op jit(solution)/shard_map/own_tile/pallas_call | solution.py:514
  12.1 0.0 collective-permute-done.top_ref
  12.1 0.0 collective-permute-done.1.bottom_ref
  12.2 0.6 %collective-permute-start.3 = (bf16[16,16,128]{2,1,0:T(8,128)(2,1)S(1)}, bf16[16,16,128]{2,1,0:T(8,128)(2,1)S(1)}, u32[]{:S(2)}, u32[]{:S(2)}) collective-permute-start(bf16[16,16,128]{2,1,0:T(8,128)(2,1)S(1)} %maximum_maximum_fusion.1), channel_id=1, source_target_pairs={{1,0},{2,1},{3,2},{4,3},{5,4},{6,5},{7,6},{0,7},{9,8},{10,9},{11,1... | collective-permute-start | bytes 196616 | tf_op jit(solution)/shard_map/ppermute | solution.py:507
  12.8 0.1 collective-permute-start.2
  12.9 0.0 collective-permute-done.4.left_ref
  12.9 0.0 collective-permute-done.5.right_ref
  12.9 5.5 %edge_windows.1 = (bf16[4,4,64,512]{3,2,1,0:T(8,128)(2,1)S(1)}, f32[4,64,256]{2,1,0:T(8,128)S(1)}, f32[2,256,256]{2,1,0:T(8,128)S(1)}, f32[256,256]{1,0:T(8,128)S(1)}) custom-call(bf16[32,32,180]{2,1,0:T(8,128)(2,1)S(1)} %get-tuple-element.30.image_ref, bf16[8,48,128]{2,1,0:T(8,128)(2,1)S(1)} %collective-permute-done.top_ref, ...), custom_call_target="tpu_custom_call" | custom-call | flops 2000000000 | bytes 4000000 | tf_op jit(solution)/shard_map/edge_windows/pallas_call | solution.py:514
  18.5 0.0 collective-permute-done.3.right_ref
  18.5 0.0 collective-permute-done.2.left_ref
  18.5 3.5 %corner_windows.1 = bf16[32,32,180]{2,1,0:T(8,128)(2,1)} custom-call(bf16[16,16,128]{2,1,0:T(8,128)(2,1)S(1)} %collective-permute-done.2.left_ref, bf16[16,16,128]{2,1,0:T(8,128)(2,1)S(1)} %collective-permute-done.3.right_ref, f32[1,180]{1,0:T(1,128)S(1)} %get-tuple-element.29.gain1_ref, f32[6,2,2,64,256]{4,3,2,1,0:T(8,128)S(1)} %get-tuple-element.33.bias, ...), custom_call_target="tpu_custom_call" | custom-call | flops 1000000000 | bytes 4000000 | tf_op jit(solution)/shard_map/corner_windows/pallas_call | solution.py:514
  (4 shorter events, 0.1 us)
Async XLA Ops:
  1.3 10.8 %collective-permute-start = (bf16[8,48,128]{2,1,0:T(8,128)(2,1)S(1)}, bf16[8,48,128]{2,1,0:T(8,128)(2,1)S(1)}, u32[]{:S(2)}, u32[]{:S(2)}) collective-permute-start(bf16[8,48,128]{2,1,0:T(8,128)(2,1)S(1)} %get-tuple-element.27), channel_id=1, source_target_pairs={{0,8},{8,16},{16,24},{24,0},{1,9},{9,17},{17,25},{25,1},{2,10},{10... | collective-permute-start | bytes 294920 | tf_op jit(solution)/shard_map/ppermute | solution.py:506
  4.3 7.8 %collective-permute-start.1 = (bf16[8,48,128]{2,1,0:T(8,128)(2,1)S(1)}, bf16[8,48,128]{2,1,0:T(8,128)(2,1)S(1)}, u32[]{:S(2)}, u32[]{:S(2)}) collective-permute-start(bf16[8,48,128]{2,1,0:T(8,128)(2,1)S(1)} %get-tuple-element.28), channel_id=1, source_target_pairs={{8,0},{16,8},{24,16},{0,24},{9,1},{17,9},{25,17},{1,25},{10,2},{18... | collective-permute-start | bytes 294920 | tf_op jit(solution)/shard_map/ppermute | solution.py:507
  5.3 7.6 %collective-permute-start.4 = (bf16[32,8,180]{2,1,0:T(8,128)(2,1)S(1)}, bf16[32,8,180]{2,1,0:T(8,128)(2,1)S(1)}, u32[]{:S(2)}, u32[]{:S(2)}) collective-permute-start(bf16[32,8,180]{2,1,0:T(8,128)(2,1)S(1)} %get-tuple-element.42), channel_id=1, source_target_pairs={{0,1},{1,2},{2,3},{3,4},{4,5},{5,6},{6,7},{7,0},{8,9},{9,10},{10,1... | collective-permute-start | bytes 276488 | tf_op jit(solution)/shard_map/ppermute | solution.py:506
  5.3 7.6 %collective-permute-start.5 = (bf16[32,8,180]{2,1,0:T(8,128)(2,1)S(1)}, bf16[32,8,180]{2,1,0:T(8,128)(2,1)S(1)}, u32[]{:S(2)}, u32[]{:S(2)}) collective-permute-start(bf16[32,8,180]{2,1,0:T(8,128)(2,1)S(1)} %get-tuple-element.43), channel_id=1, source_target_pairs={{1,0},{2,1},{3,2},{4,3},{5,4},{6,5},{7,6},{0,7},{9,8},{10,9},{11,1... | collective-permute-start | bytes 276488 | tf_op jit(solution)/shard_map/ppermute | solution.py:507
  12.2 6.3 %collective-permute-start.3 = (bf16[16,16,128]{2,1,0:T(8,128)(2,1)S(1)}, bf16[16,16,128]{2,1,0:T(8,128)(2,1)S(1)}, u32[]{:S(2)}, u32[]{:S(2)}) collective-permute-start(bf16[16,16,128]{2,1,0:T(8,128)(2,1)S(1)} %maximum_maximum_fusion.1), channel_id=1, source_target_pairs={{1,0},{2,1},{3,2},{4,3},{5,4},{6,5},{7,6},{0,7},{9,8},{10,9},{11,1... | collective-permute-start | bytes 196616 | tf_op jit(solution)/shard_map/ppermute | solution.py:507
  12.8 5.6 %collective-permute-start.2 = (bf16[16,16,128]{2,1,0:T(8,128)(2,1)S(1)}, bf16[16,16,128]{2,1,0:T(8,128)(2,1)S(1)}, u32[]{:S(2)}, u32[]{:S(2)}) collective-permute-start(bf16[16,16,128]{2,1,0:T(8,128)(2,1)S(1)} %maximum_maximum_fusion), channel_id=1, source_target_pairs={{0,1},{1,2},{2,3},{3,4},{4,5},{5,6},{6,7},{7,0},{8,9},{9,10},{10,1... | collective-permute-start | bytes 196616 | tf_op jit(solution)/shard_map/ppermute | solution.py:506

commit v19 on v15

--- a/solution.py
+++ b/solution.py
@@ -252,6 +252,8 @@
         g2[:, 0:channels] = gain2_ref[...]
         for tap in range(9):
             wc[tap * LANES : tap * LANES + channels, 0:channels] = conv_ref[tap // 3, tap % 3]
+            if tap % 3 == 2:
+                yield
 
     def norm(br):
         at = slice(br * SIDE, (br + 1) * SIDE)
@@ -273,8 +275,8 @@
 
     for br in range(blocks_r):
         norm(br)
-    weave([expand_bias(table_ref, padded, strip, bias), *[project(br) for br in range(blocks_r)]], 3)
-    weights()
+    tasks = [expand_bias(table_ref, padded, strip, bias), *[project(br) for br in range(blocks_r)]]
+    weave([*tasks, weights()], 3)
 
 
 def edge_kernel(
@@ -401,7 +403,7 @@
 
 
 def corner_kernel(
-    left_ref, right_ref, gain1_ref,
+    top_ref, bottom_ref, gain1_ref,
     bias, query, kv, wkv, wp, wc, w1, w2, g2, kv_edge, corner_base, out_mid, out_edge,
     out_hbm,
     normed, out_ref, sems,
@@ -437,12 +439,11 @@
 
     def project(pair):
         for i in (2 * pair, 2 * pair + 1):
-            ref = (left_ref, right_ref)[i % 2]
+            ref = (top_ref, bottom_ref)[i // 2]
             inside = (1.0 - out_row[i // 2]) * (1.0 - out_col[i % 2])
             mark = marks(channels, out_row[i // 2] + out_col[i % 2])
             normed[i, :, HALF:] = jnp.broadcast_to(mark, (AREA, HALF))
-            values = ref[i // 2 * SIDE : (i // 2 + 1) * SIDE].astype(F32)
-            values = unpack(values[:, :SIDE], values[:, SIDE:], i % 2 == 0, channels)
+            values = ref[...].astype(F32)[:, i % 2 * SIDE : (i % 2 + 1) * SIDE]
             normed[i, :, 0:channels] = layer_norm(values.reshape(AREA, channels), gain1 * inside)
         yield
         both = dot(normed[2 * pair : 2 * pair + 2].reshape(-1, LANES).astype(BF16), wkv[...])
@@ -539,8 +540,8 @@
         (image, gain1, table, qkv_weight),
         range(4),
     )
+    left, right = exchange(first_cols, last_cols, "col")
     top, bottom = exchange(first_rows, last_rows, "row")
-    left, right = exchange(first_cols, last_cols, "col")
     fetched = (gain2, proj_weight, conv_weight, fc1_weight, fc2)
     hidden = -(-fc1_weight.shape[1] // 128) * 128
     bias, query, kv, normed, wkv, wp, wc, w1, w2, g2 = call(
@@ -569,14 +570,9 @@
         (tile, gain1, table, qkv_weight, gain2, proj_weight, conv_weight, fc1_weight, fc2),
         range(4, 9),
     )
-    def ends(start, rest):
-        parts = [(start, start + SHIFT), (cols + rest, cols + rest + SHIFT)]
-        return jnp.concatenate(
-            [jnp.concatenate([x[:, a:b] for a, b in parts], axis=1) for x in (top, bottom)]
-        )
-
-    first, last = ends(0, 0), ends(cols - SHIFT, cols // 2 - SHIFT)
-    left_corner, right_corner = exchange(first, last, "col")
+    first = jnp.concatenate([left[:SHIFT], right[:SHIFT]], axis=1)
+    last = jnp.concatenate([left[rows - SHIFT :], right[rows - SHIFT :]], axis=1)
+    top_corner, bottom_corner = exchange(first, last, "row")
     kv_edge, corner_base, out_edge, out_mid = call(
         edge_kernel,
         "edge_windows",
@@ -600,7 +596,7 @@
         [jax.ShapeDtypeStruct(image.shape, BF16)],
         [((4, AREA, LANES), F32), (image.shape, BF16), pltpu.SemaphoreType.DMA((3,))],
         1_000_000_000,
-        (left_corner, right_corner, gain1, bias, query, kv, wkv, wp, wc, w1, w2, g2,
+        (top_corner, bottom_corner, gain1, bias, query, kv, wkv, wp, wc, w1, w2, g2,
          kv_edge, corner_base, out_mid, out_edge),
     )
     return out

time: 22.3 us -> 23.3 us (1.045)
  starting transfers between devices: 8.26 us -> 9.66 us
  Pallas kernels: 13.7 us -> 13.4 us
    ppermute x3, starting transfers between devices: 5.2 us -> 7.14 us  [exchange(): lax.ppermute(low, axis, [((i + 1) % count, i) for i in range(count)])]
    ppermute x3, starting transfers between devices: 3.05 us -> 2.53 us  [exchange(): lax.ppermute(high, axis, [(i, (i + 1) % count) for i in range(count)])]
    pallas_call x4, Pallas kernels: 13.7 us -> 13.4 us  [call(): pl.pallas_call(kernel, out_shape=[out if isinstance(out, jax.ShapeDtypeSt...]
  transfers between devices with their start and end apart: 6 -> 6, of which waited for: 0 -> 0; matrix products, arithmetic and copies ran while one was open for 0% -> 0% of each run, Pallas kernels for 40% -> 38%
where the time goes in v19:
time: 23.3 us; the launch traced here: 23.2 us
  Pallas kernels  13.4 us (58%)
  starting transfers between devices  9.66 us (41%)
    pallas_call x4, Pallas kernels, call(): pl.pallas_call(kernel, out_shape=[out if isinstance(out, jax.ShapeDtypeSt...  13.4 us
    ppermute x3, starting transfers between devices, exchange(): lax.ppermute(low, axis, [((i + 1) % count, i) for i in range(count)])  7.14 us
    ppermute x3, starting transfers between devices, exchange(): lax.ppermute(high, axis, [(i, (i + 1) % count) for i in range(count)])  2.53 us
  transfers between devices with their start and end apart: 6, of which 0 were waited for; matrix products, arithmetic and copies ran while one was open for 0% of the time, Pallas kernels for 38%

profile of v19, /device:TPU:0, one launch (start us, length us, event | category | flops | bytes accessed | tf_op | source)
XLA Modules:
  0.0 23.2 jit_solution(17059880197681121708)
XLA Ops:
  0.0 1.3 %cut_halo.1 = (bf16[32,32,180]{2,1,0:T(8,128)(2,1)S(1)}, f32[1,180]{1,0:T(1,128)S(1)}, f32[6,961]{1,0:T(8,128)S(1)}, bf16[180,540]{1,0:T(8,128)(2,1)S(1)}, bf16[...) custom-call(bf16[32,32,180]{2,1,0:T(8,128)(2,1)} %image_hbm.1, ...), custom_call_target="tpu_custom_call" | custom-call | flops 1000000 | bytes 4000000 | tf_op jit(solution)/shard_map/cut_halo/pallas_call | solution.py:513
  1.3 0.5 %collective-permute-start = (bf16[32,8,180]{2,1,0:T(8,128)(2,1)S(1)}, bf16[32,8,180]{2,1,0:T(8,128)(2,1)S(1)}, u32[]{:S(2)}, u32[]{:S(2)}) collective-permute-start(bf16[32,8,180]{2,1,0:T(8,128)(2,1)S(1)} %get-tuple-element.27), channel_id=1, source_target_pairs={{0,1},{1,2},{2,3},{3,4},{4,5},{5,6},{6,7},{7,0},{8,9},{9,10},{10,1... | collective-permute-start | bytes 276488 | tf_op jit(solution)/shard_map/ppermute | solution.py:505
  1.8 4.1 %collective-permute-start.1 = (bf16[32,8,180]{2,1,0:T(8,128)(2,1)S(1)}, bf16[32,8,180]{2,1,0:T(8,128)(2,1)S(1)}, u32[]{:S(2)}, u32[]{:S(2)}) collective-permute-start(bf16[32,8,180]{2,1,0:T(8,128)(2,1)S(1)} %get-tuple-element.28), channel_id=1, source_target_pairs={{1,0},{2,1},{3,2},{4,3},{5,4},{6,5},{7,6},{0,7},{9,8},{10,9},{11,1... | collective-permute-start | bytes 276488 | tf_op jit(solution)/shard_map/ppermute | solution.py:506
  5.9 1.9 %collective-permute-start.4 = (bf16[8,48,128]{2,1,0:T(8,128)(2,1)S(1)}, bf16[8,48,128]{2,1,0:T(8,128)(2,1)S(1)}, u32[]{:S(2)}, u32[]{:S(2)}) collective-permute-start(bf16[8,48,128]{2,1,0:T(8,128)(2,1)S(1)} %get-tuple-element.42), channel_id=1, source_target_pairs={{0,8},{8,16},{16,24},{24,0},{1,9},{9,17},{17,25},{25,1},{2,10},{10... | collective-permute-start | bytes 294920 | tf_op jit(solution)/shard_map/ppermute | solution.py:505
  7.9 1.0 %collective-permute-start.5 = (bf16[8,48,128]{2,1,0:T(8,128)(2,1)S(1)}, bf16[8,48,128]{2,1,0:T(8,128)(2,1)S(1)}, u32[]{:S(2)}, u32[]{:S(2)}) collective-permute-start(bf16[8,48,128]{2,1,0:T(8,128)(2,1)S(1)} %get-tuple-element.43), channel_id=1, source_target_pairs={{8,0},{16,8},{24,16},{0,24},{9,1},{17,9},{25,17},{1,25},{10,2},{18... | collective-permute-start | bytes 294920 | tf_op jit(solution)/shard_map/ppermute | solution.py:506
  8.9 3.2 %own_tile.1 = (f32[6,2,2,64,256]{4,3,2,1,0:T(8,128)S(1)}, bf16[4,4,64,256]{3,2,1,0:T(8,128)(2,1)S(1)}, bf16[4,4,64,512]{3,2,1,0:T(8,128)(2,1)S(1)}, f32[32,32,25...) custom-call(bf16[32,32,180]{2,1,0:T(8,128)(2,1)S(1)} %get-tuple-elem, ...), custom_call_target="tpu_custom_call" | custom-call | flops 2000000000 | bytes 4000000 | tf_op jit(solution)/shard_map/own_tile/pallas_call | solution.py:513
  12.1 0.0 collective-permute-done.left_ref
  12.1 0.0 collective-permute-done.1.right_ref
  12.1 2.0 %collective-permute-start.3 = (bf16[8,16,180]{2,1,0:T(8,128)(2,1)S(1)}, bf16[8,16,180]{2,1,0:T(8,128)(2,1)S(1)}, u32[]{:S(2)}, u32[]{:S(2)}) collective-permute-start(bf16[8,16,180]{2,1,0:T(8,128)(2,1)S(1)} %pad_maximum_fusion.1), channel_id=1, source_target_pairs={{8,0},{16,8},{24,16},{0,24},{9,1},{17,9},{25,17},{1,25},{10,2},{18... | collective-permute-start | bytes 138248 | tf_op jit(solution)/shard_map/ppermute | solution.py:506
  14.2 0.1 collective-permute-start.2
  14.3 0.0 collective-permute-done.4.top_ref
  14.3 0.0 collective-permute-done.5.bottom_ref
  14.3 5.5 %edge_windows.1 = (bf16[4,4,64,512]{3,2,1,0:T(8,128)(2,1)S(1)}, f32[4,64,256]{2,1,0:T(8,128)S(1)}, f32[2,256,256]{2,1,0:T(8,128)S(1)}, f32[256,256]{1,0:T(8,128)S(1)}) custom-call(bf16[32,32,180]{2,1,0:T(8,128)(2,1)S(1)} %get-tuple-element.30.image_ref, bf16[8,48,128]{2,1,0:T(8,128)(2,1)S(1)} %collective-permute-done.4.top_ref, ...), custom_call_target="tpu_custom_call" | custom-call | flops 2000000000 | bytes 4000000 | tf_op jit(solution)/shard_map/edge_windows/pallas_call | solution.py:513
  19.8 0.0 collective-permute-done.3.bottom_ref
  19.8 0.0 collective-permute-done.2.top_ref
  19.8 3.3 %corner_windows.1 = bf16[32,32,180]{2,1,0:T(8,128)(2,1)} custom-call(bf16[8,16,180]{2,1,0:T(8,128)(2,1)S(1)} %collective-permute-done.2.top_ref, bf16[8,16,180]{2,1,0:T(8,128)(2,1)S(1)} %collective-permute-done.3.bottom_ref, f32[1,180]{1,0:T(1,128)S(1)} %get-tuple-element.29.gain1_ref, f32[6,2,2,64,256]{4,3,2,1,0:T(8,128)S(1)} %get-tuple-element.33.bias, ...), custom_call_target="tpu_custom_call" | custom-call | flops 1000000000 | bytes 4000000 | tf_op jit(solution)/shard_map/corner_windows/pallas_call | solution.py:513
  (4 shorter events, 0.0 us)
Async XLA Ops:
  1.3 10.7 %collective-permute-start = (bf16[32,8,180]{2,1,0:T(8,128)(2,1)S(1)}, bf16[32,8,180]{2,1,0:T(8,128)(2,1)S(1)}, u32[]{:S(2)}, u32[]{:S(2)}) collective-permute-start(bf16[32,8,180]{2,1,0:T(8,128)(2,1)S(1)} %get-tuple-element.27), channel_id=1, source_target_pairs={{0,1},{1,2},{2,3},{3,4},{4,5},{5,6},{6,7},{7,0},{8,9},{9,10},{10,1... | collective-permute-start | bytes 276488 | tf_op jit(solution)/shard_map/ppermute | solution.py:505
  1.8 10.3 %collective-permute-start.1 = (bf16[32,8,180]{2,1,0:T(8,128)(2,1)S(1)}, bf16[32,8,180]{2,1,0:T(8,128)(2,1)S(1)}, u32[]{:S(2)}, u32[]{:S(2)}) collective-permute-start(bf16[32,8,180]{2,1,0:T(8,128)(2,1)S(1)} %get-tuple-element.28), channel_id=1, source_target_pairs={{1,0},{2,1},{3,2},{4,3},{5,4},{6,5},{7,6},{0,7},{9,8},{10,9},{11,1... | collective-permute-start | bytes 276488 | tf_op jit(solution)/shard_map/ppermute | solution.py:506
  5.9 8.3 %collective-permute-start.4 = (bf16[8,48,128]{2,1,0:T(8,128)(2,1)S(1)}, bf16[8,48,128]{2,1,0:T(8,128)(2,1)S(1)}, u32[]{:S(2)}, u32[]{:S(2)}) collective-permute-start(bf16[8,48,128]{2,1,0:T(8,128)(2,1)S(1)} %get-tuple-element.42), channel_id=1, source_target_pairs={{0,8},{8,16},{16,24},{24,0},{1,9},{9,17},{17,25},{25,1},{2,10},{10... | collective-permute-start | bytes 294920 | tf_op jit(solution)/shard_map/ppermute | solution.py:505
  7.9 6.4 %collective-permute-start.5 = (bf16[8,48,128]{2,1,0:T(8,128)(2,1)S(1)}, bf16[8,48,128]{2,1,0:T(8,128)(2,1)S(1)}, u32[]{:S(2)}, u32[]{:S(2)}) collective-permute-start(bf16[8,48,128]{2,1,0:T(8,128)(2,1)S(1)} %get-tuple-element.43), channel_id=1, source_target_pairs={{8,0},{16,8},{24,16},{0,24},{9,1},{17,9},{25,17},{1,25},{10,2},{18... | collective-permute-start | bytes 294920 | tf_op jit(solution)/shard_map/ppermute | solution.py:506
  12.1 7.7 %collective-permute-start.3 = (bf16[8,16,180]{2,1,0:T(8,128)(2,1)S(1)}, bf16[8,16,180]{2,1,0:T(8,128)(2,1)S(1)}, u32[]{:S(2)}, u32[]{:S(2)}) collective-permute-start(bf16[8,16,180]{2,1,0:T(8,128)(2,1)S(1)} %pad_maximum_fusion.1), channel_id=1, source_target_pairs={{8,0},{16,8},{24,16},{0,24},{9,1},{17,9},{25,17},{1,25},{10,2},{18... | collective-permute-start | bytes 138248 | tf_op jit(solution)/shard_map/ppermute | solution.py:506
  14.2 5.6 %collective-permute-start.2 = (bf16[8,16,180]{2,1,0:T(8,128)(2,1)S(1)}, bf16[8,16,180]{2,1,0:T(8,128)(2,1)S(1)}, u32[]{:S(2)}, u32[]{:S(2)}) collective-permute-start(bf16[8,16,180]{2,1,0:T(8,128)(2,1)S(1)} %pad_maximum_fusion), channel_id=1, source_target_pairs={{0,8},{8,16},{16,24},{24,0},{1,9},{9,17},{17,25},{25,1},{2,10},{10... | collective-permute-start | bytes 138248 | tf_op jit(solution)/shard_map/ppermute | solution.py:505

commit v20 on v18

--- a/solution.py
+++ b/solution.py
@@ -490,7 +490,13 @@
         return after(lambda: len(done) == 4, make)
 
     project()
-    weave([unit(0), unit(1), unit(2), unit(3), tail()], 2)
+    units = [unit(i) for i in range(4)]
+    next(units[0])
+    for i in range(4):
+        if i < 3:
+            next(units[i + 1])
+        weave([units[i]], 1)
+    weave([tail()], 1)
     writes[0].wait()
     for r in (0, rows - SIDE):
         at = slice(r, r + SIDE)

time: 22.2 us -> 22.1 us (level)
  no operation moved by 1% of the time
where the time goes in v20:
time: 22.1 us; the launch traced here: 21.9 us
  Pallas kernels  13.5 us (61%)
  starting transfers between devices  8.26 us (37%)
    pallas_call x4, Pallas kernels, call(): pl.pallas_call(kernel, out_shape=[out if isinstance(out, jax.ShapeDtypeSt...  13.5 us
    ppermute x3, starting transfers between devices, exchange(): lax.ppermute(low, axis, [((i + 1) % count, i) for i in range(count)])  5.21 us
    ppermute x3, starting transfers between devices, exchange(): lax.ppermute(high, axis, [(i, (i + 1) % count) for i in range(count)])  3.05 us
  transfers between devices with their start and end apart: 6, of which 0 were waited for; matrix products, arithmetic and copies ran while one was open for 0% of the time, Pallas kernels for 40%

profile of v20, /device:TPU:0, one launch (start us, length us, event | category | flops | bytes accessed | tf_op | source)
XLA Modules:
  0.0 21.9 jit_solution(7405190713930465991)
XLA Ops:
  0.0 1.3 %cut_halo.1 = (bf16[32,32,180]{2,1,0:T(8,128)(2,1)S(1)}, f32[1,180]{1,0:T(1,128)S(1)}, f32[6,961]{1,0:T(8,128)S(1)}, bf16[180,540]{1,0:T(8,128)(2,1)S(1)}, bf16[...) custom-call(bf16[32,32,180]{2,1,0:T(8,128)(2,1)} %image_hbm.1, ...), custom_call_target="tpu_custom_call" | custom-call | flops 1000000 | bytes 4000000 | tf_op jit(solution)/shard_map/cut_halo/pallas_call | solution.py:520
  1.3 3.0 %collective-permute-start = (bf16[8,48,128]{2,1,0:T(8,128)(2,1)S(1)}, bf16[8,48,128]{2,1,0:T(8,128)(2,1)S(1)}, u32[]{:S(2)}, u32[]{:S(2)}) collective-permute-start(bf16[8,48,128]{2,1,0:T(8,128)(2,1)S(1)} %get-tuple-element.27), channel_id=1, source_target_pairs={{0,8},{8,16},{16,24},{24,0},{1,9},{9,17},{17,25},{25,1},{2,10},{10... | collective-permute-start | bytes 294920 | tf_op jit(solution)/shard_map/ppermute | solution.py:512
  4.3 1.0 %collective-permute-start.1 = (bf16[8,48,128]{2,1,0:T(8,128)(2,1)S(1)}, bf16[8,48,128]{2,1,0:T(8,128)(2,1)S(1)}, u32[]{:S(2)}, u32[]{:S(2)}) collective-permute-start(bf16[8,48,128]{2,1,0:T(8,128)(2,1)S(1)} %get-tuple-element.28), channel_id=1, source_target_pairs={{8,0},{16,8},{24,16},{0,24},{9,1},{17,9},{25,17},{1,25},{10,2},{18... | collective-permute-start | bytes 294920 | tf_op jit(solution)/shard_map/ppermute | solution.py:513
  5.3 0.0 collective-permute-start.4
  5.3 3.5 %collective-permute-start.5 = (bf16[32,8,180]{2,1,0:T(8,128)(2,1)S(1)}, bf16[32,8,180]{2,1,0:T(8,128)(2,1)S(1)}, u32[]{:S(2)}, u32[]{:S(2)}) collective-permute-start(bf16[32,8,180]{2,1,0:T(8,128)(2,1)S(1)} %get-tuple-element.43), channel_id=1, source_target_pairs={{1,0},{2,1},{3,2},{4,3},{5,4},{6,5},{7,6},{0,7},{9,8},{10,9},{11,1... | collective-permute-start | bytes 276488 | tf_op jit(solution)/shard_map/ppermute | solution.py:513
  8.9 3.2 %own_tile.1 = (f32[6,2,2,64,256]{4,3,2,1,0:T(8,128)S(1)}, bf16[4,4,64,256]{3,2,1,0:T(8,128)(2,1)S(1)}, bf16[4,4,64,512]{3,2,1,0:T(8,128)(2,1)S(1)}, f32[32,32,25...) custom-call(bf16[32,32,180]{2,1,0:T(8,128)(2,1)S(1)} %get-tuple-elem, ...), custom_call_target="tpu_custom_call" | custom-call | flops 2000000000 | bytes 4000000 | tf_op jit(solution)/shard_map/own_tile/pallas_call | solution.py:520
  12.1 0.0 collective-permute-done.top_ref
  12.1 0.0 collective-permute-done.1.bottom_ref
  12.2 0.6 %collective-permute-start.3 = (bf16[16,16,128]{2,1,0:T(8,128)(2,1)S(1)}, bf16[16,16,128]{2,1,0:T(8,128)(2,1)S(1)}, u32[]{:S(2)}, u32[]{:S(2)}) collective-permute-start(bf16[16,16,128]{2,1,0:T(8,128)(2,1)S(1)} %maximum_maximum_fusion.1), channel_id=1, source_target_pairs={{1,0},{2,1},{3,2},{4,3},{5,4},{6,5},{7,6},{0,7},{9,8},{10,9},{11,1... | collective-permute-start | bytes 196616 | tf_op jit(solution)/shard_map/ppermute | solution.py:513
  12.8 0.1 collective-permute-start.2
  12.9 0.0 collective-permute-done.4.left_ref
  12.9 0.0 collective-permute-done.5.right_ref
  12.9 5.5 %edge_windows.1 = (bf16[4,4,64,512]{3,2,1,0:T(8,128)(2,1)S(1)}, f32[4,64,256]{2,1,0:T(8,128)S(1)}, f32[2,256,256]{2,1,0:T(8,128)S(1)}, f32[256,256]{1,0:T(8,128)S(1)}) custom-call(bf16[32,32,180]{2,1,0:T(8,128)(2,1)S(1)} %get-tuple-element.30.image_ref, bf16[8,48,128]{2,1,0:T(8,128)(2,1)S(1)} %collective-permute-done.top_ref, ...), custom_call_target="tpu_custom_call" | custom-call | flops 2000000000 | bytes 4000000 | tf_op jit(solution)/shard_map/edge_windows/pallas_call | solution.py:520
  18.5 0.0 collective-permute-done.3.right_ref
  18.5 0.0 collective-permute-done.2.left_ref
  18.5 3.5 %corner_windows.1 = bf16[32,32,180]{2,1,0:T(8,128)(2,1)} custom-call(bf16[16,16,128]{2,1,0:T(8,128)(2,1)S(1)} %collective-permute-done.2.left_ref, bf16[16,16,128]{2,1,0:T(8,128)(2,1)S(1)} %collective-permute-done.3.right_ref, f32[1,180]{1,0:T(1,128)S(1)} %get-tuple-element.29.gain1_ref, f32[6,2,2,64,256]{4,3,2,1,0:T(8,128)S(1)} %get-tuple-element.33.bias, ...), custom_call_target="tpu_custom_call" | custom-call | flops 1000000000 | bytes 4000000 | tf_op jit(solution)/shard_map/corner_windows/pallas_call | solution.py:520
  (4 shorter events, 0.1 us)
Async XLA Ops:
  1.3 10.8 %collective-permute-start = (bf16[8,48,128]{2,1,0:T(8,128)(2,1)S(1)}, bf16[8,48,128]{2,1,0:T(8,128)(2,1)S(1)}, u32[]{:S(2)}, u32[]{:S(2)}) collective-permute-start(bf16[8,48,128]{2,1,0:T(8,128)(2,1)S(1)} %get-tuple-element.27), channel_id=1, source_target_pairs={{0,8},{8,16},{16,24},{24,0},{1,9},{9,17},{17,25},{25,1},{2,10},{10... | collective-permute-start | bytes 294920 | tf_op jit(solution)/shard_map/ppermute | solution.py:512
  4.3 7.8 %collective-permute-start.1 = (bf16[8,48,128]{2,1,0:T(8,128)(2,1)S(1)}, bf16[8,48,128]{2,1,0:T(8,128)(2,1)S(1)}, u32[]{:S(2)}, u32[]{:S(2)}) collective-permute-start(bf16[8,48,128]{2,1,0:T(8,128)(2,1)S(1)} %get-tuple-element.28), channel_id=1, source_target_pairs={{8,0},{16,8},{24,16},{0,24},{9,1},{17,9},{25,17},{1,25},{10,2},{18... | collective-permute-start | bytes 294920 | tf_op jit(solution)/shard_map/ppermute | solution.py:513
  5.3 7.6 %collective-permute-start.4 = (bf16[32,8,180]{2,1,0:T(8,128)(2,1)S(1)}, bf16[32,8,180]{2,1,0:T(8,128)(2,1)S(1)}, u32[]{:S(2)}, u32[]{:S(2)}) collective-permute-start(bf16[32,8,180]{2,1,0:T(8,128)(2,1)S(1)} %get-tuple-element.42), channel_id=1, source_target_pairs={{0,1},{1,2},{2,3},{3,4},{4,5},{5,6},{6,7},{7,0},{8,9},{9,10},{10,1... | collective-permute-start | bytes 276488 | tf_op jit(solution)/shard_map/ppermute | solution.py:512
  5.3 7.6 %collective-permute-start.5 = (bf16[32,8,180]{2,1,0:T(8,128)(2,1)S(1)}, bf16[32,8,180]{2,1,0:T(8,128)(2,1)S(1)}, u32[]{:S(2)}, u32[]{:S(2)}) collective-permute-start(bf16[32,8,180]{2,1,0:T(8,128)(2,1)S(1)} %get-tuple-element.43), channel_id=1, source_target_pairs={{1,0},{2,1},{3,2},{4,3},{5,4},{6,5},{7,6},{0,7},{9,8},{10,9},{11,1... | collective-permute-start | bytes 276488 | tf_op jit(solution)/shard_map/ppermute | solution.py:513
  12.2 6.3 %collective-permute-start.3 = (bf16[16,16,128]{2,1,0:T(8,128)(2,1)S(1)}, bf16[16,16,128]{2,1,0:T(8,128)(2,1)S(1)}, u32[]{:S(2)}, u32[]{:S(2)}) collective-permute-start(bf16[16,16,128]{2,1,0:T(8,128)(2,1)S(1)} %maximum_maximum_fusion.1), channel_id=1, source_target_pairs={{1,0},{2,1},{3,2},{4,3},{5,4},{6,5},{7,6},{0,7},{9,8},{10,9},{11,1... | collective-permute-start | bytes 196616 | tf_op jit(solution)/shard_map/ppermute | solution.py:513
  12.8 5.6 %collective-permute-start.2 = (bf16[16,16,128]{2,1,0:T(8,128)(2,1)S(1)}, bf16[16,16,128]{2,1,0:T(8,128)(2,1)S(1)}, u32[]{:S(2)}, u32[]{:S(2)}) collective-permute-start(bf16[16,16,128]{2,1,0:T(8,128)(2,1)S(1)} %maximum_maximum_fusion), channel_id=1, source_target_pairs={{0,1},{1,2},{2,3},{3,4},{4,5},{5,6},{6,7},{7,0},{8,9},{9,10},{10,1... | collective-permute-start | bytes 196616 | tf_op jit(solution)/shard_map/ppermute | solution.py:512

commit v21 on v15

--- a/solution.py
+++ b/solution.py
@@ -207,15 +207,69 @@
 
 
 def own_kernel(
-    image_ref, gain1_ref, table_ref, qkv_ref, gain2_hbm, proj_hbm, conv_hbm, fc1_hbm, fc2_hbm,
-    bias, query, kv, normed, wkv, wp, wc, w1, w2, g2,
+    image_ref, gain1_ref, table_ref, qkv_ref,
+    bias, query, kv, normed, wkv,
     padded, strip, wq,
-    gain2_ref, proj_ref, conv_ref, fc1_ref, fc2_ref, sems,
 ):
     rows, cols, channels = image_ref.shape
     head_dim = channels // HEADS
     flag_lane, one_lane = channels, channels + 1
     blocks_r, blocks_c = rows // SIDE, cols // SIDE
+    for ref in (wq, wkv):
+        ref[...] = jnp.zeros_like(ref)
+    special = lax.broadcasted_iota(jnp.int32, (16, LANES), 0) + 176
+    lanes16 = lax.broadcasted_iota(jnp.int32, (16, LANES), 1)
+    wq[176:192, :] = one_hot((special == one_lane) & (lanes16 == flag_lane))
+    wkv[176:192, 0:LANES] = jnp.where(
+        (special == flag_lane) & (lanes16 == flag_lane), MASKED, 0.0
+    ).astype(BF16)
+    normed[:, :, HALF:] = jnp.broadcast_to(marks(channels, 0.0)[None], (rows, cols, HALF))
+
+    gain1 = gain1_ref[...]
+    scale = head_dim**-0.5 * LOG2E
+
+    wq[0:channels, 0:channels] = qkv_ref[:, 0:channels]
+    wkv[0:channels, 0:channels] = qkv_ref[:, channels : 2 * channels]
+    wkv[0:channels, LANES : LANES + channels] = qkv_ref[:, 2 * channels :]
+
+    def norm(br):
+        at = slice(br * SIDE, (br + 1) * SIDE)
+        normed[at, :, 0:channels] = layer_norm(image_ref[at].astype(F32), gain1)
+
+    def project(br):
+        pixels = normed[br * SIDE : (br + 1) * SIDE].astype(BF16).reshape(-1, LANES)
+        q = dot(pixels, wq[...])
+        yield
+        both = dot(pixels, wkv[...]).reshape(SIDE, cols, 2 * LANES)
+        q = (q * scale).reshape(SIDE, cols, LANES)
+        for bc in range(blocks_c):
+            part = slice(bc * SIDE, (bc + 1) * SIDE)
+            query[br, bc] = q[:, part].reshape(AREA, LANES).astype(BF16)
+        yield
+        for bc in range(blocks_c):
+            part = slice(bc * SIDE, (bc + 1) * SIDE)
+            kv[br, bc] = both[:, part].reshape(AREA, 2 * LANES).astype(BF16)
+
+    for br in range(blocks_r):
+        norm(br)
+    weave([expand_bias(table_ref, padded, strip, bias), *[project(br) for br in range(blocks_r)]], 3)
+
+
+def edge_kernel(
+    image_ref, top_ref, bottom_ref, left_ref, right_ref, gain1_ref,
+    bias, query, kv, normed, wkv, gain2_hbm, proj_hbm, conv_hbm, fc1_hbm, fc2_hbm,
+    kv_edge, corner_base, out_edge, out_mid, wp, wc, w1, w2, g2,
+    halo, base, shifted,
+    gain2_ref, proj_ref, conv_ref, fc1_ref, fc2_ref, sems,
+):
+    rows, cols, channels = image_ref.shape
+    head_dim = channels // HEADS
+    row, last_row = lax.axis_index("row"), lax.axis_size("row") - 1
+    col, last_col = lax.axis_index("col"), lax.axis_size("col") - 1
+    gain1 = gain1_ref[...]
+    outside = [(row == 0).astype(F32), (row == last_row).astype(F32),
+               (col == 0).astype(F32), (col == last_col).astype(F32)]
+
     fetches = [
         pltpu.make_async_copy(source, target, sems.at[i])
         for i, (source, target) in enumerate(
@@ -226,24 +280,12 @@
     for fetch in fetches:
         fetch.start()
 
-    for ref in (wq, wkv, wp, wc, w1, w2, g2):
-        ref[...] = jnp.zeros_like(ref)
-    special = lax.broadcasted_iota(jnp.int32, (16, LANES), 0) + 176
-    lanes16 = lax.broadcasted_iota(jnp.int32, (16, LANES), 1)
-    wq[176:192, :] = one_hot((special == one_lane) & (lanes16 == flag_lane))
-    wkv[176:192, 0:LANES] = jnp.where(
-        (special == flag_lane) & (lanes16 == flag_lane), MASKED, 0.0
-    ).astype(BF16)
-    normed[:, :, HALF:] = jnp.broadcast_to(marks(channels, 0.0)[None], (rows, cols, HALF))
-
-    gain1 = gain1_ref[...]
-    scale = head_dim**-0.5 * LOG2E
-
-    wq[0:channels, 0:channels] = qkv_ref[:, 0:channels]
-    wkv[0:channels, 0:channels] = qkv_ref[:, channels : 2 * channels]
-    wkv[0:channels, LANES : LANES + channels] = qkv_ref[:, 2 * channels :]
+    loaded = []
 
     def weights():
+        for ref in (wp, wc, w1, w2, g2):
+            ref[...] = jnp.zeros_like(ref)
+        yield
         for fetch in fetches:
             fetch.wait()
         wp[0:channels, 0:channels] = proj_ref[...]
@@ -252,44 +294,9 @@
         g2[:, 0:channels] = gain2_ref[...]
         for tap in range(9):
             wc[tap * LANES : tap * LANES + channels, 0:channels] = conv_ref[tap // 3, tap % 3]
-
-    def norm(br):
-        at = slice(br * SIDE, (br + 1) * SIDE)
-        normed[at, :, 0:channels] = layer_norm(image_ref[at].astype(F32), gain1)
-
-    def project(br):
-        pixels = normed[br * SIDE : (br + 1) * SIDE].astype(BF16).reshape(-1, LANES)
-        q = dot(pixels, wq[...])
-        yield
-        both = dot(pixels, wkv[...]).reshape(SIDE, cols, 2 * LANES)
-        q = (q * scale).reshape(SIDE, cols, LANES)
-        for bc in range(blocks_c):
-            part = slice(bc * SIDE, (bc + 1) * SIDE)
-            query[br, bc] = q[:, part].reshape(AREA, LANES).astype(BF16)
-        yield
-        for bc in range(blocks_c):
-            part = slice(bc * SIDE, (bc + 1) * SIDE)
-            kv[br, bc] = both[:, part].reshape(AREA, 2 * LANES).astype(BF16)
-
-    for br in range(blocks_r):
-        norm(br)
-    weave([expand_bias(table_ref, padded, strip, bias), *[project(br) for br in range(blocks_r)]], 3)
-    weights()
-
-
-def edge_kernel(
-    image_ref, top_ref, bottom_ref, left_ref, right_ref, gain1_ref,
-    bias, query, kv, normed, wkv, wp, wc, w1, w2, g2,
-    kv_edge, corner_base, out_edge, out_mid,
-    halo, base, shifted,
-):
-    rows, cols, channels = image_ref.shape
-    head_dim = channels // HEADS
-    row, last_row = lax.axis_index("row"), lax.axis_size("row") - 1
-    col, last_col = lax.axis_index("col"), lax.axis_size("col") - 1
-    gain1 = gain1_ref[...]
-    outside = [(row == 0).astype(F32), (row == last_row).astype(F32),
-               (col == 0).astype(F32), (col == last_col).astype(F32)]
+            if tap % 3 == 2:
+                yield
+        loaded.append(True)
 
     for r in (0, SHIFT + rows):
         for c in (0, SHIFT + cols):
@@ -393,9 +400,10 @@
 
         return after(lambda: i in done and i + 1 in done, make)
 
+    conv = lambda br: after(lambda: bool(loaded), lambda: convolve(br))
     weave(
-        [unit(4), band(0), band(1), unit(5), band(2), band(3), tile(), unit(0), convolve(0), unit(1),
-         convolve(1), unit(2), convolve(2), unit(3), convolve(3), tail(4), tail(0), tail(2)],
+        [unit(4), band(0), band(1), unit(5), band(2), band(3), weights(), tile(), unit(0), conv(0), unit(1),
+         conv(1), unit(2), conv(2), unit(3), conv(3), tail(4), tail(0), tail(2)],
         3,
     )
 
@@ -543,7 +551,7 @@
     left, right = exchange(first_cols, last_cols, "col")
     fetched = (gain2, proj_weight, conv_weight, fc1_weight, fc2)
     hidden = -(-fc1_weight.shape[1] // 128) * 128
-    bias, query, kv, normed, wkv, wp, wc, w1, w2, g2 = call(
+    bias, query, kv, normed, wkv = call(
         own_kernel,
         "own_tile",
         [
@@ -552,6 +560,31 @@
             ((blocks_r, blocks_c, AREA, 2 * LANES), BF16),
             ((rows, cols, LANES), F32),
             ((LANES, 2 * LANES), BF16),
+        ],
+        [
+            ((8, 1024), F32),
+            ((4, 8 * WIN, 128), F32),
+            ((LANES, LANES), BF16),
+        ],
+        2_000_000_000,
+        (tile, gain1, table, qkv_weight),
+    )
+    def ends(start, rest):
+        parts = [(start, start + SHIFT), (cols + rest, cols + rest + SHIFT)]
+        return jnp.concatenate(
+            [jnp.concatenate([x[:, a:b] for a, b in parts], axis=1) for x in (top, bottom)]
+        )
+
+    first, last = ends(0, 0), ends(cols - SHIFT, cols // 2 - SHIFT)
+    left_corner, right_corner = exchange(first, last, "col")
+    kv_edge, corner_base, out_edge, out_mid, wp, wc, w1, w2, g2 = call(
+        edge_kernel,
+        "edge_windows",
+        [
+            ((4, blocks_c, AREA, 2 * LANES), BF16),
+            ((4, AREA, LANES), F32),
+            ((2, 4 * AREA, LANES), F32),
+            ((4 * AREA, LANES), F32),
             ((LANES, LANES), BF16),
             ((9 * LANES, LANES), BF16),
             ((LANES, hidden), BF16),
@@ -559,40 +592,15 @@
             ((1, LANES), F32),
         ],
         [
-            ((8, 1024), F32),
-            ((4, 8 * WIN, 128), F32),
-            ((LANES, LANES), BF16),
+            ((rows + 2 * SHIFT, cols + 2 * SHIFT, LANES), F32),
+            ((blocks_r, blocks_c, AREA, LANES), F32),
+            ((3, rows + 2, cols, LANES), BF16),
             *[(x.shape, x.dtype) for x in fetched],
             pltpu.SemaphoreType.DMA((len(fetched),)),
         ],
         2_000_000_000,
-        (tile, gain1, table, qkv_weight, gain2, proj_weight, conv_weight, fc1_weight, fc2),
-        range(4, 9),
-    )
-    def ends(start, rest):
-        parts = [(start, start + SHIFT), (cols + rest, cols + rest + SHIFT)]
-        return jnp.concatenate(
-            [jnp.concatenate([x[:, a:b] for a, b in parts], axis=1) for x in (top, bottom)]
-        )
-
-    first, last = ends(0, 0), ends(cols - SHIFT, cols // 2 - SHIFT)
-    left_corner, right_corner = exchange(first, last, "col")
-    kv_edge, corner_base, out_edge, out_mid = call(
-        edge_kernel,
-        "edge_windows",
-        [
-            ((4, blocks_c, AREA, 2 * LANES), BF16),
-            ((4, AREA, LANES), F32),
-            ((2, 4 * AREA, LANES), F32),
-            ((4 * AREA, LANES), F32),
-        ],
-        [
-            ((rows + 2 * SHIFT, cols + 2 * SHIFT, LANES), F32),
-            ((blocks_r, blocks_c, AREA, LANES), F32),
-            ((3, rows + 2, cols, LANES), BF16),
-        ],
-        2_000_000_000,
-        (tile, top, bottom, left, right, gain1, bias, query, kv, normed, wkv, wp, wc, w1, w2, g2),
+        (tile, top, bottom, left, right, gain1, bias, query, kv, normed, wkv, *fetched),
+        range(11, 16),
     )
     (out,) = call(
         corner_kernel,

time: 22.3 us -> 23.2 us (1.040)
  starting transfers between devices: 8.26 us -> 9.31 us
    ppermute x3, starting transfers between devices: 5.2 us -> 6.25 us  [exchange(): lax.ppermute(low, axis, [((i + 1) % count, i) for i in range(count)])]
  transfers between devices with their start and end apart: 6 -> 6, of which waited for: 0 -> 0; matrix products, arithmetic and copies ran while one was open for 0% -> 0% of each run, Pallas kernels for 40% -> 38%
where the time goes in v21:
time: 23.2 us; the launch traced here: 23 us
  Pallas kernels  13.6 us (59%)
  starting transfers between devices  9.31 us (40%)
    pallas_call x4, Pallas kernels, call(): pl.pallas_call(kernel, out_shape=[out if isinstance(out, jax.ShapeDtypeSt...  13.6 us
    ppermute x3, starting transfers between devices, exchange(): lax.ppermute(low, axis, [((i + 1) % count, i) for i in range(count)])  6.25 us
    ppermute x3, starting transfers between devices, exchange(): lax.ppermute(high, axis, [(i, (i + 1) % count) for i in range(count)])  3.05 us
  transfers between devices with their start and end apart: 6, of which 0 were waited for; matrix products, arithmetic and copies ran while one was open for 0% of the time, Pallas kernels for 38%

profile of v21, /device:TPU:0, one launch (start us, length us, event | category | flops | bytes accessed | tf_op | source)
XLA Modules:
  0.0 23.0 jit_solution(14126750427167269620)
XLA Ops:
  0.0 1.3 %cut_halo.1 = (bf16[32,32,180]{2,1,0:T(8,128)(2,1)S(1)}, f32[1,180]{1,0:T(1,128)S(1)}, f32[6,961]{1,0:T(8,128)S(1)}, bf16[180,540]{1,0:T(8,128)(2,1)S(1)}, bf16[...) custom-call(bf16[32,32,180]{2,1,0:T(8,128)(2,1)} %image_hbm.1, ...), custom_call_target="tpu_custom_call" | custom-call | flops 1000000 | bytes 4000000 | tf_op jit(solution)/shard_map/cut_halo/pallas_call | solution.py:520
  1.3 3.0 %collective-permute-start = (bf16[8,48,128]{2,1,0:T(8,128)(2,1)S(1)}, bf16[8,48,128]{2,1,0:T(8,128)(2,1)S(1)}, u32[]{:S(2)}, u32[]{:S(2)}) collective-permute-start(bf16[8,48,128]{2,1,0:T(8,128)(2,1)S(1)} %get-tuple-element.27), channel_id=1, source_target_pairs={{0,8},{8,16},{16,24},{24,0},{1,9},{9,17},{17,25},{25,1},{2,10},{10... | collective-permute-start | bytes 294920 | tf_op jit(solution)/shard_map/ppermute | solution.py:512
  4.3 1.0 %collective-permute-start.1 = (bf16[8,48,128]{2,1,0:T(8,128)(2,1)S(1)}, bf16[8,48,128]{2,1,0:T(8,128)(2,1)S(1)}, u32[]{:S(2)}, u32[]{:S(2)}) collective-permute-start(bf16[8,48,128]{2,1,0:T(8,128)(2,1)S(1)} %get-tuple-element.28), channel_id=1, source_target_pairs={{8,0},{16,8},{24,16},{0,24},{9,1},{17,9},{25,17},{1,25},{10,2},{18... | collective-permute-start | bytes 294920 | tf_op jit(solution)/shard_map/ppermute | solution.py:513
  5.3 0.0 collective-permute-start.4
  5.3 3.5 %collective-permute-start.5 = (bf16[32,8,180]{2,1,0:T(8,128)(2,1)S(1)}, bf16[32,8,180]{2,1,0:T(8,128)(2,1)S(1)}, u32[]{:S(2)}, u32[]{:S(2)}) collective-permute-start(bf16[32,8,180]{2,1,0:T(8,128)(2,1)S(1)} %get-tuple-element.38), channel_id=1, source_target_pairs={{1,0},{2,1},{3,2},{4,3},{5,4},{6,5},{7,6},{0,7},{9,8},{10,9},{11,1... | collective-permute-start | bytes 276488 | tf_op jit(solution)/shard_map/ppermute | solution.py:513
  8.9 2.0 %own_tile.1 = (f32[6,2,2,64,256]{4,3,2,1,0:T(8,128)S(1)}, bf16[4,4,64,256]{3,2,1,0:T(8,128)(2,1)S(1)}, bf16[4,4,64,512]{3,2,1,0:T(8,128)(2,1)S(1)}, f32[32,32,256]{2,1,0:T(8,128)S(1)}, bf16[256,512]{1,0:T(8,128)(2,1)S(1)}) custom-call(bf16[32,32,180]{2,1,0:T(8,128)(2,1)S(1)} %get-tuple-element.30.image_ref, f32[1,180]{1,0:T(1,128)S(1)} %get-tuple-element.29.gain1_ref, ...), custom_call_target="tpu_custom_call" | custom-call | flops 2000000000 | bytes 4000000 | tf_op jit(solution)/shard_map/own_tile/pallas_call | solution.py:520
  10.9 0.0 collective-permute-done.top_ref
  10.9 0.0 collective-permute-done.1.bottom_ref
  11.0 1.7 %collective-permute-start.3 = (bf16[16,16,128]{2,1,0:T(8,128)(2,1)S(1)}, bf16[16,16,128]{2,1,0:T(8,128)(2,1)S(1)}, u32[]{:S(2)}, u32[]{:S(2)}) collective-permute-start(bf16[16,16,128]{2,1,0:T(8,128)(2,1)S(1)} %maximum_maximum_fusion.1), channel_id=1, source_target_pairs={{1,0},{2,1},{3,2},{4,3},{5,4},{6,5},{7,6},{0,7},{9,8},{10,9},{11,1... | collective-permute-start | bytes 196616 | tf_op jit(solution)/shard_map/ppermute | solution.py:513
  12.7 0.1 collective-permute-start.2
  12.8 0.0 collective-permute-done.4.left_ref
  12.8 0.0 collective-permute-done.5.right_ref
  12.8 6.8 %edge_windows.1 = (bf16[4,4,64,512]{3,2,1,0:T(8,128)(2,1)S(1)}, f32[4,64,256]{2,1,0:T(8,128)S(1)}, f32[2,256,256]{2,1,0:T(8,128)S(1)}, f32[256,256]{1,0:T(8,128)...) custom-call(bf16[32,32,180]{2,1,0:T(8,128)(2,1)S(1)} %get-tuple-elem, ...), custom_call_target="tpu_custom_call" | custom-call | flops 2000000000 | bytes 4000000 | tf_op jit(solution)/shard_map/edge_windows/pallas_call | solution.py:520
  19.6 0.0 collective-permute-done.3.right_ref
  19.6 0.0 collective-permute-done.2.left_ref
  19.6 3.5 %corner_windows.1 = bf16[32,32,180]{2,1,0:T(8,128)(2,1)} custom-call(bf16[16,16,128]{2,1,0:T(8,128)(2,1)S(1)} %collective-permute-done.2.left_ref, bf16[16,16,128]{2,1,0:T(8,128)(2,1)S(1)} %collective-permute-done.3.right_ref, f32[1,180]{1,0:T(1,128)S(1)} %get-tuple-element.29.gain1_ref, f32[6,2,2,64,256]{4,3,2,1,0:T(8,128)S(1)} %get-tuple-element.33.bias, ...), custom_call_target="tpu_custom_call" | custom-call | flops 1000000000 | bytes 4000000 | tf_op jit(solution)/shard_map/corner_windows/pallas_call | solution.py:520
  (4 shorter events, 0.1 us)
Async XLA Ops:
  1.3 9.6 %collective-permute-start = (bf16[8,48,128]{2,1,0:T(8,128)(2,1)S(1)}, bf16[8,48,128]{2,1,0:T(8,128)(2,1)S(1)}, u32[]{:S(2)}, u32[]{:S(2)}) collective-permute-start(bf16[8,48,128]{2,1,0:T(8,128)(2,1)S(1)} %get-tuple-element.27), channel_id=1, source_target_pairs={{0,8},{8,16},{16,24},{24,0},{1,9},{9,17},{17,25},{25,1},{2,10},{10... | collective-permute-start | bytes 294920 | tf_op jit(solution)/shard_map/ppermute | solution.py:512
  4.3 6.6 %collective-permute-start.1 = (bf16[8,48,128]{2,1,0:T(8,128)(2,1)S(1)}, bf16[8,48,128]{2,1,0:T(8,128)(2,1)S(1)}, u32[]{:S(2)}, u32[]{:S(2)}) collective-permute-start(bf16[8,48,128]{2,1,0:T(8,128)(2,1)S(1)} %get-tuple-element.28), channel_id=1, source_target_pairs={{8,0},{16,8},{24,16},{0,24},{9,1},{17,9},{25,17},{1,25},{10,2},{18... | collective-permute-start | bytes 294920 | tf_op jit(solution)/shard_map/ppermute | solution.py:513
  5.3 7.4 %collective-permute-start.4 = (bf16[32,8,180]{2,1,0:T(8,128)(2,1)S(1)}, bf16[32,8,180]{2,1,0:T(8,128)(2,1)S(1)}, u32[]{:S(2)}, u32[]{:S(2)}) collective-permute-start(bf16[32,8,180]{2,1,0:T(8,128)(2,1)S(1)} %get-tuple-element.37), channel_id=1, source_target_pairs={{0,1},{1,2},{2,3},{3,4},{4,5},{5,6},{6,7},{7,0},{8,9},{9,10},{10,1... | collective-permute-start | bytes 276488 | tf_op jit(solution)/shard_map/ppermute | solution.py:512
  5.3 7.4 %collective-permute-start.5 = (bf16[32,8,180]{2,1,0:T(8,128)(2,1)S(1)}, bf16[32,8,180]{2,1,0:T(8,128)(2,1)S(1)}, u32[]{:S(2)}, u32[]{:S(2)}) collective-permute-start(bf16[32,8,180]{2,1,0:T(8,128)(2,1)S(1)} %get-tuple-element.38), channel_id=1, source_target_pairs={{1,0},{2,1},{3,2},{4,3},{5,4},{6,5},{7,6},{0,7},{9,8},{10,9},{11,1... | collective-permute-start | bytes 276488 | tf_op jit(solution)/shard_map/ppermute | solution.py:513
  11.0 8.6 %collective-permute-start.3 = (bf16[16,16,128]{2,1,0:T(8,128)(2,1)S(1)}, bf16[16,16,128]{2,1,0:T(8,128)(2,1)S(1)}, u32[]{:S(2)}, u32[]{:S(2)}) collective-permute-start(bf16[16,16,128]{2,1,0:T(8,128)(2,1)S(1)} %maximum_maximum_fusion.1), channel_id=1, source_target_pairs={{1,0},{2,1},{3,2},{4,3},{5,4},{6,5},{7,6},{0,7},{9,8},{10,9},{11,1... | collective-permute-start | bytes 196616 | tf_op jit(solution)/shard_map/ppermute | solution.py:513
  12.7 6.9 %collective-permute-start.2 = (bf16[16,16,128]{2,1,0:T(8,128)(2,1)S(1)}, bf16[16,16,128]{2,1,0:T(8,128)(2,1)S(1)}, u32[]{:S(2)}, u32[]{:S(2)}) collective-permute-start(bf16[16,16,128]{2,1,0:T(8,128)(2,1)S(1)} %maximum_maximum_fusion), channel_id=1, source_target_pairs={{0,1},{1,2},{2,3},{3,4},{4,5},{5,6},{6,7},{7,0},{8,9},{9,10},{10,1... | collective-permute-start | bytes 196616 | tf_op jit(solution)/shard_map/ppermute | solution.py:512

commit v22 on v15

--- a/solution.py
+++ b/solution.py
@@ -39,13 +39,6 @@
     return values * lax.rsqrt(spread + 1e-05) * norm_gain
 
 
-def layer_norm_padded(values, norm_gain, channels):
-    centre = jnp.sum(values, axis=-1, keepdims=True) * (1.0 / channels)
-    values = jnp.where(lanes_of() < channels, values - centre, 0.0)
-    spread = jnp.sum(values * values, axis=-1, keepdims=True) * (1.0 / channels)
-    return values * lax.rsqrt(spread + 1e-05) * norm_gain
-
-
 def dot(a, b):
     return jnp.dot(a, b, preferred_element_type=F32)
 
@@ -151,14 +144,14 @@
 def finish(heads_out, base, wp, gain2, w1, w2, channels, put):
     attended = dot(heads_out, wp[...])
     yield
-    state1 = base() + attended.astype(BF16).astype(F32)
-    normed2 = layer_norm_padded(state1, gain2, channels).astype(BF16)
+    state1 = (base() + attended.astype(BF16).astype(F32))[:, :channels]
+    normed2 = layer_norm(state1, gain2).astype(BF16)
     yield
     hidden = dot(normed2, w1[...])
     yield
     hidden = gelu(hidden).astype(BF16)
     yield
-    put(state1 + dot(hidden, w2[...]))
+    put(state1 + dot_nt(hidden, w2[...]))
 
 
 def after(ready, make):
@@ -207,10 +200,10 @@
 
 
 def own_kernel(
-    image_ref, gain1_ref, table_ref, qkv_ref, gain2_hbm, proj_hbm, conv_hbm, fc1_hbm, fc2_hbm,
-    bias, query, kv, normed, wkv, wp, wc, w1, w2, g2,
+    image_ref, gain1_ref, table_ref, qkv_ref, proj_hbm, conv_hbm,
+    bias, query, kv, normed, wkv, wp, wc,
     padded, strip, wq,
-    gain2_ref, proj_ref, conv_ref, fc1_ref, fc2_ref, sems,
+    proj_ref, conv_ref, sems,
 ):
     rows, cols, channels = image_ref.shape
     head_dim = channels // HEADS
@@ -219,14 +212,13 @@
     fetches = [
         pltpu.make_async_copy(source, target, sems.at[i])
         for i, (source, target) in enumerate(
-            ((conv_hbm, conv_ref), (proj_hbm, proj_ref), (gain2_hbm, gain2_ref), (fc1_hbm, fc1_ref),
-             (fc2_hbm, fc2_ref))
+            ((conv_hbm, conv_ref), (proj_hbm, proj_ref))
         )
     ]
     for fetch in fetches:
         fetch.start()
 
-    for ref in (wq, wkv, wp, wc, w1, w2, g2):
+    for ref in (wq, wkv, wp, wc):
         ref[...] = jnp.zeros_like(ref)
     special = lax.broadcasted_iota(jnp.int32, (16, LANES), 0) + 176
     lanes16 = lax.broadcasted_iota(jnp.int32, (16, LANES), 1)
@@ -247,11 +239,10 @@
         for fetch in fetches:
             fetch.wait()
         wp[0:channels, 0:channels] = proj_ref[...]
-        w1[0:channels, 0 : fc1_ref.shape[1]] = fc1_ref[...]
-        w2[0 : fc2_ref.shape[1], 0:channels] = fc2_ref[...].astype(F32).T.astype(BF16)
-        g2[:, 0:channels] = gain2_ref[...]
         for tap in range(9):
             wc[tap * LANES : tap * LANES + channels, 0:channels] = conv_ref[tap // 3, tap % 3]
+            if tap % 3 == 2:
+                yield
 
     def norm(br):
         at = slice(br * SIDE, (br + 1) * SIDE)
@@ -273,8 +264,8 @@
 
     for br in range(blocks_r):
         norm(br)
-    weave([expand_bias(table_ref, padded, strip, bias), *[project(br) for br in range(blocks_r)]], 3)
-    weights()
+    tasks = [expand_bias(table_ref, padded, strip, bias), *[project(br) for br in range(blocks_r)]]
+    weave([*tasks, weights()], 3)
 
 
 def edge_kernel(
@@ -541,9 +532,8 @@
     )
     top, bottom = exchange(first_rows, last_rows, "row")
     left, right = exchange(first_cols, last_cols, "col")
-    fetched = (gain2, proj_weight, conv_weight, fc1_weight, fc2)
-    hidden = -(-fc1_weight.shape[1] // 128) * 128
-    bias, query, kv, normed, wkv, wp, wc, w1, w2, g2 = call(
+    fetched = (proj_weight, conv_weight)
+    bias, query, kv, normed, wkv, wp, wc = call(
         own_kernel,
         "own_tile",
         [
@@ -554,9 +544,6 @@
             ((LANES, 2 * LANES), BF16),
             ((LANES, LANES), BF16),
             ((9 * LANES, LANES), BF16),
-            ((LANES, hidden), BF16),
-            ((hidden, LANES), BF16),
-            ((1, LANES), F32),
         ],
         [
             ((8, 1024), F32),
@@ -566,8 +553,8 @@
             pltpu.SemaphoreType.DMA((len(fetched),)),
         ],
         2_000_000_000,
-        (tile, gain1, table, qkv_weight, gain2, proj_weight, conv_weight, fc1_weight, fc2),
-        range(4, 9),
+        (tile, gain1, table, qkv_weight, proj_weight, conv_weight),
+        range(4, 6),
     )
     def ends(start, rest):
         parts = [(start, start + SHIFT), (cols + rest, cols + rest + SHIFT)]
@@ -583,8 +570,8 @@
         [
             ((4, blocks_c, AREA, 2 * LANES), BF16),
             ((4, AREA, LANES), F32),
-            ((2, 4 * AREA, LANES), F32),
-            ((4 * AREA, LANES), F32),
+            ((2, 4 * AREA, channels), F32),
+            ((4 * AREA, channels), F32),
         ],
         [
             ((rows + 2 * SHIFT, cols + 2 * SHIFT, LANES), F32),
@@ -592,7 +579,7 @@
             ((3, rows + 2, cols, LANES), BF16),
         ],
         2_000_000_000,
-        (tile, top, bottom, left, right, gain1, bias, query, kv, normed, wkv, wp, wc, w1, w2, g2),
+        (tile, top, bottom, left, right, gain1, bias, query, kv, normed, wkv, wp, wc, fc1_weight, fc2, gain2),
     )
     (out,) = call(
         corner_kernel,
@@ -600,7 +587,7 @@
         [jax.ShapeDtypeStruct(image.shape, BF16)],
         [((4, AREA, LANES), F32), (image.shape, BF16), pltpu.SemaphoreType.DMA((3,))],
         1_000_000_000,
-        (left_corner, right_corner, gain1, bias, query, kv, wkv, wp, wc, w1, w2, g2,
+        (left_corner, right_corner, gain1, bias, query, kv, wkv, wp, wc, fc1_weight, fc2, gain2,
          kv_edge, corner_base, out_mid, out_edge),
     )
     return out

time: 22.3 us -> 21.8 us (0.978)
  Pallas kernels: 13.7 us -> 12.5 us
  starting transfers between devices: 8.26 us -> 8.69 us
  waiting for transfers between devices: 0.02 us -> 0.25 us
    pallas_call x4, Pallas kernels: 13.7 us -> 12.5 us  [call(): pl.pallas_call(kernel, out_shape=[out if isinstance(out, jax.ShapeDtypeSt...]
    ppermute x3, starting transfers between devices: 5.2 us -> 5.64 us  [exchange(): lax.ppermute(low, axis, [((i + 1) % count, i) for i in range(count)])]
    ppermute x3, waiting for transfers between devices: 0.01 us -> 0.24 us  [exchange(): lax.ppermute(high, axis, [(i, (i + 1) % count) for i in range(count)])]
  transfers between devices with their start and end apart: 6 -> 6, of which waited for: 0 -> 1; matrix products, arithmetic and copies ran while one was open for 0% -> 0% of each run, Pallas kernels for 40% -> 36%
where the time goes in v22:
time: 21.8 us; the launch traced here: 21.7 us
  Pallas kernels  12.5 us (57%)
  starting transfers between devices  8.69 us (40%)
  waiting for transfers between devices  0.25 us (1%)
    pallas_call x4, Pallas kernels, call(): pl.pallas_call(kernel, out_shape=[out if isinstance(out, jax.ShapeDtypeSt...  12.5 us
    ppermute x3, starting transfers between devices, exchange(): lax.ppermute(low, axis, [((i + 1) % count, i) for i in range(count)])  5.64 us
    ppermute x3, starting transfers between devices, exchange(): lax.ppermute(high, axis, [(i, (i + 1) % count) for i in range(count)])  3.05 us
  transfers between devices with their start and end apart: 6, of which 1 were waited for; matrix products, arithmetic and copies ran while one was open for 0% of the time, Pallas kernels for 36%

profile of v22, /device:TPU:0, one launch (start us, length us, event | category | flops | bytes accessed | tf_op | source)
XLA Modules:
  0.0 21.7 jit_solution(15283788686998734192)
XLA Ops:
  0.0 1.3 %cut_halo.1 = (bf16[32,32,180]{2,1,0:T(8,128)(2,1)S(1)}, f32[1,180]{1,0:T(1,128)S(1)}, f32[6,961]{1,0:T(8,128)S(1)}, bf16[180,540]{1,0:T(8,128)(2,1)S(1)}, bf16[...) custom-call(bf16[32,32,180]{2,1,0:T(8,128)(2,1)} %image_hbm.1, ...), custom_call_target="tpu_custom_call" | custom-call | flops 1000000 | bytes 4000000 | tf_op jit(solution)/shard_map/cut_halo/pallas_call | solution.py:503
  1.3 3.0 %collective-permute-start = (bf16[8,48,128]{2,1,0:T(8,128)(2,1)S(1)}, bf16[8,48,128]{2,1,0:T(8,128)(2,1)S(1)}, u32[]{:S(2)}, u32[]{:S(2)}) collective-permute-start(bf16[8,48,128]{2,1,0:T(8,128)(2,1)S(1)} %get-tuple-element.24), channel_id=1, source_target_pairs={{0,8},{8,16},{16,24},{24,0},{1,9},{9,17},{17,25},{25,1},{2,10},{10... | collective-permute-start | bytes 294920 | tf_op jit(solution)/shard_map/ppermute | solution.py:495
  4.3 1.0 %collective-permute-start.1 = (bf16[8,48,128]{2,1,0:T(8,128)(2,1)S(1)}, bf16[8,48,128]{2,1,0:T(8,128)(2,1)S(1)}, u32[]{:S(2)}, u32[]{:S(2)}) collective-permute-start(bf16[8,48,128]{2,1,0:T(8,128)(2,1)S(1)} %get-tuple-element.25), channel_id=1, source_target_pairs={{8,0},{16,8},{24,16},{0,24},{9,1},{17,9},{25,17},{1,25},{10,2},{18... | collective-permute-start | bytes 294920 | tf_op jit(solution)/shard_map/ppermute | solution.py:496
  5.3 0.0 collective-permute-start.4
  5.3 3.5 %collective-permute-start.5 = (bf16[32,8,180]{2,1,0:T(8,128)(2,1)S(1)}, bf16[32,8,180]{2,1,0:T(8,128)(2,1)S(1)}, u32[]{:S(2)}, u32[]{:S(2)}) collective-permute-start(bf16[32,8,180]{2,1,0:T(8,128)(2,1)S(1)} %get-tuple-element.37), channel_id=1, source_target_pairs={{1,0},{2,1},{3,2},{4,3},{5,4},{6,5},{7,6},{0,7},{9,8},{10,9},{11,1... | collective-permute-start | bytes 276488 | tf_op jit(solution)/shard_map/ppermute | solution.py:496
  8.9 0.0 copy-start
  8.9 0.0 copy-start.1
  8.9 0.0 copy-start.2
  8.9 2.6 %own_tile.1 = (f32[6,2,2,64,256]{4,3,2,1,0:T(8,128)S(1)}, bf16[4,4,64,256]{3,2,1,0:T(8,128)(2,1)S(1)}, bf16[4,4,64,512]{3,2,1,0:T(8,128)(2,1)S(1)}, f32[32,32,25...) custom-call(bf16[32,32,180]{2,1,0:T(8,128)(2,1)S(1)} %get-tuple-elem, ...), custom_call_target="tpu_custom_call" | custom-call | flops 2000000000 | bytes 4000000 | tf_op jit(solution)/shard_map/own_tile/pallas_call | solution.py:503
  11.5 0.0 collective-permute-done.top_ref
  11.6 0.0 collective-permute-done.1.bottom_ref
  11.6 1.1 %collective-permute-start.3 = (bf16[16,16,128]{2,1,0:T(8,128)(2,1)S(1)}, bf16[16,16,128]{2,1,0:T(8,128)(2,1)S(1)}, u32[]{:S(2)}, u32[]{:S(2)}) collective-permute-start(bf16[16,16,128]{2,1,0:T(8,128)(2,1)S(1)} %maximum_maximum_fusion.1), channel_id=1, source_target_pairs={{1,0},{2,1},{3,2},{4,3},{5,4},{6,5},{7,6},{0,7},{9,8},{10,9},{11,1... | collective-permute-start | bytes 196616 | tf_op jit(solution)/shard_map/ppermute | solution.py:496
  12.7 0.1 collective-permute-start.2
  12.8 0.0 collective-permute-done.4.left_ref
  12.8 0.0 collective-permute-done.5.right_ref
  12.8 0.0 copy-done
  12.8 0.0 copy-done.1
  12.8 0.0 copy-done.2
  12.8 5.2 %edge_windows.1 = (bf16[4,4,64,512]{3,2,1,0:T(8,128)(2,1)S(1)}, f32[4,64,256]{2,1,0:T(8,128)S(1)}, f32[2,256,180]{2,1,0:T(8,128)S(1)}, f32[256,180]{1,0:T(8,128)S(1)}) custom-call(bf16[32,32,180]{2,1,0:T(8,128)(2,1)S(1)} %get-tuple-element.27.image_ref, bf16[8,48,128]{2,1,0:T(8,128)(2,1)S(1)} %collective-permute-done.top_ref, ...), custom_call_target="tpu_custom_call" | custom-call | flops 2000000000 | bytes 4000000 | tf_op jit(solution)/shard_map/edge_windows/pallas_call | solution.py:503
  18.0 0.0 collective-permute-done.3.right_ref
  18.0 0.2 %collective-permute-done.2.left_ref = bf16[16,16,128]{2,1,0:T(8,128)(2,1)S(1)} collective-permute-done((bf16[16,16,128]{2,1,0:T(8,128)(2,1)S(1)}, bf16[16,16,128]{2,1,0:T(8,128)(2,1)S(1)}, u32[]{:S(2)}, u32[]{:S(2)}) %collective-permute-start.2) | collective-permute-done | bytes 65568 | tf_op jit(solution)/shard_map/ppermute | solution.py:495
  18.2 3.4 %corner_windows.1 = bf16[32,32,180]{2,1,0:T(8,128)(2,1)} custom-call(bf16[16,16,128]{2,1,0:T(8,128)(2,1)S(1)} %collective-permute-done.2.left_ref, bf16[16,16,128]{2,1,0:T(8,128)(2,1)S(1)} %collective-permute-done.3.right_ref, f32[1,180]{1,0:T(1,128)S(1)} %get-tuple-element.26.gain1_ref, f32[6,2,2,64,256]{4,3,2,1,0:T(8,128)S(1)} %get-tuple-element.30.bias, ...), custom_call_target="tpu_custom_call" | custom-call | flops 1000000000 | bytes 4000000 | tf_op jit(solution)/shard_map/corner_windows/pallas_call | solution.py:503
  (4 shorter events, 0.1 us)
Async XLA Ops:
  1.3 10.2 %collective-permute-start = (bf16[8,48,128]{2,1,0:T(8,128)(2,1)S(1)}, bf16[8,48,128]{2,1,0:T(8,128)(2,1)S(1)}, u32[]{:S(2)}, u32[]{:S(2)}) collective-permute-start(bf16[8,48,128]{2,1,0:T(8,128)(2,1)S(1)} %get-tuple-element.24), channel_id=1, source_target_pairs={{0,8},{8,16},{16,24},{24,0},{1,9},{9,17},{17,25},{25,1},{2,10},{10... | collective-permute-start | bytes 294920 | tf_op jit(solution)/shard_map/ppermute | solution.py:495
  4.3 7.2 %collective-permute-start.1 = (bf16[8,48,128]{2,1,0:T(8,128)(2,1)S(1)}, bf16[8,48,128]{2,1,0:T(8,128)(2,1)S(1)}, u32[]{:S(2)}, u32[]{:S(2)}) collective-permute-start(bf16[8,48,128]{2,1,0:T(8,128)(2,1)S(1)} %get-tuple-element.25), channel_id=1, source_target_pairs={{8,0},{16,8},{24,16},{0,24},{9,1},{17,9},{25,17},{1,25},{10,2},{18... | collective-permute-start | bytes 294920 | tf_op jit(solution)/shard_map/ppermute | solution.py:496
  5.3 7.4 %collective-permute-start.4 = (bf16[32,8,180]{2,1,0:T(8,128)(2,1)S(1)}, bf16[32,8,180]{2,1,0:T(8,128)(2,1)S(1)}, u32[]{:S(2)}, u32[]{:S(2)}) collective-permute-start(bf16[32,8,180]{2,1,0:T(8,128)(2,1)S(1)} %get-tuple-element.36), channel_id=1, source_target_pairs={{0,1},{1,2},{2,3},{3,4},{4,5},{5,6},{6,7},{7,0},{8,9},{9,10},{10,1... | collective-permute-start | bytes 276488 | tf_op jit(solution)/shard_map/ppermute | solution.py:495
  5.3 7.4 %collective-permute-start.5 = (bf16[32,8,180]{2,1,0:T(8,128)(2,1)S(1)}, bf16[32,8,180]{2,1,0:T(8,128)(2,1)S(1)}, u32[]{:S(2)}, u32[]{:S(2)}) collective-permute-start(bf16[32,8,180]{2,1,0:T(8,128)(2,1)S(1)} %get-tuple-element.37), channel_id=1, source_target_pairs={{1,0},{2,1},{3,2},{4,3},{5,4},{6,5},{7,6},{0,7},{9,8},{10,9},{11,1... | collective-permute-start | bytes 276488 | tf_op jit(solution)/shard_map/ppermute | solution.py:496
  8.9 3.9 %copy-start = (bf16[180,360]{1,0:T(8,128)(2,1)S(1)}, bf16[180,360]{1,0:T(8,128)(2,1)}, u32[]{:S(2)}) copy-start(bf16[180,360]{1,0:T(8,128)(2,1)} %w1.3) | copy-start | bytes 388804
  8.9 3.9 %copy-start.1 = (bf16[360,180]{0,1:T(8,128)(2,1)S(1)}, bf16[360,180]{0,1:T(8,128)(2,1)}, u32[]{:S(2)}) copy-start(bf16[360,180]{0,1:T(8,128)(2,1)} %param.17) | copy-start | bytes 388804
  8.9 3.9 %copy-start.2 = (f32[180]{0:T(256)S(1)}, f32[180]{0:T(256)}, u32[]{:S(2)}) copy-start(f32[180]{0:T(256)} %param.11) | copy-start | bytes 2164
  11.6 6.4 %collective-permute-start.3 = (bf16[16,16,128]{2,1,0:T(8,128)(2,1)S(1)}, bf16[16,16,128]{2,1,0:T(8,128)(2,1)S(1)}, u32[]{:S(2)}, u32[]{:S(2)}) collective-permute-start(bf16[16,16,128]{2,1,0:T(8,128)(2,1)S(1)} %maximum_maximum_fusion.1), channel_id=1, source_target_pairs={{1,0},{2,1},{3,2},{4,3},{5,4},{6,5},{7,6},{0,7},{9,8},{10,9},{11,1... | collective-permute-start | bytes 196616 | tf_op jit(solution)/shard_map/ppermute | solution.py:496
  12.7 5.5 %collective-permute-start.2 = (bf16[16,16,128]{2,1,0:T(8,128)(2,1)S(1)}, bf16[16,16,128]{2,1,0:T(8,128)(2,1)S(1)}, u32[]{:S(2)}, u32[]{:S(2)}) collective-permute-start(bf16[16,16,128]{2,1,0:T(8,128)(2,1)S(1)} %maximum_maximum_fusion), channel_id=1, source_target_pairs={{0,1},{1,2},{2,3},{3,4},{4,5},{5,6},{6,7},{7,0},{8,9},{9,10},{10,1... | collective-permute-start | bytes 196616 | tf_op jit(solution)/shard_map/ppermute | solution.py:495

commit v23 on v22

--- a/solution.py
+++ b/solution.py
@@ -219,7 +219,11 @@
         fetch.start()
 
     for ref in (wq, wkv, wp, wc):
-        ref[...] = jnp.zeros_like(ref)
+        for r in range(0, ref.shape[0], LANES):
+            edge = slice(r + channels // 16 * 16, r + LANES)
+            ref[edge] = jnp.zeros_like(ref[edge])
+        for c in range(HALF, ref.shape[1], LANES):
+            ref[:, c : c + HALF] = jnp.zeros((ref.shape[0], HALF), BF16)
     special = lax.broadcasted_iota(jnp.int32, (16, LANES), 0) + 176
     lanes16 = lax.broadcasted_iota(jnp.int32, (16, LANES), 1)
     wq[176:192, :] = one_hot((special == one_lane) & (lanes16 == flag_lane))

time: 21.8 us -> 21.8 us (level)
  no operation moved by 1% of the time
where the time goes in v23:
time: 21.8 us; the launch traced here: 21.7 us
  Pallas kernels  12.6 us (58%)
  starting transfers between devices  8.58 us (39%)
  waiting for transfers between devices  0.25 us (1%)
    pallas_call x4, Pallas kernels, call(): pl.pallas_call(kernel, out_shape=[out if isinstance(out, jax.ShapeDtypeSt...  12.6 us
    ppermute x3, starting transfers between devices, exchange(): lax.ppermute(low, axis, [((i + 1) % count, i) for i in range(count)])  5.53 us
    ppermute x3, starting transfers between devices, exchange(): lax.ppermute(high, axis, [(i, (i + 1) % count) for i in range(count)])  3.05 us
  transfers between devices with their start and end apart: 6, of which 1 were waited for; matrix products, arithmetic and copies ran while one was open for 0% of the time, Pallas kernels for 36%

profile of v23, /device:TPU:0, one launch (start us, length us, event | category | flops | bytes accessed | tf_op | source)
XLA Modules:
  0.0 21.7 jit_solution(17985790604759586970)
XLA Ops:
  0.0 1.3 %cut_halo.1 = (bf16[32,32,180]{2,1,0:T(8,128)(2,1)S(1)}, f32[1,180]{1,0:T(1,128)S(1)}, f32[6,961]{1,0:T(8,128)S(1)}, bf16[180,540]{1,0:T(8,128)(2,1)S(1)}, bf16[...) custom-call(bf16[32,32,180]{2,1,0:T(8,128)(2,1)} %image_hbm.1, ...), custom_call_target="tpu_custom_call" | custom-call | flops 1000000 | bytes 4000000 | tf_op jit(solution)/shard_map/cut_halo/pallas_call | solution.py:507
  1.3 3.0 %collective-permute-start = (bf16[8,48,128]{2,1,0:T(8,128)(2,1)S(1)}, bf16[8,48,128]{2,1,0:T(8,128)(2,1)S(1)}, u32[]{:S(2)}, u32[]{:S(2)}) collective-permute-start(bf16[8,48,128]{2,1,0:T(8,128)(2,1)S(1)} %get-tuple-element.24), channel_id=1, source_target_pairs={{0,8},{8,16},{16,24},{24,0},{1,9},{9,17},{17,25},{25,1},{2,10},{10... | collective-permute-start | bytes 294920 | tf_op jit(solution)/shard_map/ppermute | solution.py:499
  4.3 1.0 %collective-permute-start.1 = (bf16[8,48,128]{2,1,0:T(8,128)(2,1)S(1)}, bf16[8,48,128]{2,1,0:T(8,128)(2,1)S(1)}, u32[]{:S(2)}, u32[]{:S(2)}) collective-permute-start(bf16[8,48,128]{2,1,0:T(8,128)(2,1)S(1)} %get-tuple-element.25), channel_id=1, source_target_pairs={{8,0},{16,8},{24,16},{0,24},{9,1},{17,9},{25,17},{1,25},{10,2},{18... | collective-permute-start | bytes 294920 | tf_op jit(solution)/shard_map/ppermute | solution.py:500
  5.3 0.0 collective-permute-start.4
  5.3 3.5 %collective-permute-start.5 = (bf16[32,8,180]{2,1,0:T(8,128)(2,1)S(1)}, bf16[32,8,180]{2,1,0:T(8,128)(2,1)S(1)}, u32[]{:S(2)}, u32[]{:S(2)}) collective-permute-start(bf16[32,8,180]{2,1,0:T(8,128)(2,1)S(1)} %get-tuple-element.37), channel_id=1, source_target_pairs={{1,0},{2,1},{3,2},{4,3},{5,4},{6,5},{7,6},{0,7},{9,8},{10,9},{11,1... | collective-permute-start | bytes 276488 | tf_op jit(solution)/shard_map/ppermute | solution.py:500
  8.9 0.0 copy-start
  8.9 0.0 copy-start.1
  8.9 0.0 copy-start.2
  8.9 2.7 %own_tile.1 = (f32[6,2,2,64,256]{4,3,2,1,0:T(8,128)S(1)}, bf16[4,4,64,256]{3,2,1,0:T(8,128)(2,1)S(1)}, bf16[4,4,64,512]{3,2,1,0:T(8,128)(2,1)S(1)}, f32[32,32,25...) custom-call(bf16[32,32,180]{2,1,0:T(8,128)(2,1)S(1)} %get-tuple-elem, ...), custom_call_target="tpu_custom_call" | custom-call | flops 2000000000 | bytes 4000000 | tf_op jit(solution)/shard_map/own_tile/pallas_call | solution.py:507
  11.6 0.0 collective-permute-done.top_ref
  11.7 0.0 collective-permute-done.1.bottom_ref
  11.7 1.0 %collective-permute-start.3 = (bf16[16,16,128]{2,1,0:T(8,128)(2,1)S(1)}, bf16[16,16,128]{2,1,0:T(8,128)(2,1)S(1)}, u32[]{:S(2)}, u32[]{:S(2)}) collective-permute-start(bf16[16,16,128]{2,1,0:T(8,128)(2,1)S(1)} %maximum_maximum_fusion.1), channel_id=1, source_target_pairs={{1,0},{2,1},{3,2},{4,3},{5,4},{6,5},{7,6},{0,7},{9,8},{10,9},{11,1... | collective-permute-start | bytes 196616 | tf_op jit(solution)/shard_map/ppermute | solution.py:500
  12.7 0.1 collective-permute-start.2
  12.8 0.0 collective-permute-done.4.left_ref
  12.8 0.0 collective-permute-done.5.right_ref
  12.8 0.0 copy-done
  12.8 0.0 copy-done.1
  12.8 0.0 copy-done.2
  12.8 5.2 %edge_windows.1 = (bf16[4,4,64,512]{3,2,1,0:T(8,128)(2,1)S(1)}, f32[4,64,256]{2,1,0:T(8,128)S(1)}, f32[2,256,180]{2,1,0:T(8,128)S(1)}, f32[256,180]{1,0:T(8,128)S(1)}) custom-call(bf16[32,32,180]{2,1,0:T(8,128)(2,1)S(1)} %get-tuple-element.27.image_ref, bf16[8,48,128]{2,1,0:T(8,128)(2,1)S(1)} %collective-permute-done.top_ref, ...), custom_call_target="tpu_custom_call" | custom-call | flops 2000000000 | bytes 4000000 | tf_op jit(solution)/shard_map/edge_windows/pallas_call | solution.py:507
  18.0 0.0 collective-permute-done.3.right_ref
  18.0 0.2 %collective-permute-done.2.left_ref = bf16[16,16,128]{2,1,0:T(8,128)(2,1)S(1)} collective-permute-done((bf16[16,16,128]{2,1,0:T(8,128)(2,1)S(1)}, bf16[16,16,128]{2,1,0:T(8,128)(2,1)S(1)}, u32[]{:S(2)}, u32[]{:S(2)}) %collective-permute-start.2) | collective-permute-done | bytes 65568 | tf_op jit(solution)/shard_map/ppermute | solution.py:499
  18.2 3.4 %corner_windows.1 = bf16[32,32,180]{2,1,0:T(8,128)(2,1)} custom-call(bf16[16,16,128]{2,1,0:T(8,128)(2,1)S(1)} %collective-permute-done.2.left_ref, bf16[16,16,128]{2,1,0:T(8,128)(2,1)S(1)} %collective-permute-done.3.right_ref, f32[1,180]{1,0:T(1,128)S(1)} %get-tuple-element.26.gain1_ref, f32[6,2,2,64,256]{4,3,2,1,0:T(8,128)S(1)} %get-tuple-element.30.bias, ...), custom_call_target="tpu_custom_call" | custom-call | flops 1000000000 | bytes 4000000 | tf_op jit(solution)/shard_map/corner_windows/pallas_call | solution.py:507
  (4 shorter events, 0.1 us)
Async XLA Ops:
  1.3 10.3 %collective-permute-start = (bf16[8,48,128]{2,1,0:T(8,128)(2,1)S(1)}, bf16[8,48,128]{2,1,0:T(8,128)(2,1)S(1)}, u32[]{:S(2)}, u32[]{:S(2)}) collective-permute-start(bf16[8,48,128]{2,1,0:T(8,128)(2,1)S(1)} %get-tuple-element.24), channel_id=1, source_target_pairs={{0,8},{8,16},{16,24},{24,0},{1,9},{9,17},{17,25},{25,1},{2,10},{10... | collective-permute-start | bytes 294920 | tf_op jit(solution)/shard_map/ppermute | solution.py:499
  4.3 7.3 %collective-permute-start.1 = (bf16[8,48,128]{2,1,0:T(8,128)(2,1)S(1)}, bf16[8,48,128]{2,1,0:T(8,128)(2,1)S(1)}, u32[]{:S(2)}, u32[]{:S(2)}) collective-permute-start(bf16[8,48,128]{2,1,0:T(8,128)(2,1)S(1)} %get-tuple-element.25), channel_id=1, source_target_pairs={{8,0},{16,8},{24,16},{0,24},{9,1},{17,9},{25,17},{1,25},{10,2},{18... | collective-permute-start | bytes 294920 | tf_op jit(solution)/shard_map/ppermute | solution.py:500
  5.3 7.4 %collective-permute-start.4 = (bf16[32,8,180]{2,1,0:T(8,128)(2,1)S(1)}, bf16[32,8,180]{2,1,0:T(8,128)(2,1)S(1)}, u32[]{:S(2)}, u32[]{:S(2)}) collective-permute-start(bf16[32,8,180]{2,1,0:T(8,128)(2,1)S(1)} %get-tuple-element.36), channel_id=1, source_target_pairs={{0,1},{1,2},{2,3},{3,4},{4,5},{5,6},{6,7},{7,0},{8,9},{9,10},{10,1... | collective-permute-start | bytes 276488 | tf_op jit(solution)/shard_map/ppermute | solution.py:499
  5.3 7.4 %collective-permute-start.5 = (bf16[32,8,180]{2,1,0:T(8,128)(2,1)S(1)}, bf16[32,8,180]{2,1,0:T(8,128)(2,1)S(1)}, u32[]{:S(2)}, u32[]{:S(2)}) collective-permute-start(bf16[32,8,180]{2,1,0:T(8,128)(2,1)S(1)} %get-tuple-element.37), channel_id=1, source_target_pairs={{1,0},{2,1},{3,2},{4,3},{5,4},{6,5},{7,6},{0,7},{9,8},{10,9},{11,1... | collective-permute-start | bytes 276488 | tf_op jit(solution)/shard_map/ppermute | solution.py:500
  8.9 3.9 %copy-start = (bf16[180,360]{1,0:T(8,128)(2,1)S(1)}, bf16[180,360]{1,0:T(8,128)(2,1)}, u32[]{:S(2)}) copy-start(bf16[180,360]{1,0:T(8,128)(2,1)} %w1.3) | copy-start | bytes 388804
  8.9 3.9 %copy-start.1 = (bf16[360,180]{0,1:T(8,128)(2,1)S(1)}, bf16[360,180]{0,1:T(8,128)(2,1)}, u32[]{:S(2)}) copy-start(bf16[360,180]{0,1:T(8,128)(2,1)} %param.17) | copy-start | bytes 388804
  8.9 3.9 %copy-start.2 = (f32[180]{0:T(256)S(1)}, f32[180]{0:T(256)}, u32[]{:S(2)}) copy-start(f32[180]{0:T(256)} %param.11) | copy-start | bytes 2164
  11.7 6.3 %collective-permute-start.3 = (bf16[16,16,128]{2,1,0:T(8,128)(2,1)S(1)}, bf16[16,16,128]{2,1,0:T(8,128)(2,1)S(1)}, u32[]{:S(2)}, u32[]{:S(2)}) collective-permute-start(bf16[16,16,128]{2,1,0:T(8,128)(2,1)S(1)} %maximum_maximum_fusion.1), channel_id=1, source_target_pairs={{1,0},{2,1},{3,2},{4,3},{5,4},{6,5},{7,6},{0,7},{9,8},{10,9},{11,1... | collective-permute-start | bytes 196616 | tf_op jit(solution)/shard_map/ppermute | solution.py:500
  12.7 5.5 %collective-permute-start.2 = (bf16[16,16,128]{2,1,0:T(8,128)(2,1)S(1)}, bf16[16,16,128]{2,1,0:T(8,128)(2,1)S(1)}, u32[]{:S(2)}, u32[]{:S(2)}) collective-permute-start(bf16[16,16,128]{2,1,0:T(8,128)(2,1)S(1)} %maximum_maximum_fusion), channel_id=1, source_target_pairs={{0,1},{1,2},{2,3},{3,4},{4,5},{5,6},{6,7},{7,0},{8,9},{9,10},{10,1... | collective-permute-start | bytes 196616 | tf_op jit(solution)/shard_map/ppermute | solution.py:499
